TPU v7x, 32 devices: a whole 2x2x4 slice. The times are simulated.
32 devices in a mesh: ctx: 8 (over y, x, core), wt: 4 (over z).
Axes of the slice: x: 2, y: 2, z: 4, core: 2. Of those that a mesh axis runs over, the one named last changes fastest.
Arguments:
- layer_input: bfloat16 [4, 6144, 1024], P('wt', 'ctx'), may hold values from -6 to 6
- attention_gain: bfloat16 [1024], P(('ctx', 'wt')), may hold values from 0.5 to 1.5
- query_weight: bfloat16 [1024, 1024], P(('ctx', 'wt')), may hold values from -0.75 to 0.75
- key_matrix: bfloat16 [1024, 512], P(('ctx', 'wt')), may hold values from -0.75 to 0.75
- value_matrix: bfloat16 [1024, 512], P(('ctx', 'wt')), may hold values from -0.5 to 0.5
- output_weight: bfloat16 [1024, 1024], P(None, ('ctx', 'wt')), may hold values from -1.75 to 1.75
- mixture_gain: bfloat16 [1024], P(('ctx', 'wt')), may hold values from 0.5 to 1.5
- router_weight: bfloat16 [1024, 32], P(('ctx', 'wt')), may hold values from -0.09375 to 0.09375
- gate_weight: bfloat16 [32, 1024, 512], P('wt', 'ctx'), may hold values from -0.375 to 0.375
- up_weight: bfloat16 [32, 1024, 512], P('wt', 'ctx'), may hold values from -0.375 to 0.375
- down_weight: bfloat16 [32, 512, 1024], P('wt', None, 'ctx'), may hold values from -1.5 to 1.5
- expert_routes: int32 [4, 6144, 8], P('wt', 'ctx'), may hold values from 0 to 31, all different within a row; in each aligned block of 768 rows (0 to 767, 768 to 1535, ..., all dimensions but the last counted through in order) at most 336 rows name the same one
- prompt_deal: int32 [4, 16], P('wt'), may hold values from 0 to 15, as said below
- output_grad: bfloat16 [4, 6144, 1024], P('wt', 'ctx'), may hold values from -6 to 6
Outputs:
- layer_output: bfloat16 [4, 6144, 1024], P('wt', 'ctx')
- input_grad: bfloat16 [4, 6144, 1024], P('wt', 'ctx')
- attention_gain_grad: float32 [1024], P(('ctx', 'wt'))
- query_grad: float32 [1024, 1024], P(('ctx', 'wt'))
- key_grad: float32 [1024, 512], P(('ctx', 'wt'))
- value_grad: float32 [1024, 512], P(('ctx', 'wt'))
- output_proj_grad: float32 [1024, 1024], P(None, ('ctx', 'wt'))
- mixture_gain_grad: float32 [1024], P(('ctx', 'wt'))
- router_grad: float32 [1024, 32], P(('ctx', 'wt'))
- gate_grad: float32 [32, 1024, 512], P('wt', 'ctx')
- up_grad: float32 [32, 1024, 512], P('wt', 'ctx')
- down_grad: float32 [32, 512, 1024], P('wt', None, 'ctx')
Inputs may be any that keep to these rules, and one draw needn't show every extreme that they name: `expert_routes`: each token names 8 different experts. In the 768 rows of one device (aligned blocks of the first two dimensions taken together), no expert is named by more than 336 tokens, and in some block one expert is named by exactly 336. `prompt_deal`: each row is a permutation of the prompt's 16 blocks of 128 tokens; entries 2c and 2c + 1 add up to 15.
All inputs are finite; a program needn't handle non-finite values.
Results may differ from a plain program's by a relative error of at most 0.02.
Values may be sent and summed in bfloat16 or wider, within the bound.
A program may use at most 384 MiB of HBM per device.

v0:
```python
import jax
import jax.numpy as jnp
from jax import lax
from jax.sharding import PartitionSpec as P

MODEL_WIDTH = 1024
HQ = 16
KEY_VALUE_HEADS = 8
HEAD_SIZE = 64
EXPERTS = 32
TOP = 8
PROMPT = 2048
CLEN = 256
CONT_DEV = 2
QUERIES_PER_KEY = 2


att_scale = 0.015625
resid_scale = 0.22
norm_eps = 1e-06
rope_base = 10000.0
masked_score = -1e30


def rope_tables(positions):
    middle = HEAD_SIZE // 2
    frequency = jnp.power(
        jnp.float32(rope_base), -2.0 * jnp.arange(middle, dtype=jnp.float32) / HEAD_SIZE
    )
    angles = positions.astype(jnp.float32)[:, None] * frequency[None, :]
    cosine_table = jnp.cos(angles)
    sinusoid_table = jnp.sin(angles)
    return (
        jnp.concatenate([cosine_table, cosine_table], 1),
        jnp.concatenate([sinusoid_table, sinusoid_table], 1),
    )


def apply_turning(values, cosine_table, sinusoid_table, heads, direction):
    shaped = values.reshape(values.shape[0], heads, HEAD_SIZE)
    middle = HEAD_SIZE // 2
    turned = jnp.concatenate([-shaped[..., middle:], shaped[..., :middle]], -1)
    rotated = shaped * cosine_table[:, None, :] + direction * turned * sinusoid_table[:, None, :]
    return rotated.reshape(values.shape)


def norm_forward(values, gain):
    inverse = lax.rsqrt(jnp.mean(values * values, -1, keepdims=True) + norm_eps)
    return (values * inverse * gain, inverse)


def norm_backward(values, inverse, gain, grad_out):
    scaled = gain * grad_out
    gain_grad = jnp.sum(grad_out * values * inverse, 0)
    projection = jnp.mean(scaled * values, -1, keepdims=True)
    return (inverse * scaled - values * inverse * inverse * inverse * projection, gain_grad)


def per_device(
    layer_input,
    attention_gain,
    query_weight,
    key_matrix,
    value_matrix,
    output_weight,
    mixture_gain,
    router_weight,
    gate_weight,
    up_weight,
    down_weight,
    expert_routes,
    prompt_deal,
    output_grad,
):
    tok_rows = layer_input.shape[1]
    prompt_local = tok_rows - CONT_DEV * CLEN
    block_rows = prompt_local // 2
    context_size = lax.axis_size("ctx")
    shard_count = lax.axis_size("wt")
    expert_count = gate_weight.shape[0]
    capacity = 8 * ((tok_rows * TOP * 7 // (4 * EXPERTS) + 7) // 8)
    prompt_total = prompt_local * context_size
    inputs = layer_input[0].astype(jnp.float32)
    routes = expert_routes[0]
    deal_row = prompt_deal[0]
    gathered = (
        lax.all_gather(attention_gain, ("ctx", "wt"), axis=0, tiled=True),
        lax.all_gather(mixture_gain, ("ctx", "wt"), axis=0, tiled=True),
        lax.all_gather(query_weight, ("ctx", "wt"), axis=0, tiled=True),
        lax.all_gather(key_matrix, ("ctx", "wt"), axis=0, tiled=True),
        lax.all_gather(value_matrix, ("ctx", "wt"), axis=0, tiled=True),
        lax.all_gather(router_weight, ("ctx", "wt"), axis=0, tiled=True),
        lax.all_gather(output_weight, ("ctx", "wt"), axis=1, tiled=True),
    )
    first_gain = gathered[0].astype(jnp.float32)
    second_gain = gathered[1].astype(jnp.float32)
    query_full = gathered[2]
    key_full = gathered[3]
    value_full = gathered[4]
    router_full = gathered[5]
    output_full = gathered[6]
    gate_full, up_full, down_full = (
        lax.all_gather(gate_weight, "ctx", axis=1, tiled=True),
        lax.all_gather(up_weight, "ctx", axis=1, tiled=True),
        lax.all_gather(down_weight, "ctx", axis=2, tiled=True),
    )
    normed_float, inverse_one = norm_forward(inputs, first_gain)
    normed_one = normed_float.astype(jnp.bfloat16)
    raw_queries = jnp.dot(normed_one, query_full, preferred_element_type=jnp.float32)
    unrotated_keys = jnp.dot(normed_one, key_full, preferred_element_type=jnp.float32)
    raw_values = jnp.dot(normed_one, value_full, preferred_element_type=jnp.float32)
    local_rows = jnp.arange(tok_rows, dtype=jnp.int32)
    slot_index = jnp.minimum(
        2 * lax.axis_index("ctx") + local_rows // block_rows, 2 * context_size - 1
    )
    prompt_place = deal_row[slot_index] * block_rows + local_rows % block_rows
    positions = jnp.where(
        local_rows < prompt_local, prompt_place, PROMPT + (local_rows - prompt_local) % CLEN
    )
    cosine_table, sinusoid_table = rope_tables(positions)
    turned_query = apply_turning(raw_queries, cosine_table, sinusoid_table, HQ, 1.0).astype(
        jnp.bfloat16
    )
    spun_key = apply_turning(
        unrotated_keys, cosine_table, sinusoid_table, KEY_VALUE_HEADS, 1.0
    ).astype(jnp.bfloat16)
    value_low = raw_values.astype(jnp.bfloat16)
    prompt_keys, prompt_values = (
        lax.all_gather(spun_key[:prompt_local], "ctx", axis=0, tiled=True),
        lax.all_gather(value_low[:prompt_local], "ctx", axis=0, tiled=True),
    )
    all_keys = jnp.concatenate([prompt_keys, spun_key[prompt_local:]], 0)
    all_values = jnp.concatenate([prompt_values, value_low[prompt_local:]], 0)
    gathered_rows = jnp.arange(prompt_total, dtype=jnp.int32)
    key_place = jnp.concatenate(
        [
            deal_row[gathered_rows // block_rows] * block_rows + gathered_rows % block_rows,
            positions[prompt_local:],
        ]
    )
    query_segment = jnp.where(local_rows < prompt_local, -1, (local_rows - prompt_local) // CLEN)
    key_segment = jnp.concatenate(
        [jnp.full((prompt_total,), -1, jnp.int32), query_segment[prompt_local:]]
    )
    allowed = ((key_segment[None, :] == -1) | (key_segment[None, :] == query_segment[:, None])) & (
        key_place[None, :] <= positions[:, None]
    )

    def head_slices(head_group):
        query_part = lax.dynamic_slice_in_dim(
            turned_query, head_group * QUERIES_PER_KEY * HEAD_SIZE, QUERIES_PER_KEY * HEAD_SIZE, 1
        ).reshape(tok_rows, QUERIES_PER_KEY, HEAD_SIZE)
        key_part = lax.dynamic_slice_in_dim(all_keys, head_group * HEAD_SIZE, HEAD_SIZE, 1)
        value_part = lax.dynamic_slice_in_dim(all_values, head_group * HEAD_SIZE, HEAD_SIZE, 1)
        scores = att_scale * jnp.einsum(
            "trd,kd->rtk", query_part, key_part, preferred_element_type=jnp.float32
        )
        return (query_part, key_part, value_part, jnp.where(allowed[None], scores, masked_score))

    def head_ahead_step(head_group):
        query_part, key_part, value_part, scores = head_slices(head_group)
        row_max = jnp.max(scores, -1, keepdims=True)
        exponent = jnp.exp(scores - row_max)
        row_total = jnp.sum(exponent, -1, keepdims=True)
        weights_low = (exponent / row_total).astype(jnp.bfloat16)
        attended = jnp.einsum(
            "rtk,kd->trd", weights_low, value_part, preferred_element_type=jnp.float32
        )
        return (attended.astype(jnp.bfloat16), row_max + jnp.log(row_total))

    per_head_outputs, logarithm_totals = lax.map(
        head_ahead_step, jnp.arange(KEY_VALUE_HEADS, dtype=jnp.int32)
    )
    attended_low = jnp.transpose(per_head_outputs, (1, 0, 2, 3)).reshape(tok_rows, HQ * HEAD_SIZE)
    branch = jnp.dot(attended_low, output_full, preferred_element_type=jnp.float32)
    middle = inputs + resid_scale * branch
    normed_mid, inverse_two = norm_forward(middle, second_gain)
    normed_two = normed_mid.astype(jnp.bfloat16)
    logits = jnp.dot(normed_two, router_full, preferred_element_type=jnp.float32)
    chosen = jnp.take_along_axis(logits, routes, 1)
    chosen_exp = jnp.exp(chosen - jnp.max(chosen, -1, keepdims=True))
    gates = chosen_exp / jnp.sum(chosen_exp, -1, keepdims=True)
    pairs = routes.reshape(-1)
    selection = (pairs[:, None] == jnp.arange(EXPERTS, dtype=jnp.int32)[None, :]).astype(jnp.int32)
    slot_numbers = jnp.sum((jnp.cumsum(selection, 0) - selection) * selection, 1)
    buffer_row = pairs * capacity + slot_numbers
    token_index = jnp.arange(tok_rows * TOP, dtype=jnp.int32) // TOP
    outgoing = (
        jnp.zeros((EXPERTS * capacity, MODEL_WIDTH), jnp.bfloat16)
        .at[buffer_row]
        .set(normed_two[token_index])
    )
    received = lax.all_to_all(
        outgoing.reshape(shard_count, expert_count, capacity, MODEL_WIDTH),
        "wt",
        split_axis=0,
        concat_axis=0,
        tiled=True,
    )
    gate_part = jnp.einsum(
        "sjcd,jdf->sjcf", received, gate_full, preferred_element_type=jnp.float32
    )
    up_part = jnp.einsum("sjcd,jdf->sjcf", received, up_full, preferred_element_type=jnp.float32)
    activated = (jax.nn.silu(gate_part) * up_part).astype(jnp.bfloat16)
    expert_out = jnp.einsum(
        "sjcf,jfd->sjcd", activated, down_full, preferred_element_type=jnp.float32
    ).astype(jnp.bfloat16)
    returned = lax.all_to_all(expert_out, "wt", split_axis=0, concat_axis=0, tiled=True).reshape(
        EXPERTS * capacity, MODEL_WIDTH
    )
    picked = returned[buffer_row].reshape(tok_rows, TOP, MODEL_WIDTH).astype(jnp.float32)
    mixture = jnp.sum(gates[:, :, None] * picked, 1)
    layer_output = (middle + resid_scale * mixture).astype(jnp.bfloat16)
    out_grad = output_grad[0].astype(jnp.float32)
    grad_mixture = resid_scale * out_grad
    grad_gates = jnp.sum(grad_mixture[:, None, :] * picked, -1)
    grad_chosen = gates * (grad_gates - jnp.sum(gates * grad_gates, -1, keepdims=True))
    grad_pick = (
        (gates[:, :, None] * grad_mixture[:, None, :])
        .astype(jnp.bfloat16)
        .reshape(tok_rows * TOP, MODEL_WIDTH)
    )
    outgoing_grad = (
        jnp.zeros((EXPERTS * capacity, MODEL_WIDTH), jnp.bfloat16).at[buffer_row].set(grad_pick)
    )
    grad_expert_out = lax.all_to_all(
        outgoing_grad.reshape(shard_count, expert_count, capacity, MODEL_WIDTH),
        "wt",
        split_axis=0,
        concat_axis=0,
        tiled=True,
    )
    grad_down = jnp.einsum(
        "sjcf,sjcd->jfd", activated, grad_expert_out, preferred_element_type=jnp.float32
    )
    grad_activated = jnp.einsum(
        "sjcd,jfd->sjcf", grad_expert_out, down_full, preferred_element_type=jnp.float32
    )
    sigmoid_part = jax.nn.sigmoid(gate_part)
    grad_gate_part = (
        grad_activated * up_part * sigmoid_part * (1.0 + gate_part * (1.0 - sigmoid_part))
    ).astype(jnp.bfloat16)
    grad_up_part = (grad_activated * gate_part * sigmoid_part).astype(jnp.bfloat16)
    grad_gate = jnp.einsum(
        "sjcd,sjcf->jdf", received, grad_gate_part, preferred_element_type=jnp.float32
    )
    grad_up = jnp.einsum(
        "sjcd,sjcf->jdf", received, grad_up_part, preferred_element_type=jnp.float32
    )
    grad_received = jnp.einsum(
        "sjcf,jdf->sjcd", grad_gate_part, gate_full, preferred_element_type=jnp.float32
    )
    grad_received = (
        grad_received
        + jnp.einsum("sjcf,jdf->sjcd", grad_up_part, up_full, preferred_element_type=jnp.float32)
    ).astype(jnp.bfloat16)
    grad_returned = lax.all_to_all(
        grad_received, "wt", split_axis=0, concat_axis=0, tiled=True
    ).reshape(EXPERTS * capacity, MODEL_WIDTH)
    gate_share, up_share, down_share = (
        lax.psum_scatter(
            grad_gate.astype(jnp.bfloat16), "ctx", scatter_dimension=1, tiled=True
        ).astype(jnp.float32),
        lax.psum_scatter(
            grad_up.astype(jnp.bfloat16), "ctx", scatter_dimension=1, tiled=True
        ).astype(jnp.float32),
        lax.psum_scatter(
            grad_down.astype(jnp.bfloat16), "ctx", scatter_dimension=2, tiled=True
        ).astype(jnp.float32),
    )
    grad_logits = jnp.sum(
        grad_chosen[:, :, None] * selection.reshape(tok_rows, TOP, EXPERTS).astype(jnp.float32), 1
    ).astype(jnp.bfloat16)
    router_share = jnp.einsum(
        "td,te->de", normed_two, grad_logits, preferred_element_type=jnp.float32
    )
    grad_normed_two = jnp.sum(
        grad_returned[buffer_row].reshape(tok_rows, TOP, MODEL_WIDTH).astype(jnp.float32), 1
    )
    grad_normed_two = grad_normed_two + jnp.einsum(
        "te,de->td", grad_logits, router_full, preferred_element_type=jnp.float32
    )
    grad_mid_norm, second_gain_grad = norm_backward(
        middle, inverse_two, second_gain, grad_normed_two
    )
    grad_middle = out_grad + grad_mid_norm
    grad_branch = (resid_scale * grad_middle).astype(jnp.bfloat16)
    output_share = jnp.einsum(
        "tf,td->fd", attended_low, grad_branch, preferred_element_type=jnp.float32
    )
    grad_attended = jnp.einsum(
        "td,fd->tf", grad_branch, output_full, preferred_element_type=jnp.float32
    ).astype(jnp.bfloat16)

    def head_reverse_step(packed):
        head_group, log_sum = packed
        query_part, key_part, value_part, scores = head_slices(head_group)
        grad_part = lax.dynamic_slice_in_dim(
            grad_attended, head_group * QUERIES_PER_KEY * HEAD_SIZE, QUERIES_PER_KEY * HEAD_SIZE, 1
        ).reshape(tok_rows, QUERIES_PER_KEY, HEAD_SIZE)
        chance = jnp.exp(scores - log_sum)
        grad_chance = jnp.einsum(
            "trd,kd->rtk", grad_part, value_part, preferred_element_type=jnp.float32
        )
        centre = jnp.sum(chance * grad_chance, -1, keepdims=True)
        grad_scores = (chance * (grad_chance - centre)).astype(jnp.bfloat16)
        grad_query = att_scale * jnp.einsum(
            "rtk,kd->trd", grad_scores, key_part, preferred_element_type=jnp.float32
        )
        grad_key = att_scale * jnp.einsum(
            "rtk,trd->kd", grad_scores, query_part, preferred_element_type=jnp.float32
        )
        grad_value = jnp.einsum(
            "rtk,trd->kd",
            chance.astype(jnp.bfloat16),
            grad_part,
            preferred_element_type=jnp.float32,
        )
        return (grad_query, grad_key, grad_value)

    head_queries, per_head_keys, per_head_values = lax.map(
        head_reverse_step, (jnp.arange(KEY_VALUE_HEADS, dtype=jnp.int32), logarithm_totals)
    )
    query_all_grad = jnp.transpose(head_queries, (1, 0, 2, 3)).reshape(tok_rows, HQ * HEAD_SIZE)
    key_total_gradient = jnp.transpose(per_head_keys, (1, 0, 2)).reshape(
        -1, KEY_VALUE_HEADS * HEAD_SIZE
    )
    value_total_gradient = jnp.transpose(per_head_values, (1, 0, 2)).reshape(
        -1, KEY_VALUE_HEADS * HEAD_SIZE
    )
    owned_key, owned_value = (
        lax.psum_scatter(
            key_total_gradient[:prompt_total].astype(jnp.bfloat16),
            "ctx",
            scatter_dimension=0,
            tiled=True,
        ).astype(jnp.float32),
        lax.psum_scatter(
            value_total_gradient[:prompt_total].astype(jnp.bfloat16),
            "ctx",
            scatter_dimension=0,
            tiled=True,
        ).astype(jnp.float32),
    )
    key_resident = jnp.concatenate([owned_key, key_total_gradient[prompt_total:]], 0)
    value_local = jnp.concatenate([owned_value, value_total_gradient[prompt_total:]], 0)
    grad_query_low = apply_turning(query_all_grad, cosine_table, sinusoid_table, HQ, -1.0).astype(
        jnp.bfloat16
    )
    key_gradient_narrow = apply_turning(
        key_resident, cosine_table, sinusoid_table, KEY_VALUE_HEADS, -1.0
    ).astype(jnp.bfloat16)
    grad_value_low = value_local.astype(jnp.bfloat16)
    query_share = jnp.einsum(
        "td,tf->df", normed_one, grad_query_low, preferred_element_type=jnp.float32
    )
    key_share = jnp.einsum(
        "td,tf->df", normed_one, key_gradient_narrow, preferred_element_type=jnp.float32
    )
    value_share = jnp.einsum(
        "td,tf->df", normed_one, grad_value_low, preferred_element_type=jnp.float32
    )
    grad_normed_one = jnp.einsum(
        "tf,df->td", grad_query_low, query_full, preferred_element_type=jnp.float32
    )
    grad_normed_one = grad_normed_one + jnp.einsum(
        "tf,df->td", key_gradient_narrow, key_full, preferred_element_type=jnp.float32
    )
    grad_normed_one = grad_normed_one + jnp.einsum(
        "tf,df->td", grad_value_low, value_full, preferred_element_type=jnp.float32
    )
    grad_input_norm, first_gain_grad = norm_backward(
        inputs, inverse_one, first_gain, grad_normed_one
    )
    input_grad = (grad_middle + grad_input_norm).astype(jnp.bfloat16)
    summed = (
        lax.psum_scatter(first_gain_grad, ("ctx", "wt"), scatter_dimension=0, tiled=True),
        lax.psum_scatter(second_gain_grad, ("ctx", "wt"), scatter_dimension=0, tiled=True),
        lax.psum_scatter(query_share, ("ctx", "wt"), scatter_dimension=0, tiled=True),
        lax.psum_scatter(key_share, ("ctx", "wt"), scatter_dimension=0, tiled=True),
        lax.psum_scatter(value_share, ("ctx", "wt"), scatter_dimension=0, tiled=True),
        lax.psum_scatter(router_share, ("ctx", "wt"), scatter_dimension=0, tiled=True),
        lax.psum_scatter(output_share, ("ctx", "wt"), scatter_dimension=1, tiled=True),
    )
    return (
        layer_output[None],
        input_grad[None],
        summed[0],
        summed[2],
        summed[3],
        summed[4],
        summed[6],
        summed[1],
        summed[5],
        gate_share,
        up_share,
        down_share,
    )


def solution(mesh):
    return jax.shard_map(
        per_device,
        mesh=mesh,
        in_specs=(
            P("wt", "ctx", None),
            P(("ctx", "wt")),
            P(("ctx", "wt"), None),
            P(("ctx", "wt"), None),
            P(("ctx", "wt"), None),
            P(None, ("ctx", "wt")),
            P(("ctx", "wt")),
            P(("ctx", "wt"), None),
            P("wt", "ctx", None),
            P("wt", "ctx", None),
            P("wt", None, "ctx"),
            P("wt", "ctx", None),
            P("wt", None),
            P("wt", "ctx", None),
        ),
        out_specs=(
            P("wt", "ctx", None),
            P("wt", "ctx", None),
            P(("ctx", "wt")),
            P(("ctx", "wt"), None),
            P(("ctx", "wt"), None),
            P(("ctx", "wt"), None),
            P(None, ("ctx", "wt")),
            P(("ctx", "wt")),
            P(("ctx", "wt"), None),
            P("wt", "ctx", None),
            P("wt", "ctx", None),
            P("wt", None, "ctx"),
        ),
        check_vma=False,
    )
```

profile of v0, /device:TPU:0, one launch (start us, length us, event | category | flops | bytes accessed | tf_op | source)
XLA Modules:
  0.0 4091.9 jit_solution(9333301279424212456)
XLA Ops:
  11.1 42.0 %all-reduce.6 = (bf16[1024]{0:T(1024)(128)(2,1)S(1)}, bf16[1024]{0:T(1024)(128)(2,1)S(1)}) all-reduce(bf16[1024]{0:T(1024)(128)(2,1)S(1)} %dynamic-update-slice, bf16[1024]{0:T(1024)(128)(2,1)S(1)} %dynamic-update-slice.1), channel_id=1, replica_groups=mesh['ctx'=8,'wt'=4] {'ctx','wt'}, use_global_device_ids=true, to_apply=%add.1 | all-reduce | flops 2048 | bytes 8192
  84.2 39.1 all-gather.14.cloned.1.call-done
  244.2 164.6 %while.32 = (s32[]{:T(128)}, bf16[8,768,2,64]{1,3,2,0:T(8,128)(2,1)}, f32[8,2,768,1]{2,1,3,0:T(2,128)}, s32[8]{0:T(128)S(1)}, bf16[2560,512]{0,1:T(8,128)(2,1)},...) while((s32[]{:T(128)}, ...), condition=%wide.region_4.5_spmd.clone, body=%wide.region_1.4_spmd.clone.sunk | while | flops 1061779968 | bytes 56571672 | solution.py:171
  415.2 84.1 %scatter_custom_fusion = bf16[10752,1024]{1,0:T(8,128)(2,1)} fusion(s32[6144]{0:T(1024)} %bitcast.471, bf16[768,1024]{1,0:T(8,128)(2,1)S(1)} %multiply_convert_fusion.1, s32[6144]{0:T(1024)} %broadcast_clamp_fusion.1, bf16[]{:T(256)} %constant.268.clone.1), kind=kCustom, calls=%fused_computation.100 | custom fusion | bytes 22020608 | tf_op jit(solution)/shard_map/scatter | solution.py:191
  508.4 534.1 %all_gather.44 = bf16[1024,32]{1,0:T(8,128)(2,1)S(1)} all-gather(bf16[32,32]{1,0:T(8,128)(2,1)S(1)} %copy-done.72), channel_id=1, replica_groups=mesh['ctx'=8,'wt'=4] {'ctx','wt'}, dimensions={0}, use_global_device_ids=true | all-gather | bytes 67584 | tf_op jit(solution)/shard_map/all_gather | solution.py:92
  1047.6 49.5 %gather_fusion.2 = f32[6144]{0:T(1024)S(1)} fusion(f32[768,32]{0,1:T(8,128)S(1)} %fusion.190, s32[6144]{0:T(1024)S(1)} %reshape.764), kind=kCustom, calls=%fused_computation.3 | custom fusion | bytes 98304 | tf_op jit(solution)/shard_map/jit(take_along_axis)/gather | solution.py:180
  1105.1 42.7 %scatter_custom_fusion.1 = bf16[10752,1024]{1,0:T(8,128)(2,1)} fusion(s32[6144]{0:T(1024)} %bitcast.472, f32[768,1024]{1,0:T(8,128)S(1)} %convert_multiply_fusion.2, f32[6144]{0:T(1024)S(1)} %exponential_divide_fusion, bf16[]{:T(256)} %constant.268.clone.1), kind=kCustom, calls=%fused_computation.99 | custom fusion | flops 12582912 | bytes 25190912 | tf_op jit(solution)/shard_map/scatter | solution.py:224
  1237.1 33.6 all-gather.26.cloned.1.call-done
  1270.7 355.6 %all-to-all-done.2 = bf16[4,8,336,1024]{3,2,1,0:T(8,128)(2,1)} async-done(((bf16[4,8,336,1024]{3,2,1,0:T(8,128)(2,1)}), bf16[4,8,336,1024]{3,2,1,0:T(8,128)(2,1)}, u32[]{:S(2)}, u32[]{:S(2)}) %all-to-all-start.2) | async-done | bytes 22020128 | tf_op jit(solution)/shard_map/all_to_all | solution.py:226
  1626.4 37.7 fusion.55
  1783.6 402.5 %all-to-all-done.1 = bf16[4,8,336,1024]{3,2,1,0:T(8,128)(2,1)} async-done(((bf16[4,8,336,1024]{3,2,1,0:T(8,128)(2,1)}), bf16[4,8,336,1024]{3,2,1,0:T(8,128)(2,1)}, u32[]{:S(2)}, u32[]{:S(2)}) %all-to-all-start.1) | async-done | bytes 22020128 | tf_op jit(solution)/shard_map/all_to_all | solution.py:208
  2195.1 42.0 %gather_fusion = bf16[6144,1024]{1,0:T(8,128)(2,1)} fusion(bf16[10752,1024]{1,0:T(8,128)(2,1)} %bitcast.45, s32[6144]{0:T(1024)} %broadcast_clamp_fusion), kind=kCustom, calls=%fused_computation.1 | custom fusion | bytes 25190400 | tf_op jit(solution)/shard_map/gather | solution.py:211
  2251.4 417.4 %all-to-all-done.3 = bf16[4,8,336,1024]{3,2,1,0:T(8,128)(2,1)} async-done(((bf16[4,8,336,1024]{3,2,1,0:T(8,128)(2,1)}), bf16[4,8,336,1024]{3,2,1,0:T(8,128)(2,1)}, u32[]{:S(2)}, u32[]{:S(2)}) %all-to-all-start.3) | async-done | bytes 22020128 | tf_op jit(solution)/shard_map/all_to_all | solution.py:257
  2668.7 41.6 %gather_fusion.1 = bf16[6144,1024]{1,0:T(8,128)(2,1)} fusion(bf16[10752,1024]{1,0:T(8,128)(2,1)} %bitcast.57, s32[6144]{0:T(1024)} %broadcast_clamp_fusion), kind=kCustom, calls=%fused_computation.2 | custom fusion | bytes 25190400 | tf_op jit(solution)/shard_map/gather | solution.py:278
  2728.6 333.3 %while.33 = (s32[]{:T(128)}, f32[8,768,2,64]{1,3,2,0:T(8,128)}, f32[8,2560,64]{1,2,0:T(8,128)}, bf16[8,2560,64]{1,2,0:T(8,128)(2,1)}, s32[8]{0:T(128)S(1)}, /*in...) while((s32[]{:T(128)}, f32[8,768,2,64]{1,3,2,0:T(8,128)}, ...), condition=%wide.region_21.22_spmd.clone, body=%wide.region_19.21_spmd.clone.sunk | while | flops 2560096768 | bytes 128971160 | solution.py:321
  3190.1 34.3 reduce-scatter.31.cloned.1.call-done
  3232.3 67.2 %reduce-scatter.27.cloned.1.call-done = bf16[8,128,512]{2,1,0:T(8,128)(2,1)} async-done(((bf16[8,1024,512]{2,1,0:T(8,128)(2,1)}), bf16[8,128,512]{2,1,0:T(8,128)(2,1)}) %reduce-scatter.27.cloned.1.call-update) | async-done | bytes 1048592 | tf_op jit(solution)/shard_map/reduce_scatter | solution.py:261
  3302.4 71.8 %reduce-scatter.29.cloned.1.call-done = bf16[8,128,512]{2,1,0:T(8,128)(2,1)} async-done(((bf16[8,1024,512]{2,1,0:T(8,128)(2,1)}), bf16[8,128,512]{2,1,0:T(8,128)(2,1)}) %reduce-scatter.29.cloned.1.call-update) | async-done | bytes 1048592 | tf_op jit(solution)/shard_map/reduce_scatter | solution.py:264
  3387.1 39.4 all-reduce.5
  3432.7 78.4 %reduce-scatter.25.cloned.1.call-done = f32[32,32]{1,0:T(8,128)} async-done(((f32[1024,32]{1,0:T(8,128)}), f32[32,32]{1,0:T(8,128)}) %reduce-scatter.25.cloned.1.call-update) | async-done | bytes 4112 | tf_op jit(solution)/shard_map/reduce_scatter | solution.py:382
  3511.1 137.6 %reduce-scatter.21.cloned.1.call-done = f32[32,512]{1,0:T(8,128)} async-done(((f32[1024,512]{1,0:T(8,128)}), f32[32,512]{1,0:T(8,128)}) %reduce-scatter.21.cloned.1.call-update) | async-done | bytes 65552 | tf_op jit(solution)/shard_map/reduce_scatter | solution.py:381
  3648.7 138.9 %reduce-scatter.19.cloned.1.call-done = f32[32,512]{1,0:T(8,128)} async-done(((f32[1024,512]{1,0:T(8,128)}), f32[32,512]{1,0:T(8,128)}) %reduce-scatter.19.cloned.1.call-update) | async-done | bytes 65552 | tf_op jit(solution)/shard_map/reduce_scatter | solution.py:380
  3787.6 148.0 %reduce-scatter.17.cloned.1.call-done = f32[32,1024]{1,0:T(8,128)} async-done(((f32[1024,1024]{1,0:T(8,128)}), f32[32,1024]{1,0:T(8,128)}) %reduce-scatter.17.cloned.1.call-update) | async-done | bytes 131088 | tf_op jit(solution)/shard_map/reduce_scatter | solution.py:379
  3935.6 149.4 %reduce-scatter.23.cloned.1.call-done = f32[1024,32]{0,1:T(8,128)} async-done(((f32[1024,1024]{0,1:T(8,128)}), f32[1024,32]{0,1:T(8,128)}) %reduce-scatter.23.cloned.1.call-update) | async-done | bytes 131088 | tf_op jit(solution)/shard_map/reduce_scatter | solution.py:383
  (540 shorter events, 1067.0 us)
Async XLA Ops:
  7.2 60.4 %all-gather.10.cloned.1.call-start = ((), (), s32[]{:S(2)}) async-start(), calls=%async_computation.14 | async-start | bytes 1081344 | tf_op jit(solution)/shard_map/all_gather | solution.py:91
  7.9 115.4 %all-gather.14.cloned.1.call-start = ((), (), s32[]{:S(2)}) async-start(), calls=%async_computation.16 | async-start | bytes 1081344 | tf_op jit(solution)/shard_map/all_gather | solution.py:90
  8.7 173.2 %all-gather.18.cloned.1.call-start = ((), (), s32[]{:S(2)}) async-start(), calls=%async_computation.18 | async-start | bytes 2162688 | tf_op jit(solution)/shard_map/all_gather | solution.py:89
  9.4 201.5 %all-gather.12.cloned.1.call-start = ((), (), s32[]{:S(2)}) async-start(), calls=%async_computation.15 | async-start | bytes 2359296 | tf_op jit(solution)/shard_map/all_gather | solution.py:130
  71.9 169.0 %all-gather.16.cloned.1.call-start = ((), (), s32[]{:S(2)}) async-start(), calls=%async_computation.17 | async-start | bytes 2359296 | tf_op jit(solution)/shard_map/all_gather | solution.py:129
  130.0 278.9 %all-gather.20.cloned.1.call-start = ((), (), s32[]{:S(2)}) async-start(), calls=%async_computation.19 | async-start | bytes 2162688 | tf_op jit(solution)/shard_map/all_gather | solution.py:93
  499.2 648.5 %all-to-all-start = ((bf16[4,8,336,1024]{3,2,1,0:T(8,128)(2,1)}), bf16[4,8,336,1024]{3,2,1,0:T(8,128)(2,1)}, u32[]{:S(2)}, u32[]{:S(2)}) async-start(bf16[4,8,336,1024]{3,2,1,0:T(8,128)(2,1)} %bitcast.437), calls=%async_computation | async-start | bytes 44040192 | tf_op jit(solution)/shard_map/all_to_all | solution.py:193
  507.3 649.9 %all-gather.24.cloned.1.call-start = ((), (), s32[]{:S(2)}) async-start(), calls=%async_computation.21 | async-start | bytes 9437184 | tf_op jit(solution)/shard_map/all_gather | solution.py:104
  1147.8 478.6 %all-to-all-start.2 = ((bf16[4,8,336,1024]{3,2,1,0:T(8,128)(2,1)}), bf16[4,8,336,1024]{3,2,1,0:T(8,128)(2,1)}, u32[]{:S(2)}, u32[]{:S(2)}) async-start(bf16[4,8,336,1024]{3,2,1,0:T(8,128)(2,1)} %bitcast.438), calls=%async_computation.2 | async-start | bytes 44040192 | tf_op jit(solution)/shard_map/all_to_all | solution.py:226
  1155.6 57.2 %all-gather.22.cloned.1.call-start = ((), (), s32[]{:S(2)}) async-start(), calls=%async_computation.20 | async-start | bytes 9437184 | tf_op jit(solution)/shard_map/all_gather | solution.py:103
  1156.4 114.3 %all-gather.26.cloned.1.call-start = ((), (), s32[]{:S(2)}) async-start(), calls=%async_computation.22 | async-start | bytes 9437184 | tf_op jit(solution)/shard_map/all_gather | solution.py:105
  1703.5 482.6 %all-to-all-start.1 = ((bf16[4,8,336,1024]{3,2,1,0:T(8,128)(2,1)}), bf16[4,8,336,1024]{3,2,1,0:T(8,128)(2,1)}, u32[]{:S(2)}, u32[]{:S(2)}) async-start(bf16[4,8,336,1024]{3,2,1,0:T(8,128)(2,1)} %copy.92), calls=%async_computation.1 | async-start | bytes 44040192 | tf_op jit(solution)/shard_map/all_to_all | solution.py:208
  1783.6 411.2 %copy-start.60 = (f32[768]{0:T(1024)S(1)}, f32[768]{0:T(1024)}, u32[]{:S(2)}) copy-start(f32[768]{0:T(1024)} %copy-done.59) | copy-start | bytes 9220
  2186.1 482.6 %all-to-all-start.3 = ((bf16[4,8,336,1024]{3,2,1,0:T(8,128)(2,1)}), bf16[4,8,336,1024]{3,2,1,0:T(8,128)(2,1)}, u32[]{:S(2)}, u32[]{:S(2)}) async-start(bf16[4,8,336,1024]{3,2,1,0:T(8,128)(2,1)} %copy.94), calls=%async_computation.3 | async-start | bytes 44040192 | tf_op jit(solution)/shard_map/all_to_all | solution.py:257
  2194.1 969.4 %reduce-scatter.15.cloned.1.call-start = ((), (), s32[]{:S(2)}) async-start(), calls=%async_computation.24 | async-start | bytes 2359296 | tf_op jit(solution)/shard_map/reduce_scatter | solution.py:338
  3065.1 104.0 %reduce-scatter.13.cloned.1.call-start = ((), (), s32[]{:S(2)}) async-start(), calls=%async_computation.23 | async-start | bytes 2359296 | tf_op jit(solution)/shard_map/reduce_scatter | solution.py:332
  3069.0 155.4 %reduce-scatter.31.cloned.1.call-start = ((), (), s32[]{:S(2)}) async-start(), calls=%async_computation.32 | async-start | bytes 9437184
  3116.5 183.0 %reduce-scatter.27.cloned.1.call-start = ((), (), s32[]{:S(2)}) async-start(), calls=%async_computation.30 | async-start | bytes 9437184 | tf_op jit(solution)/shard_map/reduce_scatter | solution.py:261
  3138.5 235.7 %reduce-scatter.29.cloned.1.call-start = ((), (), s32[]{:S(2)}) async-start(), calls=%async_computation.31 | async-start | bytes 9437184 | tf_op jit(solution)/shard_map/reduce_scatter | solution.py:264
  3159.8 351.3 %reduce-scatter.25.cloned.1.call-start = ((), (), s32[]{:S(2)}) async-start(), calls=%async_computation.29 | async-start | bytes 540672 | tf_op jit(solution)/shard_map/reduce_scatter | solution.py:382
  3163.4 485.3 %reduce-scatter.21.cloned.1.call-start = ((), (), s32[]{:S(2)}) async-start(), calls=%async_computation.27 | async-start | bytes 2162688 | tf_op jit(solution)/shard_map/reduce_scatter | solution.py:381
  3167.3 620.2 %reduce-scatter.19.cloned.1.call-start = ((), (), s32[]{:S(2)}) async-start(), calls=%async_computation.26 | async-start | bytes 2162688 | tf_op jit(solution)/shard_map/reduce_scatter | solution.py:380
  3174.9 760.6 %reduce-scatter.17.cloned.1.call-start = ((), (), s32[]{:S(2)}) async-start(), calls=%async_computation.25 | async-start | bytes 4325376 | tf_op jit(solution)/shard_map/reduce_scatter | solution.py:379
  3183.6 901.4 %reduce-scatter.23.cloned.1.call-start = ((), (), s32[]{:S(2)}) async-start(), calls=%async_computation.28 | async-start | bytes 4325376 | tf_op jit(solution)/shard_map/reduce_scatter | solution.py:383
  (96 other events, 2897.2 us)
Sparse Core Ops, SparseCore 0:
  11.0 56.5 all-gather.9
  70.6 52.7 all-gather.13
  126.3 55.5 all-gather.17
  184.2 26.7 all-gather.11
  212.7 28.1 all-gather.15
  243.7 56.4 all-gather.19
  510.0 54.8 all-gather.23
  1158.4 54.4 all-gather.21
  1214.7 55.9 all-gather.25
  3065.2 38.9 reduce-scatter.14
  3108.5 41.2 reduce-scatter.12
  3153.0 71.2 reduce-scatter.30
  3228.2 71.2 reduce-scatter.26
  3302.9 71.2 reduce-scatter.28
  3376.9 134.1 reduce-scatter.24
  3513.8 134.8 reduce-scatter.20
  3651.5 136.0 reduce-scatter.18
  3790.3 145.2 reduce-scatter.16
  3938.4 146.5 reduce-scatter.22
where the time goes:
time: 4100 us; the launch traced here: 4090 us
  waiting for transfers between devices  2180 us (53%)
  blocking collectives  616 us (15%)
  matrix products  570 us (14%)
  local copies, waits for them, and re-layouts  371 us (9%)
  other arithmetic  281 us (7%)
    all_gather x1, blocking collectives, per_device(): lax.all_gather(router_weight, ('ctx', 'wt'), axis=0, tiled=True)  534 us
    all_to_all x1, waiting for transfers between devices, per_device(): lax.all_to_all(grad_received, 'wt', split_axis=0, concat_axis=0, tiled=True)  417 us
    all_to_all x1, waiting for transfers between devices, per_device(): lax.all_to_all(expert_out, 'wt', split_axis=0, concat_axis=0, tiled=True)  403 us
    all_to_all x1, waiting for transfers between devices, per_device(): lax.all_to_all(outgoing_grad.reshape(shard_count, expert_count, capacity,...  356 us
    reduce_scatter x1, waiting for transfers between devices, per_device(): lax.psum_scatter(output_share, ('ctx', 'wt'), scatter_dimension=1, tiled=...  149 us
    reduce_scatter x1, waiting for transfers between devices, per_device(): lax.psum_scatter(query_share, ('ctx', 'wt'), scatter_dimension=0, tiled=T...  148 us
    reduce_scatter x1, waiting for transfers between devices, per_device(): lax.psum_scatter(key_share, ('ctx', 'wt'), scatter_dimension=0, tiled=True)  139 us
    reduce_scatter x1, waiting for transfers between devices, per_device(): lax.psum_scatter(value_share, ('ctx', 'wt'), scatter_dimension=0, tiled=T...  138 us
  transfers between devices with their start and end apart: 23, of which 18 were waited for; matrix products, arithmetic and copies ran while one was open for 16% of the time, Pallas kernels for 0%

commit v1 on v0

v1 whole, which is shorter than its diff:
```python
import functools

import jax
import jax.numpy as jnp
from jax import lax
from jax.experimental import pallas as pl
from jax.experimental.pallas import tpu as pltpu
from jax.sharding import PartitionSpec as P

MODEL_WIDTH = 1024
HQ = 16
KEY_VALUE_HEADS = 8
HEAD_SIZE = 64
EXPERTS = 32
TOP = 8
PROMPT = 2048
CLEN = 256
CONT_DEV = 2
FF = 512
QTILE = 128
KV_WIDTH = KEY_VALUE_HEADS * HEAD_SIZE
ALL = ("ctx", "wt")

att_scale = 0.015625
resid_scale = 0.22
norm_eps = 1e-06
rope_base = 10000.0
masked_score = -1e30

bf16 = jnp.bfloat16
f32 = jnp.float32
VMEM_LIMIT = 60 * 1024 * 1024

NT = (((1,), (1,)), ((), ()))
TN = (((0,), (0,)), ((), ()))


def dot(a, b):
    return jnp.dot(a, b, preferred_element_type=f32)


def dot_nt(a, b):
    return lax.dot_general(a, b, NT, preferred_element_type=f32)


def dot_tn(a, b):
    return lax.dot_general(a, b, TN, preferred_element_type=f32)


def turn_tile(values, cosine, sine, direction):
    middle = HEAD_SIZE // 2
    first = lax.broadcasted_iota(jnp.int32, values.shape, 1) % HEAD_SIZE < middle
    turned = jnp.where(first, -pltpu.roll(values, 128 - middle, 1), pltpu.roll(values, middle, 1))
    return values * cosine + direction * turned * sine


def project_kernel(places, x_ref, cos_ref, sin_ref, *refs, counts):
    pieces = refs[: len(counts)]
    normed_ref, q_ref, kv_ref, qkv_ref, out_ref, rest_ref, gains_ref = refs[len(counts) :]
    rows = MODEL_WIDTH // sum(counts)
    at = 0
    for piece, count in zip(pieces, counts):
        for i in range(count):
            source = slice(i * rows, (i + 1) * rows)
            target = pl.ds(pl.multiple_of(places[at] * rows, rows), rows)
            qkv_ref[target, :] = piece[source, :2048]
            out_ref[target, :] = piece[source, 2048:3072]
            rest_ref[target, :] = piece[source, 3072:]
            at += 1
    gains = rest_ref[...].astype(f32).T[EXPERTS : EXPERTS + 8]
    gains_ref[...] = gains
    x = x_ref[...].astype(f32)
    inverse = lax.rsqrt(jnp.mean(x * x, -1, keepdims=True) + norm_eps)
    normed_ref[...] = (x * inverse * gains[:1]).astype(bf16)
    for c in range(8):
        raw = dot(normed_ref[...], qkv_ref[:, 256 * c : 256 * (c + 1)])
        for h in range(2):
            part = raw[:, 128 * h : 128 * (h + 1)]
            if c < 6:
                part = turn_tile(part, cos_ref[...], sin_ref[...], 1.0)
            column = 256 * c + 128 * h
            if column < 1024:
                q_ref[:, column : column + 128] = part.astype(bf16)
            else:
                kv_ref[:, column - 1024 : column - 896] = part.astype(bf16)


def project(x, cosine, sine, pieces, counts, places):
    tok = x.shape[0]
    shape = jax.ShapeDtypeStruct
    whole = pl.BlockSpec(memory_space=pltpu.VMEM)
    return pl.pallas_call(
        functools.partial(project_kernel, counts=counts),
        in_specs=[pl.BlockSpec(memory_space=pltpu.SMEM)] + [whole] * (3 + len(pieces)),
        out_specs=[whole] * 7,
        out_shape=[
            shape((tok, MODEL_WIDTH), bf16),
            shape((tok, HQ * HEAD_SIZE), bf16),
            shape((tok, 2 * KV_WIDTH), bf16),
            shape((MODEL_WIDTH, 2048), bf16),
            shape((MODEL_WIDTH, 1024), bf16),
            shape((MODEL_WIDTH, 128), bf16),
            shape((8, MODEL_WIDTH), f32),
        ],
        compiler_params=pltpu.CompilerParams(vmem_limit_bytes=VMEM_LIMIT),
        cost_estimate=pl.CostEstimate(
            flops=3_300_000_000, bytes_accessed=22_000_000, transcendentals=0
        ),
        name="project",
    )(places, x, cosine, sine, *pieces)


def outer_kernel(mine, a_ref, b_ref, out_ref):
    out_ref[...] = dot_tn(a_ref[...], b_ref[...]).astype(bf16)


def outer(a, b):
    tok, columns = b.shape
    mine = lax.axis_index("ctx").astype(jnp.int32).reshape(1)
    return pl.pallas_call(
        outer_kernel,
        grid_spec=pltpu.PrefetchScalarGridSpec(
            num_scalar_prefetch=1,
            grid=(8,),
            in_specs=[
                pl.BlockSpec((tok, 128), lambda m, mine: (0, m ^ mine[0])),
                pl.BlockSpec((tok, columns), lambda m, mine: (0, 0)),
            ],
            out_specs=pl.BlockSpec((128, columns), lambda m, mine: (m, 0)),
        ),
        out_shape=jax.ShapeDtypeStruct((MODEL_WIDTH, columns), bf16),
        compiler_params=pltpu.CompilerParams(vmem_limit_bytes=VMEM_LIMIT),
        cost_estimate=pl.CostEstimate(
            flops=2 * tok * MODEL_WIDTH * columns, bytes_accessed=8_000_000, transcendentals=0
        ),
        name="outer",
    )(mine, a, b)


def gather_keys(k_ref, scratch, slots, block_rows):
    for b in range(PROMPT // block_rows):
        start = pl.multiple_of(slots[b] * block_rows, block_rows)
        scratch[b * block_rows : (b + 1) * block_rows, :] = k_ref[pl.ds(start, block_rows), :]


def pair_rows(ref, start, rows, j):
    both = ref[pl.ds(start, rows), 2 * HEAD_SIZE * j : 2 * HEAD_SIZE * (j + 1)]
    return jnp.concatenate([both[:, :HEAD_SIZE], both[:, HEAD_SIZE:]], 0)


def attention_forward_kernel(
    slots, starts, q_ref, k_ref, v_ref, kc_ref, vc_ref, o_ref, lse_ref, k_scr, v_scr, *, block_rows
):
    tok = q_ref.shape[0]
    prompt_local = 2 * block_rows
    gather_keys(k_ref, k_scr, slots, block_rows)
    gather_keys(v_ref, v_scr, slots, block_rows)

    def store(start, rows, j, out, m, total, at):
        out = (out / total).astype(bf16)
        lse = m + jnp.log(total)
        o_ref[pl.ds(start, rows), 2 * HEAD_SIZE * j : 2 * HEAD_SIZE * (j + 1)] = jnp.concatenate(
            [out[:rows], out[rows:]], 1
        )
        row = jnp.broadcast_to(lse, (2 * rows, 128)).T[:1]
        lse_ref[0, 2 * j : 2 * j + 2, pl.ds(at, rows)] = jnp.concatenate(
            [row[:, :rows], row[:, rows:]], 0
        )

    for j in range(2):
        lanes = slice(HEAD_SIZE * j, HEAD_SIZE * (j + 1))

        def tile(i, _):
            start = pl.multiple_of(prompt_local + i * QTILE, 64)
            per = CLEN // QTILE
            seg = pl.multiple_of((i // per) * CLEN, CLEN)
            q = pair_rows(q_ref, start, QTILE, j) * bf16(att_scale)
            s1 = dot_nt(q, k_scr[:, lanes])
            s2 = dot_nt(q, kc_ref[pl.ds(seg, CLEN), lanes])
            place = lax.broadcasted_iota(jnp.int32, s2.shape, 0) % QTILE + (i % per) * QTILE
            s2 = jnp.where(lax.broadcasted_iota(jnp.int32, s2.shape, 1) <= place, s2, masked_score)
            m = jnp.maximum(jnp.max(s1, 1, keepdims=True), jnp.max(s2, 1, keepdims=True))
            e1 = jnp.exp(s1 - m)
            e2 = jnp.exp(s2 - m)
            total = jnp.sum(e1, 1, keepdims=True) + jnp.sum(e2, 1, keepdims=True)
            out = dot(e1.astype(bf16), v_scr[:, lanes])
            out = out + dot(e2.astype(bf16), vc_ref[pl.ds(seg, CLEN), lanes])
            store(start, QTILE, j, out, m, total, pl.multiple_of(i * QTILE, QTILE))
            return 0

        lax.fori_loop(0, CONT_DEV * CLEN // QTILE, tile, 0)

        for half, keys in enumerate((PROMPT // 2, PROMPT)):
            start = pl.multiple_of(starts[half], block_rows)
            q = pair_rows(q_ref, start, block_rows, j) * bf16(att_scale)
            s = dot_nt(q, k_scr[:keys, lanes])
            place = lax.broadcasted_iota(jnp.int32, s.shape, 0) % block_rows + starts[2 + half]
            s = jnp.where(lax.broadcasted_iota(jnp.int32, s.shape, 1) <= place, s, masked_score)
            m = jnp.max(s, 1, keepdims=True)
            e = jnp.exp(s - m)
            total = jnp.sum(e, 1, keepdims=True)
            out = dot(e.astype(bf16), v_scr[:keys, lanes])
            store(
                start, block_rows, j, out, m, total, CONT_DEV * CLEN + half * block_rows
            )


def attention_forward(q, kv, kv_own, slots, starts, block_rows):
    tok = q.shape[0]
    own = kv_own.shape[0]
    pairs = KEY_VALUE_HEADS // 2
    spec = pl.BlockSpec
    return pl.pallas_call(
        functools.partial(attention_forward_kernel, block_rows=block_rows),
        grid_spec=pltpu.PrefetchScalarGridSpec(
            num_scalar_prefetch=2,
            grid=(pairs,),
            in_specs=[
                spec((tok, 4 * HEAD_SIZE), lambda g, *_: (0, g)),
                spec((PROMPT, 2 * HEAD_SIZE), lambda g, *_: (0, g)),
                spec((PROMPT, 2 * HEAD_SIZE), lambda g, *_: (0, pairs + g)),
                spec((own, 2 * HEAD_SIZE), lambda g, *_: (0, g)),
                spec((own, 2 * HEAD_SIZE), lambda g, *_: (0, pairs + g)),
            ],
            out_specs=[
                spec((tok, 4 * HEAD_SIZE), lambda g, *_: (0, g)),
                spec((1, 4, tok), lambda g, *_: (g, 0, 0)),
            ],
            scratch_shapes=[
                pltpu.VMEM((PROMPT, 2 * HEAD_SIZE), bf16),
                pltpu.VMEM((PROMPT, 2 * HEAD_SIZE), bf16),
            ],
        ),
        out_shape=[
            jax.ShapeDtypeStruct((tok, HQ * HEAD_SIZE), bf16),
            jax.ShapeDtypeStruct((pairs, 4, tok), f32),
        ],
        compiler_params=pltpu.CompilerParams(vmem_limit_bytes=VMEM_LIMIT),
        cost_estimate=pl.CostEstimate(
            flops=60_000_000_000, bytes_accessed=12_000_000, transcendentals=25_000_000
        ),
        name="attention_forward",
    )(slots, starts, q, kv, kv, kv_own, kv_own)


def attention_backward_kernel(
    slots,
    starts,
    q_ref,
    do_ref,
    k_ref,
    v_ref,
    kc_ref,
    vc_ref,
    lse_ref,
    o_ref,
    cos_ref,
    sin_ref,
    dq_ref,
    dk_ref,
    dv_ref,
    dkc_ref,
    dvc_ref,
    k_scr,
    v_scr,
    dk_acc,
    dv_acc,
    dq_acc,
    *,
    block_rows,
):
    prompt_local = 2 * block_rows
    gather_keys(k_ref, k_scr, slots, block_rows)
    gather_keys(v_ref, v_scr, slots, block_rows)
    dk_acc[...] = jnp.zeros_like(dk_acc)
    dv_acc[...] = jnp.zeros_like(dv_acc)
    dkc_ref[...] = jnp.zeros_like(dkc_ref)
    dvc_ref[...] = jnp.zeros_like(dvc_ref)

    def row_pair(ref, start, rows, j):
        both = ref[0, 2 * j : 2 * j + 2, pl.ds(start, rows)]
        return jnp.concatenate([both[:1], both[1:]], 1)

    def centre(start, rows, j, d_out):
        product = d_out.astype(f32) * pair_rows(o_ref, start, rows, j).astype(f32)
        ones = jnp.ones((8, HEAD_SIZE), f32)
        return lax.dot_general(
            ones, product, NT, precision=lax.Precision.HIGHEST, preferred_element_type=f32
        )[:1]

    def part(k, v, q, d_out, lse, delta, allowed):
        s = dot_nt(k, q)
        if allowed is not None:
            s = jnp.where(allowed(s.shape), s, masked_score)
        p = jnp.exp(s - lse)
        d_p = dot_nt(v, d_out)
        d_s = (p * (d_p - delta)).astype(bf16)
        return dot_tn(d_s, k), dot(d_s, q), dot(p.astype(bf16), d_out)

    def store(start, rows, j, d_q):
        d_q = d_q * att_scale
        dq_acc[pl.ds(start, rows), 2 * HEAD_SIZE * j : 2 * HEAD_SIZE * (j + 1)] = jnp.concatenate(
            [d_q[:rows], d_q[rows:]], 1
        )

    for j in range(2):
        lanes = slice(HEAD_SIZE * j, HEAD_SIZE * (j + 1))

        def tile(i, _):
            start = pl.multiple_of(prompt_local + i * QTILE, 64)
            per = CLEN // QTILE
            seg = pl.multiple_of((i // per) * CLEN, CLEN)
            own = pl.ds(seg, CLEN)
            q = pair_rows(q_ref, start, QTILE, j) * bf16(att_scale)
            d_out = pair_rows(do_ref, start, QTILE, j)
            lane_start = pl.multiple_of(i * QTILE, QTILE)
            lse = row_pair(lse_ref, lane_start, QTILE, j)
            delta = centre(start, QTILE, j, d_out)

            def allowed(shape):
                place = lax.broadcasted_iota(jnp.int32, shape, 1) % QTILE + (i % per) * QTILE
                return lax.broadcasted_iota(jnp.int32, shape, 0) <= place

            a, b, c = part(k_scr[:, lanes], v_scr[:, lanes], q, d_out, lse, delta, None)
            dk_acc[:, lanes] += b
            dv_acc[:, lanes] += c
            d_q = a
            a, b, c = part(
                kc_ref[own, lanes], vc_ref[own, lanes], q, d_out, lse, delta, allowed
            )
            dkc_ref[own, lanes] += b
            dvc_ref[own, lanes] += c
            store(start, QTILE, j, d_q + a)
            return 0

        lax.fori_loop(0, CONT_DEV * CLEN // QTILE, tile, 0)

        for half, keys in enumerate((PROMPT // 2, PROMPT)):
            start = pl.multiple_of(starts[half], block_rows)
            q = pair_rows(q_ref, start, block_rows, j) * bf16(att_scale)
            d_out = pair_rows(do_ref, start, block_rows, j)
            at = CONT_DEV * CLEN + half * block_rows
            lse = row_pair(lse_ref, at, block_rows, j)
            delta = centre(start, block_rows, j, d_out)

            def allowed(shape):
                place = lax.broadcasted_iota(jnp.int32, shape, 1) % block_rows + starts[2 + half]
                return lax.broadcasted_iota(jnp.int32, shape, 0) <= place

            a, b, c = part(
                k_scr[:keys, lanes], v_scr[:keys, lanes], q, d_out, lse, delta, allowed
            )
            dk_acc[:keys, lanes] += b
            dv_acc[:keys, lanes] += c
            store(start, block_rows, j, a)

    for b in range(PROMPT // block_rows):
        start = pl.multiple_of(slots[b] * block_rows, block_rows)
        rows = slice(b * block_rows, (b + 1) * block_rows)
        dk_ref[pl.ds(start, block_rows), :] = dk_acc[rows, :].astype(bf16)
        dv_ref[pl.ds(start, block_rows), :] = dv_acc[rows, :].astype(bf16)
    for c in range(2):
        lanes = slice(128 * c, 128 * (c + 1))
        dq_ref[:, lanes] = turn_tile(dq_acc[:, lanes], cos_ref[...], sin_ref[...], -1.0).astype(
            bf16
        )


def attention_backward(
    q, d_out, kv, kv_own, lse, attended, cosine, sine, slots, starts, block_rows
):
    tok = q.shape[0]
    own = kv_own.shape[0]
    pairs = KEY_VALUE_HEADS // 2
    spec = pl.BlockSpec
    wide = spec((tok, 4 * HEAD_SIZE), lambda g, *_: (0, g))
    first = spec((PROMPT, 2 * HEAD_SIZE), lambda g, *_: (0, g))
    first_own = spec((own, 2 * HEAD_SIZE), lambda g, *_: (0, g))
    row = spec((1, 4, tok), lambda g, *_: (g, 0, 0))
    table = spec((tok, 128), lambda g, *_: (0, 0))
    return pl.pallas_call(
        functools.partial(attention_backward_kernel, block_rows=block_rows),
        grid_spec=pltpu.PrefetchScalarGridSpec(
            num_scalar_prefetch=2,
            grid=(pairs,),
            in_specs=[
                wide,
                wide,
                first,
                spec((PROMPT, 2 * HEAD_SIZE), lambda g, *_: (0, pairs + g)),
                first_own,
                spec((own, 2 * HEAD_SIZE), lambda g, *_: (0, pairs + g)),
                row,
                wide,
                table,
                table,
            ],
            out_specs=[wide, first, first, first_own, first_own],
            scratch_shapes=[
                pltpu.VMEM((PROMPT, 2 * HEAD_SIZE), bf16),
                pltpu.VMEM((PROMPT, 2 * HEAD_SIZE), bf16),
                pltpu.VMEM((PROMPT, 2 * HEAD_SIZE), f32),
                pltpu.VMEM((PROMPT, 2 * HEAD_SIZE), f32),
                pltpu.VMEM((tok, 4 * HEAD_SIZE), f32),
            ],
        ),
        out_shape=[
            jax.ShapeDtypeStruct((tok, HQ * HEAD_SIZE), bf16),
            jax.ShapeDtypeStruct((PROMPT, KV_WIDTH), bf16),
            jax.ShapeDtypeStruct((PROMPT, KV_WIDTH), bf16),
            jax.ShapeDtypeStruct((own, KV_WIDTH), f32),
            jax.ShapeDtypeStruct((own, KV_WIDTH), f32),
        ],
        compiler_params=pltpu.CompilerParams(vmem_limit_bytes=VMEM_LIMIT),
        cost_estimate=pl.CostEstimate(
            flops=120_000_000_000, bytes_accessed=24_000_000, transcendentals=25_000_000
        ),
        name="attention_backward",
    )(slots, starts, q, d_out, kv, kv, kv_own, kv_own, lse, attended, cosine, sine)


def expert_kernel(
    a2_ref,
    df_ref,
    rank_ref,
    gate_ref,
    wg_ref,
    wu_ref,
    wd_ref,
    mix_ref,
    da_ref,
    dg_ref,
    x_ref,
    dy_ref,
    z_ref,
    dgate_ref,
    dup_ref,
    mix_acc,
    da_acc,
    *,
    capacity,
):
    e = pl.program_id(0)

    @pl.when(e == 0)
    def _():
        mix_acc[...] = jnp.zeros_like(mix_acc)
        da_acc[...] = jnp.zeros_like(da_acc)

    rank = rank_ref[0]
    gates = gate_ref[0]
    tok = rank.shape[1]
    slot = lax.broadcasted_iota(jnp.int32, (capacity, tok), 0).astype(f32)
    hit = slot == rank
    chosen = hit.astype(f32).astype(bf16)
    gate = jnp.sum(jnp.where(hit, gates, 0.0), 1, keepdims=True)
    x = dot(chosen, a2_ref[...]).astype(bf16)
    d_mix = resid_scale * dot(chosen, df_ref[...])
    wg = wg_ref[:, 0].reshape(MODEL_WIDTH, FF)
    wu = wu_ref[:, 0].reshape(MODEL_WIDTH, FF)
    wd = jnp.concatenate([wd_ref[c, 0] for c in range(wd_ref.shape[0])], 1)
    g = dot(x, wg)
    u = dot(x, wu)
    sig = jax.nn.sigmoid(g)
    z = (g * sig * u).astype(bf16)
    y = dot(z, wd).astype(bf16).astype(f32)
    d_gate_value = jnp.sum(d_mix * y, 1, keepdims=True)
    dg_ref[0] = jnp.sum(jnp.where(hit, d_gate_value, 0.0), 0, keepdims=True)
    mix_acc[...] += dot_tn(chosen, (gate * y).astype(bf16))
    d_y = (gate * d_mix).astype(bf16)
    d_z = dot_nt(d_y, wd)
    d_g = (d_z * u * sig * (1.0 + g * (1.0 - sig))).astype(bf16)
    d_u = (d_z * g * sig).astype(bf16)
    d_r = (dot_nt(d_g, wg) + dot_nt(d_u, wu)).astype(bf16)
    da_acc[...] += dot_tn(chosen, d_r)
    x_ref[0] = x
    dy_ref[0] = d_y
    z_ref[0] = z
    dgate_ref[0] = d_g
    dup_ref[0] = d_u

    @pl.when(e == pl.num_programs(0) - 1)
    def _():
        mix_ref[...] = mix_acc[...].astype(bf16)
        da_ref[...] = da_acc[...].astype(bf16)


def expert_pass(a2, df, rank, gates, wg, wu, wd, capacity):
    tok = a2.shape[0]
    parts, experts = wg.shape[0], wg.shape[1]
    spec = pl.BlockSpec
    whole = spec((tok, MODEL_WIDTH), lambda e: (0, 0))
    row = spec((1, 1, tok), lambda e: (e, 0, 0))
    up = spec((parts, 1, MODEL_WIDTH // parts, FF), lambda e: (0, e, 0, 0))
    rows_wide = spec((1, capacity, MODEL_WIDTH), lambda e: (e, 0, 0))
    rows_thin = spec((1, capacity, FF), lambda e: (e, 0, 0))
    shape = jax.ShapeDtypeStruct
    return pl.pallas_call(
        functools.partial(expert_kernel, capacity=capacity),
        grid=(experts,),
        in_specs=[
            whole,
            whole,
            row,
            row,
            up,
            up,
            spec((parts, 1, FF, MODEL_WIDTH // parts), lambda e: (0, e, 0, 0)),
        ],
        out_specs=[whole, whole, row, rows_wide, rows_wide, rows_thin, rows_thin, rows_thin],
        out_shape=[
            shape((tok, MODEL_WIDTH), bf16),
            shape((tok, MODEL_WIDTH), bf16),
            shape((experts, 1, tok), f32),
            shape((experts, capacity, MODEL_WIDTH), bf16),
            shape((experts, capacity, MODEL_WIDTH), bf16),
            shape((experts, capacity, FF), bf16),
            shape((experts, capacity, FF), bf16),
            shape((experts, capacity, FF), bf16),
        ],
        scratch_shapes=[
            pltpu.VMEM((tok, MODEL_WIDTH), f32),
            pltpu.VMEM((tok, MODEL_WIDTH), f32),
        ],
        compiler_params=pltpu.CompilerParams(vmem_limit_bytes=VMEM_LIMIT),
        cost_estimate=pl.CostEstimate(
            flops=35_000_000_000, bytes_accessed=50_000_000, transcendentals=1_500_000
        ),
        name="expert_pass",
    )(a2, df, rank.reshape(experts, 1, tok), gates.reshape(experts, 1, tok), wg, wu, wd)


def weight_grad_kernel(*refs, sources, parts):
    rows = refs[: 5 * sources]
    gate_ref, up_ref, down_ref = refs[5 * sources :]
    width = MODEL_WIDTH // parts

    def add(which, other):
        total = None
        for s in range(sources):
            term = dot_tn(rows[5 * s + which][0], rows[5 * s + other][0])
            total = term if total is None else total + term
        return total

    gate_ref[...] = add(0, 3).astype(bf16).reshape(gate_ref.shape)
    up_ref[...] = add(0, 4).astype(bf16).reshape(up_ref.shape)
    down = add(2, 1).astype(bf16)
    for c in range(parts):
        down_ref[c, 0] = down[:, c * width : (c + 1) * width]


def weight_grads(rows, parts):
    sources = len(rows)
    experts, capacity = rows[0][0].shape[:2]
    spec = pl.BlockSpec
    wide = spec((1, capacity, MODEL_WIDTH), lambda e: (e, 0, 0))
    thin = spec((1, capacity, FF), lambda e: (e, 0, 0))
    up = (parts, experts, MODEL_WIDTH // parts, FF)
    down = (parts, experts, FF, MODEL_WIDTH // parts)
    up_spec = spec((parts, 1) + up[2:], lambda e: (0, e, 0, 0))
    return pl.pallas_call(
        functools.partial(weight_grad_kernel, sources=sources, parts=parts),
        grid=(experts,),
        in_specs=[wide, wide, thin, thin, thin] * sources,
        out_specs=[up_spec, up_spec, spec((parts, 1) + down[2:], lambda e: (0, e, 0, 0))],
        out_shape=[
            jax.ShapeDtypeStruct(up, bf16),
            jax.ShapeDtypeStruct(up, bf16),
            jax.ShapeDtypeStruct(down, bf16),
        ],
        compiler_params=pltpu.CompilerParams(vmem_limit_bytes=VMEM_LIMIT),
        cost_estimate=pl.CostEstimate(
            flops=34_000_000_000, bytes_accessed=100_000_000, transcendentals=0
        ),
        name="weight_grads",
    )(*[a for source in rows for a in source])


def swap(x, mask):
    return lax.ppermute(x, "ctx", [(i, i ^ mask) for i in range(lax.axis_size("ctx"))])


def blocks_ctx(x):
    half = x.shape[0] // 2
    near, far = swap(x, 2), swap(x, 4)
    diagonal = jnp.concatenate([swap(near[:half], 4), swap(far[half:], 2)], 0)
    even = [x, near, far, diagonal]
    odd = [swap(block, 1) for block in even]
    return [b for pair in zip(even, odd) for b in pair]


def gather_ctx(x):
    if lax.axis_size("ctx") != 8:
        return lax.all_gather(x, "ctx", axis=0, tiled=True)
    return jnp.concatenate(blocks_ctx(x), 0)


def scatter_ctx(x):
    if lax.axis_size("ctx") != 8:
        return lax.psum_scatter(x, "ctx", scatter_dimension=0, tiled=True).astype(f32)
    rows = x.shape[0] // 8
    half = rows // 2
    block = [x[m * rows : (m + 1) * rows] for m in range(8)]
    diagonal, near, far, own = (
        block[m].astype(f32) + swap(block[m + 1], 1).astype(f32) for m in (6, 2, 4, 0)
    )
    diagonal = diagonal.astype(bf16)
    near_top = near[:half] + swap(diagonal[:half], 4).astype(f32)
    far_end = far[half:] + swap(diagonal[half:], 2).astype(f32)
    near = jnp.concatenate([near_top.astype(bf16), near[half:].astype(bf16)], 0)
    far = jnp.concatenate([far[:half].astype(bf16), far_end.astype(bf16)], 0)
    return own + swap(near, 2).astype(f32) + swap(far, 4).astype(f32)


def shift(x, distance):
    n = lax.axis_size("wt")
    return lax.ppermute(x, "wt", [(i, (i + distance) % n) for i in range(n)])


def gather_all(x):
    ctx, wt = lax.axis_size("ctx"), lax.axis_size("wt")
    if ctx != 8 or wt != 4:
        return [lax.all_gather(x, ALL, axis=0, tiled=True)], [1], jnp.zeros((1,), jnp.int32)
    ctx_index, wt_index = lax.axis_index("ctx"), lax.axis_index("wt")
    others = jnp.concatenate([shift(x, d) for d in (1, 2, 3)], 0)
    pieces = blocks_ctx(x) + blocks_ctx(others)
    m = jnp.arange(8, dtype=jnp.int32)
    own = (ctx_index ^ m) * wt + wt_index
    d = jnp.arange(1, 4, dtype=jnp.int32)
    rest = ((ctx_index ^ m) * wt)[:, None] + ((wt_index - d) % wt)[None, :]
    places = jnp.concatenate([own, rest.reshape(-1)]).astype(jnp.int32)
    return pieces, [1] * 8 + [3] * 8, places


def outer_sum(a, b):
    ctx, wt = lax.axis_size("ctx"), lax.axis_size("wt")
    if ctx != 8 or wt != 4:
        return lax.psum_scatter(
            dot_tn(a, b).astype(bf16), ALL, scatter_dimension=0, tiled=True
        ).astype(f32)
    part = scatter_ctx(outer(a, b))
    rows = part.shape[0] // wt
    low = part.astype(bf16)
    at = lambda d: ((lax.axis_index("wt") + d) % wt) * rows
    total = lax.dynamic_slice_in_dim(part, at(0), rows, 0)
    for d in range(1, wt):
        total = total + shift(lax.dynamic_slice_in_dim(low, at(d), rows, 0), d).astype(f32)
    return total


def spread_sum(x):
    return jnp.sum(lax.all_to_all(x, ALL, 0, 0, tiled=True), 0)


def after(x, *others):
    return lax.optimization_barrier((x,) + others)[0]


def rope_tables(positions, width):
    middle = HEAD_SIZE // 2
    frequency = jnp.power(
        jnp.float32(rope_base), -2.0 * jnp.arange(middle, dtype=f32) / HEAD_SIZE
    )
    angles = positions.astype(f32)[:, None] * frequency[None, :]
    times = width // middle
    return jnp.tile(jnp.cos(angles), (1, times)), jnp.tile(jnp.sin(angles), (1, times))


def turn(values, cosine, sine, direction):
    middle = HEAD_SIZE // 2
    first = lax.broadcasted_iota(jnp.int32, values.shape, 1) % HEAD_SIZE < middle
    turned = jnp.where(first, -jnp.roll(values, -middle, 1), jnp.roll(values, middle, 1))
    width = values.shape[1]
    return values * cosine[:, :width] + direction * turned * sine[:, :width]


def norm_forward(values, gain):
    inverse = lax.rsqrt(jnp.mean(values * values, -1, keepdims=True) + norm_eps)
    return (values * inverse * gain, inverse)


def norm_backward(values, inverse, gain, grad_out):
    scaled = gain * grad_out
    gain_grad = jnp.sum(grad_out * values * inverse, 0)
    projection = jnp.mean(scaled * values, -1, keepdims=True)
    return (inverse * scaled - values * inverse * inverse * inverse * projection, gain_grad)


def per_device(
    layer_input,
    attention_gain,
    query_weight,
    key_matrix,
    value_matrix,
    output_weight,
    mixture_gain,
    router_weight,
    gate_weight,
    up_weight,
    down_weight,
    expert_routes,
    prompt_deal,
    output_grad,
):
    tok = layer_input.shape[1]
    prompt_local = tok - CONT_DEV * CLEN
    block_rows = prompt_local // 2
    context_size = lax.axis_size("ctx")
    shard_count = lax.axis_size("wt")
    expert_count = gate_weight.shape[0]
    capacity = 8 * ((tok * TOP * 7 // (4 * EXPERTS) + 7) // 8)
    ctx_index = lax.axis_index("ctx")
    wt_index = lax.axis_index("wt")
    inputs = layer_input[0].astype(f32)
    routes = expert_routes[0]
    deal_row = prompt_deal[0]
    out_low = output_grad[0]
    out_grad = out_low.astype(f32)

    own_rows = query_weight.shape[0]
    packed = jnp.concatenate(
        [
            query_weight,
            key_matrix,
            value_matrix,
            output_weight.T,
            router_weight,
            attention_gain[:, None],
            mixture_gain[:, None],
            jnp.zeros((own_rows, 94), bf16),
        ],
        1,
    )
    pieces, counts, block_places = gather_all(packed)

    gate_full = lax.all_gather(gate_weight, "ctx", axis=0, tiled=False)
    up_full = lax.all_gather(up_weight, "ctx", axis=0, tiled=False)
    down_full = lax.all_gather(down_weight, "ctx", axis=0, tiled=False)

    mask = jnp.any(
        routes[:, :, None] == jnp.arange(EXPERTS, dtype=jnp.int32)[None, None, :], 1
    )
    order = jnp.arange(tok, dtype=jnp.int32)
    before = (order[None, :] < order[:, None]).astype(bf16)
    rank = jnp.where(mask, dot(before, mask.astype(bf16)), -1.0)
    ranks = lax.all_to_all(
        rank.T.reshape(shard_count, expert_count, tok), "wt", 0, 0, tiled=True
    )
    grads_in = [out_low] + [shift(out_low, d) for d in range(1, shard_count)]

    local_rows = jnp.arange(tok, dtype=jnp.int32)
    mine = lax.dynamic_slice_in_dim(deal_row, 2 * ctx_index, 2, 0)
    prompt_place = (
        jnp.where(local_rows < block_rows, mine[0], mine[1]) * block_rows
        + local_rows % block_rows
    )
    positions = jnp.where(
        local_rows < prompt_local, prompt_place, PROMPT + (local_rows - prompt_local) % CLEN
    )
    cosine, sine = rope_tables(positions, 128)
    normed_one, turned_query, kv_low, qkv_full, output_t, rest, gain_rows = project(
        layer_input[0], cosine, sine, pieces, counts, block_places
    )
    router_full = rest[:, :EXPERTS]
    first_gain, second_gain = gain_rows[0], gain_rows[1]
    inverse_one = lax.rsqrt(jnp.mean(inputs * inputs, -1, keepdims=True) + norm_eps)
    kv_own = kv_low[prompt_local:]
    kv_all = gather_ctx(kv_low[:prompt_local])

    order = jnp.arange(2 * context_size, dtype=jnp.int32)
    place_of = jnp.sum(jnp.where(deal_row[None, :] == order[:, None], order[None, :], 0), 1)
    if context_size == 8:
        place_of = ((place_of // 2) ^ ctx_index) * 2 + place_of % 2
    low = (mine[0] > mine[1]).astype(jnp.int32)
    starts = jnp.stack(
        [
            low * block_rows,
            (1 - low) * block_rows,
            jnp.min(mine) * block_rows,
            jnp.max(mine) * block_rows,
        ]
    ).astype(jnp.int32)
    attended, lse = attention_forward(turned_query, kv_all, kv_own, place_of, starts, block_rows)

    branch = dot_nt(attended, output_t)
    middle = inputs + resid_scale * branch
    normed_mid, inverse_two = norm_forward(middle, second_gain)
    normed_two = normed_mid.astype(bf16)
    logits = dot(normed_two, router_full)
    top = jnp.max(jnp.where(mask, logits, masked_score), -1, keepdims=True)
    raised = jnp.where(mask, jnp.exp(jnp.where(mask, logits - top, 0.0)), 0.0)
    gates = raised / jnp.sum(raised, -1, keepdims=True)

    gates_out = gates.T.reshape(shard_count, expert_count, tok)
    arrived, gates_in = [normed_two], []
    for d in range(shard_count):
        piece = lax.dynamic_index_in_dim(gates_out, (wt_index + d) % shard_count, 0, False)
        gates_in.append(shift(piece, d) if d else piece)
    sequence = [0, 1, shard_count - 1] + list(range(2, shard_count - 1))
    got = {0: normed_two}
    for d in sequence[1:3]:
        got[d] = shift(normed_two, d)
    mixed, returned, gate_grads, rows = {}, {}, {}, []
    for d in sequence:
        source = (wt_index - d) % shard_count
        rank_in = lax.dynamic_index_in_dim(ranks, source, 0, False)
        mix, d_a, d_gate, *kept = expert_pass(
            got[d], grads_in[d], rank_in, gates_in[d], gate_full, up_full, down_full, capacity
        )
        rows.append(kept)
        d_gate = d_gate.reshape(expert_count, tok)
        back = shard_count - d
        mixed[d] = mix
        if d == 0:
            for other in sequence[3:]:
                got[other] = shift(after(normed_two, mix), other)
        returned[d] = shift(d_a, back) if d else d_a
        gate_grads[d] = shift(d_gate, back) if d else d_gate
    gate_grad, up_grad, down_grad = weight_grads(rows, context_size)
    returned[0] = after(returned[0], gate_grad)
    gate_share = lax.psum_scatter(gate_grad, "ctx", scatter_dimension=0, tiled=False).astype(f32)
    up_share = lax.psum_scatter(up_grad, "ctx", scatter_dimension=0, tiled=False).astype(f32)
    down_share = lax.psum_scatter(down_grad, "ctx", scatter_dimension=0, tiled=False).astype(f32)

    stacked = jnp.stack([gate_grads[d] for d in range(shard_count)], 0)
    stacked = jnp.roll(stacked, wt_index, 0).reshape(EXPERTS, tok).T
    grad_logits = (gates * (stacked - jnp.sum(gates * stacked, -1, keepdims=True))).astype(bf16)
    grad_normed_two = sum(returned[d].astype(f32) for d in range(shard_count))
    grad_normed_two = grad_normed_two + dot_nt(grad_logits, router_full)
    grad_mid_norm, second_gain_grad = norm_backward(
        middle, inverse_two, second_gain, grad_normed_two
    )
    grad_middle = out_grad + grad_mid_norm
    grad_branch = (resid_scale * grad_middle).astype(bf16)
    grad_attended = dot(grad_branch, output_t).astype(bf16)
    output_share = outer_sum(grad_branch, attended)
    devices = context_size * shard_count
    small = jnp.concatenate(
        [
            dot_tn(normed_two, grad_logits).reshape(devices, own_rows * EXPERTS),
            second_gain_grad.reshape(devices, own_rows),
        ],
        1,
    )
    small = spread_sum(small)

    mixture = mixed[0].astype(f32)
    for d in sequence[1:]:
        mixture = mixture + shift(after(mixed[d], returned[d]), shard_count - d).astype(f32)
    layer_output = (middle + resid_scale * mixture).astype(bf16)

    grad_query_low, d_key, d_value, d_key_own, d_value_own = attention_backward(
        turned_query,
        grad_attended,
        kv_all,
        kv_own,
        lse,
        attended,
        cosine,
        sine,
        place_of,
        starts,
        block_rows,
    )
    owned = scatter_ctx(jnp.concatenate([d_key, d_value], 1))
    d_key_all = jnp.concatenate([owned[:, :KV_WIDTH], d_key_own], 0)
    d_value_all = jnp.concatenate([owned[:, KV_WIDTH:], d_value_own], 0)
    grad_key_low = turn(
        d_key_all, jnp.tile(cosine, (1, 4)), jnp.tile(sine, (1, 4)), -1.0
    ).astype(bf16)
    grad_qkv = jnp.concatenate([grad_query_low, grad_key_low, d_value_all.astype(bf16)], 1)
    qkv_share = outer_sum(normed_one, grad_qkv)
    grad_normed_one = dot_nt(grad_qkv, qkv_full)
    grad_input_norm, first_gain_grad = norm_backward(
        inputs, inverse_one, first_gain, grad_normed_one
    )
    input_grad = (grad_middle + grad_input_norm).astype(bf16)

    first_gain_share = spread_sum(first_gain_grad.reshape(devices, own_rows))
    return (
        layer_output[None],
        input_grad[None],
        first_gain_share,
        qkv_share[:, :1024],
        qkv_share[:, 1024:1536],
        qkv_share[:, 1536:],
        output_share.T,
        small[own_rows * EXPERTS :],
        small[: own_rows * EXPERTS].reshape(own_rows, EXPERTS),
        gate_share,
        up_share,
        down_share,
    )


def solution(mesh):
    return jax.shard_map(
        per_device,
        mesh=mesh,
        in_specs=(
            P("wt", "ctx", None),
            P(("ctx", "wt")),
            P(("ctx", "wt"), None),
            P(("ctx", "wt"), None),
            P(("ctx", "wt"), None),
            P(None, ("ctx", "wt")),
            P(("ctx", "wt")),
            P(("ctx", "wt"), None),
            P("wt", "ctx", None),
            P("wt", "ctx", None),
            P("wt", None, "ctx"),
            P("wt", "ctx", None),
            P("wt", None),
            P("wt", "ctx", None),
        ),
        out_specs=(
            P("wt", "ctx", None),
            P("wt", "ctx", None),
            P(("ctx", "wt")),
            P(("ctx", "wt"), None),
            P(("ctx", "wt"), None),
            P(("ctx", "wt"), None),
            P(None, ("ctx", "wt")),
            P(("ctx", "wt")),
            P(("ctx", "wt"), None),
            P("wt", "ctx", None),
            P("wt", "ctx", None),
            P("wt", None, "ctx"),
        ),
        check_vma=False,
    )
```

time: 4100 us -> 1040 us (0.25)
  waiting for transfers between devices: 2180 us -> 327 us
  blocking collectives: 616 us -> 0 us
  matrix products: 570 us -> 22 us
  Pallas kernels: 0 us -> 447 us
  local copies, waits for them, and re-layouts: 371 us -> 60.3 us
  other arithmetic: 281 us -> 56.4 us
  starting transfers between devices: 32.7 us -> 96.8 us
    all_to_all x4 -> x3, waiting for transfers between devices: 1180 us -> 105 us  [the longest x2 105 us: spread_sum(): return jnp.sum(lax.all_to_all(x, ALL, 0, 0, tiled=True), 0)]
    reduce_scatter x9 -> x3, waiting for transfers between devices: 791 us -> 0.01 us  [the longest x1 0.01 us: per_device(): lax.psum_scatter(down_grad, 'ctx', scatter_dimension=0, tiled=False)]
    dot_general x80 -> x7, matrix products: 570 us -> 22 us  [the longest x3 16.8 us: dot_nt(): return lax.dot_general(a, b, NT, preferred_element_type=f32)]
    all_gather x1 -> x0, blocking collectives: 534 us -> none  [per_device(): lax.all_gather(router_weight, ('ctx', 'wt'), axis=0, tiled=True)]
    pallas_call x0 -> x10, Pallas kernels: none -> 447 us  [the longest x4 202 us: expert_pass(): pl.pallas_call(functools.partial(expert_kernel, capacity=capacity), grid=...]
    ppermute x0 -> x75, waiting for transfers between devices: none -> 220 us  [the longest x27 140 us: shift(): return lax.ppermute(x, 'wt', [(i, (i + distance) % n) for i in range(n)])]
    all_gather x9 -> x3, waiting for transfers between devices: 178 us -> 0.01 us  [the longest x1 0.01 us: per_device(): gate_full = lax.all_gather(gate_weight, 'ctx', axis=0, tiled=False)]
    gather x7 -> x0, local copies, waits for them, and re-layouts: 135 us -> none  [the longest x4 50.9 us: per_device(): chosen = jnp.take_along_axis(logits, routes, 1)]
  transfers between devices with their start and end apart: 23 -> 84, of which waited for: 18 -> 19; matrix products, arithmetic and copies ran while one was open for 16% -> 12% of each run, Pallas kernels for 0% -> 33%
where the time goes in v1:
time: 1040 us; the launch traced here: 1030 us
  Pallas kernels  447 us (43%)
  waiting for transfers between devices  327 us (31%)
  starting transfers between devices  96.8 us (9%)
  local copies, waits for them, and re-layouts  60.3 us (6%)
  other arithmetic  56.4 us (5%)
  matrix products  22 us (2%)
  between operations  18.7 us (2%)
    pallas_call x4, Pallas kernels, expert_pass(): pl.pallas_call(functools.partial(expert_kernel, capacity=capacity), grid=...  202 us
    ppermute x27, waiting for transfers between devices, shift(): return lax.ppermute(x, 'wt', [(i, (i + distance) % n) for i in range(n)])  140 us
    all_to_all x2, waiting for transfers between devices, spread_sum(): return jnp.sum(lax.all_to_all(x, ALL, 0, 0, tiled=True), 0)  105 us
    pallas_call x1, Pallas kernels, attention_backward(): pl.pallas_call(functools.partial(attention_backward_kernel, block_rows=bl...  97.3 us
    ppermute x48, waiting for transfers between devices, swap(): lax.ppermute(x, 'ctx', [(i, i ^ mask) for i in range(lax.axis_size('ctx'))])  80.8 us
    pallas_call x1, Pallas kernels, attention_forward(): pl.pallas_call(functools.partial(attention_forward_kernel, block_rows=blo...  60.7 us
    pallas_call x1, Pallas kernels, weight_grads(): pl.pallas_call(functools.partial(weight_grad_kernel, sources=sources, par...  60.1 us
    ppermute x27, starting transfers between devices, shift(): return lax.ppermute(x, 'wt', [(i, (i + distance) % n) for i in range(n)])  50.5 us
  transfers between devices with their start and end apart: 84, of which 19 were waited for; matrix products, arithmetic and copies ran while one was open for 12% of the time, Pallas kernels for 33%

profile of v1, /device:TPU:0, one launch (start us, length us, event | category | flops | bytes accessed | tf_op | source)
XLA Modules:
  0.0 1028.5 jit_solution(17551269423991965206)
XLA Ops:
  24.0 6.3 collective-permute-done.9
  36.7 17.3 %collective-permute-done.12.refs_10_ = bf16[96,3200]{1,0:T(8,128)(2,1)S(1)} collective-permute-done((bf16[96,3200]{1,0:T(8,128)(2,1)S(1)}, bf16[96,3200]{1,0:T(8,128)(2,1)S(1)}, u32[]{:S(2)}, u32[]{:S(2)}) %collective-permute-start.12) | collective-permute-done | bytes 614432 | tf_op jit(solution)/shard_map/ppermute | solution.py:580
  63.7 13.9 %collective-permute-done.16 = bf16[48,3200]{1,0:T(8,128)(2,1)S(1)} collective-permute-done((bf16[48,3200]{1,0:T(8,128)(2,1)S(1)}, bf16[48,3200]{1,0:T(8,128)(2,1)S(1)}, u32[]{:S(2)}, u32[]{:S(2)}) %collective-permute-start.16) | collective-permute-done | bytes 307232 | tf_op jit(solution)/shard_map/ppermute | solution.py:580
  77.7 7.6 collective-permute-done.17
  91.8 9.5 project.1
  128.2 6.6 collective-permute-done.24
  142.0 60.7 %attention_forward.1 = (bf16[768,1024]{1,0:T(8,128)(2,1)}, f32[4,4,768]{2,1,0:T(4,128)}) custom-call(s32[16]{0:T(128)} %fusion.58.slots, s32[4]{0:T(128)} %pad_add_fusion.starts, bf16[768,1024]{1,0:T(8,128)(2,1)} %get-tuple-element.66.q_ref, bf16[2048,1024]{1,0:T(8,128)(2,1)} %constant_dynamic-update-slice_fusion.7.k_ref.v_ref, ...), custom_call_target="tpu_custom_call" | custom-call | flops 60000002048 | bytes 12000000 | tf_op jit(solution)/shard_map/attention_forward/pallas_call | solution.py:213
  225.7 50.5 %expert_pass.4 = (bf16[768,1024]{1,0:T(8,128)(2,1)}, bf16[768,1024]{1,0:T(8,128)(2,1)}, f32[8,1,768]{2,1,0:T(1,128)}, bf16[8,336,1024]{2,1,0:T(8,128)(2,1)}, bf1...) custom-call(bf16[768,1024]{1,0:T(8,128)(2,1)} %copy-done.4, ...), custom_call_target="tpu_custom_call" | custom-call | flops 35000000512 | bytes 50000000 | tf_op jit(solution)/shard_map/expert_pass/pallas_call | solution.py:498
  278.2 13.9 %collective-permute-done.32.a2_ref = bf16[768,1024]{1,0:T(8,128)(2,1)} collective-permute-done((bf16[768,1024]{1,0:T(8,128)(2,1)S(1)}, bf16[768,1024]{1,0:T(8,128)(2,1)}, u32[]{:S(2)}, u32[]{:S(2)}) %collective-permute-start.32) | collective-permute-done | bytes 1572896 | tf_op jit(solution)/shard_map/ppermute | solution.py:617
  292.1 50.5 %expert_pass.6 = (bf16[768,1024]{1,0:T(8,128)(2,1)}, bf16[768,1024]{1,0:T(8,128)(2,1)}, f32[8,1,768]{2,1,0:T(1,128)}, bf16[8,336,1024]{2,1,0:T(8,128)(2,1)}, bf1...) custom-call(bf16[768,1024]{1,0:T(8,128)(2,1)} %collective-permute-do, ...), custom_call_target="tpu_custom_call" | custom-call | flops 35000000512 | bytes 50000000 | tf_op jit(solution)/shard_map/expert_pass/pallas_call | solution.py:498
  342.6 50.7 %expert_pass.5 = (bf16[768,1024]{1,0:T(8,128)(2,1)}, bf16[768,1024]{1,0:T(8,128)(2,1)}, f32[8,1,768]{2,1,0:T(1,128)}, bf16[8,336,1024]{2,1,0:T(8,128)(2,1)}, bf1...) custom-call(bf16[768,1024]{1,0:T(8,128)(2,1)} %collective-permute-do, ...), custom_call_target="tpu_custom_call" | custom-call | flops 35000000512 | bytes 50000000 | tf_op jit(solution)/shard_map/expert_pass/pallas_call | solution.py:498
  394.6 50.5 %expert_pass.7 = (bf16[768,1024]{1,0:T(8,128)(2,1)}, bf16[768,1024]{1,0:T(8,128)(2,1)}, f32[8,1,768]{2,1,0:T(1,128)}, bf16[8,336,1024]{2,1,0:T(8,128)(2,1)}, bf1...) custom-call(bf16[768,1024]{1,0:T(8,128)(2,1)} %copy-done.68, ...), custom_call_target="tpu_custom_call" | custom-call | flops 35000000512 | bytes 50000000 | tf_op jit(solution)/shard_map/expert_pass/pallas_call | solution.py:498
  445.1 60.1 %weight_grads.1 = (bf16[8,8,128,512]{3,2,1,0:T(8,128)(2,1)}, bf16[8,8,128,512]{3,2,1,0:T(8,128)(2,1)}, bf16[8,8,512,128]{3,2,1,0:T(8,128)(2,1)}) custom-call(bf16[8,336,1024]{2,1,0:T(8,128)(2,1)} %get-tuple-element.84.refs_0_, bf16[8,336,1024]{2,1,0:T(8,128)(2,1)} %get-tuple-element.85.refs_1_, bf16[8,336,512]{2,1,0:T(8,128)(2,1)} %get-tuple-element.86.refs_2_, ...), custom_call_target="tpu_custom_call" | custom-call | flops 33999998976 | bytes 100000000 | tf_op jit(solution)/shard_map/weight_grads/pallas_call | solution.py:561
  521.8 64.1 %collective-permute-done.43 = f32[8,768]{1,0:T(8,128)} collective-permute-done((f32[8,768]{1,0:T(8,128)}, f32[8,768]{1,0:T(8,128)}, u32[]{:S(2)}, u32[]{:S(2)}) %collective-permute-start.43) | collective-permute-done | bytes 24608 | tf_op jit(solution)/shard_map/ppermute | solution.py:617
  595.9 54.4 %collective-permute-done.40 = bf16[768,1024]{1,0:T(8,128)(2,1)} collective-permute-done((bf16[768,1024]{1,0:T(8,128)(2,1)}, bf16[768,1024]{1,0:T(8,128)(2,1)}, u32[]{:S(2)}, u32[]{:S(2)}) %collective-permute-start.40) | collective-permute-done | bytes 1572896 | tf_op jit(solution)/shard_map/ppermute | solution.py:617
  662.4 97.3 %attention_backward.1 = (bf16[768,1024]{1,0:T(8,128)(2,1)}, bf16[2048,512]{1,0:T(8,128)(2,1)}, bf16[2048,512]{1,0:T(8,128)(2,1)}, f32[512,512]{1,0:T(8,128)}, f32[512,512]{1,0:T(8,128)}) custom-call(s32[16]{0:T(128)} %fusion.58.slots, s32[4]{0:T(128)} %pad_add_fusion.starts, bf16[768,1024]{1,0:T(8,128)(2,1)} %get-tuple-element.66.q_ref, ...), custom_call_target="tpu_custom_call" | custom-call | flops 120000004096 | bytes 24000000 | tf_op jit(solution)/shard_map/attention_backward/pallas_call | solution.py:381
  767.2 7.9 outer.3
  786.2 5.6 collective-permute-done.48
  792.9 5.7 collective-permute-done.51
  804.4 9.0 collective-permute-done.49
  825.0 9.3 outer.2
  878.7 7.5 fusion.9
  891.2 105.0 %all-to-all-done.1 = f32[32,1,32]{2,1,0:T(1,128)S(1)} async-done(((f32[32,1,32]{2,1,0:T(1,128)}), f32[32,1,32]{2,1,0:T(1,128)S(1)}, u32[]{:S(2)}, u32[]{:S(2)}) %all-to-all-start.1) | async-done | bytes 4128 | tf_op jit(solution)/shard_map/all_to_all | solution.py:652
  1002.5 8.2 fusion.14
  (466 shorter events, 237.6 us)
Async XLA Ops:
  7.2 218.5 %all-gather.7.cloned.1.call-start = ((), (), s32[]{:S(2)}) async-start(), calls=%async_computation.9 | async-start | bytes 9437184 | tf_op jit(solution)/shard_map/all_gather | solution.py:736
  7.9 217.7 %all-gather.9.cloned.1.call-start = ((), (), s32[]{:S(2)}) async-start(), calls=%async_computation.10 | async-start | bytes 9437184 | tf_op jit(solution)/shard_map/all_gather | solution.py:737
  8.7 217.0 %all-gather.11.cloned.1.call-start = ((), (), s32[]{:S(2)}) async-start(), calls=%async_computation.11 | async-start | bytes 9437184 | tf_op jit(solution)/shard_map/all_gather | solution.py:738
  106.8 109.2 %all-to-all-start = ((f32[4,8,768]{2,1,0:T(8,128)}), f32[4,8,768]{2,1,0:T(8,128)S(1)}, u32[]{:S(2)}, u32[]{:S(2)}) async-start(f32[4,8,768]{2,1,0:T(8,128)} %fusion.21), calls=%async_computation | async-start | bytes 196608 | tf_op jit(solution)/shard_map/all_to_all | solution.py:746
  111.1 901.8 %reduce-scatter.8.cloned.1.call-start = ((), (), s32[]{:S(2)}) async-start(), calls=%async_computation.8 | async-start | bytes 9437184 | tf_op jit(solution)/shard_map/reduce_scatter | solution.py:823
  111.1 165.1 %collective-permute-start.33 = (bf16[768,1024]{1,0:T(8,128)(2,1)}, bf16[768,1024]{1,0:T(8,128)(2,1)}, u32[]{:S(2)}, u32[]{:S(2)}) collective-permute-start(bf16[768,1024]{1,0:T(8,128)(2,1)} %bitcast.14.df_ref), channel_id=1, source_target_pairs={{0,3},{1,0},{2,1},{3,2},{4,7},{5,4},{6,5},{7,6},{8,11},{9,8},{10,9... | collective-permute-start | bytes 4718600 | tf_op jit(solution)/shard_map/ppermute | solution.py:617
  134.8 258.5 %collective-permute-start.38 = (bf16[768,1024]{1,0:T(8,128)(2,1)}, bf16[768,1024]{1,0:T(8,128)(2,1)}, u32[]{:S(2)}, u32[]{:S(2)}) collective-permute-start(bf16[768,1024]{1,0:T(8,128)(2,1)} %bitcast.14.df_ref), channel_id=1, source_target_pairs={{0,2},{1,3},{2,0},{3,1},{4,6},{5,7},{6,4},{7,5},{8,10},{9,11},{10,... | collective-permute-start | bytes 4718600 | tf_op jit(solution)/shard_map/ppermute | solution.py:617
  219.1 123.5 %collective-permute-start.28 = (bf16[768,1024]{1,0:T(8,128)(2,1)}, bf16[768,1024]{1,0:T(8,128)(2,1)}, u32[]{:S(2)}, u32[]{:S(2)}) collective-permute-start(bf16[768,1024]{1,0:T(8,128)(2,1)} %bitcast.14.df_ref), channel_id=1, source_target_pairs={{0,1},{1,2},{2,3},{3,0},{4,5},{5,6},{6,7},{7,4},{8,9},{9,10},{10,1... | collective-permute-start | bytes 4718600 | tf_op jit(solution)/shard_map/ppermute | solution.py:617
  222.2 69.9 %collective-permute-start.32 = (bf16[768,1024]{1,0:T(8,128)(2,1)S(1)}, bf16[768,1024]{1,0:T(8,128)(2,1)}, u32[]{:S(2)}, u32[]{:S(2)}) collective-permute-start(bf16[768,1024]{1,0:T(8,128)(2,1)S(1)} %multiply_convert_fusion.1.a2_ref), channel_id=1, source_target_pairs={{0,3},{1,0},{2,1},{3,2},{4,7},{5,4},{6,5},{7,6},{8,11},{9,8},{10,9... | collective-permute-start | bytes 4718600 | tf_op jit(solution)/shard_map/ppermute | solution.py:617
  224.2 118.4 %collective-permute-start.27 = (bf16[768,1024]{1,0:T(8,128)(2,1)S(1)}, bf16[768,1024]{1,0:T(8,128)(2,1)}, u32[]{:S(2)}, u32[]{:S(2)}) collective-permute-start(bf16[768,1024]{1,0:T(8,128)(2,1)S(1)} %multiply_convert_fusion.1.a2_ref), channel_id=1, source_target_pairs={{0,1},{1,2},{2,3},{3,0},{4,5},{5,6},{6,7},{7,4},{8,9},{9,10},{10,1... | collective-permute-start | bytes 4718600 | tf_op jit(solution)/shard_map/ppermute | solution.py:617
  276.2 117.1 %collective-permute-start.37 = (bf16[768,1024]{1,0:T(8,128)(2,1)}, bf16[768,1024]{1,0:T(8,128)(2,1)S(1)}, u32[]{:S(2)}, u32[]{:S(2)}) collective-permute-start(bf16[768,1024]{1,0:T(8,128)(2,1)} %copy-done.4), channel_id=1, source_target_pairs={{0,2},{1,3},{2,0},{3,1},{4,6},{5,7},{6,4},{7,5},{8,10},{9,11},{10,... | collective-permute-start | bytes 4718600 | tf_op jit(solution)/shard_map/ppermute | solution.py:617
  505.2 510.4 %reduce-scatter.6.cloned.1.call-start = ((), (), s32[]{:S(2)}) async-start(), calls=%async_computation.7 | async-start | bytes 9437184 | tf_op jit(solution)/shard_map/reduce_scatter | solution.py:822
  505.8 512.6 %reduce-scatter.4.cloned.1.call-start = ((), (), s32[]{:S(2)}) async-start(), calls=%async_computation.6 | async-start | bytes 9437184 | tf_op jit(solution)/shard_map/reduce_scatter | solution.py:821
  508.6 78.6 %collective-permute-start.44 = (f32[8,768]{1,0:T(8,128)}, f32[8,768]{1,0:T(8,128)}, u32[]{:S(2)}, u32[]{:S(2)}) collective-permute-start(f32[8,768]{1,0:T(8,128)} %bitcast.123), channel_id=1, source_target_pairs={{0,1},{1,2},{2,3},{3,0},{4,5},{5,6},{6,7},{7,4},{8,9},{9,10},{10,1... | collective-permute-start | bytes 73736 | tf_op jit(solution)/shard_map/ppermute | solution.py:617
  513.1 82.8 %collective-permute-start.35 = (bf16[768,1024]{1,0:T(8,128)(2,1)}, bf16[768,1024]{1,0:T(8,128)(2,1)}, u32[]{:S(2)}, u32[]{:S(2)}) collective-permute-start(bf16[768,1024]{1,0:T(8,128)(2,1)} %get-tuple-element.77), channel_id=1, source_target_pairs={{0,1},{1,2},{2,3},{3,0},{4,5},{5,6},{6,7},{7,4},{8,9},{9,10},{10,1... | collective-permute-start | bytes 4718600 | tf_op jit(solution)/shard_map/ppermute | solution.py:617
  513.1 82.8 %collective-permute-start.30 = (bf16[768,1024]{1,0:T(8,128)(2,1)}, bf16[768,1024]{1,0:T(8,128)(2,1)}, u32[]{:S(2)}, u32[]{:S(2)}) collective-permute-start(bf16[768,1024]{1,0:T(8,128)(2,1)} %get-tuple-element.74), channel_id=1, source_target_pairs={{0,3},{1,0},{2,1},{3,2},{4,7},{5,4},{6,5},{7,6},{8,11},{9,8},{10,9... | collective-permute-start | bytes 4718600 | tf_op jit(solution)/shard_map/ppermute | solution.py:617
  517.5 68.4 %collective-permute-start.43 = (f32[8,768]{1,0:T(8,128)}, f32[8,768]{1,0:T(8,128)}, u32[]{:S(2)}, u32[]{:S(2)}) collective-permute-start(f32[8,768]{1,0:T(8,128)} %bitcast.124), channel_id=1, source_target_pairs={{0,2},{1,3},{2,0},{3,1},{4,6},{5,7},{6,4},{7,5},{8,10},{9,11},{10,... | collective-permute-start | bytes 73736 | tf_op jit(solution)/shard_map/ppermute | solution.py:617
  518.8 131.5 %collective-permute-start.40 = (bf16[768,1024]{1,0:T(8,128)(2,1)}, bf16[768,1024]{1,0:T(8,128)(2,1)}, u32[]{:S(2)}, u32[]{:S(2)}) collective-permute-start(bf16[768,1024]{1,0:T(8,128)(2,1)} %get-tuple-element.81), channel_id=1, source_target_pairs={{0,2},{1,3},{2,0},{3,1},{4,6},{5,7},{6,4},{7,5},{8,10},{9,11},{10,... | collective-permute-start | bytes 4718600 | tf_op jit(solution)/shard_map/ppermute | solution.py:617
  856.5 142.8 %collective-permute-start.36 = (bf16[768,1024]{1,0:T(8,128)(2,1)}, bf16[768,1024]{1,0:T(8,128)(2,1)}, u32[]{:S(2)}, u32[]{:S(2)}) collective-permute-start(bf16[768,1024]{1,0:T(8,128)(2,1)} %get-tuple-element.78), channel_id=1, source_target_pairs={{0,1},{1,2},{2,3},{3,0},{4,5},{5,6},{6,7},{7,4},{8,9},{9,10},{10,1... | collective-permute-start | bytes 4718600 | tf_op jit(solution)/shard_map/ppermute | solution.py:617
  860.4 142.1 %collective-permute-start.31 = (bf16[768,1024]{1,0:T(8,128)(2,1)}, bf16[768,1024]{1,0:T(8,128)(2,1)}, u32[]{:S(2)}, u32[]{:S(2)}) collective-permute-start(bf16[768,1024]{1,0:T(8,128)(2,1)} %get-tuple-element.75), channel_id=1, source_target_pairs={{0,3},{1,0},{2,1},{3,2},{4,7},{5,4},{6,5},{7,6},{8,11},{9,8},{10,9... | collective-permute-start | bytes 4718600 | tf_op jit(solution)/shard_map/ppermute | solution.py:617
  863.9 138.6 %collective-permute-start.41 = (bf16[768,1024]{1,0:T(8,128)(2,1)}, bf16[768,1024]{1,0:T(8,128)(2,1)}, u32[]{:S(2)}, u32[]{:S(2)}) collective-permute-start(bf16[768,1024]{1,0:T(8,128)(2,1)} %get-tuple-element.82), channel_id=1, source_target_pairs={{0,2},{1,3},{2,0},{3,1},{4,6},{5,7},{6,4},{7,5},{8,10},{9,11},{10,... | collective-permute-start | bytes 4718600 | tf_op jit(solution)/shard_map/ppermute | solution.py:617
  875.7 120.9 %collective-permute-start.57 = (bf16[128,2048]{1,0:T(8,128)(2,1)}, bf16[128,2048]{1,0:T(8,128)(2,1)}, u32[]{:S(2)}, u32[]{:S(2)}) collective-permute-start(bf16[128,2048]{1,0:T(8,128)(2,1)} %pad_maximum_fusion.4), channel_id=1, source_target_pairs={{0,8},{4,12},{8,0},{12,4},{16,24},{20,28},{24,16},{28,20},{1,9},{5... | collective-permute-start | bytes 1572872 | tf_op jit(solution)/shard_map/ppermute | solution.py:580
  878.1 118.5 %collective-permute-start.60 = (bf16[128,2048]{1,0:T(8,128)(2,1)}, bf16[128,2048]{1,0:T(8,128)(2,1)}, u32[]{:S(2)}, u32[]{:S(2)}) collective-permute-start(bf16[128,2048]{1,0:T(8,128)(2,1)} %pad_maximum_fusion.5), channel_id=1, source_target_pairs={{0,16},{4,20},{8,24},{12,28},{16,0},{20,4},{24,8},{28,12},{1,17},{... | collective-permute-start | bytes 1572872 | tf_op jit(solution)/shard_map/ppermute | solution.py:580
  886.9 109.2 %all-to-all-start.1 = ((f32[32,1,32]{2,1,0:T(1,128)}), f32[32,1,32]{2,1,0:T(1,128)S(1)}, u32[]{:S(2)}, u32[]{:S(2)}) async-start(f32[32,1,32]{2,1,0:T(1,128)} %all_to_all.16), calls=%async_computation.1 | async-start | bytes 32768 | tf_op jit(solution)/shard_map/all_to_all | solution.py:652
  (138 other events, 3305.1 us)
Sparse Core Ops, SparseCore 0:
  9.9 73.1 all-gather.6
  85.0 63.2 all-gather.8
  150.2 55.2 all-gather.10
  505.3 85.9 reduce-scatter.7
  595.1 71.2 reduce-scatter.5
  669.7 71.2 reduce-scatter.3

commit v2 on v1

v2 whole, which is shorter than its diff:
```python
import functools

import jax
import jax.numpy as jnp
from jax import lax
from jax.experimental import pallas as pl
from jax.experimental.pallas import tpu as pltpu
from jax.sharding import PartitionSpec as P

MODEL_WIDTH = 1024
HQ = 16
KEY_VALUE_HEADS = 8
HEAD_SIZE = 64
EXPERTS = 32
TOP = 8
PROMPT = 2048
CLEN = 256
CONT_DEV = 2
FF = 512
QTILE = 128
KV_WIDTH = KEY_VALUE_HEADS * HEAD_SIZE
ALL = ("ctx", "wt")

att_scale = 0.015625
resid_scale = 0.22
norm_eps = 1e-06
rope_base = 10000.0
masked_score = -1e30

bf16 = jnp.bfloat16
f32 = jnp.float32
VMEM_LIMIT = 60 * 1024 * 1024
SMALL = pl.CostEstimate(flops=1_000_000_000, bytes_accessed=1_000_000, transcendentals=0)

NT = (((1,), (1,)), ((), ()))
TN = (((0,), (0,)), ((), ()))


def dot(a, b):
    return jnp.dot(a, b, preferred_element_type=f32)


def dot_nt(a, b):
    return lax.dot_general(a, b, NT, preferred_element_type=f32)


def dot_tn(a, b):
    return lax.dot_general(a, b, TN, preferred_element_type=f32)


def turn_tile(values, cosine, sine, direction):
    middle = HEAD_SIZE // 2
    first = lax.broadcasted_iota(jnp.int32, values.shape, 1) % HEAD_SIZE < middle
    turned = jnp.where(first, -pltpu.roll(values, 128 - middle, 1), pltpu.roll(values, middle, 1))
    return values * cosine + direction * turned * sine


def project_kernel(places, x_ref, cos_ref, sin_ref, *refs, counts):
    pieces = refs[: len(counts)]
    normed_ref, q_ref, *kv_refs, qkv_ref, out_ref, rest_ref, gains_ref = refs[len(counts) :]
    rows = MODEL_WIDTH // sum(counts)
    at = 0
    for piece, count in zip(pieces, counts):
        for i in range(count):
            source = slice(i * rows, (i + 1) * rows)
            target = pl.ds(pl.multiple_of(places[at] * rows, rows), rows)
            qkv_ref[target, :] = piece[source, :2048]
            out_ref[target, :] = piece[source, 2048:3072]
            rest_ref[target, :] = piece[source, 3072:]
            at += 1
    gains = rest_ref[...].astype(f32).T[EXPERTS : EXPERTS + 8]
    gains_ref[...] = gains
    x = x_ref[...].astype(f32)
    inverse = lax.rsqrt(jnp.mean(x * x, -1, keepdims=True) + norm_eps)
    normed_ref[...] = (x * inverse * gains[:1]).astype(bf16)
    for c in range(8):
        raw = dot(normed_ref[...], qkv_ref[:, 256 * c : 256 * (c + 1)])
        for h in range(2):
            part = raw[:, 128 * h : 128 * (h + 1)]
            if c < 6:
                part = turn_tile(part, cos_ref[...], sin_ref[...], 1.0)
            column = 256 * c + 128 * h
            if column < 1024:
                q_ref[:, column : column + 128] = part.astype(bf16)
            else:
                column -= 1024
                at = column // KV_WIDTH * 256 + column % 256
                kv_refs[column % KV_WIDTH // 256][:, at : at + 128] = part.astype(bf16)


def project(x, cosine, sine, pieces, counts, places):
    tok = x.shape[0]
    shape = jax.ShapeDtypeStruct
    whole = pl.BlockSpec(memory_space=pltpu.VMEM)
    return pl.pallas_call(
        functools.partial(project_kernel, counts=counts),
        in_specs=[pl.BlockSpec(memory_space=pltpu.SMEM)] + [whole] * (3 + len(pieces)),
        out_specs=[whole] * 8,
        out_shape=[
            shape((tok, MODEL_WIDTH), bf16),
            shape((tok, HQ * HEAD_SIZE), bf16),
            shape((tok, KV_WIDTH), bf16),
            shape((tok, KV_WIDTH), bf16),
            shape((MODEL_WIDTH, 2048), bf16),
            shape((MODEL_WIDTH, 1024), bf16),
            shape((MODEL_WIDTH, 128), bf16),
            shape((8, MODEL_WIDTH), f32),
        ],
        compiler_params=pltpu.CompilerParams(vmem_limit_bytes=VMEM_LIMIT),
        cost_estimate=SMALL,
        name="project",
    )(places, x, cosine, sine, *pieces)


def outer_kernel(mine, a_ref, b_ref, out_ref):
    out_ref[...] = dot_tn(a_ref[...], b_ref[...]).astype(bf16)


def outer(a, b):
    tok, columns = b.shape
    mine = lax.axis_index("ctx").astype(jnp.int32).reshape(1)
    return pl.pallas_call(
        outer_kernel,
        grid_spec=pltpu.PrefetchScalarGridSpec(
            num_scalar_prefetch=1,
            grid=(8,),
            in_specs=[
                pl.BlockSpec((tok, 128), lambda m, mine: (0, m ^ mine[0])),
                pl.BlockSpec((tok, columns), lambda m, mine: (0, 0)),
            ],
            out_specs=pl.BlockSpec((128, columns), lambda m, mine: (m, 0)),
        ),
        out_shape=jax.ShapeDtypeStruct((MODEL_WIDTH, columns), bf16),
        compiler_params=pltpu.CompilerParams(vmem_limit_bytes=VMEM_LIMIT),
        cost_estimate=SMALL,
        name="outer",
    )(mine, a, b)


def gather_keys(pieces, scratch, places, block_rows):
    at = 0
    for piece in pieces:
        for b in range(piece.shape[0] // block_rows):
            start = pl.multiple_of(places[at] * block_rows, block_rows)
            scratch[pl.ds(start, block_rows), :] = piece[b * block_rows : (b + 1) * block_rows, :]
            at += 1


def pair_rows(ref, start, rows, j):
    both = ref[pl.ds(start, rows), 2 * HEAD_SIZE * j : 2 * HEAD_SIZE * (j + 1)]
    return jnp.concatenate([both[:, :HEAD_SIZE], both[:, HEAD_SIZE:]], 0)


def attention_forward_kernel(places, starts, q_ref, *refs, block_rows, pieces):
    k_refs, v_refs = refs[:pieces], refs[pieces : 2 * pieces]
    kc_ref, vc_ref, o_ref, lse_ref, k_scr, v_scr = refs[2 * pieces :]
    prompt_local = 2 * block_rows
    gather_keys(k_refs, k_scr, places, block_rows)
    gather_keys(v_refs, v_scr, places, block_rows)

    def store(start, rows, j, out, m, total, at):
        out = (out / total).astype(bf16)
        lse = m + jnp.log(total)
        o_ref[pl.ds(start, rows), 2 * HEAD_SIZE * j : 2 * HEAD_SIZE * (j + 1)] = jnp.concatenate(
            [out[:rows], out[rows:]], 1
        )
        row = jnp.broadcast_to(lse, (2 * rows, 128)).T[:1]
        lse_ref[0, 2 * j : 2 * j + 2, pl.ds(at, rows)] = jnp.concatenate(
            [row[:, :rows], row[:, rows:]], 0
        )

    def tile(i, _):
        start = pl.multiple_of(prompt_local + i * QTILE, 64)
        per = CLEN // QTILE
        seg = pl.multiple_of((i // per) * CLEN, CLEN)
        for j in range(2):
            lanes = slice(HEAD_SIZE * j, HEAD_SIZE * (j + 1))
            q = pair_rows(q_ref, start, QTILE, j) * bf16(att_scale)
            s1 = dot_nt(q, k_scr[:, lanes])
            s2 = dot_nt(q, kc_ref[pl.ds(seg, CLEN), lanes])
            place = lax.broadcasted_iota(jnp.int32, s2.shape, 0) % QTILE + (i % per) * QTILE
            s2 = jnp.where(lax.broadcasted_iota(jnp.int32, s2.shape, 1) <= place, s2, masked_score)
            m = jnp.maximum(jnp.max(s1, 1, keepdims=True), jnp.max(s2, 1, keepdims=True))
            e1 = jnp.exp(s1 - m)
            e2 = jnp.exp(s2 - m)
            total = jnp.sum(e1, 1, keepdims=True) + jnp.sum(e2, 1, keepdims=True)
            out = dot(e1.astype(bf16), v_scr[:, lanes])
            out = out + dot(e2.astype(bf16), vc_ref[pl.ds(seg, CLEN), lanes])
            store(start, QTILE, j, out, m, total, pl.multiple_of(i * QTILE, QTILE))
        return 0

    lax.fori_loop(0, CONT_DEV * CLEN // QTILE, tile, 0)

    for half, keys in enumerate((PROMPT // 2, PROMPT)):
        start = pl.multiple_of(starts[half], block_rows)
        for j in range(2):
            lanes = slice(HEAD_SIZE * j, HEAD_SIZE * (j + 1))
            q = pair_rows(q_ref, start, block_rows, j) * bf16(att_scale)
            s = dot_nt(q, k_scr[:keys, lanes])
            place = lax.broadcasted_iota(jnp.int32, s.shape, 0) % block_rows + starts[2 + half]
            s = jnp.where(lax.broadcasted_iota(jnp.int32, s.shape, 1) <= place, s, masked_score)
            m = jnp.max(s, 1, keepdims=True)
            e = jnp.exp(s - m)
            total = jnp.sum(e, 1, keepdims=True)
            out = dot(e.astype(bf16), v_scr[:keys, lanes])
            store(start, block_rows, j, out, m, total, CONT_DEV * CLEN + half * block_rows)


def key_specs(pieces, own):
    spec = pl.BlockSpec
    keys = [spec((p.shape[0], 128), lambda g, *_: (0, g)) for p in pieces]
    values = [spec((p.shape[0], 128), lambda g, *_: (0, 2 + g)) for p in pieces]
    ours = [spec((own, 128), lambda g, *_: (0, g)), spec((own, 128), lambda g, *_: (0, 2 + g))]
    return keys + values + ours


def attention_forward(q, pieces, kv_own, places, starts, block_rows, half):
    tok = q.shape[0]
    spec = pl.BlockSpec
    return pl.pallas_call(
        functools.partial(
            attention_forward_kernel, block_rows=block_rows, pieces=len(pieces)
        ),
        grid_spec=pltpu.PrefetchScalarGridSpec(
            num_scalar_prefetch=2,
            grid=(2,),
            in_specs=[spec((tok, 256), lambda g, *_: (0, 2 * half + g))]
            + key_specs(pieces, kv_own.shape[0]),
            out_specs=[
                spec((tok, 256), lambda g, *_: (0, g)),
                spec((1, 4, tok), lambda g, *_: (g, 0, 0)),
            ],
            scratch_shapes=[
                pltpu.VMEM((PROMPT, 2 * HEAD_SIZE), bf16),
                pltpu.VMEM((PROMPT, 2 * HEAD_SIZE), bf16),
            ],
        ),
        out_shape=[
            jax.ShapeDtypeStruct((tok, HQ * HEAD_SIZE // 2), bf16),
            jax.ShapeDtypeStruct((2, 4, tok), f32),
        ],
        compiler_params=pltpu.CompilerParams(vmem_limit_bytes=VMEM_LIMIT),
        cost_estimate=SMALL,
        name="attention_forward",
    )(places, starts, q, *pieces, *pieces, kv_own, kv_own)


def attention_backward_kernel(
    places, starts, q_ref, do_ref, lse_ref, o_ref, cos_ref, sin_ref, *refs, block_rows, pieces
):
    k_refs, v_refs = refs[:pieces], refs[pieces : 2 * pieces]
    kc_ref, vc_ref, dq_ref, dkv_ref, dkc_ref, dvc_ref = refs[2 * pieces : 2 * pieces + 6]
    k_scr, v_scr, dk_acc, dv_acc, dq_acc = refs[2 * pieces + 6 :]
    prompt_local = 2 * block_rows
    gather_keys(k_refs, k_scr, places, block_rows)
    gather_keys(v_refs, v_scr, places, block_rows)
    dk_acc[...] = jnp.zeros_like(dk_acc)
    dv_acc[...] = jnp.zeros_like(dv_acc)
    dkc_ref[...] = jnp.zeros_like(dkc_ref)
    dvc_ref[...] = jnp.zeros_like(dvc_ref)

    def row_pair(ref, start, rows, j):
        both = ref[0, 2 * j : 2 * j + 2, pl.ds(start, rows)]
        return jnp.concatenate([both[:1], both[1:]], 1)

    def centre(start, rows, j, d_out):
        product = d_out.astype(f32) * pair_rows(o_ref, start, rows, j).astype(f32)
        ones = jnp.ones((8, HEAD_SIZE), f32)
        return lax.dot_general(
            ones, product, NT, precision=lax.Precision.HIGHEST, preferred_element_type=f32
        )[:1]

    def part(k, v, q, d_out, lse, delta, allowed):
        s = dot_nt(k, q)
        if allowed is not None:
            s = jnp.where(allowed(s.shape), s, masked_score)
        p = jnp.exp(s - lse)
        d_p = dot_nt(v, d_out)
        d_s = (p * (d_p - delta)).astype(bf16)
        return dot_tn(d_s, k), dot(d_s, q), dot(p.astype(bf16), d_out)

    def store(start, rows, j, d_q):
        d_q = d_q * att_scale
        dq_acc[pl.ds(start, rows), 2 * HEAD_SIZE * j : 2 * HEAD_SIZE * (j + 1)] = jnp.concatenate(
            [d_q[:rows], d_q[rows:]], 1
        )

    def tile(i, _):
        start = pl.multiple_of(prompt_local + i * QTILE, 64)
        per = CLEN // QTILE
        seg = pl.multiple_of((i // per) * CLEN, CLEN)
        own = pl.ds(seg, CLEN)
        lane_start = pl.multiple_of(i * QTILE, QTILE)

        def allowed(shape):
            place = lax.broadcasted_iota(jnp.int32, shape, 1) % QTILE + (i % per) * QTILE
            return lax.broadcasted_iota(jnp.int32, shape, 0) <= place

        for j in range(2):
            lanes = slice(HEAD_SIZE * j, HEAD_SIZE * (j + 1))
            q = pair_rows(q_ref, start, QTILE, j) * bf16(att_scale)
            d_out = pair_rows(do_ref, start, QTILE, j)
            lse = row_pair(lse_ref, lane_start, QTILE, j)
            delta = centre(start, QTILE, j, d_out)
            a, b, c = part(k_scr[:, lanes], v_scr[:, lanes], q, d_out, lse, delta, None)
            dk_acc[:, lanes] += b
            dv_acc[:, lanes] += c
            d_q = a
            a, b, c = part(
                kc_ref[own, lanes], vc_ref[own, lanes], q, d_out, lse, delta, allowed
            )
            dkc_ref[own, lanes] += b
            dvc_ref[own, lanes] += c
            store(start, QTILE, j, d_q + a)
        return 0

    lax.fori_loop(0, CONT_DEV * CLEN // QTILE, tile, 0)

    for half, keys in enumerate((PROMPT // 2, PROMPT)):
        start = pl.multiple_of(starts[half], block_rows)
        at = CONT_DEV * CLEN + half * block_rows

        def allowed(shape):
            place = lax.broadcasted_iota(jnp.int32, shape, 1) % block_rows + starts[2 + half]
            return lax.broadcasted_iota(jnp.int32, shape, 0) <= place

        for j in range(2):
            lanes = slice(HEAD_SIZE * j, HEAD_SIZE * (j + 1))
            q = pair_rows(q_ref, start, block_rows, j) * bf16(att_scale)
            d_out = pair_rows(do_ref, start, block_rows, j)
            lse = row_pair(lse_ref, at, block_rows, j)
            delta = centre(start, block_rows, j, d_out)
            a, b, c = part(
                k_scr[:keys, lanes], v_scr[:keys, lanes], q, d_out, lse, delta, allowed
            )
            dk_acc[:keys, lanes] += b
            dv_acc[:keys, lanes] += c
            store(start, block_rows, j, a)

    g = pl.program_id(0)
    key_lanes = pl.ds(pl.multiple_of(g * 128, 128), 128)
    value_lanes = pl.ds(pl.multiple_of(256 + g * 128, 128), 128)
    for b in range(PROMPT // block_rows):
        source = pl.ds(pl.multiple_of(places[b] * block_rows, block_rows), block_rows)
        rows = slice(b * block_rows, (b + 1) * block_rows)
        dkv_ref[rows, key_lanes] = dk_acc[source, :].astype(bf16)
        dkv_ref[rows, value_lanes] = dv_acc[source, :].astype(bf16)
    for c in range(2):
        lanes = slice(128 * c, 128 * (c + 1))
        dq_ref[:, lanes] = turn_tile(dq_acc[:, lanes], cos_ref[...], sin_ref[...], -1.0).astype(
            bf16
        )


def attention_backward(
    q, d_out, lse, attended, cosine, sine, pieces, kv_own, places, starts, block_rows, half
):
    tok = q.shape[0]
    own = kv_own.shape[0]
    spec = pl.BlockSpec
    wide = spec((tok, 256), lambda g, *_: (0, 2 * half + g))
    ours = spec((own, 128), lambda g, *_: (0, g))
    table = spec((tok, 128), lambda g, *_: (0, 0))
    return pl.pallas_call(
        functools.partial(
            attention_backward_kernel, block_rows=block_rows, pieces=len(pieces)
        ),
        grid_spec=pltpu.PrefetchScalarGridSpec(
            num_scalar_prefetch=2,
            grid=(2,),
            in_specs=[wide, wide, spec((1, 4, tok), lambda g, *_: (g, 0, 0)), wide, table, table]
            + key_specs(pieces, own),
            out_specs=[
                spec((tok, 256), lambda g, *_: (0, g)),
                spec((PROMPT, KV_WIDTH), lambda g, *_: (0, 0)),
                ours,
                ours,
            ],
            scratch_shapes=[
                pltpu.VMEM((PROMPT, 2 * HEAD_SIZE), bf16),
                pltpu.VMEM((PROMPT, 2 * HEAD_SIZE), bf16),
                pltpu.VMEM((PROMPT, 2 * HEAD_SIZE), f32),
                pltpu.VMEM((PROMPT, 2 * HEAD_SIZE), f32),
                pltpu.VMEM((tok, 4 * HEAD_SIZE), f32),
            ],
        ),
        out_shape=[
            jax.ShapeDtypeStruct((tok, HQ * HEAD_SIZE // 2), bf16),
            jax.ShapeDtypeStruct((PROMPT, KV_WIDTH), bf16),
            jax.ShapeDtypeStruct((own, KV_WIDTH // 2), f32),
            jax.ShapeDtypeStruct((own, KV_WIDTH // 2), f32),
        ],
        compiler_params=pltpu.CompilerParams(vmem_limit_bytes=VMEM_LIMIT),
        cost_estimate=SMALL,
        name="attention_backward",
    )(places, starts, q, d_out, lse, attended, cosine, sine, *pieces, *pieces, kv_own, kv_own)


def expert_kernel(
    counts,
    a2_ref,
    df_ref,
    rank_ref,
    gate_ref,
    wg_ref,
    wu_ref,
    wd_ref,
    mix_ref,
    da_ref,
    dg_ref,
    x_ref,
    dy_ref,
    z_ref,
    dgate_ref,
    dup_ref,
    mix_acc,
    da_acc,
    *,
    sizes,
):
    e = pl.program_id(0)

    @pl.when(e == 0)
    def _():
        mix_acc[...] = jnp.zeros_like(mix_acc)
        da_acc[...] = jnp.zeros_like(da_acc)

    def body(size):
        rank = rank_ref[0]
        gates = gate_ref[0]
        tok = rank.shape[1]
        slot = lax.broadcasted_iota(jnp.int32, (size, tok), 0).astype(f32)
        hit = slot == rank
        chosen = hit.astype(f32).astype(bf16)
        gate = jnp.sum(jnp.where(hit, gates, 0.0), 1, keepdims=True)
        x = dot(chosen, a2_ref[...]).astype(bf16)
        d_mix = resid_scale * dot(chosen, df_ref[...])
        wg = wg_ref[:, 0].reshape(MODEL_WIDTH, FF)
        wu = wu_ref[:, 0].reshape(MODEL_WIDTH, FF)
        wd = jnp.concatenate([wd_ref[c, 0] for c in range(wd_ref.shape[0])], 1)
        g = dot(x, wg)
        u = dot(x, wu)
        sig = jax.nn.sigmoid(g)
        z = (g * sig * u).astype(bf16)
        y = dot(z, wd).astype(bf16).astype(f32)
        d_gate_value = jnp.sum(d_mix * y, 1, keepdims=True)
        dg_ref[0] = jnp.sum(jnp.where(hit, d_gate_value, 0.0), 0, keepdims=True)
        mix_acc[...] += dot_tn(chosen, (gate * y).astype(bf16))
        d_y = (gate * d_mix).astype(bf16)
        d_z = dot_nt(d_y, wd)
        d_g = (d_z * u * sig * (1.0 + g * (1.0 - sig))).astype(bf16)
        d_u = (d_z * g * sig).astype(bf16)
        d_r = (dot_nt(d_g, wg) + dot_nt(d_u, wu)).astype(bf16)
        da_acc[...] += dot_tn(chosen, d_r)
        for ref, value in (
            (x_ref, x),
            (dy_ref, d_y),
            (z_ref, z),
            (dgate_ref, d_g),
            (dup_ref, d_u),
        ):
            ref[0, :size] = value
            if size < ref.shape[1]:
                ref[0, size:] = jnp.zeros((ref.shape[1] - size, ref.shape[2]), bf16)

    least = -1
    for size in sizes:
        pl.when((counts[e] > least) & (counts[e] <= size))(functools.partial(body, size))
        least = size

    @pl.when(e == pl.num_programs(0) - 1)
    def _():
        mix_ref[...] = mix_acc[...].astype(bf16)
        da_ref[...] = da_acc[...].astype(bf16)


def expert_pass(a2, df, rank, gates, wg, wu, wd, capacity):
    tok = a2.shape[0]
    parts, experts = wg.shape[0], wg.shape[1]
    sizes = sorted({min(size, capacity) for size in (128, 192, 256, capacity)})
    counts = (jnp.max(rank, 1) + 1.0).astype(jnp.int32)
    spec = pl.BlockSpec
    whole = spec((tok, MODEL_WIDTH), lambda e, *_: (0, 0))
    row = spec((1, 1, tok), lambda e, *_: (e, 0, 0))
    up = spec((parts, 1, MODEL_WIDTH // parts, FF), lambda e, *_: (0, e, 0, 0))
    down = spec((parts, 1, FF, MODEL_WIDTH // parts), lambda e, *_: (0, e, 0, 0))
    rows_wide = spec((1, capacity, MODEL_WIDTH), lambda e, *_: (e, 0, 0))
    rows_thin = spec((1, capacity, FF), lambda e, *_: (e, 0, 0))
    shape = jax.ShapeDtypeStruct
    return pl.pallas_call(
        functools.partial(expert_kernel, sizes=sizes),
        grid_spec=pltpu.PrefetchScalarGridSpec(
            num_scalar_prefetch=1,
            grid=(experts,),
            in_specs=[whole, whole, row, row, up, up, down],
            out_specs=[whole, whole, row, rows_wide, rows_wide, rows_thin, rows_thin, rows_thin],
            scratch_shapes=[
                pltpu.VMEM((tok, MODEL_WIDTH), f32),
                pltpu.VMEM((tok, MODEL_WIDTH), f32),
            ],
        ),
        out_shape=[
            shape((tok, MODEL_WIDTH), bf16),
            shape((tok, MODEL_WIDTH), bf16),
            shape((experts, 1, tok), f32),
            shape((experts, capacity, MODEL_WIDTH), bf16),
            shape((experts, capacity, MODEL_WIDTH), bf16),
            shape((experts, capacity, FF), bf16),
            shape((experts, capacity, FF), bf16),
            shape((experts, capacity, FF), bf16),
        ],
        compiler_params=pltpu.CompilerParams(vmem_limit_bytes=VMEM_LIMIT),
        cost_estimate=SMALL,
        name="expert_pass",
    )(counts, a2, df, rank.reshape(experts, 1, tok), gates.reshape(experts, 1, tok), wg, wu, wd)


def up_grad_kernel(*refs, sources):
    rows = refs[: 3 * sources]
    gate_ref, up_ref = refs[3 * sources :]
    for n, out_ref in ((1, gate_ref), (2, up_ref)):
        total = None
        for s in range(sources):
            term = dot_tn(rows[3 * s][0], rows[3 * s + n][0])
            total = term if total is None else total + term
        out_ref[...] = total.astype(bf16).reshape(out_ref.shape)


def down_grad_kernel(*refs, sources, parts):
    rows, down_ref = refs[: 2 * sources], refs[-1]
    width = MODEL_WIDTH // parts
    total = None
    for s in range(sources):
        term = dot_tn(rows[2 * s][0], rows[2 * s + 1][0])
        total = term if total is None else total + term
    total = total.astype(bf16)
    for c in range(parts):
        down_ref[c, 0] = total[:, c * width : (c + 1) * width]


def row_specs(rows):
    return [pl.BlockSpec((1,) + a.shape[1:], lambda e: (e, 0, 0)) for r in rows for a in r]


def up_weight_grads(rows, parts):
    experts = rows[0][0].shape[0]
    shape = (parts, experts, MODEL_WIDTH // parts, FF)
    out = pl.BlockSpec((parts, 1) + shape[2:], lambda e: (0, e, 0, 0))
    return pl.pallas_call(
        functools.partial(up_grad_kernel, sources=len(rows)),
        grid=(experts,),
        in_specs=row_specs(rows),
        out_specs=[out, out],
        out_shape=[jax.ShapeDtypeStruct(shape, bf16)] * 2,
        compiler_params=pltpu.CompilerParams(vmem_limit_bytes=VMEM_LIMIT),
        cost_estimate=SMALL,
        name="up_weight_grads",
    )(*[a for r in rows for a in r])


def down_weight_grads(rows, parts):
    experts = rows[0][0].shape[0]
    shape = (parts, experts, FF, MODEL_WIDTH // parts)
    return pl.pallas_call(
        functools.partial(down_grad_kernel, sources=len(rows), parts=parts),
        grid=(experts,),
        in_specs=row_specs(rows),
        out_specs=pl.BlockSpec((parts, 1) + shape[2:], lambda e: (0, e, 0, 0)),
        out_shape=jax.ShapeDtypeStruct(shape, bf16),
        compiler_params=pltpu.CompilerParams(vmem_limit_bytes=VMEM_LIMIT),
        cost_estimate=SMALL,
        name="down_weight_grads",
    )(*[a for r in rows for a in r])


def swap(x, mask):
    return lax.ppermute(x, "ctx", [(i, i ^ mask) for i in range(lax.axis_size("ctx"))])


def blocks_ctx(x):
    half = x.shape[0] // 2
    near, far = swap(x, 2), swap(x, 4)
    diagonal = jnp.concatenate([swap(near[:half], 4), swap(far[half:], 2)], 0)
    even = [x, near, far, diagonal]
    odd = [swap(block, 1) for block in even]
    return [b for pair in zip(even, odd) for b in pair]


def gather_ctx(x):
    if lax.axis_size("ctx") != 8:
        return [lax.all_gather(x, "ctx", axis=0, tiled=True)]
    return blocks_ctx(x)


def scatter_ctx(x):
    if lax.axis_size("ctx") != 8:
        return lax.psum_scatter(x, "ctx", scatter_dimension=0, tiled=True).astype(f32)
    rows = x.shape[0] // 8
    half = rows // 2
    block = [x[m * rows : (m + 1) * rows] for m in range(8)]
    diagonal, near, far, own = (
        block[m].astype(f32) + swap(block[m + 1], 1).astype(f32) for m in (6, 2, 4, 0)
    )
    diagonal = diagonal.astype(bf16)
    near_top = near[:half] + swap(diagonal[:half], 4).astype(f32)
    far_end = far[half:] + swap(diagonal[half:], 2).astype(f32)
    near = jnp.concatenate([near_top.astype(bf16), near[half:].astype(bf16)], 0)
    far = jnp.concatenate([far[:half].astype(bf16), far_end.astype(bf16)], 0)
    return own + swap(near, 2).astype(f32) + swap(far, 4).astype(f32)


def shift(x, distance):
    n = lax.axis_size("wt")
    return lax.ppermute(x, "wt", [(i, (i + distance) % n) for i in range(n)])


def beside(results, *arrivals):
    out = lax.optimization_barrier((results, arrivals))
    return (out[0],) + tuple(out[1])


def gather_all(x):
    ctx, wt = lax.axis_size("ctx"), lax.axis_size("wt")
    if ctx != 8 or wt != 4:
        return [lax.all_gather(x, ALL, axis=0, tiled=True)], [1], jnp.zeros((1,), jnp.int32), x
    ctx_index, wt_index = lax.axis_index("ctx"), lax.axis_index("wt")
    others = jnp.concatenate([shift(x, d) for d in (1, 2, 3)], 0)
    pieces = blocks_ctx(x) + blocks_ctx(others)
    m = jnp.arange(8, dtype=jnp.int32)
    own = (ctx_index ^ m) * wt + wt_index
    d = jnp.arange(1, 4, dtype=jnp.int32)
    rest = ((ctx_index ^ m) * wt)[:, None] + ((wt_index - d) % wt)[None, :]
    places = jnp.concatenate([own, rest.reshape(-1)]).astype(jnp.int32)
    return pieces, [1] * 8 + [3] * 8, places, others


def outer_sum(a, b):
    ctx, wt = lax.axis_size("ctx"), lax.axis_size("wt")
    if ctx != 8 or wt != 4:
        return lax.psum_scatter(
            dot_tn(a, b).astype(bf16), ALL, scatter_dimension=0, tiled=True
        ).astype(f32)
    part = scatter_ctx(outer(a, b))
    rows = part.shape[0] // wt
    low = part.astype(bf16)
    at = lambda d: ((lax.axis_index("wt") + d) % wt) * rows
    total = lax.dynamic_slice_in_dim(part, at(0), rows, 0)
    for d in range(1, wt):
        total = total + shift(lax.dynamic_slice_in_dim(low, at(d), rows, 0), d).astype(f32)
    return total


def spread_sum(x):
    return jnp.sum(lax.all_to_all(x, ALL, 0, 0, tiled=True), 0)


def after(x, *others):
    return lax.optimization_barrier((x,) + others)[0]


def rope_tables(positions, width):
    middle = HEAD_SIZE // 2
    frequency = jnp.power(
        jnp.float32(rope_base), -2.0 * jnp.arange(middle, dtype=f32) / HEAD_SIZE
    )
    angles = positions.astype(f32)[:, None] * frequency[None, :]
    times = width // middle
    return jnp.tile(jnp.cos(angles), (1, times)), jnp.tile(jnp.sin(angles), (1, times))


def turn(values, cosine, sine, direction):
    middle = HEAD_SIZE // 2
    first = lax.broadcasted_iota(jnp.int32, values.shape, 1) % HEAD_SIZE < middle
    turned = jnp.where(first, -jnp.roll(values, -middle, 1), jnp.roll(values, middle, 1))
    width = values.shape[1]
    return values * cosine[:, :width] + direction * turned * sine[:, :width]


def norm_forward(values, gain):
    inverse = lax.rsqrt(jnp.mean(values * values, -1, keepdims=True) + norm_eps)
    return (values * inverse * gain, inverse)


def norm_backward(values, inverse, gain, grad_out):
    scaled = gain * grad_out
    gain_grad = jnp.sum(grad_out * values * inverse, 0)
    projection = jnp.mean(scaled * values, -1, keepdims=True)
    return (inverse * scaled - values * inverse * inverse * inverse * projection, gain_grad)


def per_device(
    layer_input,
    attention_gain,
    query_weight,
    key_matrix,
    value_matrix,
    output_weight,
    mixture_gain,
    router_weight,
    gate_weight,
    up_weight,
    down_weight,
    expert_routes,
    prompt_deal,
    output_grad,
):
    tok = layer_input.shape[1]
    prompt_local = tok - CONT_DEV * CLEN
    block_rows = prompt_local // 2
    context_size = lax.axis_size("ctx")
    shard_count = lax.axis_size("wt")
    expert_count = gate_weight.shape[0]
    capacity = 8 * ((tok * TOP * 7 // (4 * EXPERTS) + 7) // 8)
    ctx_index = lax.axis_index("ctx")
    wt_index = lax.axis_index("wt")
    inputs = layer_input[0].astype(f32)
    routes = expert_routes[0]
    deal_row = prompt_deal[0]
    out_low = output_grad[0]
    out_grad = out_low.astype(f32)

    own_rows = query_weight.shape[0]
    packed = jnp.concatenate(
        [
            query_weight,
            key_matrix,
            value_matrix,
            output_weight.T,
            router_weight,
            attention_gain[:, None],
            mixture_gain[:, None],
            jnp.zeros((own_rows, 94), bf16),
        ],
        1,
    )
    pieces, counts, block_places, first_part = gather_all(packed)

    gate_full = lax.all_gather(gate_weight, "ctx", axis=0, tiled=False)
    up_full = lax.all_gather(up_weight, "ctx", axis=0, tiled=False)
    down_full = lax.all_gather(down_weight, "ctx", axis=0, tiled=False)

    mask = jnp.any(
        routes[:, :, None] == jnp.arange(EXPERTS, dtype=jnp.int32)[None, None, :], 1
    )
    order = jnp.arange(tok, dtype=jnp.int32)
    before = (order[None, :] < order[:, None]).astype(bf16)
    rank = jnp.where(mask, dot(before, mask.astype(bf16)), -1.0)
    ranks = lax.all_to_all(
        rank.T.reshape(shard_count, expert_count, tok), "wt", 0, 0, tiled=True
    )
    last = shard_count - 1
    grads_in = {0: out_low, last: shift(after(out_low, first_part), -1)}

    pieces, grads_in[last] = beside(pieces, grads_in[last])
    local_rows = jnp.arange(tok, dtype=jnp.int32)
    mine = lax.dynamic_slice_in_dim(deal_row, 2 * ctx_index, 2, 0)
    prompt_place = (
        jnp.where(local_rows < block_rows, mine[0], mine[1]) * block_rows
        + local_rows % block_rows
    )
    positions = jnp.where(
        local_rows < prompt_local, prompt_place, PROMPT + (local_rows - prompt_local) % CLEN
    )
    cosine, sine = rope_tables(positions, 128)
    normed_one, turned_query, *kv_low, qkv_full, output_t, rest, gain_rows = project(
        layer_input[0], cosine, sine, pieces, counts, block_places
    )
    router_full = rest[:, :EXPERTS]
    first_gain, second_gain = gain_rows[0], gain_rows[1]
    inverse_one = lax.rsqrt(jnp.mean(inputs * inputs, -1, keepdims=True) + norm_eps)
    kv_own = [low[prompt_local:] for low in kv_low]
    kv_pieces = [gather_ctx(low[:prompt_local]) for low in kv_low]

    places = deal_row
    if context_size == 8:
        pairs = deal_row.reshape(2, 2, 2, 2)
        for axis, bit in ((0, 4), (1, 2), (2, 1)):
            pairs = jnp.where(ctx_index & bit > 0, jnp.flip(pairs, axis), pairs)
        places = pairs.reshape(-1)
    low = (mine[0] > mine[1]).astype(jnp.int32)
    starts = jnp.stack(
        [
            low * block_rows,
            (1 - low) * block_rows,
            jnp.min(mine) * block_rows,
            jnp.max(mine) * block_rows,
        ]
    ).astype(jnp.int32)
    heads = []
    for half in range(2):
        result = attention_forward(
            turned_query, kv_pieces[half], kv_own[half], places, starts, block_rows, half
        )
        d = last - 1 - half
        grads_in[d] = shift(grads_in[d + 1], -1)
        result, grads_in[d] = beside(result, grads_in[d])
        if half == 0:
            turned_query = after(turned_query, result[0])
        heads.append(result)
    for d in range(last - 3, 0, -1):
        grads_in[d] = shift(grads_in[d + 1], -1)
    attended = jnp.concatenate([out for out, _ in heads], 1)
    lse = [row for _, row in heads]

    branch = dot_nt(attended, output_t)
    middle = inputs + resid_scale * branch
    normed_mid, inverse_two = norm_forward(middle, second_gain)
    normed_two = normed_mid.astype(bf16)
    logits = dot(normed_two, router_full)
    top = jnp.max(jnp.where(mask, logits, masked_score), -1, keepdims=True)
    raised = jnp.where(mask, jnp.exp(jnp.where(mask, logits - top, 0.0)), 0.0)
    gates = raised / jnp.sum(raised, -1, keepdims=True)

    gates_out = gates.T.reshape(shard_count, expert_count, tok)
    gates_in = []
    for d in range(shard_count):
        piece = lax.dynamic_index_in_dim(gates_out, (wt_index + d) % shard_count, 0, False)
        gates_in.append(shift(piece, d) if d else piece)
    got = {0: normed_two}
    partial, mixed, gate_grads, rows = {}, {}, {}, []
    carried = None

    def add(a, b):
        return b if a is None else (a.astype(f32) + b.astype(f32)).astype(bf16)

    for d in [0] + list(range(last, 0, -1)):
        source = (wt_index - d) % shard_count
        rank_in = lax.dynamic_index_in_dim(ranks, source, 0, False)
        result = expert_pass(
            got[d], grads_in[d], rank_in, gates_in[d], gate_full, up_full, down_full, capacity
        )
        coming = d - 1 if d else last
        if coming:
            result, got[coming] = beside(result, shift(got[(coming + 1) % shard_count], -1))
        if 0 < d <= last - 2:
            carried = shift(after(add(carried, partial[d + 2]), got[d]), -1)
            result, carried = beside(result, carried)
        mixed[d], partial[d], d_gate, *kept = result
        rows.append(kept)
        d_gate = d_gate.reshape(expert_count, tok)
        gate_grads[d] = shift(d_gate, shard_count - d) if d else d_gate
        if coming:
            got[coming] = after(got[coming], partial[d])
    carried = shift(add(carried, partial[2]), -1)
    (gate_grad, up_grad), carried = beside(
        up_weight_grads([(after(r[0], partial[1]), r[3], r[4]) for r in rows], context_size),
        carried,
    )
    carried = shift(add(carried, partial[1]), -1)
    down_grad, carried = beside(
        down_weight_grads([(after(r[2], gate_grad), r[1]) for r in rows], context_size), carried
    )

    stacked = jnp.stack([gate_grads[d] for d in range(shard_count)], 0)
    stacked = jnp.roll(stacked, wt_index, 0).reshape(EXPERTS, tok).T
    grad_logits = (gates * (stacked - jnp.sum(gates * stacked, -1, keepdims=True))).astype(bf16)
    grad_normed_two = partial[0].astype(f32) + carried.astype(f32)
    grad_normed_two = grad_normed_two + dot_nt(grad_logits, router_full)
    grad_mid_norm, second_gain_grad = norm_backward(
        middle, inverse_two, second_gain, grad_normed_two
    )
    grad_middle = out_grad + grad_mid_norm
    grad_branch = (resid_scale * grad_middle).astype(bf16)
    grad_attended = dot(grad_branch, output_t).astype(bf16)
    gate_share, up_share, down_share = (
        lax.psum_scatter(grad, "ctx", scatter_dimension=0, tiled=False).astype(f32)
        for grad in (gate_grad, up_grad, down_grad)
    )
    output_share = outer_sum(grad_branch, attended)
    devices = context_size * shard_count
    small = jnp.concatenate(
        [
            dot_tn(normed_two, grad_logits).reshape(devices, own_rows * EXPERTS),
            second_gain_grad.reshape(devices, own_rows),
        ],
        1,
    )
    small = spread_sum(small)

    d_query, owned, ours = [], [], []
    carried = None
    query = after(turned_query, grad_attended)
    for half in range(2):
        result = attention_backward(
            query,
            grad_attended,
            lse[half],
            attended,
            cosine,
            sine,
            kv_pieces[half],
            kv_own[half],
            places,
            starts,
            block_rows,
            half,
        )
        d = last - half
        carried = shift(after(add(carried, mixed[d]), query), -1)
        result, carried = beside(result, carried)
        d_q, d_kv, d_key_own, d_value_own = result
        query = after(query, d_q)
        d_query.append(d_q)
        owned.append(scatter_ctx(d_kv))
        ours.append((d_key_own, d_value_own))
    for d in range(last - 2, 0, -1):
        carried = shift(add(carried, mixed[d]), -1)
    mixture = mixed[0].astype(f32) + carried.astype(f32)
    layer_output = (middle + resid_scale * mixture).astype(bf16)
    d_key, d_value = (
        jnp.concatenate(
            [
                jnp.concatenate([owned[half][:, 256 * n : 256 * n + 256], ours[half][n]], 0)
                for half in range(2)
            ],
            1,
        )
        for n in range(2)
    )
    grad_key_low = turn(d_key, jnp.tile(cosine, (1, 4)), jnp.tile(sine, (1, 4)), -1.0).astype(
        bf16
    )
    grad_qkv = jnp.concatenate(d_query + [grad_key_low, d_value.astype(bf16)], 1)
    grad_qkv, layer_output = beside(grad_qkv, layer_output)
    qkv_share = outer_sum(normed_one, grad_qkv)
    grad_normed_one = dot_nt(grad_qkv, qkv_full)
    grad_input_norm, first_gain_grad = norm_backward(
        inputs, inverse_one, first_gain, grad_normed_one
    )
    input_grad = (grad_middle + grad_input_norm).astype(bf16)

    first_gain_share = spread_sum(first_gain_grad.reshape(devices, own_rows))
    return (
        layer_output[None],
        input_grad[None],
        first_gain_share,
        qkv_share[:, :1024],
        qkv_share[:, 1024:1536],
        qkv_share[:, 1536:],
        output_share.T,
        small[own_rows * EXPERTS :],
        small[: own_rows * EXPERTS].reshape(own_rows, EXPERTS),
        gate_share,
        up_share,
        down_share,
    )


def solution(mesh):
    return jax.shard_map(
        per_device,
        mesh=mesh,
        in_specs=(
            P("wt", "ctx", None),
            P(("ctx", "wt")),
            P(("ctx", "wt"), None),
            P(("ctx", "wt"), None),
            P(("ctx", "wt"), None),
            P(None, ("ctx", "wt")),
            P(("ctx", "wt")),
            P(("ctx", "wt"), None),
            P("wt", "ctx", None),
            P("wt", "ctx", None),
            P("wt", None, "ctx"),
            P("wt", "ctx", None),
            P("wt", None),
            P("wt", "ctx", None),
        ),
        out_specs=(
            P("wt", "ctx", None),
            P("wt", "ctx", None),
            P(("ctx", "wt")),
            P(("ctx", "wt"), None),
            P(("ctx", "wt"), None),
            P(("ctx", "wt"), None),
            P(None, ("ctx", "wt")),
            P(("ctx", "wt")),
            P(("ctx", "wt"), None),
            P("wt", "ctx", None),
            P("wt", "ctx", None),
            P("wt", None, "ctx"),
        ),
        check_vma=False,
    )
```

time: 1040 us -> 955 us (0.918)
  waiting for transfers between devices: 327 us -> 275 us
  Pallas kernels: 447 us -> 399 us
  starting transfers between devices: 96.8 us -> 118 us
  local copies, waits for them, and re-layouts: 60.3 us -> 45.8 us
    all_to_all x2, waiting for transfers between devices: 105 us -> 0.01 us  [spread_sum(): return jnp.sum(lax.all_to_all(x, ALL, 0, 0, tiled=True), 0)]
    pallas_call x5 -> x6, Pallas kernels: 262 us -> 220 us  [the longest x4 156 us: expert_pass(): pl.pallas_call(functools.partial(expert_kernel, sizes=sizes), grid_spec=p...]
    all_to_all x1, waiting for transfers between devices: 0.01 us -> 31.9 us  [per_device(): lax.all_to_all(rank.T.reshape(shard_count, expert_count, tok), 'wt', 0, 0...]
    unnamed x178 -> x182, local copies, waits for them, and re-layouts: 27.9 us -> 10 us
    convert_element_type x4 -> x12, other arithmetic: 9.44 us -> 26.6 us  [the longest x4 14.2 us: add(): return b if a is None else (a.astype(f32) + b.astype(f32)).astype(bf16)]
    ppermute x48 -> x64, waiting for transfers between devices: 80.8 us -> 94.5 us  [swap(): lax.ppermute(x, 'ctx', [(i, i ^ mask) for i in range(lax.axis_size('ctx'))])]
    ppermute x48 -> x64, starting transfers between devices: 34.9 us -> 48 us  [swap(): lax.ppermute(x, 'ctx', [(i, i ^ mask) for i in range(lax.axis_size('ctx'))])]
    pallas_call x1 -> x2, Pallas kernels: 60.7 us -> 53.4 us  [attention_forward(): pl.pallas_call(functools.partial(attention_forward_kernel, block_rows=blo...]
  transfers between devices with their start and end apart: 84 -> 100, of which waited for: 19 -> 35; matrix products, arithmetic and copies ran while one was open for 12% -> 13% of each run, Pallas kernels for 33% -> 42%
where the time goes in v2:
time: 955 us; the launch traced here: 947 us
  Pallas kernels  399 us (42%)
  waiting for transfers between devices  275 us (29%)
  starting transfers between devices  118 us (12%)
  other arithmetic  66.7 us (7%)
  local copies, waits for them, and re-layouts  45.8 us (5%)
  matrix products  24.1 us (3%)
  between operations  18.7 us (2%)
    pallas_call x4, Pallas kernels, expert_pass(): pl.pallas_call(functools.partial(expert_kernel, sizes=sizes), grid_spec=p...  156 us
    ppermute x27, waiting for transfers between devices, shift(): return lax.ppermute(x, 'wt', [(i, (i + distance) % n) for i in range(n)])  146 us
    pallas_call x2, Pallas kernels, attention_backward(): pl.pallas_call(functools.partial(attention_backward_kernel, block_rows=bl...  96.9 us
    ppermute x64, waiting for transfers between devices, swap(): lax.ppermute(x, 'ctx', [(i, i ^ mask) for i in range(lax.axis_size('ctx'))])  94.5 us
    ppermute x27, starting transfers between devices, shift(): return lax.ppermute(x, 'wt', [(i, (i + distance) % n) for i in range(n)])  58.6 us
    pallas_call x2, Pallas kernels, attention_forward(): pl.pallas_call(functools.partial(attention_forward_kernel, block_rows=blo...  53.4 us
    ppermute x64, starting transfers between devices, swap(): lax.ppermute(x, 'ctx', [(i, i ^ mask) for i in range(lax.axis_size('ctx'))])  48 us
    pallas_call x1, Pallas kernels, up_weight_grads(): pl.pallas_call(functools.partial(up_grad_kernel, sources=len(rows)), grid...  40.6 us
  transfers between devices with their start and end apart: 100, of which 35 were waited for; matrix products, arithmetic and copies ran while one was open for 13% of the time, Pallas kernels for 42%

profile of v2, /device:TPU:0, one launch (start us, length us, event | category | flops | bytes accessed | tf_op | source)
XLA Modules:
  0.0 947.2 jit_solution(16410837759015785356)
XLA Ops:
  21.8 7.9 collective-permute-done.9
  41.1 12.6 %collective-permute-done.12.refs_10_ = bf16[96,3200]{1,0:T(8,128)(2,1)S(1)} collective-permute-done((bf16[96,3200]{1,0:T(8,128)(2,1)S(1)}, bf16[96,3200]{1,0:T(8,128)(2,1)S(1)}, u32[]{:S(2)}, u32[]{:S(2)}) %collective-permute-start.12) | collective-permute-done | bytes 614432 | tf_op jit(solution)/shard_map/ppermute | solution.py:577
  60.8 13.1 %collective-permute-done.16 = bf16[48,3200]{1,0:T(8,128)(2,1)S(1)} collective-permute-done((bf16[48,3200]{1,0:T(8,128)(2,1)S(1)}, bf16[48,3200]{1,0:T(8,128)(2,1)S(1)}, u32[]{:S(2)}, u32[]{:S(2)}) %collective-permute-start.16) | collective-permute-done | bytes 307232 | tf_op jit(solution)/shard_map/ppermute | solution.py:577
  92.2 11.3 %project.1 = (bf16[768,1024]{1,0:T(8,128)(2,1)}, bf16[768,1024]{1,0:T(8,128)(2,1)}, bf16[768,512]{1,0:T(8,128)(2,1)}, bf16[768,512]{1,0:T(8,128)(2,1)}, bf16[102...) custom-call(s32[32]{0:T(128)} %pad_add_fusion.1.places, ...), custom_call_target="tpu_custom_call" | custom-call | flops 1000000000 | bytes 1000000 | tf_op jit(solution)/shard_map/project/pallas_call | solution.py:95
  128.4 26.7 %attention_forward.2 = (bf16[768,512]{1,0:T(8,128)(2,1)}, f32[2,4,768]{2,1,0:T(4,128)}) custom-call(s32[16]{0:T(128)} %reshape.273.places, s32[4]{0:T(128)} %pad_add_fusion.starts, bf16[768,1024]{1,0:T(8,128)(2,1)} %get-tuple-element.283.q_ref, bf16[256,512]{1,0:T(8,128)(2,1)} %copy-done.6, bf16[256,512]{1,0:T(8,128)(2,1)} %copy-done.20, ...), custom_call_target="tpu_custom_call" | custom-call | flops 1000000000 | bytes 1000000 | tf_op jit(solution)/shard_map/attention_forward/pallas_call | solution.py:220
  158.9 11.3 %collective-permute-done.30.refs_2_.refs_10_ = bf16[256,512]{1,0:T(8,128)(2,1)S(1)} collective-permute-done((bf16[256,512]{1,0:T(8,128)(2,1)S(1)}, bf16[256,512]{1,0:T(8,128)(2,1)S(1)}, u32[]{:S(2)}, u32[]{:S(2)}) %collective-permute-start.30) | collective-permute-done | bytes 262176 | tf_op jit(solution)/shard_map/ppermute | solution.py:577
  182.0 26.7 %attention_forward.3 = (bf16[768,512]{1,0:T(8,128)(2,1)}, f32[2,4,768]{2,1,0:T(4,128)}) custom-call(s32[16]{0:T(128)} %reshape.273.places, s32[4]{0:T(128)} %pad_add_fusion.starts, bf16[768,1024]{1,0:T(8,128)(2,1)} %get-tuple-element.283.q_ref, bf16[256,512]{1,0:T(8,128)(2,1)} %copy-done.7, bf16[256,512]{1,0:T(8,128)(2,1)} %copy-done.23, ...), custom_call_target="tpu_custom_call" | custom-call | flops 1000000000 | bytes 1000000 | tf_op jit(solution)/shard_map/attention_forward/pallas_call | solution.py:220
  225.6 31.9 %all-to-all-done = f32[4,8,768]{2,1,0:T(8,128)S(1)} async-done(((f32[4,8,768]{2,1,0:T(8,128)}), f32[4,8,768]{2,1,0:T(8,128)S(1)}, u32[]{:S(2)}, u32[]{:S(2)}) %all-to-all-start) | async-done | bytes 98336 | tf_op jit(solution)/shard_map/all_to_all | solution.py:748
  263.4 40.6 %expert_pass.4 = (bf16[768,1024]{1,0:T(8,128)(2,1)}, bf16[768,1024]{1,0:T(8,128)(2,1)}, f32[8,1,768]{2,1,0:T(1,128)}, bf16[8,336,1024]{2,1,0:T(8,128)(2,1)}, bf1...) custom-call(s32[8]{0:T(128)} %add_convert_fusion.12.counts, ...), custom_call_target="tpu_custom_call" | custom-call | flops 1000000000 | bytes 1000000 | tf_op jit(solution)/shard_map/expert_pass/pallas_call | solution.py:490
  309.8 32.4 %collective-permute-done.39 = f32[8,768]{1,0:T(8,128)S(1)} collective-permute-done((f32[8,768]{1,0:T(8,128)S(1)}, f32[8,768]{1,0:T(8,128)S(1)}, u32[]{:S(2)}, u32[]{:S(2)}) %collective-permute-start.39) | collective-permute-done | bytes 24608 | tf_op jit(solution)/shard_map/ppermute | solution.py:614
  342.8 38.4 %expert_pass.5 = (bf16[768,1024]{1,0:T(8,128)(2,1)}, bf16[768,1024]{1,0:T(8,128)(2,1)}, f32[8,1,768]{2,1,0:T(1,128)}, bf16[8,336,1024]{2,1,0:T(8,128)(2,1)}, bf1...) custom-call(s32[8]{0:T(128)} %add_convert_fusion.9.counts, ...), custom_call_target="tpu_custom_call" | custom-call | flops 1000000000 | bytes 1000000 | tf_op jit(solution)/shard_map/expert_pass/pallas_call | solution.py:490
  388.1 32.4 %collective-permute-done.41 = f32[8,768]{1,0:T(8,128)S(1)} collective-permute-done((f32[8,768]{1,0:T(8,128)S(1)}, f32[8,768]{1,0:T(8,128)S(1)}, u32[]{:S(2)}, u32[]{:S(2)}) %collective-permute-start.41) | collective-permute-done | bytes 24608 | tf_op jit(solution)/shard_map/ppermute | solution.py:614
  421.0 37.9 %expert_pass.6 = (bf16[768,1024]{1,0:T(8,128)(2,1)}, bf16[768,1024]{1,0:T(8,128)(2,1)}, f32[8,1,768]{2,1,0:T(1,128)}, bf16[8,336,1024]{2,1,0:T(8,128)(2,1)}, bf1...) custom-call(s32[8]{0:T(128)} %add_convert_fusion.10.counts, ...), custom_call_target="tpu_custom_call" | custom-call | flops 1000000000 | bytes 1000000 | tf_op jit(solution)/shard_map/expert_pass/pallas_call | solution.py:490
  467.5 31.3 %collective-permute-done.43 = f32[8,768]{1,0:T(8,128)S(1)} collective-permute-done((f32[8,768]{1,0:T(8,128)S(1)}, f32[8,768]{1,0:T(8,128)S(1)}, u32[]{:S(2)}, u32[]{:S(2)}) %collective-permute-start.43) | collective-permute-done | bytes 24608 | tf_op jit(solution)/shard_map/ppermute | solution.py:614
  499.5 38.9 %expert_pass.7 = (bf16[768,1024]{1,0:T(8,128)(2,1)}, bf16[768,1024]{1,0:T(8,128)(2,1)}, f32[8,1,768]{2,1,0:T(1,128)}, bf16[8,336,1024]{2,1,0:T(8,128)(2,1)}, bf1...) custom-call(s32[8]{0:T(128)} %add_convert_fusion.11.counts, ...), custom_call_target="tpu_custom_call" | custom-call | flops 1000000000 | bytes 1000000 | tf_op jit(solution)/shard_map/expert_pass/pallas_call | solution.py:490
  542.1 40.6 %up_weight_grads.1 = (bf16[8,8,128,512]{3,2,1,0:T(8,128)(2,1)}, bf16[8,8,128,512]{3,2,1,0:T(8,128)(2,1)}) custom-call(bf16[8,336,1024]{2,1,0:T(8,128)(2,1)} %get-tuple-element.238.refs_0_, bf16[8,336,512]{2,1,0:T(8,128)(2,1)} %get-tuple-element.239.refs_1_, bf16[8,336,512]{2,1,0:T(8,128)(2,1)} %get-tuple-element.240.refs_2_, ...), custom_call_target="tpu_custom_call" | custom-call | flops 1000000000 | bytes 1000000 | tf_op jit(solution)/shard_map/up_weight_grads/pallas_call | solution.py:549
  600.3 23.9 %down_weight_grads.1 = bf16[8,8,512,128]{3,2,1,0:T(8,128)(2,1)} custom-call(bf16[8,336,512]{2,1,0:T(8,128)(2,1)} %get-tuple-element.257.refs_0_, bf16[8,336,1024]{2,1,0:T(8,128)(2,1)} %get-tuple-element.258.refs_1_, bf16[8,336,512]{2,1,0:T(8,128)(2,1)} %get-tuple-element.260.refs_2_, bf16[8,336,1024]{2,1,0:T(8,128)(2,1)} %get-tuple-element.261.refs_3_, ...), custom_call_target="tpu_custom_call" | custom-call | flops 1000000000 | bytes 1000000 | tf_op jit(solution)/shard_map/down_weight_grads/pallas_call | solution.py:564
  624.2 8.9 collective-permute-done.46
  647.9 7.6 outer.3
  675.3 48.5 %attention_backward.2 = (bf16[768,512]{1,0:T(8,128)(2,1)}, bf16[2048,512]{1,0:T(8,128)(2,1)}, f32[512,256]{1,0:T(8,128)}, f32[512,256]{1,0:T(8,128)}) custom-call(s32[16]{0:T(128)} %reshape.273.places, s32[4]{0:T(128)} %pad_add_fusion.starts, bf16[768,1024]{1,0:T(8,128)(2,1)} %get-tuple-element.283.q_ref, bf16[768,1024]{1,0:T(8,128)(2,1)} %convolution_convert_fusion.do_ref, ...), custom_call_target="tpu_custom_call" | custom-call | flops 1000000000 | bytes 1000000 | tf_op jit(solution)/shard_map/attention_backward/pallas_call | solution.py:364
  737.0 48.5 %attention_backward.3 = (bf16[768,512]{1,0:T(8,128)(2,1)}, bf16[2048,512]{1,0:T(8,128)(2,1)}, f32[512,256]{1,0:T(8,128)}, f32[512,256]{1,0:T(8,128)}) custom-call(s32[16]{0:T(128)} %reshape.273.places, s32[4]{0:T(128)} %pad_add_fusion.starts, bf16[768,1024]{1,0:T(8,128)(2,1)} %get-tuple-element.283.q_ref, bf16[768,1024]{1,0:T(8,128)(2,1)} %convolution_convert_fusion.do_ref, ...), custom_call_target="tpu_custom_call" | custom-call | flops 1000000000 | bytes 1000000 | tf_op jit(solution)/shard_map/attention_backward/pallas_call | solution.py:364
  798.3 10.2 %collective-permute-done.56 = bf16[256,512]{1,0:T(8,128)(2,1)S(1)} collective-permute-done((bf16[256,512]{1,0:T(8,128)(2,1)S(1)}, bf16[256,512]{1,0:T(8,128)(2,1)S(1)}, u32[]{:S(2)}, u32[]{:S(2)}) %collective-permute-start.56) | collective-permute-done | bytes 262176 | tf_op jit(solution)/shard_map/ppermute | solution.py:577
  830.5 26.6 %collective-permute-done.68 = bf16[768,1024]{1,0:T(8,128)(2,1)S(1)} collective-permute-done((bf16[768,1024]{1,0:T(8,128)(2,1)S(1)}, bf16[768,1024]{1,0:T(8,128)(2,1)S(1)}, u32[]{:S(2)}, u32[]{:S(2)}) %collective-permute-start.68) | collective-permute-done | bytes 1572896 | tf_op jit(solution)/shard_map/ppermute | solution.py:614
  859.1 9.3 outer.2
  (537 shorter events, 311.0 us)
Async XLA Ops:
  7.2 256.1 %all-gather.7.cloned.1.call-start = ((), (), s32[]{:S(2)}) async-start(), calls=%async_computation.9 | async-start | bytes 9437184 | tf_op jit(solution)/shard_map/all_gather | solution.py:738
  8.0 255.3 %all-gather.9.cloned.1.call-start = ((), (), s32[]{:S(2)}) async-start(), calls=%async_computation.10 | async-start | bytes 9437184 | tf_op jit(solution)/shard_map/all_gather | solution.py:739
  8.7 254.6 %all-gather.11.cloned.1.call-start = ((), (), s32[]{:S(2)}) async-start(), calls=%async_computation.11 | async-start | bytes 9437184 | tf_op jit(solution)/shard_map/all_gather | solution.py:740
  21.8 60.4 %collective-permute-start = (bf16[32,3200]{1,0:T(8,128)(2,1)}, bf16[32,3200]{1,0:T(8,128)(2,1)}, u32[]{:S(2)}, u32[]{:S(2)}) collective-permute-start(bf16[32,3200]{1,0:T(8,128)(2,1)} %concatenate.88.refs_0_), channel_id=1, source_target_pairs={{0,4},{4,0},{8,12},{12,8},{16,20},{20,16},{24,28},{28,24},{1,5},{5... | collective-permute-start | bytes 614408 | tf_op jit(solution)/shard_map/ppermute | solution.py:577
  33.6 53.8 %collective-permute-start.19 = (bf16[768,1024]{1,0:T(8,128)(2,1)S(1)}, bf16[768,1024]{1,0:T(8,128)(2,1)}, u32[]{:S(2)}, u32[]{:S(2)}) collective-permute-start(bf16[768,1024]{1,0:T(8,128)(2,1)S(1)} %bitcast.146), channel_id=1, source_target_pairs={{0,3},{1,0},{2,1},{3,2},{4,7},{5,4},{6,5},{7,6},{8,11},{9,8},{10,9... | collective-permute-start | bytes 4718600 | tf_op jit(solution)/shard_map/ppermute | solution.py:614
  87.4 67.7 %collective-permute-start.28 = (bf16[768,1024]{1,0:T(8,128)(2,1)}, bf16[768,1024]{1,0:T(8,128)(2,1)}, u32[]{:S(2)}, u32[]{:S(2)}) collective-permute-start(bf16[768,1024]{1,0:T(8,128)(2,1)} %collective-permute-done.19.df_ref), channel_id=1, source_target_pairs={{0,3},{1,0},{2,1},{3,2},{4,7},{5,4},{6,5},{7,6},{8,11},{9,8},{10,9... | collective-permute-start | bytes 4718600 | tf_op jit(solution)/shard_map/ppermute | solution.py:614
  155.1 55.0 %collective-permute-start.37 = (bf16[768,1024]{1,0:T(8,128)(2,1)}, bf16[768,1024]{1,0:T(8,128)(2,1)S(1)}, u32[]{:S(2)}, u32[]{:S(2)}) collective-permute-start(bf16[768,1024]{1,0:T(8,128)(2,1)} %collective-permute-done.28.df_ref), channel_id=1, source_target_pairs={{0,3},{1,0},{2,1},{3,2},{4,7},{5,4},{6,5},{7,6},{8,11},{9,8},{10,9... | collective-permute-start | bytes 4718600 | tf_op jit(solution)/shard_map/ppermute | solution.py:614
  217.7 86.2 %collective-permute-start.38 = (bf16[768,1024]{1,0:T(8,128)(2,1)}, bf16[768,1024]{1,0:T(8,128)(2,1)}, u32[]{:S(2)}, u32[]{:S(2)}) collective-permute-start(bf16[768,1024]{1,0:T(8,128)(2,1)} %multiply_convert_fusion.1.a2_ref), channel_id=1, source_target_pairs={{0,3},{1,0},{2,1},{3,2},{4,7},{5,4},{6,5},{7,6},{8,11},{9,8},{10,9... | collective-permute-start | bytes 4718600 | tf_op jit(solution)/shard_map/ppermute | solution.py:614
  225.4 706.4 %reduce-scatter.6.cloned.1.call-start = ((), (), s32[]{:S(2)}) async-start(), calls=%async_computation.7 | async-start | bytes 9437184 | tf_op jit(solution)/shard_map/reduce_scatter | solution.py:866
  304.0 77.3 %collective-permute-start.40 = (bf16[768,1024]{1,0:T(8,128)(2,1)}, bf16[768,1024]{1,0:T(8,128)(2,1)}, u32[]{:S(2)}, u32[]{:S(2)}) collective-permute-start(bf16[768,1024]{1,0:T(8,128)(2,1)} %collective-permute-done.38.a2_ref), channel_id=1, source_target_pairs={{0,3},{1,0},{2,1},{3,2},{4,7},{5,4},{6,5},{7,6},{8,11},{9,8},{10,9... | collective-permute-start | bytes 4718600 | tf_op jit(solution)/shard_map/ppermute | solution.py:614
  381.3 77.7 %collective-permute-start.42 = (bf16[768,1024]{1,0:T(8,128)(2,1)}, bf16[768,1024]{1,0:T(8,128)(2,1)}, u32[]{:S(2)}, u32[]{:S(2)}) collective-permute-start(bf16[768,1024]{1,0:T(8,128)(2,1)} %collective-permute-done.40.a2_ref), channel_id=1, source_target_pairs={{0,3},{1,0},{2,1},{3,2},{4,7},{5,4},{6,5},{7,6},{8,11},{9,8},{10,9... | collective-permute-start | bytes 4718600 | tf_op jit(solution)/shard_map/ppermute | solution.py:614
  458.9 79.5 %collective-permute-start.44 = (bf16[768,1024]{1,0:T(8,128)(2,1)}, bf16[768,1024]{1,0:T(8,128)(2,1)}, u32[]{:S(2)}, u32[]{:S(2)}) collective-permute-start(bf16[768,1024]{1,0:T(8,128)(2,1)} %get-tuple-element.236), channel_id=1, source_target_pairs={{0,3},{1,0},{2,1},{3,2},{4,7},{5,4},{6,5},{7,6},{8,11},{9,8},{10,9... | collective-permute-start | bytes 4718600 | tf_op jit(solution)/shard_map/ppermute | solution.py:614
  542.1 40.6 %collective-permute-start.45 = (bf16[768,1024]{1,0:T(8,128)(2,1)}, bf16[768,1024]{1,0:T(8,128)(2,1)}, u32[]{:S(2)}, u32[]{:S(2)}) collective-permute-start(bf16[768,1024]{1,0:T(8,128)(2,1)} %add_convert_fusion.4), channel_id=1, source_target_pairs={{0,3},{1,0},{2,1},{3,2},{4,7},{5,4},{6,5},{7,6},{8,11},{9,8},{10,9... | collective-permute-start | bytes 4718600 | tf_op jit(solution)/shard_map/ppermute | solution.py:614
  582.7 351.9 %reduce-scatter.4.cloned.1.call-start = ((), (), s32[]{:S(2)}) async-start(), calls=%async_computation.6 | async-start | bytes 9437184 | tf_op jit(solution)/shard_map/reduce_scatter | solution.py:866
  583.3 354.2 %reduce-scatter.8.cloned.1.call-start = ((), (), s32[]{:S(2)}) async-start(), calls=%async_computation.8 | async-start | bytes 9437184 | tf_op jit(solution)/shard_map/reduce_scatter | solution.py:866
  643.5 82.4 %collective-permute-start.50 = (bf16[768,1024]{1,0:T(8,128)(2,1)}, bf16[768,1024]{1,0:T(8,128)(2,1)}, u32[]{:S(2)}, u32[]{:S(2)}) collective-permute-start(bf16[768,1024]{1,0:T(8,128)(2,1)} %get-tuple-element.281), channel_id=1, source_target_pairs={{0,3},{1,0},{2,1},{3,2},{4,7},{5,4},{6,5},{7,6},{8,11},{9,8},{10,9... | collective-permute-start | bytes 4718600 | tf_op jit(solution)/shard_map/ppermute | solution.py:614
  664.4 60.5 %collective-permute-start.83 = (bf16[64,1024]{1,0:T(8,128)(2,1)}, bf16[64,1024]{1,0:T(8,128)(2,1)}, u32[]{:S(2)}, u32[]{:S(2)}) collective-permute-start(bf16[64,1024]{1,0:T(8,128)(2,1)} %get-tuple-element.367), channel_id=1, source_target_pairs={{0,16},{4,20},{8,24},{12,28},{16,0},{20,4},{24,8},{28,12},{1,17},{... | collective-permute-start | bytes 393224 | tf_op jit(solution)/shard_map/ppermute | solution.py:577
  675.0 196.4 %collective-permute-start.80 = (bf16[128,1024]{1,0:T(8,128)(2,1)}, bf16[128,1024]{1,0:T(8,128)(2,1)S(1)}, u32[]{:S(2)}, u32[]{:S(2)}) collective-permute-start(bf16[128,1024]{1,0:T(8,128)(2,1)} %get-tuple-element.336), channel_id=1, source_target_pairs={{0,4},{4,0},{8,12},{12,8},{16,20},{20,16},{24,28},{28,24},{1,5},{5... | collective-permute-start | bytes 786440 | tf_op jit(solution)/shard_map/ppermute | solution.py:577
  729.8 64.0 %collective-permute-start.51 = (bf16[768,1024]{1,0:T(8,128)(2,1)}, bf16[768,1024]{1,0:T(8,128)(2,1)}, u32[]{:S(2)}, u32[]{:S(2)}) collective-permute-start(bf16[768,1024]{1,0:T(8,128)(2,1)} %add_convert_fusion.2), channel_id=1, source_target_pairs={{0,3},{1,0},{2,1},{3,2},{4,7},{5,4},{6,5},{7,6},{8,11},{9,8},{10,9... | collective-permute-start | bytes 4718600 | tf_op jit(solution)/shard_map/ppermute | solution.py:614
  735.0 50.5 %collective-permute-start.53 = (bf16[256,512]{1,0:T(8,128)(2,1)}, bf16[256,512]{1,0:T(8,128)(2,1)S(1)}, u32[]{:S(2)}, u32[]{:S(2)}) collective-permute-start(bf16[256,512]{1,0:T(8,128)(2,1)} %get-tuple-element.346), channel_id=1, source_target_pairs={{0,4},{4,0},{8,12},{12,8},{16,20},{20,16},{24,28},{28,24},{1,5},{5... | collective-permute-start | bytes 786440 | tf_op jit(solution)/shard_map/ppermute | solution.py:577
  735.0 51.1 %collective-permute-start.54 = (bf16[256,512]{1,0:T(8,128)(2,1)}, bf16[256,512]{1,0:T(8,128)(2,1)}, u32[]{:S(2)}, u32[]{:S(2)}) collective-permute-start(bf16[256,512]{1,0:T(8,128)(2,1)} %get-tuple-element.345), channel_id=1, source_target_pairs={{0,4},{4,0},{8,12},{12,8},{16,20},{20,16},{24,28},{28,24},{1,5},{5... | collective-permute-start | bytes 786440 | tf_op jit(solution)/shard_map/ppermute | solution.py:577
  735.5 50.7 %collective-permute-start.57 = (bf16[256,512]{1,0:T(8,128)(2,1)}, bf16[256,512]{1,0:T(8,128)(2,1)}, u32[]{:S(2)}, u32[]{:S(2)}) collective-permute-start(bf16[256,512]{1,0:T(8,128)(2,1)} %get-tuple-element.344), channel_id=1, source_target_pairs={{0,4},{4,0},{8,12},{12,8},{16,20},{20,16},{24,28},{28,24},{1,5},{5... | collective-permute-start | bytes 786440 | tf_op jit(solution)/shard_map/ppermute | solution.py:577
  822.2 55.1 %collective-permute-start.84 = (bf16[128,1024]{1,0:T(8,128)(2,1)}, bf16[128,1024]{1,0:T(8,128)(2,1)}, u32[]{:S(2)}, u32[]{:S(2)}) collective-permute-start(bf16[128,1024]{1,0:T(8,128)(2,1)} %pad_maximum_fusion.8), channel_id=1, source_target_pairs={{0,8},{4,12},{8,0},{12,4},{16,24},{20,28},{24,16},{28,20},{1,9},{5... | collective-permute-start | bytes 786440 | tf_op jit(solution)/shard_map/ppermute | solution.py:577
  823.7 53.6 %collective-permute-start.87 = (bf16[128,1024]{1,0:T(8,128)(2,1)}, bf16[128,1024]{1,0:T(8,128)(2,1)}, u32[]{:S(2)}, u32[]{:S(2)}) collective-permute-start(bf16[128,1024]{1,0:T(8,128)(2,1)} %pad_maximum_fusion.9), channel_id=1, source_target_pairs={{0,16},{4,20},{8,24},{12,28},{16,0},{20,4},{24,8},{28,12},{1,17},{... | collective-permute-start | bytes 786440 | tf_op jit(solution)/shard_map/ppermute | solution.py:577
  (157 other events, 1972.4 us)
Sparse Core Ops, SparseCore 0:
  10.0 72.5 all-gather.6
  84.5 56.9 all-gather.8
  143.3 59.2 all-gather.10
  582.8 75.1 reduce-scatter.5
  661.8 73.9 reduce-scatter.3
  739.1 80.6 reduce-scatter.7

commit v3 on v2

--- a/solution.py
+++ b/solution.py
@@ -578,10 +578,17 @@
 
 
 def blocks_ctx(x):
+    return both_cores(even_blocks(x))
+
+
+def even_blocks(x):
     half = x.shape[0] // 2
     near, far = swap(x, 2), swap(x, 4)
     diagonal = jnp.concatenate([swap(near[:half], 4), swap(far[half:], 2)], 0)
-    even = [x, near, far, diagonal]
+    return [x, near, far, diagonal]
+
+
+def both_cores(even):
     odd = [swap(block, 1) for block in even]
     return [b for pair in zip(even, odd) for b in pair]
 
@@ -634,13 +641,18 @@
     return pieces, [1] * 8 + [3] * 8, places, others
 
 
-def outer_sum(a, b):
-    ctx, wt = lax.axis_size("ctx"), lax.axis_size("wt")
-    if ctx != 8 or wt != 4:
+def outer_part(a, b):
+    if lax.axis_size("ctx") != 8 or lax.axis_size("wt") != 4:
+        return dot_tn(a, b)
+    return scatter_ctx(outer(a, b))
+
+
+def row_sum(part):
+    wt = lax.axis_size("wt")
+    if lax.axis_size("ctx") != 8 or wt != 4:
         return lax.psum_scatter(
-            dot_tn(a, b).astype(bf16), ALL, scatter_dimension=0, tiled=True
+            part.astype(bf16), ALL, scatter_dimension=0, tiled=True
         ).astype(f32)
-    part = scatter_ctx(outer(a, b))
     rows = part.shape[0] // wt
     low = part.astype(bf16)
     at = lambda d: ((lax.axis_index("wt") + d) % wt) * rows
@@ -751,7 +763,7 @@
     last = shard_count - 1
     grads_in = {0: out_low, last: shift(after(out_low, first_part), -1)}
 
-    pieces, grads_in[last] = beside(pieces, grads_in[last])
+    pieces, grads_in[last], ranks = beside(pieces, grads_in[last], ranks)
     local_rows = jnp.arange(tok, dtype=jnp.int32)
     mine = lax.dynamic_slice_in_dim(deal_row, 2 * ctx_index, 2, 0)
     prompt_place = (
@@ -769,7 +781,13 @@
     first_gain, second_gain = gain_rows[0], gain_rows[1]
     inverse_one = lax.rsqrt(jnp.mean(inputs * inputs, -1, keepdims=True) + norm_eps)
     kv_own = [low[prompt_local:] for low in kv_low]
-    kv_pieces = [gather_ctx(low[:prompt_local]) for low in kv_low]
+    kv_prompt = [low[:prompt_local] for low in kv_low]
+    if context_size == 8:
+        kv_even = [even_blocks(low) for low in kv_prompt]
+        kv_even[0], turned_query = beside(kv_even[0], after(turned_query, *kv_even[1]))
+        kv_pieces = [both_cores(even) for even in kv_even]
+    else:
+        kv_pieces = [gather_ctx(low) for low in kv_prompt]
 
     places = deal_row
     if context_size == 8:
@@ -832,6 +850,8 @@
         coming = d - 1 if d else last
         if coming:
             result, got[coming] = beside(result, shift(got[(coming + 1) % shard_count], -1))
+        if d == 0:
+            result, gates_in = beside(result, gates_in)
         if 0 < d <= last - 2:
             carried = shift(after(add(carried, partial[d + 2]), got[d]), -1)
             result, carried = beside(result, carried)
@@ -847,14 +867,14 @@
         carried,
     )
     carried = shift(add(carried, partial[1]), -1)
-    down_grad, carried = beside(
+    down_grad, home = beside(
         down_weight_grads([(after(r[2], gate_grad), r[1]) for r in rows], context_size), carried
     )
 
     stacked = jnp.stack([gate_grads[d] for d in range(shard_count)], 0)
     stacked = jnp.roll(stacked, wt_index, 0).reshape(EXPERTS, tok).T
     grad_logits = (gates * (stacked - jnp.sum(gates * stacked, -1, keepdims=True))).astype(bf16)
-    grad_normed_two = partial[0].astype(f32) + carried.astype(f32)
+    grad_normed_two = partial[0].astype(f32) + home.astype(f32)
     grad_normed_two = grad_normed_two + dot_nt(grad_logits, router_full)
     grad_mid_norm, second_gain_grad = norm_backward(
         middle, inverse_two, second_gain, grad_normed_two
@@ -866,7 +886,7 @@
         lax.psum_scatter(grad, "ctx", scatter_dimension=0, tiled=False).astype(f32)
         for grad in (gate_grad, up_grad, down_grad)
     )
-    output_share = outer_sum(grad_branch, attended)
+    output_share = row_sum(outer_part(grad_branch, attended))
     devices = context_size * shard_count
     small = jnp.concatenate(
         [
@@ -877,9 +897,9 @@
     )
     small = spread_sum(small)
 
+    carried = shift(after(mixed[last], home), -1)
+    query, carried = beside(after(turned_query, grad_attended), carried)
     d_query, owned, ours = [], [], []
-    carried = None
-    query = after(turned_query, grad_attended)
     for half in range(2):
         result = attention_backward(
             query,
@@ -895,18 +915,19 @@
             block_rows,
             half,
         )
-        d = last - half
-        carried = shift(after(add(carried, mixed[d]), query), -1)
+        carried = shift(add(carried, mixed[last - 1 - half]), -1)
         result, carried = beside(result, carried)
         d_q, d_kv, d_key_own, d_value_own = result
         query = after(query, d_q)
         d_query.append(d_q)
         owned.append(scatter_ctx(d_kv))
         ours.append((d_key_own, d_value_own))
-    for d in range(last - 2, 0, -1):
+    for d in range(last - 3, 0, -1):
         carried = shift(add(carried, mixed[d]), -1)
     mixture = mixed[0].astype(f32) + carried.astype(f32)
     layer_output = (middle + resid_scale * mixture).astype(bf16)
+    d_query = jnp.concatenate(d_query, 1)
+    query_part = outer_part(normed_one, d_query)
     d_key, d_value = (
         jnp.concatenate(
             [
@@ -920,10 +941,11 @@
     grad_key_low = turn(d_key, jnp.tile(cosine, (1, 4)), jnp.tile(sine, (1, 4)), -1.0).astype(
         bf16
     )
-    grad_qkv = jnp.concatenate(d_query + [grad_key_low, d_value.astype(bf16)], 1)
-    grad_qkv, layer_output = beside(grad_qkv, layer_output)
-    qkv_share = outer_sum(normed_one, grad_qkv)
-    grad_normed_one = dot_nt(grad_qkv, qkv_full)
+    grad_kv = jnp.concatenate([grad_key_low, d_value.astype(bf16)], 1)
+    grad_kv, query_part = beside(grad_kv, query_part)
+    kv_share = row_sum(outer_part(normed_one, grad_kv))
+    query_share = row_sum(query_part)
+    grad_normed_one = dot_nt(d_query, qkv_full[:, :1024]) + dot_nt(grad_kv, qkv_full[:, 1024:])
     grad_input_norm, first_gain_grad = norm_backward(
         inputs, inverse_one, first_gain, grad_normed_one
     )
@@ -934,9 +956,9 @@
         layer_output[None],
         input_grad[None],
         first_gain_share,
-        qkv_share[:, :1024],
-        qkv_share[:, 1024:1536],
-        qkv_share[:, 1536:],
+        query_share,
+        kv_share[:, :KV_WIDTH],
+        kv_share[:, KV_WIDTH:],
         output_share.T,
         small[own_rows * EXPERTS :],
         small[: own_rows * EXPERTS].reshape(own_rows, EXPERTS),

time: 955 us -> 836 us (0.88)
  waiting for transfers between devices: 275 us -> 104 us
  starting transfers between devices: 118 us -> 143 us
  Pallas kernels: 399 us -> 409 us
    ppermute x27 -> x30, waiting for transfers between devices: 146 us -> 16.9 us  [shift(): return lax.ppermute(x, 'wt', [(i, (i + distance) % n) for i in range(n)])]
    all_to_all x1, waiting for transfers between devices: 31.9 us -> 0.01 us  [per_device(): lax.all_to_all(rank.T.reshape(shard_count, expert_count, tok), 'wt', 0, 0...]
    ppermute x64 -> x72, waiting for transfers between devices: 94.5 us -> 69.5 us  [swap(): lax.ppermute(x, 'ctx', [(i, i ^ mask) for i in range(lax.axis_size('ctx'))])]
    all_to_all x2, waiting for transfers between devices: 0.01 us -> 14.9 us  [spread_sum(): return jnp.sum(lax.all_to_all(x, ALL, 0, 0, tiled=True), 0)]
    ppermute x64 -> x72, starting transfers between devices: 48 us -> 62 us  [swap(): lax.ppermute(x, 'ctx', [(i, i ^ mask) for i in range(lax.axis_size('ctx'))])]
    ppermute x27 -> x30, starting transfers between devices: 58.6 us -> 68.8 us  [shift(): return lax.ppermute(x, 'wt', [(i, (i + distance) % n) for i in range(n)])]
    pallas_call x2 -> x3, Pallas kernels: 16.9 us -> 23.2 us  [outer(): pl.pallas_call(outer_kernel, grid_spec=pltpu.PrefetchScalarGridSpec(num_s...]
  transfers between devices with their start and end apart: 100 -> 111, of which waited for: 35 -> 27; matrix products, arithmetic and copies ran while one was open for 13% -> 17% of each run, Pallas kernels for 42% -> 50%
where the time goes in v3:
time: 836 us; the launch traced here: 824 us
  Pallas kernels  409 us (49%)
  starting transfers between devices  143 us (17%)
  waiting for transfers between devices  104 us (12%)
  other arithmetic  67.7 us (8%)
  local copies, waits for them, and re-layouts  53.8 us (6%)
  matrix products  27.3 us (3%)
  between operations  18.7 us (2%)
    pallas_call x4, Pallas kernels, expert_pass(): pl.pallas_call(functools.partial(expert_kernel, sizes=sizes), grid_spec=p...  161 us
    pallas_call x2, Pallas kernels, attention_backward(): pl.pallas_call(functools.partial(attention_backward_kernel, block_rows=bl...  96.4 us
    ppermute x72, waiting for transfers between devices, swap(): lax.ppermute(x, 'ctx', [(i, i ^ mask) for i in range(lax.axis_size('ctx'))])  69.5 us
    ppermute x30, starting transfers between devices, shift(): return lax.ppermute(x, 'wt', [(i, (i + distance) % n) for i in range(n)])  68.8 us
    ppermute x72, starting transfers between devices, swap(): lax.ppermute(x, 'ctx', [(i, i ^ mask) for i in range(lax.axis_size('ctx'))])  62 us
    pallas_call x2, Pallas kernels, attention_forward(): pl.pallas_call(functools.partial(attention_forward_kernel, block_rows=blo...  53.3 us
    pallas_call x1, Pallas kernels, up_weight_grads(): pl.pallas_call(functools.partial(up_grad_kernel, sources=len(rows)), grid...  40.6 us
    pallas_call x1, Pallas kernels, down_weight_grads(): pl.pallas_call(functools.partial(down_grad_kernel, sources=len(rows), par...  23.6 us
  transfers between devices with their start and end apart: 111, of which 27 were waited for; matrix products, arithmetic and copies ran while one was open for 17% of the time, Pallas kernels for 50%

profile of v3, /device:TPU:0, one launch (start us, length us, event | category | flops | bytes accessed | tf_op | source)
XLA Modules:
  0.0 823.8 jit_solution(9351841842953337282)
XLA Ops:
  35.8 6.9 collective-permute-start.19
  44.2 9.0 %collective-permute-done.12.refs_10_ = bf16[96,3200]{1,0:T(8,128)(2,1)S(1)} collective-permute-done((bf16[96,3200]{1,0:T(8,128)(2,1)}, bf16[96,3200]{1,0:T(8,128)(2,1)S(1)}, u32[]{:S(2)}, u32[]{:S(2)}) %collective-permute-start.12) | collective-permute-done | bytes 614432 | tf_op jit(solution)/shard_map/ppermute | solution.py:577
  62.8 11.8 %collective-permute-done.16 = bf16[48,3200]{1,0:T(8,128)(2,1)S(1)} collective-permute-done((bf16[48,3200]{1,0:T(8,128)(2,1)S(1)}, bf16[48,3200]{1,0:T(8,128)(2,1)S(1)}, u32[]{:S(2)}, u32[]{:S(2)}) %collective-permute-start.16) | collective-permute-done | bytes 307232 | tf_op jit(solution)/shard_map/ppermute | solution.py:577
  87.3 9.5 %collective-permute-start.32 = (bf16[768,1024]{1,0:T(8,128)(2,1)}, bf16[768,1024]{1,0:T(8,128)(2,1)}, u32[]{:S(2)}, u32[]{:S(2)}) collective-permute-start(bf16[768,1024]{1,0:T(8,128)(2,1)} %collective-permute-done.19.df_ref), channel_id=1, source_target_pairs={{0,3},{1,0},{2,1},{3,2},{4,7},{5,4},{6,5},{7,6},{8,11},{9,8},{10,9... | collective-permute-start | bytes 4718600 | tf_op jit(solution)/shard_map/ppermute | solution.py:621
  97.4 11.0 %project.1 = (bf16[768,1024]{1,0:T(8,128)(2,1)}, bf16[768,1024]{1,0:T(8,128)(2,1)}, bf16[768,512]{1,0:T(8,128)(2,1)}, bf16[768,512]{1,0:T(8,128)(2,1)}, bf16[102...) custom-call(s32[32]{0:T(128)} %pad_add_fusion.1.places, ...), custom_call_target="tpu_custom_call" | custom-call | flops 1000000000 | bytes 1000000 | tf_op jit(solution)/shard_map/project/pallas_call | solution.py:95
  150.1 26.7 %attention_forward.2 = (bf16[768,512]{1,0:T(8,128)(2,1)}, f32[2,4,768]{2,1,0:T(4,128)}) custom-call(s32[16]{0:T(128)} %reshape.274.places, s32[4]{0:T(128)} %pad_add_fusion.starts, bf16[768,1024]{1,0:T(8,128)(2,1)} %get-tuple-element.324.q_ref, bf16[256,512]{1,0:T(8,128)(2,1)} %copy-done.12, bf16[256,512]{1,0:T(8,128)(2,1)} %copy-done.25, ...), custom_call_target="tpu_custom_call" | custom-call | flops 1000000000 | bytes 1000000 | tf_op jit(solution)/shard_map/attention_forward/pallas_call | solution.py:220
  183.4 26.7 %attention_forward.3 = (bf16[768,512]{1,0:T(8,128)(2,1)}, f32[2,4,768]{2,1,0:T(4,128)}) custom-call(s32[16]{0:T(128)} %reshape.274.places, s32[4]{0:T(128)} %pad_add_fusion.starts, bf16[768,1024]{1,0:T(8,128)(2,1)} %get-tuple-element.324.q_ref, bf16[256,512]{1,0:T(8,128)(2,1)} %copy-done.11, bf16[256,512]{1,0:T(8,128)(2,1)} %copy-done.21, ...), custom_call_target="tpu_custom_call" | custom-call | flops 1000000000 | bytes 1000000 | tf_op jit(solution)/shard_map/attention_forward/pallas_call | solution.py:220
  232.3 39.3 %expert_pass.4 = (bf16[768,1024]{1,0:T(8,128)(2,1)}, bf16[768,1024]{1,0:T(8,128)(2,1)}, f32[8,1,768]{2,1,0:T(1,128)}, bf16[8,336,1024]{2,1,0:T(8,128)(2,1)}, bf1...) custom-call(s32[8]{0:T(128)} %get-tuple-element.450.counts, ...), custom_call_target="tpu_custom_call" | custom-call | flops 1000000000 | bytes 1000000 | tf_op jit(solution)/shard_map/expert_pass/pallas_call | solution.py:490
  276.0 39.4 %expert_pass.5 = (bf16[768,1024]{1,0:T(8,128)(2,1)}, bf16[768,1024]{1,0:T(8,128)(2,1)}, f32[8,1,768]{2,1,0:T(1,128)}, bf16[8,336,1024]{2,1,0:T(8,128)(2,1)}, bf1...) custom-call(s32[8]{0:T(128)} %get-tuple-element.447.counts, ...), custom_call_target="tpu_custom_call" | custom-call | flops 1000000000 | bytes 1000000 | tf_op jit(solution)/shard_map/expert_pass/pallas_call | solution.py:490
  315.4 6.2 collective-permute-start.43
  323.5 41.3 %expert_pass.6 = (bf16[768,1024]{1,0:T(8,128)(2,1)}, bf16[768,1024]{1,0:T(8,128)(2,1)}, f32[8,1,768]{2,1,0:T(1,128)}, bf16[8,336,1024]{2,1,0:T(8,128)(2,1)}, bf1...) custom-call(s32[8]{0:T(128)} %get-tuple-element.448.counts, ...), custom_call_target="tpu_custom_call" | custom-call | flops 1000000000 | bytes 1000000 | tf_op jit(solution)/shard_map/expert_pass/pallas_call | solution.py:490
  366.9 41.2 %expert_pass.7 = (bf16[768,1024]{1,0:T(8,128)(2,1)}, bf16[768,1024]{1,0:T(8,128)(2,1)}, f32[8,1,768]{2,1,0:T(1,128)}, bf16[8,336,1024]{2,1,0:T(8,128)(2,1)}, bf1...) custom-call(s32[8]{0:T(128)} %get-tuple-element.449.counts, ...), custom_call_target="tpu_custom_call" | custom-call | flops 1000000000 | bytes 1000000 | tf_op jit(solution)/shard_map/expert_pass/pallas_call | solution.py:490
  411.9 40.6 %up_weight_grads.1 = (bf16[8,8,128,512]{3,2,1,0:T(8,128)(2,1)}, bf16[8,8,128,512]{3,2,1,0:T(8,128)(2,1)}) custom-call(bf16[8,336,1024]{2,1,0:T(8,128)(2,1)} %get-tuple-element.276.refs_0_, bf16[8,336,512]{2,1,0:T(8,128)(2,1)} %get-tuple-element.277.refs_1_, bf16[8,336,512]{2,1,0:T(8,128)(2,1)} %get-tuple-element.278.refs_2_, ...), custom_call_target="tpu_custom_call" | custom-call | flops 1000000000 | bytes 1000000 | tf_op jit(solution)/shard_map/up_weight_grads/pallas_call | solution.py:549
  476.7 23.6 %down_weight_grads.1 = bf16[8,8,512,128]{3,2,1,0:T(8,128)(2,1)} custom-call(bf16[8,336,512]{2,1,0:T(8,128)(2,1)} %get-tuple-element.295.refs_0_, bf16[8,336,1024]{2,1,0:T(8,128)(2,1)} %get-tuple-element.296.refs_1_, bf16[8,336,512]{2,1,0:T(8,128)(2,1)} %get-tuple-element.298.refs_2_, bf16[8,336,1024]{2,1,0:T(8,128)(2,1)} %get-tuple-element.299.refs_3_, ...), custom_call_target="tpu_custom_call" | custom-call | flops 1000000000 | bytes 1000000 | tf_op jit(solution)/shard_map/down_weight_grads/pallas_call | solution.py:564
  512.4 7.7 outer.5
  563.7 14.9 %all-to-all-done.2 = f32[32,1,1056]{2,1,0:T(1,128)S(1)} async-done(((f32[32,1,1056]{2,1,0:T(1,128)}), f32[32,1,1056]{2,1,0:T(1,128)S(1)}, u32[]{:S(2)}, u32[]{:S(2)}) %all-to-all-start.2) | async-done | bytes 135200 | tf_op jit(solution)/shard_map/all_to_all | solution.py:666
  589.2 48.3 %attention_backward.2 = (bf16[768,512]{1,0:T(8,128)(2,1)}, bf16[2048,512]{1,0:T(8,128)(2,1)}, f32[512,256]{1,0:T(8,128)}, f32[512,256]{1,0:T(8,128)}) custom-call(s32[16]{0:T(128)} %reshape.274.places, s32[4]{0:T(128)} %pad_add_fusion.starts, bf16[768,1024]{1,0:T(8,128)(2,1)} %get-tuple-element.324.q_ref, bf16[768,1024]{1,0:T(8,128)(2,1)} %convolution_convert_fusion.do_ref, ...), custom_call_target="tpu_custom_call" | custom-call | flops 1000000000 | bytes 1000000 | tf_op jit(solution)/shard_map/attention_backward/pallas_call | solution.py:364
  647.8 48.1 %attention_backward.3 = (bf16[768,512]{1,0:T(8,128)(2,1)}, bf16[2048,512]{1,0:T(8,128)(2,1)}, f32[512,256]{1,0:T(8,128)}, f32[512,256]{1,0:T(8,128)}) custom-call(s32[16]{0:T(128)} %reshape.274.places, s32[4]{0:T(128)} %pad_add_fusion.starts, bf16[768,1024]{1,0:T(8,128)(2,1)} %get-tuple-element.324.q_ref, bf16[768,1024]{1,0:T(8,128)(2,1)} %convolution_convert_fusion.do_ref, ...), custom_call_target="tpu_custom_call" | custom-call | flops 1000000000 | bytes 1000000 | tf_op jit(solution)/shard_map/attention_backward/pallas_call | solution.py:364
  707.7 7.8 outer.3
  737.6 5.9 collective-permute-done.65
  748.3 7.8 outer.4
  763.8 5.9 fusion.9
  770.3 5.9 all-to-all-start.1
  790.8 6.1 fusion.19
  (574 shorter events, 313.5 us)
Async XLA Ops:
  7.3 225.0 %all-gather.7.cloned.1.call-start = ((), (), s32[]{:S(2)}) async-start(), calls=%async_computation.9 | async-start | bytes 9437184 | tf_op jit(solution)/shard_map/all_gather | solution.py:750
  8.0 224.3 %all-gather.9.cloned.1.call-start = ((), (), s32[]{:S(2)}) async-start(), calls=%async_computation.10 | async-start | bytes 9437184 | tf_op jit(solution)/shard_map/all_gather | solution.py:751
  8.8 223.5 %all-gather.11.cloned.1.call-start = ((), (), s32[]{:S(2)}) async-start(), calls=%async_computation.11 | async-start | bytes 9437184 | tf_op jit(solution)/shard_map/all_gather | solution.py:752
  21.0 65.0 %all-to-all-start = ((f32[4,8,768]{2,1,0:T(8,128)}), f32[4,8,768]{2,1,0:T(8,128)S(1)}, u32[]{:S(2)}, u32[]{:S(2)}) async-start(f32[4,8,768]{2,1,0:T(8,128)} %fusion.28), calls=%async_computation | async-start | bytes 196608 | tf_op jit(solution)/shard_map/all_to_all | solution.py:760
  24.3 784.0 %reduce-scatter.6.cloned.1.call-start = ((), (), s32[]{:S(2)}) async-start(), calls=%async_computation.7 | async-start | bytes 9437184 | tf_op jit(solution)/shard_map/reduce_scatter | solution.py:886
  25.7 56.6 %collective-permute-start = (bf16[32,3200]{1,0:T(8,128)(2,1)S(1)}, bf16[32,3200]{1,0:T(8,128)(2,1)S(1)}, u32[]{:S(2)}, u32[]{:S(2)}) collective-permute-start(bf16[32,3200]{1,0:T(8,128)(2,1)S(1)} %concatenate.97.refs_0_), channel_id=1, source_target_pairs={{0,4},{4,0},{8,12},{12,8},{16,20},{20,16},{24,28},{28,24},{1,5},{5... | collective-permute-start | bytes 614408 | tf_op jit(solution)/shard_map/ppermute | solution.py:577
  35.8 51.5 %collective-permute-start.19 = (bf16[768,1024]{1,0:T(8,128)(2,1)S(1)}, bf16[768,1024]{1,0:T(8,128)(2,1)}, u32[]{:S(2)}, u32[]{:S(2)}) collective-permute-start(bf16[768,1024]{1,0:T(8,128)(2,1)S(1)} %bitcast.144), channel_id=1, source_target_pairs={{0,3},{1,0},{2,1},{3,2},{4,7},{5,4},{6,5},{7,6},{8,11},{9,8},{10,9... | collective-permute-start | bytes 4718600 | tf_op jit(solution)/shard_map/ppermute | solution.py:621
  87.3 89.5 %collective-permute-start.32 = (bf16[768,1024]{1,0:T(8,128)(2,1)}, bf16[768,1024]{1,0:T(8,128)(2,1)}, u32[]{:S(2)}, u32[]{:S(2)}) collective-permute-start(bf16[768,1024]{1,0:T(8,128)(2,1)} %collective-permute-done.19.df_ref), channel_id=1, source_target_pairs={{0,3},{1,0},{2,1},{3,2},{4,7},{5,4},{6,5},{7,6},{8,11},{9,8},{10,9... | collective-permute-start | bytes 4718600 | tf_op jit(solution)/shard_map/ppermute | solution.py:621
  221.1 50.5 %collective-permute-start.38 = (bf16[768,1024]{1,0:T(8,128)(2,1)}, bf16[768,1024]{1,0:T(8,128)(2,1)}, u32[]{:S(2)}, u32[]{:S(2)}) collective-permute-start(bf16[768,1024]{1,0:T(8,128)(2,1)} %multiply_convert_fusion.1.a2_ref), channel_id=1, source_target_pairs={{0,3},{1,0},{2,1},{3,2},{4,7},{5,4},{6,5},{7,6},{8,11},{9,8},{10,9... | collective-permute-start | bytes 4718600 | tf_op jit(solution)/shard_map/ppermute | solution.py:621
  228.5 43.2 %collective-permute-start.40 = (f32[8,768]{1,0:T(8,128)}, f32[8,768]{1,0:T(8,128)}, u32[]{:S(2)}, u32[]{:S(2)}) collective-permute-start(f32[8,768]{1,0:T(8,128)} %get-tuple-element.432), channel_id=1, source_target_pairs={{0,2},{1,3},{2,0},{3,1},{4,6},{5,7},{6,4},{7,5},{8,10},{9,11},{10,... | collective-permute-start | bytes 73736 | tf_op jit(solution)/shard_map/ppermute | solution.py:621
  271.6 43.7 %collective-permute-start.42 = (bf16[768,1024]{1,0:T(8,128)(2,1)}, bf16[768,1024]{1,0:T(8,128)(2,1)}, u32[]{:S(2)}, u32[]{:S(2)}) collective-permute-start(bf16[768,1024]{1,0:T(8,128)(2,1)} %collective-permute-done.38.a2_ref), channel_id=1, source_target_pairs={{0,3},{1,0},{2,1},{3,2},{4,7},{5,4},{6,5},{7,6},{8,11},{9,8},{10,9... | collective-permute-start | bytes 4718600 | tf_op jit(solution)/shard_map/ppermute | solution.py:621
  315.4 49.4 %collective-permute-start.43 = (bf16[768,1024]{1,0:T(8,128)(2,1)}, bf16[768,1024]{1,0:T(8,128)(2,1)}, u32[]{:S(2)}, u32[]{:S(2)}) collective-permute-start(bf16[768,1024]{1,0:T(8,128)(2,1)} %collective-permute-done.42.a2_ref), channel_id=1, source_target_pairs={{0,3},{1,0},{2,1},{3,2},{4,7},{5,4},{6,5},{7,6},{8,11},{9,8},{10,9... | collective-permute-start | bytes 4718600 | tf_op jit(solution)/shard_map/ppermute | solution.py:621
  364.8 43.3 %collective-permute-start.44 = (bf16[768,1024]{1,0:T(8,128)(2,1)}, bf16[768,1024]{1,0:T(8,128)(2,1)}, u32[]{:S(2)}, u32[]{:S(2)}) collective-permute-start(bf16[768,1024]{1,0:T(8,128)(2,1)} %get-tuple-element.274), channel_id=1, source_target_pairs={{0,3},{1,0},{2,1},{3,2},{4,7},{5,4},{6,5},{7,6},{8,11},{9,8},{10,9... | collective-permute-start | bytes 4718600 | tf_op jit(solution)/shard_map/ppermute | solution.py:621
  452.6 358.6 %reduce-scatter.4.cloned.1.call-start = ((), (), s32[]{:S(2)}) async-start(), calls=%async_computation.6 | async-start | bytes 9437184 | tf_op jit(solution)/shard_map/reduce_scatter | solution.py:886
  540.6 96.9 %collective-permute-start.51 = (bf16[768,1024]{1,0:T(8,128)(2,1)}, bf16[768,1024]{1,0:T(8,128)(2,1)}, u32[]{:S(2)}, u32[]{:S(2)}) collective-permute-start(bf16[768,1024]{1,0:T(8,128)(2,1)} %add_convert_fusion.2), channel_id=1, source_target_pairs={{0,3},{1,0},{2,1},{3,2},{4,7},{5,4},{6,5},{7,6},{8,11},{9,8},{10,9... | collective-permute-start | bytes 4718600 | tf_op jit(solution)/shard_map/ppermute | solution.py:621
  548.6 265.4 %reduce-scatter.8.cloned.1.call-start = ((), (), s32[]{:S(2)}) async-start(), calls=%async_computation.8 | async-start | bytes 9437184 | tf_op jit(solution)/shard_map/reduce_scatter | solution.py:886
  583.9 61.3 %collective-permute-start.100 = (bf16[32,1024]{1,0:T(8,128)(2,1)}, bf16[32,1024]{1,0:T(8,128)(2,1)S(1)}, u32[]{:S(2)}, u32[]{:S(2)}) collective-permute-start(bf16[32,1024]{1,0:T(8,128)(2,1)} %get-tuple-element.406), channel_id=1, source_target_pairs={{0,2},{1,3},{2,0},{3,1},{4,6},{5,7},{6,4},{7,5},{8,10},{9,11},{10,... | collective-permute-start | bytes 196616 | tf_op jit(solution)/shard_map/ppermute | solution.py:621
  587.2 58.5 %collective-permute-start.101 = (bf16[32,1024]{1,0:T(8,128)(2,1)}, bf16[32,1024]{1,0:T(8,128)(2,1)}, u32[]{:S(2)}, u32[]{:S(2)}) collective-permute-start(bf16[32,1024]{1,0:T(8,128)(2,1)} %get-tuple-element.405), channel_id=1, source_target_pairs={{0,3},{1,0},{2,1},{3,2},{4,7},{5,4},{6,5},{7,6},{8,11},{9,8},{10,9... | collective-permute-start | bytes 196616 | tf_op jit(solution)/shard_map/ppermute | solution.py:621
  588.1 57.6 %collective-permute-start.99 = (bf16[32,1024]{1,0:T(8,128)(2,1)S(1)}, bf16[32,1024]{1,0:T(8,128)(2,1)}, u32[]{:S(2)}, u32[]{:S(2)}) collective-permute-start(bf16[32,1024]{1,0:T(8,128)(2,1)S(1)} %get-tuple-element.404), channel_id=1, source_target_pairs={{0,1},{1,2},{2,3},{3,0},{4,5},{5,6},{6,7},{7,4},{8,9},{9,10},{10,1... | collective-permute-start | bytes 196616 | tf_op jit(solution)/shard_map/ppermute | solution.py:621
  641.4 65.3 %collective-permute-start.52 = (bf16[768,1024]{1,0:T(8,128)(2,1)}, bf16[768,1024]{1,0:T(8,128)(2,1)}, u32[]{:S(2)}, u32[]{:S(2)}) collective-permute-start(bf16[768,1024]{1,0:T(8,128)(2,1)} %add_convert_fusion.1), channel_id=1, source_target_pairs={{0,3},{1,0},{2,1},{3,2},{4,7},{5,4},{6,5},{7,6},{8,11},{9,8},{10,9... | collective-permute-start | bytes 4718600 | tf_op jit(solution)/shard_map/ppermute | solution.py:621
  645.2 50.7 %collective-permute-start.54 = (bf16[256,512]{1,0:T(8,128)(2,1)}, bf16[256,512]{1,0:T(8,128)(2,1)S(1)}, u32[]{:S(2)}, u32[]{:S(2)}) collective-permute-start(bf16[256,512]{1,0:T(8,128)(2,1)} %get-tuple-element.391), channel_id=1, source_target_pairs={{0,4},{4,0},{8,12},{12,8},{16,20},{20,16},{24,28},{28,24},{1,5},{5... | collective-permute-start | bytes 786440 | tf_op jit(solution)/shard_map/ppermute | solution.py:577
  645.2 50.7 %collective-permute-start.55 = (bf16[256,512]{1,0:T(8,128)(2,1)}, bf16[256,512]{1,0:T(8,128)(2,1)}, u32[]{:S(2)}, u32[]{:S(2)}) collective-permute-start(bf16[256,512]{1,0:T(8,128)(2,1)} %get-tuple-element.390), channel_id=1, source_target_pairs={{0,4},{4,0},{8,12},{12,8},{16,20},{20,16},{24,28},{28,24},{1,5},{5... | collective-permute-start | bytes 786440 | tf_op jit(solution)/shard_map/ppermute | solution.py:577
  645.7 50.2 %collective-permute-start.58 = (bf16[256,512]{1,0:T(8,128)(2,1)}, bf16[256,512]{1,0:T(8,128)(2,1)}, u32[]{:S(2)}, u32[]{:S(2)}) collective-permute-start(bf16[256,512]{1,0:T(8,128)(2,1)} %get-tuple-element.389), channel_id=1, source_target_pairs={{0,4},{4,0},{8,12},{12,8},{16,20},{20,16},{24,28},{28,24},{1,5},{5... | collective-permute-start | bytes 786440 | tf_op jit(solution)/shard_map/ppermute | solution.py:577
  647.3 70.1 %collective-permute-start.53 = (bf16[256,512]{1,0:T(8,128)(2,1)}, bf16[256,512]{1,0:T(8,128)(2,1)}, u32[]{:S(2)}, u32[]{:S(2)}) collective-permute-start(bf16[256,512]{1,0:T(8,128)(2,1)} %get-tuple-element.388), channel_id=1, source_target_pairs={{0,4},{4,0},{8,12},{12,8},{16,20},{20,16},{24,28},{28,24},{1,5},{5... | collective-permute-start | bytes 786440 | tf_op jit(solution)/shard_map/ppermute | solution.py:577
  (171 other events, 2867.6 us)
Sparse Core Ops, SparseCore 0:
  10.0 72.7 all-gather.6
  84.6 69.3 all-gather.8
  155.9 53.0 all-gather.10
  452.7 71.2 reduce-scatter.5
  527.7 80.1 reduce-scatter.3
  611.2 71.2 reduce-scatter.7

commit v4 on v3

--- a/solution.py
+++ b/solution.py
@@ -112,29 +112,36 @@
     )(places, x, cosine, sine, *pieces)
 
 
-def outer_kernel(mine, a_ref, b_ref, out_ref):
-    out_ref[...] = dot_tn(a_ref[...], b_ref[...]).astype(bf16)
-
-
-def outer(a, b):
-    tok, columns = b.shape
+def outer_kernel(mine, *refs):
+    out_ref = refs[-1]
+    at = 0
+    for n in range(len(refs) // 2):
+        columns = refs[2 * n + 1].shape[1]
+        out_ref[:, at : at + columns] = dot_tn(refs[2 * n][...], refs[2 * n + 1][...]).astype(bf16)
+        at += columns
+
+
+def outer(*pairs):
+    tok = pairs[0][0].shape[0]
     mine = lax.axis_index("ctx").astype(jnp.int32).reshape(1)
+    specs = []
+    for _, b in pairs:
+        specs.append(pl.BlockSpec((tok, 128), lambda m, mine: (0, m ^ mine[0])))
+        specs.append(pl.BlockSpec(b.shape, lambda m, mine: (0, 0)))
+    columns = sum(b.shape[1] for _, b in pairs)
     return pl.pallas_call(
         outer_kernel,
         grid_spec=pltpu.PrefetchScalarGridSpec(
             num_scalar_prefetch=1,
             grid=(8,),
-            in_specs=[
-                pl.BlockSpec((tok, 128), lambda m, mine: (0, m ^ mine[0])),
-                pl.BlockSpec((tok, columns), lambda m, mine: (0, 0)),
-            ],
+            in_specs=specs,
             out_specs=pl.BlockSpec((128, columns), lambda m, mine: (m, 0)),
         ),
         out_shape=jax.ShapeDtypeStruct((MODEL_WIDTH, columns), bf16),
         compiler_params=pltpu.CompilerParams(vmem_limit_bytes=VMEM_LIMIT),
         cost_estimate=SMALL,
         name="outer",
-    )(mine, a, b)
+    )(mine, *[x for pair in pairs for x in pair])
 
 
 def gather_keys(pieces, scratch, places, block_rows):
@@ -641,10 +648,10 @@
     return pieces, [1] * 8 + [3] * 8, places, others
 
 
-def outer_part(a, b):
+def outer_part(*pairs):
     if lax.axis_size("ctx") != 8 or lax.axis_size("wt") != 4:
-        return dot_tn(a, b)
-    return scatter_ctx(outer(a, b))
+        return jnp.concatenate([dot_tn(a, b) for a, b in pairs], 1)
+    return scatter_ctx(outer(*pairs))
 
 
 def row_sum(part):
@@ -886,7 +893,6 @@
         lax.psum_scatter(grad, "ctx", scatter_dimension=0, tiled=False).astype(f32)
         for grad in (gate_grad, up_grad, down_grad)
     )
-    output_share = row_sum(outer_part(grad_branch, attended))
     devices = context_size * shard_count
     small = jnp.concatenate(
         [
@@ -895,7 +901,6 @@
         ],
         1,
     )
-    small = spread_sum(small)
 
     carried = shift(after(mixed[last], home), -1)
     query, carried = beside(after(turned_query, grad_attended), carried)
@@ -919,6 +924,8 @@
         result, carried = beside(result, carried)
         d_q, d_kv, d_key_own, d_value_own = result
         query = after(query, d_q)
+        if half == 0:
+            small = spread_sum(after(small, d_q))
         d_query.append(d_q)
         owned.append(scatter_ctx(d_kv))
         ours.append((d_key_own, d_value_own))
@@ -927,7 +934,7 @@
     mixture = mixed[0].astype(f32) + carried.astype(f32)
     layer_output = (middle + resid_scale * mixture).astype(bf16)
     d_query = jnp.concatenate(d_query, 1)
-    query_part = outer_part(normed_one, d_query)
+    query_part = outer_part((normed_one, d_query), (after(grad_branch, d_query), attended))
     d_key, d_value = (
         jnp.concatenate(
             [
@@ -943,8 +950,8 @@
     )
     grad_kv = jnp.concatenate([grad_key_low, d_value.astype(bf16)], 1)
     grad_kv, query_part = beside(grad_kv, query_part)
-    kv_share = row_sum(outer_part(normed_one, grad_kv))
-    query_share = row_sum(query_part)
+    kv_share = row_sum(outer_part((normed_one, grad_kv)))
+    query_share, output_share = jnp.split(row_sum(query_part), 2, 1)
     grad_normed_one = dot_nt(d_query, qkv_full[:, :1024]) + dot_nt(grad_kv, qkv_full[:, 1024:])
     grad_input_norm, first_gain_grad = norm_backward(
         inputs, inverse_one, first_gain, grad_normed_one

time: 836 us -> 832 us (level)
  waiting for transfers between devices: 104 us -> 126 us
  starting transfers between devices: 143 us -> 128 us
    ppermute x30 -> x27, waiting for transfers between devices: 16.9 us -> 38.6 us  [shift(): return lax.ppermute(x, 'wt', [(i, (i + distance) % n) for i in range(n)])]
    ppermute x72 -> x64, waiting for transfers between devices: 69.5 us -> 85.2 us  [swap(): lax.ppermute(x, 'ctx', [(i, i ^ mask) for i in range(lax.axis_size('ctx'))])]
    all_to_all x2, waiting for transfers between devices: 14.9 us -> 0.01 us  [spread_sum(): return jnp.sum(lax.all_to_all(x, ALL, 0, 0, tiled=True), 0)]
    ppermute x72 -> x64, starting transfers between devices: 62 us -> 48.2 us  [swap(): lax.ppermute(x, 'ctx', [(i, i ^ mask) for i in range(lax.axis_size('ctx'))])]
    pallas_call x3 -> x2, Pallas kernels: 23.2 us -> 17.6 us  [outer(): pl.pallas_call(outer_kernel, grid_spec=pltpu.PrefetchScalarGridSpec(num_s...]
    ppermute x30 -> x27, starting transfers between devices: 68.8 us -> 65.3 us  [shift(): return lax.ppermute(x, 'wt', [(i, (i + distance) % n) for i in range(n)])]
  transfers between devices with their start and end apart: 111 -> 100, of which waited for: 27 -> 30; matrix products, arithmetic and copies ran while one was open for 17% -> 16% of each run, Pallas kernels for 50% -> 49%
where the time goes in v4:
time: 832 us; the launch traced here: 823 us
  Pallas kernels  403 us (48%)
  starting transfers between devices  128 us (15%)
  waiting for transfers between devices  126 us (15%)
  other arithmetic  64.7 us (8%)
  local copies, waits for them, and re-layouts  56.8 us (7%)
  matrix products  25.9 us (3%)
  between operations  18.6 us (2%)
    pallas_call x4, Pallas kernels, expert_pass(): pl.pallas_call(functools.partial(expert_kernel, sizes=sizes), grid_spec=p...  161 us
    pallas_call x2, Pallas kernels, attention_backward(): pl.pallas_call(functools.partial(attention_backward_kernel, block_rows=bl...  96 us
    ppermute x64, waiting for transfers between devices, swap(): lax.ppermute(x, 'ctx', [(i, i ^ mask) for i in range(lax.axis_size('ctx'))])  85.2 us
    ppermute x27, starting transfers between devices, shift(): return lax.ppermute(x, 'wt', [(i, (i + distance) % n) for i in range(n)])  65.3 us
    pallas_call x2, Pallas kernels, attention_forward(): pl.pallas_call(functools.partial(attention_forward_kernel, block_rows=blo...  53.4 us
    ppermute x64, starting transfers between devices, swap(): lax.ppermute(x, 'ctx', [(i, i ^ mask) for i in range(lax.axis_size('ctx'))])  48.2 us
    pallas_call x1, Pallas kernels, up_weight_grads(): pl.pallas_call(functools.partial(up_grad_kernel, sources=len(rows)), grid...  40.6 us
    ppermute x27, waiting for transfers between devices, shift(): return lax.ppermute(x, 'wt', [(i, (i + distance) % n) for i in range(n)])  38.6 us
  transfers between devices with their start and end apart: 100, of which 30 were waited for; matrix products, arithmetic and copies ran while one was open for 16% of the time, Pallas kernels for 49%

profile of v4, /device:TPU:0, one launch (start us, length us, event | category | flops | bytes accessed | tf_op | source)
XLA Modules:
  0.0 823.0 jit_solution(15909557403684674386)
XLA Ops:
  35.9 6.9 collective-permute-start.19
  44.3 9.0 %collective-permute-done.12.refs_10_ = bf16[96,3200]{1,0:T(8,128)(2,1)S(1)} collective-permute-done((bf16[96,3200]{1,0:T(8,128)(2,1)}, bf16[96,3200]{1,0:T(8,128)(2,1)S(1)}, u32[]{:S(2)}, u32[]{:S(2)}) %collective-permute-start.12) | collective-permute-done | bytes 614432 | tf_op jit(solution)/shard_map/ppermute | solution.py:584
  63.1 11.7 %collective-permute-done.16 = bf16[48,3200]{1,0:T(8,128)(2,1)S(1)} collective-permute-done((bf16[48,3200]{1,0:T(8,128)(2,1)S(1)}, bf16[48,3200]{1,0:T(8,128)(2,1)S(1)}, u32[]{:S(2)}, u32[]{:S(2)}) %collective-permute-start.16) | collective-permute-done | bytes 307232 | tf_op jit(solution)/shard_map/ppermute | solution.py:584
  76.1 5.6 collective-permute-done.17
  87.4 9.5 %collective-permute-start.32 = (bf16[768,1024]{1,0:T(8,128)(2,1)}, bf16[768,1024]{1,0:T(8,128)(2,1)}, u32[]{:S(2)}, u32[]{:S(2)}) collective-permute-start(bf16[768,1024]{1,0:T(8,128)(2,1)} %collective-permute-done.19.df_ref), channel_id=1, source_target_pairs={{0,3},{1,0},{2,1},{3,2},{4,7},{5,4},{6,5},{7,6},{8,11},{9,8},{10,9... | collective-permute-start | bytes 4718600 | tf_op jit(solution)/shard_map/ppermute | solution.py:628
  97.5 11.0 %project.1 = (bf16[768,1024]{1,0:T(8,128)(2,1)}, bf16[768,1024]{1,0:T(8,128)(2,1)}, bf16[768,512]{1,0:T(8,128)(2,1)}, bf16[768,512]{1,0:T(8,128)(2,1)}, bf16[102...) custom-call(s32[32]{0:T(128)} %pad_add_fusion.1.places, ...), custom_call_target="tpu_custom_call" | custom-call | flops 1000000000 | bytes 1000000 | tf_op jit(solution)/shard_map/project/pallas_call | solution.py:95
  150.0 26.7 %attention_forward.2 = (bf16[768,512]{1,0:T(8,128)(2,1)}, f32[2,4,768]{2,1,0:T(4,128)}) custom-call(s32[16]{0:T(128)} %reshape.273.places, s32[4]{0:T(128)} %pad_add_fusion.starts, bf16[768,1024]{1,0:T(8,128)(2,1)} %get-tuple-element.326.q_ref, bf16[256,512]{1,0:T(8,128)(2,1)} %copy-done.11, bf16[256,512]{1,0:T(8,128)(2,1)} %copy-done.24, ...), custom_call_target="tpu_custom_call" | custom-call | flops 1000000000 | bytes 1000000 | tf_op jit(solution)/shard_map/attention_forward/pallas_call | solution.py:227
  183.3 26.7 %attention_forward.3 = (bf16[768,512]{1,0:T(8,128)(2,1)}, f32[2,4,768]{2,1,0:T(4,128)}) custom-call(s32[16]{0:T(128)} %reshape.273.places, s32[4]{0:T(128)} %pad_add_fusion.starts, bf16[768,1024]{1,0:T(8,128)(2,1)} %get-tuple-element.326.q_ref, bf16[256,512]{1,0:T(8,128)(2,1)} %copy-done.10, bf16[256,512]{1,0:T(8,128)(2,1)} %copy-done.20, ...), custom_call_target="tpu_custom_call" | custom-call | flops 1000000000 | bytes 1000000 | tf_op jit(solution)/shard_map/attention_forward/pallas_call | solution.py:227
  232.2 40.7 %expert_pass.4 = (bf16[768,1024]{1,0:T(8,128)(2,1)}, bf16[768,1024]{1,0:T(8,128)(2,1)}, f32[8,1,768]{2,1,0:T(1,128)}, bf16[8,336,1024]{2,1,0:T(8,128)(2,1)}, bf1...) custom-call(s32[8]{0:T(128)} %get-tuple-element.442.counts, ...), custom_call_target="tpu_custom_call" | custom-call | flops 1000000000 | bytes 1000000 | tf_op jit(solution)/shard_map/expert_pass/pallas_call | solution.py:497
  275.6 40.7 %expert_pass.5 = (bf16[768,1024]{1,0:T(8,128)(2,1)}, bf16[768,1024]{1,0:T(8,128)(2,1)}, f32[8,1,768]{2,1,0:T(1,128)}, bf16[8,336,1024]{2,1,0:T(8,128)(2,1)}, bf1...) custom-call(s32[8]{0:T(128)} %get-tuple-element.439.counts, ...), custom_call_target="tpu_custom_call" | custom-call | flops 1000000000 | bytes 1000000 | tf_op jit(solution)/shard_map/expert_pass/pallas_call | solution.py:497
  319.2 40.0 %expert_pass.6 = (bf16[768,1024]{1,0:T(8,128)(2,1)}, bf16[768,1024]{1,0:T(8,128)(2,1)}, f32[8,1,768]{2,1,0:T(1,128)}, bf16[8,336,1024]{2,1,0:T(8,128)(2,1)}, bf1...) custom-call(s32[8]{0:T(128)} %get-tuple-element.440.counts, ...), custom_call_target="tpu_custom_call" | custom-call | flops 1000000000 | bytes 1000000 | tf_op jit(solution)/shard_map/expert_pass/pallas_call | solution.py:497
  362.4 39.7 %expert_pass.7 = (bf16[768,1024]{1,0:T(8,128)(2,1)}, bf16[768,1024]{1,0:T(8,128)(2,1)}, f32[8,1,768]{2,1,0:T(1,128)}, bf16[8,336,1024]{2,1,0:T(8,128)(2,1)}, bf1...) custom-call(s32[8]{0:T(128)} %get-tuple-element.441.counts, ...), custom_call_target="tpu_custom_call" | custom-call | flops 1000000000 | bytes 1000000 | tf_op jit(solution)/shard_map/expert_pass/pallas_call | solution.py:497
  410.8 40.6 %up_weight_grads.1 = (bf16[8,8,128,512]{3,2,1,0:T(8,128)(2,1)}, bf16[8,8,128,512]{3,2,1,0:T(8,128)(2,1)}) custom-call(bf16[8,336,1024]{2,1,0:T(8,128)(2,1)} %get-tuple-element.278.refs_0_, bf16[8,336,512]{2,1,0:T(8,128)(2,1)} %get-tuple-element.279.refs_1_, bf16[8,336,512]{2,1,0:T(8,128)(2,1)} %get-tuple-element.280.refs_2_, ...), custom_call_target="tpu_custom_call" | custom-call | flops 1000000000 | bytes 1000000 | tf_op jit(solution)/shard_map/up_weight_grads/pallas_call | solution.py:556
  472.4 23.3 %down_weight_grads.1 = bf16[8,8,512,128]{3,2,1,0:T(8,128)(2,1)} custom-call(bf16[8,336,512]{2,1,0:T(8,128)(2,1)} %get-tuple-element.297.refs_0_, bf16[8,336,1024]{2,1,0:T(8,128)(2,1)} %get-tuple-element.298.refs_1_, bf16[8,336,512]{2,1,0:T(8,128)(2,1)} %get-tuple-element.300.refs_2_, bf16[8,336,1024]{2,1,0:T(8,128)(2,1)} %get-tuple-element.301.refs_3_, ...), custom_call_target="tpu_custom_call" | custom-call | flops 1000000000 | bytes 1000000 | tf_op jit(solution)/shard_map/down_weight_grads/pallas_call | solution.py:571
  495.7 7.3 collective-permute-done.46
  515.2 20.6 %collective-permute-done.50 = bf16[768,1024]{1,0:T(8,128)(2,1)S(1)} collective-permute-done((bf16[768,1024]{1,0:T(8,128)(2,1)}, bf16[768,1024]{1,0:T(8,128)(2,1)S(1)}, u32[]{:S(2)}, u32[]{:S(2)}) %collective-permute-start.50) | collective-permute-done | bytes 1572896 | tf_op jit(solution)/shard_map/ppermute | solution.py:628
  548.8 48.1 %attention_backward.2 = (bf16[768,512]{1,0:T(8,128)(2,1)}, bf16[2048,512]{1,0:T(8,128)(2,1)}, f32[512,256]{1,0:T(8,128)}, f32[512,256]{1,0:T(8,128)}) custom-call(s32[16]{0:T(128)} %reshape.273.places, s32[4]{0:T(128)} %pad_add_fusion.starts, bf16[768,1024]{1,0:T(8,128)(2,1)} %get-tuple-element.326.q_ref, bf16[768,1024]{1,0:T(8,128)(2,1)} %convolution_convert_fusion.do_ref, ...), custom_call_target="tpu_custom_call" | custom-call | flops 1000000000 | bytes 1000000 | tf_op jit(solution)/shard_map/attention_backward/pallas_call | solution.py:371
  605.3 6.8 all-to-all-start.2
  625.0 47.9 %attention_backward.3 = (bf16[768,512]{1,0:T(8,128)(2,1)}, bf16[2048,512]{1,0:T(8,128)(2,1)}, f32[512,256]{1,0:T(8,128)}, f32[512,256]{1,0:T(8,128)}) custom-call(s32[16]{0:T(128)} %reshape.273.places, s32[4]{0:T(128)} %pad_add_fusion.starts, bf16[768,1024]{1,0:T(8,128)(2,1)} %get-tuple-element.326.q_ref, bf16[768,1024]{1,0:T(8,128)(2,1)} %convolution_convert_fusion.do_ref, ...), custom_call_target="tpu_custom_call" | custom-call | flops 1000000000 | bytes 1000000 | tf_op jit(solution)/shard_map/attention_backward/pallas_call | solution.py:371
  681.4 10.0 %outer.2 = bf16[1024,2048]{1,0:T(8,128)(2,1)} custom-call(s32[1]{0:T(128)} %bitcast.33.mine, bf16[768,1024]{1,0:T(8,128)(2,1)} %get-tuple-element.343.refs_0_, bf16[768,1024]{1,0:T(8,128)(2,1)} %constant_dynamic-update-slice_fusion.19.refs_1_, bf16[768,1024]{1,0:T(8,128)(2,1)} %copy-done.14, bf16[768,1024]{1,0:T(8,128)(2,1)} %copy-done.2), custom_call_target="tpu_custom_call" | custom-call | flops 1000000000 | bytes 1000000 | tf_op jit(solution)/shard_map/outer/pallas_call | solution.py:132
  724.9 8.1 collective-permute-done.73
  735.6 7.6 outer.3
  753.7 5.9 fusion.9
  774.6 6.5 fusion.19
  (530 shorter events, 303.4 us)
Async XLA Ops:
  7.3 224.9 %all-gather.7.cloned.1.call-start = ((), (), s32[]{:S(2)}) async-start(), calls=%async_computation.9 | async-start | bytes 9437184 | tf_op jit(solution)/shard_map/all_gather | solution.py:757
  8.0 224.2 %all-gather.9.cloned.1.call-start = ((), (), s32[]{:S(2)}) async-start(), calls=%async_computation.10 | async-start | bytes 9437184 | tf_op jit(solution)/shard_map/all_gather | solution.py:758
  8.8 223.4 %all-gather.11.cloned.1.call-start = ((), (), s32[]{:S(2)}) async-start(), calls=%async_computation.11 | async-start | bytes 9437184 | tf_op jit(solution)/shard_map/all_gather | solution.py:759
  21.0 65.2 %all-to-all-start = ((f32[4,8,768]{2,1,0:T(8,128)}), f32[4,8,768]{2,1,0:T(8,128)S(1)}, u32[]{:S(2)}, u32[]{:S(2)}) async-start(f32[4,8,768]{2,1,0:T(8,128)} %fusion.28), calls=%async_computation | async-start | bytes 196608 | tf_op jit(solution)/shard_map/all_to_all | solution.py:767
  24.3 783.3 %reduce-scatter.6.cloned.1.call-start = ((), (), s32[]{:S(2)}) async-start(), calls=%async_computation.7 | async-start | bytes 9437184 | tf_op jit(solution)/shard_map/reduce_scatter | solution.py:893
  25.7 56.7 %collective-permute-start = (bf16[32,3200]{1,0:T(8,128)(2,1)S(1)}, bf16[32,3200]{1,0:T(8,128)(2,1)S(1)}, u32[]{:S(2)}, u32[]{:S(2)}) collective-permute-start(bf16[32,3200]{1,0:T(8,128)(2,1)S(1)} %concatenate.91.refs_0_), channel_id=1, source_target_pairs={{0,4},{4,0},{8,12},{12,8},{16,20},{20,16},{24,28},{28,24},{1,5},{5... | collective-permute-start | bytes 614408 | tf_op jit(solution)/shard_map/ppermute | solution.py:584
  35.9 51.6 %collective-permute-start.19 = (bf16[768,1024]{1,0:T(8,128)(2,1)S(1)}, bf16[768,1024]{1,0:T(8,128)(2,1)}, u32[]{:S(2)}, u32[]{:S(2)}) collective-permute-start(bf16[768,1024]{1,0:T(8,128)(2,1)S(1)} %bitcast.143), channel_id=1, source_target_pairs={{0,3},{1,0},{2,1},{3,2},{4,7},{5,4},{6,5},{7,6},{8,11},{9,8},{10,9... | collective-permute-start | bytes 4718600 | tf_op jit(solution)/shard_map/ppermute | solution.py:628
  87.4 89.2 %collective-permute-start.32 = (bf16[768,1024]{1,0:T(8,128)(2,1)}, bf16[768,1024]{1,0:T(8,128)(2,1)}, u32[]{:S(2)}, u32[]{:S(2)}) collective-permute-start(bf16[768,1024]{1,0:T(8,128)(2,1)} %collective-permute-done.19.df_ref), channel_id=1, source_target_pairs={{0,3},{1,0},{2,1},{3,2},{4,7},{5,4},{6,5},{7,6},{8,11},{9,8},{10,9... | collective-permute-start | bytes 4718600 | tf_op jit(solution)/shard_map/ppermute | solution.py:628
  221.0 51.9 %collective-permute-start.38 = (bf16[768,1024]{1,0:T(8,128)(2,1)}, bf16[768,1024]{1,0:T(8,128)(2,1)}, u32[]{:S(2)}, u32[]{:S(2)}) collective-permute-start(bf16[768,1024]{1,0:T(8,128)(2,1)} %multiply_convert_fusion.1.a2_ref), channel_id=1, source_target_pairs={{0,3},{1,0},{2,1},{3,2},{4,7},{5,4},{6,5},{7,6},{8,11},{9,8},{10,9... | collective-permute-start | bytes 4718600 | tf_op jit(solution)/shard_map/ppermute | solution.py:628
  228.3 44.5 %collective-permute-start.39 = (f32[8,768]{1,0:T(8,128)}, f32[8,768]{1,0:T(8,128)}, u32[]{:S(2)}, u32[]{:S(2)}) collective-permute-start(f32[8,768]{1,0:T(8,128)} %get-tuple-element.425), channel_id=1, source_target_pairs={{0,1},{1,2},{2,3},{3,0},{4,5},{5,6},{6,7},{7,4},{8,9},{9,10},{10,1... | collective-permute-start | bytes 73736 | tf_op jit(solution)/shard_map/ppermute | solution.py:628
  228.4 44.5 %collective-permute-start.40 = (f32[8,768]{1,0:T(8,128)}, f32[8,768]{1,0:T(8,128)}, u32[]{:S(2)}, u32[]{:S(2)}) collective-permute-start(f32[8,768]{1,0:T(8,128)} %get-tuple-element.424), channel_id=1, source_target_pairs={{0,2},{1,3},{2,0},{3,1},{4,6},{5,7},{6,4},{7,5},{8,10},{9,11},{10,... | collective-permute-start | bytes 73736 | tf_op jit(solution)/shard_map/ppermute | solution.py:628
  228.9 44.0 %collective-permute-start.41 = (f32[8,768]{1,0:T(8,128)}, f32[8,768]{1,0:T(8,128)}, u32[]{:S(2)}, u32[]{:S(2)}) collective-permute-start(f32[8,768]{1,0:T(8,128)} %get-tuple-element.423), channel_id=1, source_target_pairs={{0,3},{1,0},{2,1},{3,2},{4,7},{5,4},{6,5},{7,6},{8,11},{9,8},{10,9... | collective-permute-start | bytes 73736 | tf_op jit(solution)/shard_map/ppermute | solution.py:628
  272.9 43.3 %collective-permute-start.42 = (bf16[768,1024]{1,0:T(8,128)(2,1)}, bf16[768,1024]{1,0:T(8,128)(2,1)}, u32[]{:S(2)}, u32[]{:S(2)}) collective-permute-start(bf16[768,1024]{1,0:T(8,128)(2,1)} %collective-permute-done.38.a2_ref), channel_id=1, source_target_pairs={{0,3},{1,0},{2,1},{3,2},{4,7},{5,4},{6,5},{7,6},{8,11},{9,8},{10,9... | collective-permute-start | bytes 4718600 | tf_op jit(solution)/shard_map/ppermute | solution.py:628
  405.8 45.5 %collective-permute-start.45 = (bf16[768,1024]{1,0:T(8,128)(2,1)}, bf16[768,1024]{1,0:T(8,128)(2,1)}, u32[]{:S(2)}, u32[]{:S(2)}) collective-permute-start(bf16[768,1024]{1,0:T(8,128)(2,1)} %add_convert_fusion.4), channel_id=1, source_target_pairs={{0,3},{1,0},{2,1},{3,2},{4,7},{5,4},{6,5},{7,6},{8,11},{9,8},{10,9... | collective-permute-start | bytes 4718600 | tf_op jit(solution)/shard_map/ppermute | solution.py:628
  451.4 359.0 %reduce-scatter.4.cloned.1.call-start = ((), (), s32[]{:S(2)}) async-start(), calls=%async_computation.6 | async-start | bytes 9437184 | tf_op jit(solution)/shard_map/reduce_scatter | solution.py:893
  452.0 361.3 %reduce-scatter.8.cloned.1.call-start = ((), (), s32[]{:S(2)}) async-start(), calls=%async_computation.8 | async-start | bytes 9437184 | tf_op jit(solution)/shard_map/reduce_scatter | solution.py:893
  537.6 59.4 %collective-permute-start.51 = (bf16[768,1024]{1,0:T(8,128)(2,1)}, bf16[768,1024]{1,0:T(8,128)(2,1)}, u32[]{:S(2)}, u32[]{:S(2)}) collective-permute-start(bf16[768,1024]{1,0:T(8,128)(2,1)} %add_convert_fusion.2), channel_id=1, source_target_pairs={{0,3},{1,0},{2,1},{3,2},{4,7},{5,4},{6,5},{7,6},{8,11},{9,8},{10,9... | collective-permute-start | bytes 4718600 | tf_op jit(solution)/shard_map/ppermute | solution.py:628
  603.1 73.1 %collective-permute-start.52 = (bf16[768,1024]{1,0:T(8,128)(2,1)}, bf16[768,1024]{1,0:T(8,128)(2,1)}, u32[]{:S(2)}, u32[]{:S(2)}) collective-permute-start(bf16[768,1024]{1,0:T(8,128)(2,1)} %add_convert_fusion.1), channel_id=1, source_target_pairs={{0,3},{1,0},{2,1},{3,2},{4,7},{5,4},{6,5},{7,6},{8,11},{9,8},{10,9... | collective-permute-start | bytes 4718600 | tf_op jit(solution)/shard_map/ppermute | solution.py:628
  605.3 67.6 %all-to-all-start.2 = ((f32[32,1,1056]{2,1,0:T(1,128)}), f32[32,1,1056]{2,1,0:T(1,128)S(1)}, u32[]{:S(2)}, u32[]{:S(2)}) async-start(f32[32,1,1056]{2,1,0:T(1,128)} %copy.80), calls=%async_computation.2 | async-start | bytes 294912 | tf_op jit(solution)/shard_map/all_to_all | solution.py:673
  612.2 66.8 %collective-permute-start.53 = (bf16[256,512]{1,0:T(8,128)(2,1)}, bf16[256,512]{1,0:T(8,128)(2,1)}, u32[]{:S(2)}, u32[]{:S(2)}) collective-permute-start(bf16[256,512]{1,0:T(8,128)(2,1)} %get-tuple-element.383), channel_id=1, source_target_pairs={{0,4},{4,0},{8,12},{12,8},{16,20},{20,16},{24,28},{28,24},{1,5},{5... | collective-permute-start | bytes 786440 | tf_op jit(solution)/shard_map/ppermute | solution.py:584
  621.1 57.9 %collective-permute-start.57 = (bf16[256,512]{1,0:T(8,128)(2,1)}, bf16[256,512]{1,0:T(8,128)(2,1)}, u32[]{:S(2)}, u32[]{:S(2)}) collective-permute-start(bf16[256,512]{1,0:T(8,128)(2,1)} %pad_maximum_fusion.5), channel_id=1, source_target_pairs={{0,8},{4,12},{8,0},{12,4},{16,24},{20,28},{24,16},{28,20},{1,9},{5... | collective-permute-start | bytes 786440 | tf_op jit(solution)/shard_map/ppermute | solution.py:584
  623.5 55.4 %collective-permute-start.60 = (bf16[256,512]{1,0:T(8,128)(2,1)}, bf16[256,512]{1,0:T(8,128)(2,1)}, u32[]{:S(2)}, u32[]{:S(2)}) collective-permute-start(bf16[256,512]{1,0:T(8,128)(2,1)} %pad_maximum_fusion.6), channel_id=1, source_target_pairs={{0,16},{4,20},{8,24},{12,28},{16,0},{20,4},{24,8},{28,12},{1,17},{... | collective-permute-start | bytes 786440 | tf_op jit(solution)/shard_map/ppermute | solution.py:584
  746.0 47.8 %collective-permute-start.80 = (bf16[128,1024]{1,0:T(8,128)(2,1)}, bf16[128,1024]{1,0:T(8,128)(2,1)S(1)}, u32[]{:S(2)}, u32[]{:S(2)}) collective-permute-start(bf16[128,1024]{1,0:T(8,128)(2,1)} %get-tuple-element.376), channel_id=1, source_target_pairs={{0,4},{4,0},{8,12},{12,8},{16,20},{20,16},{24,28},{28,24},{1,5},{5... | collective-permute-start | bytes 786440 | tf_op jit(solution)/shard_map/ppermute | solution.py:584
  748.6 43.5 %collective-permute-start.77 = (bf16[32,2048]{1,0:T(8,128)(2,1)}, bf16[32,2048]{1,0:T(8,128)(2,1)S(1)}, u32[]{:S(2)}, u32[]{:S(2)}) collective-permute-start(bf16[32,2048]{1,0:T(8,128)(2,1)} %get-tuple-element.399), channel_id=1, source_target_pairs={{0,1},{1,2},{2,3},{3,0},{4,5},{5,6},{6,7},{7,4},{8,9},{9,10},{10,1... | collective-permute-start | bytes 393224 | tf_op jit(solution)/shard_map/ppermute | solution.py:628
  (155 other events, 2681.1 us)
Sparse Core Ops, SparseCore 0:
  10.0 72.7 all-gather.6
  84.6 69.3 all-gather.8
  156.0 53.0 all-gather.10
  451.5 72.8 reduce-scatter.5
  528.1 71.2 reduce-scatter.3
  602.7 73.6 reduce-scatter.7

commit v5 on v4

--- a/solution.py
+++ b/solution.py
@@ -57,7 +57,7 @@
 
 def project_kernel(places, x_ref, cos_ref, sin_ref, *refs, counts):
     pieces = refs[: len(counts)]
-    normed_ref, q_ref, *kv_refs, qkv_ref, out_ref, rest_ref, gains_ref = refs[len(counts) :]
+    normed_ref, q_ref, kv_ref, qkv_ref, out_ref, rest_ref, gains_ref = refs[len(counts) :]
     rows = MODEL_WIDTH // sum(counts)
     at = 0
     for piece, count in zip(pieces, counts):
@@ -84,8 +84,8 @@
                 q_ref[:, column : column + 128] = part.astype(bf16)
             else:
                 column -= 1024
-                at = column // KV_WIDTH * 256 + column % 256
-                kv_refs[column % KV_WIDTH // 256][:, at : at + 128] = part.astype(bf16)
+                at = column % KV_WIDTH // 256 * 512 + column // KV_WIDTH * 256 + column % 256
+                kv_ref[:, at : at + 128] = part.astype(bf16)
 
 
 def project(x, cosine, sine, pieces, counts, places):
@@ -95,12 +95,11 @@
     return pl.pallas_call(
         functools.partial(project_kernel, counts=counts),
         in_specs=[pl.BlockSpec(memory_space=pltpu.SMEM)] + [whole] * (3 + len(pieces)),
-        out_specs=[whole] * 8,
+        out_specs=[whole] * 7,
         out_shape=[
             shape((tok, MODEL_WIDTH), bf16),
             shape((tok, HQ * HEAD_SIZE), bf16),
-            shape((tok, KV_WIDTH), bf16),
-            shape((tok, KV_WIDTH), bf16),
+            shape((tok, 2 * KV_WIDTH), bf16),
             shape((MODEL_WIDTH, 2048), bf16),
             shape((MODEL_WIDTH, 1024), bf16),
             shape((MODEL_WIDTH, 128), bf16),
@@ -213,12 +212,12 @@
             store(start, block_rows, j, out, m, total, CONT_DEV * CLEN + half * block_rows)
 
 
-def key_specs(pieces, own):
+def key_specs(pieces, own, half):
     spec = pl.BlockSpec
-    keys = [spec((p.shape[0], 128), lambda g, *_: (0, g)) for p in pieces]
-    values = [spec((p.shape[0], 128), lambda g, *_: (0, 2 + g)) for p in pieces]
-    ours = [spec((own, 128), lambda g, *_: (0, g)), spec((own, 128), lambda g, *_: (0, 2 + g))]
-    return keys + values + ours
+    key, value = (lambda g, *_: (0, 4 * half + g)), (lambda g, *_: (0, 4 * half + 2 + g))
+    keys = [spec((p.shape[0], 128), key) for p in pieces]
+    values = [spec((p.shape[0], 128), value) for p in pieces]
+    return keys + values + [spec((own, 128), key), spec((own, 128), value)]
 
 
 def attention_forward(q, pieces, kv_own, places, starts, block_rows, half):
@@ -232,7 +231,7 @@
             num_scalar_prefetch=2,
             grid=(2,),
             in_specs=[spec((tok, 256), lambda g, *_: (0, 2 * half + g))]
-            + key_specs(pieces, kv_own.shape[0]),
+            + key_specs(pieces, kv_own.shape[0], half),
             out_specs=[
                 spec((tok, 256), lambda g, *_: (0, g)),
                 spec((1, 4, tok), lambda g, *_: (g, 0, 0)),
@@ -376,7 +375,7 @@
             num_scalar_prefetch=2,
             grid=(2,),
             in_specs=[wide, wide, spec((1, 4, tok), lambda g, *_: (g, 0, 0)), wide, table, table]
-            + key_specs(pieces, own),
+            + key_specs(pieces, own, half),
             out_specs=[
                 spec((tok, 256), lambda g, *_: (0, g)),
                 spec((PROMPT, KV_WIDTH), lambda g, *_: (0, 0)),
@@ -409,22 +408,13 @@
     df_ref,
     rank_ref,
     gate_ref,
-    wg_ref,
-    wu_ref,
-    wd_ref,
-    mix_ref,
-    da_ref,
-    dg_ref,
-    x_ref,
-    dy_ref,
-    z_ref,
-    dgate_ref,
-    dup_ref,
-    mix_acc,
-    da_acc,
-    *,
+    *refs,
     sizes,
+    pieces,
 ):
+    weights, refs = refs[: 3 * pieces], refs[3 * pieces :]
+    wg_refs, wu_refs, wd_refs = (weights[n * pieces : (n + 1) * pieces] for n in range(3))
+    mix_ref, da_ref, dg_ref, x_ref, dy_ref, z_ref, dgate_ref, dup_ref, mix_acc, da_acc = refs
     e = pl.program_id(0)
 
     @pl.when(e == 0)
@@ -442,9 +432,9 @@
         gate = jnp.sum(jnp.where(hit, gates, 0.0), 1, keepdims=True)
         x = dot(chosen, a2_ref[...]).astype(bf16)
         d_mix = resid_scale * dot(chosen, df_ref[...])
-        wg = wg_ref[:, 0].reshape(MODEL_WIDTH, FF)
-        wu = wu_ref[:, 0].reshape(MODEL_WIDTH, FF)
-        wd = jnp.concatenate([wd_ref[c, 0] for c in range(wd_ref.shape[0])], 1)
+        wg = jnp.concatenate([ref[:, 0].reshape(-1, FF) for ref in wg_refs], 0)
+        wu = jnp.concatenate([ref[:, 0].reshape(-1, FF) for ref in wu_refs], 0)
+        wd = jnp.concatenate([ref[c, 0] for ref in wd_refs for c in range(ref.shape[0])], 1)
         g = dot(x, wg)
         u = dot(x, wu)
         sig = jax.nn.sigmoid(g)
@@ -483,23 +473,25 @@
 
 def expert_pass(a2, df, rank, gates, wg, wu, wd, capacity):
     tok = a2.shape[0]
-    parts, experts = wg.shape[0], wg.shape[1]
+    parts, experts = wg[0].shape[0], wg[0].shape[1]
+    pieces = len(wg)
     sizes = sorted({min(size, capacity) for size in (128, 192, 256, capacity)})
     counts = (jnp.max(rank, 1) + 1.0).astype(jnp.int32)
     spec = pl.BlockSpec
     whole = spec((tok, MODEL_WIDTH), lambda e, *_: (0, 0))
     row = spec((1, 1, tok), lambda e, *_: (e, 0, 0))
-    up = spec((parts, 1, MODEL_WIDTH // parts, FF), lambda e, *_: (0, e, 0, 0))
-    down = spec((parts, 1, FF, MODEL_WIDTH // parts), lambda e, *_: (0, e, 0, 0))
+    width = wg[0].shape[2]
+    up = spec((parts, 1, width, FF), lambda e, *_: (0, e, 0, 0))
+    down = spec((parts, 1, FF, width), lambda e, *_: (0, e, 0, 0))
     rows_wide = spec((1, capacity, MODEL_WIDTH), lambda e, *_: (e, 0, 0))
     rows_thin = spec((1, capacity, FF), lambda e, *_: (e, 0, 0))
     shape = jax.ShapeDtypeStruct
     return pl.pallas_call(
-        functools.partial(expert_kernel, sizes=sizes),
+        functools.partial(expert_kernel, sizes=sizes, pieces=pieces),
         grid_spec=pltpu.PrefetchScalarGridSpec(
             num_scalar_prefetch=1,
             grid=(experts,),
-            in_specs=[whole, whole, row, row, up, up, down],
+            in_specs=[whole, whole, row, row] + [up] * (2 * pieces) + [down] * pieces,
             out_specs=[whole, whole, row, rows_wide, rows_wide, rows_thin, rows_thin, rows_thin],
             scratch_shapes=[
                 pltpu.VMEM((tok, MODEL_WIDTH), f32),
@@ -519,21 +511,24 @@
         compiler_params=pltpu.CompilerParams(vmem_limit_bytes=VMEM_LIMIT),
         cost_estimate=SMALL,
         name="expert_pass",
-    )(counts, a2, df, rank.reshape(experts, 1, tok), gates.reshape(experts, 1, tok), wg, wu, wd)
-
-
-def up_grad_kernel(*refs, sources):
+    )(counts, a2, df, rank.reshape(experts, 1, tok), gates.reshape(experts, 1, tok), *wg, *wu, *wd)
+
+
+def up_grad_kernel(order, *refs, sources):
     rows = refs[: 3 * sources]
     gate_ref, up_ref = refs[3 * sources :]
+    width = gate_ref.shape[2]
     for n, out_ref in ((1, gate_ref), (2, up_ref)):
         total = None
         for s in range(sources):
             term = dot_tn(rows[3 * s][0], rows[3 * s + n][0])
             total = term if total is None else total + term
-        out_ref[...] = total.astype(bf16).reshape(out_ref.shape)
-
-
-def down_grad_kernel(*refs, sources, parts):
+        total = total.astype(bf16)
+        for c in range(out_ref.shape[0]):
+            out_ref[order[c], 0] = total[c * width : (c + 1) * width]
+
+
+def down_grad_kernel(order, *refs, sources, parts):
     rows, down_ref = refs[: 2 * sources], refs[-1]
     width = MODEL_WIDTH // parts
     total = None
@@ -542,68 +537,60 @@
         total = term if total is None else total + term
     total = total.astype(bf16)
     for c in range(parts):
-        down_ref[c, 0] = total[:, c * width : (c + 1) * width]
+        down_ref[order[c], 0] = total[:, c * width : (c + 1) * width]
 
 
 def row_specs(rows):
-    return [pl.BlockSpec((1,) + a.shape[1:], lambda e: (e, 0, 0)) for r in rows for a in r]
-
-
-def up_weight_grads(rows, parts):
+    return [pl.BlockSpec((1,) + a.shape[1:], lambda e, *_: (e, 0, 0)) for r in rows for a in r]
+
+
+def up_weight_grads(rows, order):
+    parts = order.shape[0]
     experts = rows[0][0].shape[0]
     shape = (parts, experts, MODEL_WIDTH // parts, FF)
-    out = pl.BlockSpec((parts, 1) + shape[2:], lambda e: (0, e, 0, 0))
+    out = pl.BlockSpec((parts, 1) + shape[2:], lambda e, *_: (0, e, 0, 0))
     return pl.pallas_call(
         functools.partial(up_grad_kernel, sources=len(rows)),
-        grid=(experts,),
-        in_specs=row_specs(rows),
-        out_specs=[out, out],
+        grid_spec=pltpu.PrefetchScalarGridSpec(
+            num_scalar_prefetch=1,
+            grid=(experts,),
+            in_specs=row_specs(rows),
+            out_specs=[out, out],
+        ),
         out_shape=[jax.ShapeDtypeStruct(shape, bf16)] * 2,
         compiler_params=pltpu.CompilerParams(vmem_limit_bytes=VMEM_LIMIT),
         cost_estimate=SMALL,
         name="up_weight_grads",
-    )(*[a for r in rows for a in r])
-
-
-def down_weight_grads(rows, parts):
+    )(order, *[a for r in rows for a in r])
+
+
+def down_weight_grads(rows, order):
+    parts = order.shape[0]
     experts = rows[0][0].shape[0]
     shape = (parts, experts, FF, MODEL_WIDTH // parts)
     return pl.pallas_call(
         functools.partial(down_grad_kernel, sources=len(rows), parts=parts),
-        grid=(experts,),
-        in_specs=row_specs(rows),
-        out_specs=pl.BlockSpec((parts, 1) + shape[2:], lambda e: (0, e, 0, 0)),
+        grid_spec=pltpu.PrefetchScalarGridSpec(
+            num_scalar_prefetch=1,
+            grid=(experts,),
+            in_specs=row_specs(rows),
+            out_specs=pl.BlockSpec((parts, 1) + shape[2:], lambda e, *_: (0, e, 0, 0)),
+        ),
         out_shape=jax.ShapeDtypeStruct(shape, bf16),
         compiler_params=pltpu.CompilerParams(vmem_limit_bytes=VMEM_LIMIT),
         cost_estimate=SMALL,
         name="down_weight_grads",
-    )(*[a for r in rows for a in r])
+    )(order, *[a for r in rows for a in r])
 
 
 def swap(x, mask):
     return lax.ppermute(x, "ctx", [(i, i ^ mask) for i in range(lax.axis_size("ctx"))])
 
 
-def blocks_ctx(x):
-    return both_cores(even_blocks(x))
-
-
-def even_blocks(x):
-    half = x.shape[0] // 2
-    near, far = swap(x, 2), swap(x, 4)
-    diagonal = jnp.concatenate([swap(near[:half], 4), swap(far[half:], 2)], 0)
-    return [x, near, far, diagonal]
-
-
-def both_cores(even):
-    odd = [swap(block, 1) for block in even]
-    return [b for pair in zip(even, odd) for b in pair]
-
-
-def gather_ctx(x):
+def gather_ctx(x, rows):
     if lax.axis_size("ctx") != 8:
-        return [lax.all_gather(x, "ctx", axis=0, tiled=True)]
-    return blocks_ctx(x)
+        return lax.all_gather(x[:rows], "ctx", axis=0, tiled=True)
+    return plane_gather(x, rows)
 
 
 def scatter_ctx(x):
@@ -623,6 +610,171 @@
     return own + swap(near, 2).astype(f32) + swap(far, 4).astype(f32)
 
 
+MESH = pl.DeviceIdType.MESH
+ANY = pl.BlockSpec(memory_space=pl.ANY)
+
+
+def partner(mask):
+    me = lax.axis_index("ctx")
+    return me + mask - 2 * mask * ((me // mask) % 2)
+
+
+def ahead(distance):
+    return (lax.axis_index("wt") + distance) % lax.axis_size("wt")
+
+
+class Copies:
+    def __init__(self, send, recv):
+        self.send, self.recv, self.made = send, recv, {}
+
+    def start(self, name, source, target, device):
+        n = len(self.made)
+        self.made[name] = copy = pltpu.make_async_remote_copy(
+            src_ref=source,
+            dst_ref=target,
+            send_sem=self.send.at[n],
+            recv_sem=self.recv.at[n],
+            device_id=device,
+            device_id_type=MESH,
+        )
+        copy.start()
+
+    def arrived(self, name):
+        self.made[name].wait_recv()
+
+    def close(self):
+        for copy in self.made.values():
+            copy.wait_send()
+
+
+def greet(devices):
+    barrier = pltpu.get_barrier_semaphore()
+    for device in devices:
+        pl.semaphore_signal(barrier, inc=1, device_id=device, device_id_type=MESH)
+    pl.semaphore_wait(barrier, len(devices))
+
+
+def plane_steps(copies, block, half, key):
+    side, near, far = ({"ctx": partner(m)} for m in (1, 2, 4))
+    top, end = (lambda m: block(m, 0, half)), (lambda m: block(m, half, half))
+
+    def first():
+        copies.start((key, 2), block(0), block(2), near)
+        copies.start((key, 4), block(0), block(4), far)
+        copies.start((key, 1), block(0), block(1), side)
+
+    def second():
+        copies.arrived((key, 2))
+        copies.start((key, 6), top(2), top(6), far)
+        copies.start((key, 3), block(2), block(3), side)
+
+    def third():
+        copies.arrived((key, 4))
+        copies.start((key, 7), end(4), end(6), near)
+        copies.start((key, 5), block(4), block(5), side)
+
+    def fourth():
+        copies.arrived((key, 6))
+        copies.arrived((key, 7))
+        copies.start((key, 8), block(6), block(7), side)
+
+    def last():
+        for m in (1, 3, 5, 8):
+            copies.arrived((key, m))
+
+    return [first, second, third, fourth, last]
+
+
+def plane_gather_kernel(x_ref, out_ref, send, recv, own_sem):
+    rows = out_ref.shape[0] // 8
+    greet([{"ctx": partner(m)} for m in (1, 2, 4)])
+    own = pltpu.make_async_copy(x_ref.at[pl.ds(0, rows)], out_ref.at[pl.ds(0, rows)], own_sem)
+    own.start()
+    copies = Copies(send, recv)
+
+    def block(m, start=0, count=rows):
+        if m == 0:
+            return x_ref.at[pl.ds(start, count)]
+        return out_ref.at[pl.ds(m * rows + start, count)]
+
+    for step in plane_steps(copies, block, rows // 2, 0):
+        step()
+    own.wait()
+    copies.close()
+
+
+def plane_gather(x, rows):
+    return pl.pallas_call(
+        plane_gather_kernel,
+        in_specs=[ANY],
+        out_specs=ANY,
+        out_shape=jax.ShapeDtypeStruct((8 * rows, x.shape[1]), x.dtype),
+        scratch_shapes=[
+            pltpu.SemaphoreType.DMA((8,)),
+            pltpu.SemaphoreType.DMA((8,)),
+            pltpu.SemaphoreType.DMA,
+        ],
+        compiler_params=pltpu.CompilerParams(collective_id=1, has_side_effects=True),
+        cost_estimate=SMALL,
+        name="plane_gather",
+    )(x)
+
+
+def packed_gather_kernel(x_ref, out_ref, send, recv, own_sem):
+    rows = x_ref.shape[0]
+    greet(
+        [{"ctx": partner(m)} for m in (1, 2, 4)] + [{"wt": ahead(d)} for d in (1, 2, 3)]
+    )
+    own = pltpu.make_async_copy(x_ref, out_ref.at[pl.ds(0, rows)], own_sem)
+    own.start()
+    copies = Copies(send, recv)
+
+    def block_of(d):
+        def block(m, start=0, count=rows):
+            if m == 0 and d == 0:
+                return x_ref.at[pl.ds(start, count)]
+            return out_ref.at[pl.ds((4 * m + d) * rows + start, count)]
+
+        return block
+
+    for d in (1, 3, 2):
+        copies.start(d, x_ref, block_of(d)(0), {"wt": ahead(d)})
+    steps = {d: plane_steps(copies, block_of(d), rows // 2, ("plane", d)) for d in range(4)}
+    steps[0][0]()
+    for d, before in ((1, 0), (3, 1), (2, 3)):
+        copies.arrived(d)
+        steps[d][0]()
+        steps[before][1]()
+        steps[before][2]()
+        if d != 1:
+            steps[{3: 0, 2: 1}[d]][3]()
+    steps[2][1]()
+    steps[2][2]()
+    steps[3][3]()
+    steps[2][3]()
+    for d in range(4):
+        steps[d][4]()
+    own.wait()
+    copies.close()
+
+
+def packed_gather(x):
+    return pl.pallas_call(
+        packed_gather_kernel,
+        in_specs=[ANY],
+        out_specs=ANY,
+        out_shape=jax.ShapeDtypeStruct((32 * x.shape[0], x.shape[1]), x.dtype),
+        scratch_shapes=[
+            pltpu.SemaphoreType.DMA((35,)),
+            pltpu.SemaphoreType.DMA((35,)),
+            pltpu.SemaphoreType.DMA,
+        ],
+        compiler_params=pltpu.CompilerParams(collective_id=2, has_side_effects=True),
+        cost_estimate=SMALL,
+        name="packed_gather",
+    )(x)
+
+
 def shift(x, distance):
     n = lax.axis_size("wt")
     return lax.ppermute(x, "wt", [(i, (i + distance) % n) for i in range(n)])
@@ -636,16 +788,12 @@
 def gather_all(x):
     ctx, wt = lax.axis_size("ctx"), lax.axis_size("wt")
     if ctx != 8 or wt != 4:
-        return [lax.all_gather(x, ALL, axis=0, tiled=True)], [1], jnp.zeros((1,), jnp.int32), x
+        return [lax.all_gather(x, ALL, axis=0, tiled=True)], [1], jnp.zeros((1,), jnp.int32)
     ctx_index, wt_index = lax.axis_index("ctx"), lax.axis_index("wt")
-    others = jnp.concatenate([shift(x, d) for d in (1, 2, 3)], 0)
-    pieces = blocks_ctx(x) + blocks_ctx(others)
     m = jnp.arange(8, dtype=jnp.int32)
-    own = (ctx_index ^ m) * wt + wt_index
-    d = jnp.arange(1, 4, dtype=jnp.int32)
-    rest = ((ctx_index ^ m) * wt)[:, None] + ((wt_index - d) % wt)[None, :]
-    places = jnp.concatenate([own, rest.reshape(-1)]).astype(jnp.int32)
-    return pieces, [1] * 8 + [3] * 8, places, others
+    d = jnp.arange(4, dtype=jnp.int32)
+    places = ((ctx_index ^ m) * wt)[:, None] + ((wt_index - d) % wt)[None, :]
+    return [packed_gather(x)], [32], places.reshape(-1).astype(jnp.int32)
 
 
 def outer_part(*pairs):
@@ -752,11 +900,40 @@
         ],
         1,
     )
-    pieces, counts, block_places, first_part = gather_all(packed)
-
-    gate_full = lax.all_gather(gate_weight, "ctx", axis=0, tiled=False)
-    up_full = lax.all_gather(up_weight, "ctx", axis=0, tiled=False)
-    down_full = lax.all_gather(down_weight, "ctx", axis=0, tiled=False)
+    pieces, counts, block_places = gather_all(packed)
+
+    core = ctx_index % 2
+    if context_size == 8:
+        chips = [[0, 2, 4, 6], [1, 3, 5, 7]]
+        expert_weights = [
+            [lax.all_gather(w, "ctx", axis=0, tiled=False, axis_index_groups=chips)]
+            for w in (gate_weight, up_weight, down_weight)
+        ]
+        four = 2 * jnp.arange(4, dtype=jnp.int32)
+        width_order = jnp.concatenate([four + core, four + 1 - core]).astype(jnp.int32)
+    else:
+        expert_weights = [
+            [lax.all_gather(w, "ctx", axis=0, tiled=False)]
+            for w in (gate_weight, up_weight, down_weight)
+        ]
+        width_order = jnp.arange(context_size, dtype=jnp.int32)
+
+    def to_line(x):
+        if context_size != 8:
+            return x
+        x = x.reshape(tok, 4, 2, 128)
+        ours, others = (x[:, :, n].reshape(tok, 512) for n in range(2))
+        return jnp.where(
+            core == 0, jnp.concatenate([ours, others], 1), jnp.concatenate([others, ours], 1)
+        )
+
+    def from_line(x):
+        if context_size != 8:
+            return x
+        ours, others = (x[:, 512 * n : 512 * n + 512].reshape(tok, 4, 128) for n in range(2))
+        return jnp.where(
+            core == 0, jnp.stack([ours, others], 2), jnp.stack([others, ours], 2)
+        ).reshape(tok, MODEL_WIDTH)
 
     mask = jnp.any(
         routes[:, :, None] == jnp.arange(EXPERTS, dtype=jnp.int32)[None, None, :], 1
@@ -768,9 +945,10 @@
         rank.T.reshape(shard_count, expert_count, tok), "wt", 0, 0, tiled=True
     )
     last = shard_count - 1
-    grads_in = {0: out_low, last: shift(after(out_low, first_part), -1)}
-
-    pieces, grads_in[last], ranks = beside(pieces, grads_in[last], ranks)
+    out_line = to_line(out_low)
+    grads_in = {0: out_line, last: shift(after(out_line, pieces[0]), -1)}
+
+    pieces, ranks = beside(pieces, ranks)
     local_rows = jnp.arange(tok, dtype=jnp.int32)
     mine = lax.dynamic_slice_in_dim(deal_row, 2 * ctx_index, 2, 0)
     prompt_place = (
@@ -781,20 +959,14 @@
         local_rows < prompt_local, prompt_place, PROMPT + (local_rows - prompt_local) % CLEN
     )
     cosine, sine = rope_tables(positions, 128)
-    normed_one, turned_query, *kv_low, qkv_full, output_t, rest, gain_rows = project(
+    normed_one, turned_query, kv_low, qkv_full, output_t, rest, gain_rows = project(
         layer_input[0], cosine, sine, pieces, counts, block_places
     )
     router_full = rest[:, :EXPERTS]
     first_gain, second_gain = gain_rows[0], gain_rows[1]
     inverse_one = lax.rsqrt(jnp.mean(inputs * inputs, -1, keepdims=True) + norm_eps)
-    kv_own = [low[prompt_local:] for low in kv_low]
-    kv_prompt = [low[:prompt_local] for low in kv_low]
-    if context_size == 8:
-        kv_even = [even_blocks(low) for low in kv_prompt]
-        kv_even[0], turned_query = beside(kv_even[0], after(turned_query, *kv_even[1]))
-        kv_pieces = [both_cores(even) for even in kv_even]
-    else:
-        kv_pieces = [gather_ctx(low) for low in kv_prompt]
+    kv_own = kv_low[prompt_local:]
+    kv_pieces, grads_in[last] = beside([gather_ctx(kv_low, prompt_local)], grads_in[last])
 
     places = deal_row
     if context_size == 8:
@@ -814,11 +986,17 @@
     heads = []
     for half in range(2):
         result = attention_forward(
-            turned_query, kv_pieces[half], kv_own[half], places, starts, block_rows, half
+            turned_query, kv_pieces, kv_own, places, starts, block_rows, half
         )
         d = last - 1 - half
         grads_in[d] = shift(grads_in[d + 1], -1)
         result, grads_in[d] = beside(result, grads_in[d])
+        if context_size == 8:
+            for weights in expert_weights[half : 2 * half + 1]:
+                result, sibling = beside(
+                    result, swap(after(weights[0], turned_query, *kv_pieces), 1)
+                )
+                weights.append(sibling)
         if half == 0:
             turned_query = after(turned_query, result[0])
         heads.append(result)
@@ -841,7 +1019,7 @@
     for d in range(shard_count):
         piece = lax.dynamic_index_in_dim(gates_out, (wt_index + d) % shard_count, 0, False)
         gates_in.append(shift(piece, d) if d else piece)
-    got = {0: normed_two}
+    got = {0: to_line(normed_two)}
     partial, mixed, gate_grads, rows = {}, {}, {}, []
     carried = None
 
@@ -852,7 +1030,7 @@
         source = (wt_index - d) % shard_count
         rank_in = lax.dynamic_index_in_dim(ranks, source, 0, False)
         result = expert_pass(
-            got[d], grads_in[d], rank_in, gates_in[d], gate_full, up_full, down_full, capacity
+            got[d], grads_in[d], rank_in, gates_in[d], *expert_weights, capacity
         )
         coming = d - 1 if d else last
         if coming:
@@ -870,18 +1048,18 @@
             got[coming] = after(got[coming], partial[d])
     carried = shift(add(carried, partial[2]), -1)
     (gate_grad, up_grad), carried = beside(
-        up_weight_grads([(after(r[0], partial[1]), r[3], r[4]) for r in rows], context_size),
+        up_weight_grads([(after(r[0], partial[1]), r[3], r[4]) for r in rows], width_order),
         carried,
     )
     carried = shift(add(carried, partial[1]), -1)
     down_grad, home = beside(
-        down_weight_grads([(after(r[2], gate_grad), r[1]) for r in rows], context_size), carried
+        down_weight_grads([(after(r[2], gate_grad), r[1]) for r in rows], width_order), carried
     )
 
     stacked = jnp.stack([gate_grads[d] for d in range(shard_count)], 0)
     stacked = jnp.roll(stacked, wt_index, 0).reshape(EXPERTS, tok).T
     grad_logits = (gates * (stacked - jnp.sum(gates * stacked, -1, keepdims=True))).astype(bf16)
-    grad_normed_two = partial[0].astype(f32) + home.astype(f32)
+    grad_normed_two = from_line(partial[0].astype(f32) + home.astype(f32))
     grad_normed_two = grad_normed_two + dot_nt(grad_logits, router_full)
     grad_mid_norm, second_gain_grad = norm_backward(
         middle, inverse_two, second_gain, grad_normed_two
@@ -913,8 +1091,8 @@
             attended,
             cosine,
             sine,
-            kv_pieces[half],
-            kv_own[half],
+            kv_pieces,
+            kv_own,
             places,
             starts,
             block_rows,
@@ -931,7 +1109,7 @@
         ours.append((d_key_own, d_value_own))
     for d in range(last - 3, 0, -1):
         carried = shift(add(carried, mixed[d]), -1)
-    mixture = mixed[0].astype(f32) + carried.astype(f32)
+    mixture = from_line(mixed[0].astype(f32) + carried.astype(f32))
     layer_output = (middle + resid_scale * mixture).astype(bf16)
     d_query = jnp.concatenate(d_query, 1)
     query_part = outer_part((normed_one, d_query), (after(grad_branch, d_query), attended))

time: 832 us -> 957 us (1.15)
  Pallas kernels: 403 us -> 503 us
  local copies, waits for them, and re-layouts: 56.8 us -> 110 us
  starting transfers between devices: 128 us -> 87.4 us
  other arithmetic: 64.7 us -> 95.5 us
  waiting for transfers between devices: 126 us -> 111 us
    pallas_call x4 -> x6, Pallas kernels: 161 us -> 260 us  [the longest x4 175 us: expert_pass(): pl.pallas_call(functools.partial(expert_kernel, sizes=sizes, pieces=piece...]
    ppermute x64 -> x35, waiting for transfers between devices: 85.2 us -> 27.9 us  [swap(): lax.ppermute(x, 'ctx', [(i, i ^ mask) for i in range(lax.axis_size('ctx'))])]
    ppermute x64 -> x35, starting transfers between devices: 48.2 us -> 21.9 us  [swap(): lax.ppermute(x, 'ctx', [(i, i ^ mask) for i in range(lax.axis_size('ctx'))])]
    all_to_all x1, waiting for transfers between devices: 0.01 us -> 24.5 us  [per_device(): lax.all_to_all(rank.T.reshape(shard_count, expert_count, tok), 'wt', 0, 0...]
    ppermute x27 -> x24, starting transfers between devices: 65.3 us -> 46.9 us  [shift(): return lax.ppermute(x, 'wt', [(i, (i + distance) % n) for i in range(n)])]
    another operation x0 -> x8, local copies, waits for them, and re-layouts: none -> 16.9 us  [the longest x4 10.9 us: from_line(): jnp.stack([ours, others], 2)]
    select_n x1 -> x4, other arithmetic: 0.01 us -> 13.2 us  [the longest x1 8.56 us: from_line(): jnp.where(core == 0, jnp.stack([ours, others], 2), jnp.stack([others, our...]
    slice x12 -> x5, local copies, waits for them, and re-layouts: 6.7 us -> 19.9 us  [the longest x2 14.9 us: to_line(): ours, others = (x[:, :, n].reshape(tok, 512) for n in range(2))]
  transfers between devices with their start and end apart: 100 -> 68, of which waited for: 30 -> 19; matrix products, arithmetic and copies ran while one was open for 16% -> 20% of each run, Pallas kernels for 49% -> 53%
where the time goes in v5:
time: 957 us; the launch traced here: 948 us
  Pallas kernels  503 us (53%)
  waiting for transfers between devices  111 us (12%)
  local copies, waits for them, and re-layouts  110 us (11%)
  other arithmetic  95.5 us (10%)
  starting transfers between devices  87.4 us (9%)
  matrix products  24.1 us (3%)
  between operations  18.5 us (2%)
    pallas_call x4, Pallas kernels, expert_pass(): pl.pallas_call(functools.partial(expert_kernel, sizes=sizes, pieces=piece...  175 us
    pallas_call x2, Pallas kernels, attention_backward(): pl.pallas_call(functools.partial(attention_backward_kernel, block_rows=bl...  97.2 us
    pallas_call x2, Pallas kernels, attention_forward(): pl.pallas_call(functools.partial(attention_forward_kernel, block_rows=blo...  53.1 us
    pallas_call x1, Pallas kernels, packed_gather(): pl.pallas_call(packed_gather_kernel, in_specs=[ANY], out_specs=ANY, out_s...  52.4 us
    ppermute x24, waiting for transfers between devices, shift(): return lax.ppermute(x, 'wt', [(i, (i + distance) % n) for i in range(n)])  48.6 us
    ppermute x24, starting transfers between devices, shift(): return lax.ppermute(x, 'wt', [(i, (i + distance) % n) for i in range(n)])  46.9 us
    pallas_call x1, Pallas kernels, up_weight_grads(): pl.pallas_call(functools.partial(up_grad_kernel, sources=len(rows)), grid...  41.2 us
    pallas_call x1, Pallas kernels, plane_gather(): pl.pallas_call(plane_gather_kernel, in_specs=[ANY], out_specs=ANY, out_sh...  33 us
  transfers between devices with their start and end apart: 68, of which 19 were waited for; matrix products, arithmetic and copies ran while one was open for 20% of the time, Pallas kernels for 53%

profile of v5, /device:TPU:0, one launch (start us, length us, event | category | flops | bytes accessed | tf_op | source)
XLA Modules:
  0.0 948.4 jit_solution(4572294892805155355)
XLA Ops:
  10.8 8.9 slice_reduce_fusion.1
  20.6 52.4 %packed_gather.1.refs_0_ = bf16[1024,3200]{1,0:T(8,128)(2,1)} custom-call(bf16[32,3200]{1,0:T(8,128)(2,1)} %concatenate.87.x_ref), custom_call_target="tpu_custom_call" | custom-call | flops 1000000000 | bytes 1000000 | tf_op jit(solution)/shard_map/packed_gather/pallas_call | solution.py:762
  93.0 24.5 %all-to-all-done = f32[4,8,768]{2,1,0:T(8,128)S(1)} async-done(((f32[4,8,768]{2,1,0:T(8,128)}), f32[4,8,768]{2,1,0:T(8,128)S(1)}, u32[]{:S(2)}, u32[]{:S(2)}) %all-to-all-start) | async-done | bytes 98336 | tf_op jit(solution)/shard_map/all_to_all | solution.py:944
  117.5 8.9 project.1
  126.4 33.0 %plane_gather.1.refs_0_.refs_1_ = bf16[2048,1024]{1,0:T(8,128)(2,1)} custom-call(bf16[768,1024]{1,0:T(8,128)(2,1)} %get-tuple-element.174.x_ref), custom_call_target="tpu_custom_call" | custom-call | flops 1000000000 | bytes 1000000 | tf_op jit(solution)/shard_map/plane_gather/pallas_call | solution.py:707
  166.2 26.5 %attention_forward.2 = (bf16[768,512]{1,0:T(8,128)(2,1)}, f32[2,4,768]{2,1,0:T(4,128)}) custom-call(s32[16]{0:T(128)} %reshape.289.places, s32[4]{0:T(128)} %get-tuple-element.430.starts, bf16[768,1024]{1,0:T(8,128)(2,1)} %get-tuple-element.308.q_ref, bf16[2048,1024]{1,0:T(8,128)(2,1)} %plane_gather.1.refs_0_.refs_1_, ...), custom_call_target="tpu_custom_call" | custom-call | flops 1000000000 | bytes 1000000 | tf_op jit(solution)/shard_map/attention_forward/pallas_call | solution.py:226
  197.5 6.9 all-gather.11.cloned.1.call-done
  209.2 26.6 %attention_forward.3 = (bf16[768,512]{1,0:T(8,128)(2,1)}, f32[2,4,768]{2,1,0:T(4,128)}) custom-call(s32[16]{0:T(128)} %reshape.289.places, s32[4]{0:T(128)} %get-tuple-element.430.starts, bf16[768,1024]{1,0:T(8,128)(2,1)} %get-tuple-element.308.q_ref, bf16[2048,1024]{1,0:T(8,128)(2,1)} %plane_gather.1.refs_0_.refs_1_, ...), custom_call_target="tpu_custom_call" | custom-call | flops 1000000000 | bytes 1000000 | tf_op jit(solution)/shard_map/attention_forward/pallas_call | solution.py:226
  235.8 6.3 collective-permute-done.3.df_ref
  290.4 50.9 %expert_pass.4 = (bf16[768,1024]{1,0:T(8,128)(2,1)}, bf16[768,1024]{1,0:T(8,128)(2,1)}, f32[8,1,768]{2,1,0:T(1,128)}, bf16[8,336,1024]{2,1,0:T(8,128)(2,1)}, bf1...) custom-call(s32[8]{0:T(128)} %get-tuple-element.438.counts, ...), custom_call_target="tpu_custom_call" | custom-call | flops 1000000000 | bytes 1000000 | tf_op jit(solution)/shard_map/expert_pass/pallas_call | solution.py:489
  345.8 39.9 %expert_pass.5 = (bf16[768,1024]{1,0:T(8,128)(2,1)}, bf16[768,1024]{1,0:T(8,128)(2,1)}, f32[8,1,768]{2,1,0:T(1,128)}, bf16[8,336,1024]{2,1,0:T(8,128)(2,1)}, bf1...) custom-call(s32[8]{0:T(128)} %get-tuple-element.435.counts, ...), custom_call_target="tpu_custom_call" | custom-call | flops 1000000000 | bytes 1000000 | tf_op jit(solution)/shard_map/expert_pass/pallas_call | solution.py:489
  388.9 42.5 %expert_pass.6 = (bf16[768,1024]{1,0:T(8,128)(2,1)}, bf16[768,1024]{1,0:T(8,128)(2,1)}, f32[8,1,768]{2,1,0:T(1,128)}, bf16[8,336,1024]{2,1,0:T(8,128)(2,1)}, bf1...) custom-call(s32[8]{0:T(128)} %get-tuple-element.436.counts, ...), custom_call_target="tpu_custom_call" | custom-call | flops 1000000000 | bytes 1000000 | tf_op jit(solution)/shard_map/expert_pass/pallas_call | solution.py:489
  432.9 41.6 %expert_pass.7 = (bf16[768,1024]{1,0:T(8,128)(2,1)}, bf16[768,1024]{1,0:T(8,128)(2,1)}, f32[8,1,768]{2,1,0:T(1,128)}, bf16[8,336,1024]{2,1,0:T(8,128)(2,1)}, bf1...) custom-call(s32[8]{0:T(128)} %get-tuple-element.437.counts, ...), custom_call_target="tpu_custom_call" | custom-call | flops 1000000000 | bytes 1000000 | tf_op jit(solution)/shard_map/expert_pass/pallas_call | solution.py:489
  480.8 41.2 %up_weight_grads.1 = (bf16[8,8,128,512]{3,2,1,0:T(8,128)(2,1)}, bf16[8,8,128,512]{3,2,1,0:T(8,128)(2,1)}) custom-call(s32[8]{0:T(128)} %pad_add_fusion.1.order, bf16[8,336,1024]{2,1,0:T(8,128)(2,1)} %get-tuple-element.260.refs_0_, bf16[8,336,512]{2,1,0:T(8,128)(2,1)} %get-tuple-element.261.refs_1_, bf16[8,336,512]{2,1,0:T(8,128)(2,1)} %get-tuple-element.262.refs_2_, ...), custom_call_target="tpu_custom_call" | custom-call | flops 1000000000 | bytes 1000000 | tf_op jit(solution)/shard_map/up_weight_grads/pallas_call | solution.py:552
  539.3 24.2 %down_weight_grads.1 = bf16[8,8,512,128]{3,2,1,0:T(8,128)(2,1)} custom-call(s32[8]{0:T(128)} %pad_add_fusion.1.order, bf16[8,336,512]{2,1,0:T(8,128)(2,1)} %get-tuple-element.279.refs_0_, bf16[8,336,1024]{2,1,0:T(8,128)(2,1)} %get-tuple-element.280.refs_1_, bf16[8,336,512]{2,1,0:T(8,128)(2,1)} %get-tuple-element.282.refs_2_, ...), custom_call_target="tpu_custom_call" | custom-call | flops 1000000000 | bytes 1000000 | tf_op jit(solution)/shard_map/down_weight_grads/pallas_call | solution.py:571
  563.5 8.2 collective-permute-done.14
  581.7 8.6 maximum_select_fusion
  608.5 22.7 %collective-permute-done.18 = bf16[768,1024]{1,0:T(8,128)(2,1)S(1)} collective-permute-done((bf16[768,1024]{1,0:T(8,128)(2,1)}, bf16[768,1024]{1,0:T(8,128)(2,1)S(1)}, u32[]{:S(2)}, u32[]{:S(2)}) %collective-permute-start.18) | collective-permute-done | bytes 1572896 | tf_op jit(solution)/shard_map/ppermute | solution.py:780
  641.5 48.8 %attention_backward.2 = (bf16[768,512]{1,0:T(8,128)(2,1)}, bf16[2048,512]{1,0:T(8,128)(2,1)}, f32[512,256]{1,0:T(8,128)}, f32[512,256]{1,0:T(8,128)}) custom-call(s32[16]{0:T(128)} %reshape.289.places, s32[4]{0:T(128)} %get-tuple-element.430.starts, bf16[768,1024]{1,0:T(8,128)(2,1)} %get-tuple-element.308.q_ref, ...), custom_call_target="tpu_custom_call" | custom-call | flops 1000000000 | bytes 1000000 | tf_op jit(solution)/shard_map/attention_backward/pallas_call | solution.py:370
  700.1 7.6 all-to-all-start.2
  720.9 48.4 %attention_backward.3 = (bf16[768,512]{1,0:T(8,128)(2,1)}, bf16[2048,512]{1,0:T(8,128)(2,1)}, f32[512,256]{1,0:T(8,128)}, f32[512,256]{1,0:T(8,128)}) custom-call(s32[16]{0:T(128)} %reshape.289.places, s32[4]{0:T(128)} %get-tuple-element.430.starts, bf16[768,1024]{1,0:T(8,128)(2,1)} %get-tuple-element.308.q_ref, ...), custom_call_target="tpu_custom_call" | custom-call | flops 1000000000 | bytes 1000000 | tf_op jit(solution)/shard_map/attention_backward/pallas_call | solution.py:370
  777.1 10.0 %outer.2 = bf16[1024,2048]{1,0:T(8,128)(2,1)} custom-call(s32[1]{0:T(128)} %bitcast.43.mine, bf16[768,1024]{1,0:T(8,128)(2,1)} %get-tuple-element.325.refs_0_, bf16[768,1024]{1,0:T(8,128)(2,1)} %constant_dynamic-update-slice_fusion.10.refs_1_, bf16[768,1024]{1,0:T(8,128)(2,1)} %copy-done.14, bf16[768,1024]{1,0:T(8,128)(2,1)} %copy-done.3), custom_call_target="tpu_custom_call" | custom-call | flops 1000000000 | bytes 1000000 | tf_op jit(solution)/shard_map/outer/pallas_call | solution.py:131
  848.9 8.2 collective-permute-done.41
  860.1 7.6 outer.3
  (421 shorter events, 325.3 us)
Async XLA Ops:
  7.2 152.3 %all-gather.7.cloned.1.call-start = ((), (), s32[]{:S(2)}) async-start(), calls=%async_computation.9 | async-start | bytes 5242880 | tf_op jit(solution)/shard_map/all_gather | solution.py:909
  7.9 189.6 %all-gather.9.cloned.1.call-start = ((), (), s32[]{:S(2)}) async-start(), calls=%async_computation.10 | async-start | bytes 5242880 | tf_op jit(solution)/shard_map/all_gather | solution.py:909
  8.7 195.7 %all-gather.11.cloned.1.call-start = ((), (), s32[]{:S(2)}) async-start(), calls=%async_computation.11 | async-start | bytes 5242880 | tf_op jit(solution)/shard_map/all_gather | solution.py:909
  73.8 85.7 %collective-permute-start = (bf16[768,1024]{1,0:T(8,128)(2,1)S(1)}, bf16[768,1024]{1,0:T(8,128)(2,1)}, u32[]{:S(2)}, u32[]{:S(2)}) collective-permute-start(bf16[768,1024]{1,0:T(8,128)(2,1)S(1)} %maximum_select_fusion.2.df_ref), channel_id=1, source_target_pairs={{0,3},{1,0},{2,1},{3,2},{4,7},{5,4},{6,5},{7,6},{8,11},{9,8},{10,9... | collective-permute-start | bytes 4718600 | tf_op jit(solution)/shard_map/ppermute | solution.py:780
  84.1 848.7 %reduce-scatter.6.cloned.1.call-start = ((), (), s32[]{:S(2)}) async-start(), calls=%async_computation.7 | async-start | bytes 9437184 | tf_op jit(solution)/shard_map/reduce_scatter | solution.py:1071
  197.5 46.4 %collective-permute-start.4 = (bf16[4,8,128,512]{3,2,1,0:T(8,128)(2,1)}, bf16[4,8,128,512]{3,2,1,0:T(8,128)(2,1)}, u32[]{:S(2)}, u32[]{:S(2)}) collective-permute-start(bf16[4,8,128,512]{3,2,1,0:T(8,128)(2,1)} %bitcast.151), channel_id=1, source_target_pairs={{0,4},{4,0},{8,12},{12,8},{16,20},{20,16},{24,28},{28,24},{1,5},{5... | collective-permute-start | bytes 12582920 | tf_op jit(solution)/shard_map/ppermute | solution.py:587
  278.1 63.2 %collective-permute-start.6 = (bf16[768,1024]{1,0:T(8,128)(2,1)}, bf16[768,1024]{1,0:T(8,128)(2,1)}, u32[]{:S(2)}, u32[]{:S(2)}) collective-permute-start(bf16[768,1024]{1,0:T(8,128)(2,1)} %maximum_select_fusion.3.a2_ref), channel_id=1, source_target_pairs={{0,3},{1,0},{2,1},{3,2},{4,7},{5,4},{6,5},{7,6},{8,11},{9,8},{10,9... | collective-permute-start | bytes 4718600 | tf_op jit(solution)/shard_map/ppermute | solution.py:780
  286.6 54.8 %collective-permute-start.7 = (f32[8,768]{1,0:T(8,128)S(1)}, f32[8,768]{1,0:T(8,128)S(1)}, u32[]{:S(2)}, u32[]{:S(2)}) collective-permute-start(f32[8,768]{1,0:T(8,128)S(1)} %get-tuple-element.415), channel_id=1, source_target_pairs={{0,1},{1,2},{2,3},{3,0},{4,5},{5,6},{6,7},{7,4},{8,9},{9,10},{10,1... | collective-permute-start | bytes 73736 | tf_op jit(solution)/shard_map/ppermute | solution.py:780
  286.6 54.8 %collective-permute-start.8 = (f32[8,768]{1,0:T(8,128)S(1)}, f32[8,768]{1,0:T(8,128)S(1)}, u32[]{:S(2)}, u32[]{:S(2)}) collective-permute-start(f32[8,768]{1,0:T(8,128)S(1)} %get-tuple-element.414), channel_id=1, source_target_pairs={{0,2},{1,3},{2,0},{3,1},{4,6},{5,7},{6,4},{7,5},{8,10},{9,11},{10,... | collective-permute-start | bytes 73736 | tf_op jit(solution)/shard_map/ppermute | solution.py:780
  287.1 54.2 %collective-permute-start.9 = (f32[8,768]{1,0:T(8,128)S(1)}, f32[8,768]{1,0:T(8,128)S(1)}, u32[]{:S(2)}, u32[]{:S(2)}) collective-permute-start(f32[8,768]{1,0:T(8,128)S(1)} %get-tuple-element.413), channel_id=1, source_target_pairs={{0,3},{1,0},{2,1},{3,2},{4,7},{5,4},{6,5},{7,6},{8,11},{9,8},{10,9... | collective-permute-start | bytes 73736 | tf_op jit(solution)/shard_map/ppermute | solution.py:780
  341.3 44.3 %collective-permute-start.10 = (bf16[768,1024]{1,0:T(8,128)(2,1)}, bf16[768,1024]{1,0:T(8,128)(2,1)}, u32[]{:S(2)}, u32[]{:S(2)}) collective-permute-start(bf16[768,1024]{1,0:T(8,128)(2,1)} %collective-permute-done.6.a2_ref), channel_id=1, source_target_pairs={{0,3},{1,0},{2,1},{3,2},{4,7},{5,4},{6,5},{7,6},{8,11},{9,8},{10,9... | collective-permute-start | bytes 4718600 | tf_op jit(solution)/shard_map/ppermute | solution.py:780
  385.7 45.7 %collective-permute-start.11 = (bf16[768,1024]{1,0:T(8,128)(2,1)}, bf16[768,1024]{1,0:T(8,128)(2,1)}, u32[]{:S(2)}, u32[]{:S(2)}) collective-permute-start(bf16[768,1024]{1,0:T(8,128)(2,1)} %collective-permute-done.10.a2_ref), channel_id=1, source_target_pairs={{0,3},{1,0},{2,1},{3,2},{4,7},{5,4},{6,5},{7,6},{8,11},{9,8},{10,9... | collective-permute-start | bytes 4718600 | tf_op jit(solution)/shard_map/ppermute | solution.py:780
  478.3 43.8 %collective-permute-start.13 = (bf16[768,1024]{1,0:T(8,128)(2,1)}, bf16[768,1024]{1,0:T(8,128)(2,1)}, u32[]{:S(2)}, u32[]{:S(2)}) collective-permute-start(bf16[768,1024]{1,0:T(8,128)(2,1)} %add_convert_fusion.4), channel_id=1, source_target_pairs={{0,3},{1,0},{2,1},{3,2},{4,7},{5,4},{6,5},{7,6},{8,11},{9,8},{10,9... | collective-permute-start | bytes 4718600 | tf_op jit(solution)/shard_map/ppermute | solution.py:780
  522.1 413.5 %reduce-scatter.4.cloned.1.call-start = ((), (), s32[]{:S(2)}) async-start(), calls=%async_computation.6 | async-start | bytes 9437184 | tf_op jit(solution)/shard_map/reduce_scatter | solution.py:1071
  633.0 57.3 %collective-permute-start.19 = (bf16[768,1024]{1,0:T(8,128)(2,1)}, bf16[768,1024]{1,0:T(8,128)(2,1)}, u32[]{:S(2)}, u32[]{:S(2)}) collective-permute-start(bf16[768,1024]{1,0:T(8,128)(2,1)} %add_convert_fusion.2), channel_id=1, source_target_pairs={{0,3},{1,0},{2,1},{3,2},{4,7},{5,4},{6,5},{7,6},{8,11},{9,8},{10,9... | collective-permute-start | bytes 4718600 | tf_op jit(solution)/shard_map/ppermute | solution.py:780
  696.2 80.0 %collective-permute-start.20 = (bf16[768,1024]{1,0:T(8,128)(2,1)}, bf16[768,1024]{1,0:T(8,128)(2,1)}, u32[]{:S(2)}, u32[]{:S(2)}) collective-permute-start(bf16[768,1024]{1,0:T(8,128)(2,1)} %add_convert_fusion.1), channel_id=1, source_target_pairs={{0,3},{1,0},{2,1},{3,2},{4,7},{5,4},{6,5},{7,6},{8,11},{9,8},{10,9... | collective-permute-start | bytes 4718600 | tf_op jit(solution)/shard_map/ppermute | solution.py:780
  700.1 71.3 %all-to-all-start.2 = ((f32[32,1,1056]{2,1,0:T(1,128)}), f32[32,1,1056]{2,1,0:T(1,128)S(1)}, u32[]{:S(2)}, u32[]{:S(2)}) async-start(f32[32,1,1056]{2,1,0:T(1,128)} %copy.154), calls=%async_computation.2 | async-start | bytes 294912 | tf_op jit(solution)/shard_map/all_to_all | solution.py:821
  707.7 230.8 %reduce-scatter.8.cloned.1.call-start = ((), (), s32[]{:S(2)}) async-start(), calls=%async_computation.8 | async-start | bytes 9437184 | tf_op jit(solution)/shard_map/reduce_scatter | solution.py:1071
  707.9 66.8 %collective-permute-start.21 = (bf16[256,512]{1,0:T(8,128)(2,1)}, bf16[256,512]{1,0:T(8,128)(2,1)}, u32[]{:S(2)}, u32[]{:S(2)}) collective-permute-start(bf16[256,512]{1,0:T(8,128)(2,1)} %get-tuple-element.371), channel_id=1, source_target_pairs={{0,4},{4,0},{8,12},{12,8},{16,20},{20,16},{24,28},{28,24},{1,5},{5... | collective-permute-start | bytes 786440 | tf_op jit(solution)/shard_map/ppermute | solution.py:587
  712.9 61.8 %collective-permute-start.25 = (bf16[256,512]{1,0:T(8,128)(2,1)S(1)}, bf16[256,512]{1,0:T(8,128)(2,1)}, u32[]{:S(2)}, u32[]{:S(2)}) collective-permute-start(bf16[256,512]{1,0:T(8,128)(2,1)S(1)} %pad_maximum_fusion.4), channel_id=1, source_target_pairs={{0,8},{4,12},{8,0},{12,4},{16,24},{20,28},{24,16},{28,20},{1,9},{5... | collective-permute-start | bytes 786440 | tf_op jit(solution)/shard_map/ppermute | solution.py:587
  716.9 57.8 %collective-permute-start.28 = (bf16[256,512]{1,0:T(8,128)(2,1)}, bf16[256,512]{1,0:T(8,128)(2,1)}, u32[]{:S(2)}, u32[]{:S(2)}) collective-permute-start(bf16[256,512]{1,0:T(8,128)(2,1)} %pad_maximum_fusion.5), channel_id=1, source_target_pairs={{0,16},{4,20},{8,24},{12,28},{16,0},{20,4},{24,8},{28,12},{1,17},{... | collective-permute-start | bytes 786440 | tf_op jit(solution)/shard_map/ppermute | solution.py:587
  802.3 46.6 %collective-permute-start.37 = (bf16[128,2048]{1,0:T(8,128)(2,1)}, bf16[128,2048]{1,0:T(8,128)(2,1)}, u32[]{:S(2)}, u32[]{:S(2)}) collective-permute-start(bf16[128,2048]{1,0:T(8,128)(2,1)} %get-tuple-element.351), channel_id=1, source_target_pairs={{0,4},{4,0},{8,12},{12,8},{16,20},{20,16},{24,28},{28,24},{1,5},{5... | collective-permute-start | bytes 1572872 | tf_op jit(solution)/shard_map/ppermute | solution.py:587
  870.5 48.6 %collective-permute-start.48 = (bf16[128,1024]{1,0:T(8,128)(2,1)}, bf16[128,1024]{1,0:T(8,128)(2,1)S(1)}, u32[]{:S(2)}, u32[]{:S(2)}) collective-permute-start(bf16[128,1024]{1,0:T(8,128)(2,1)} %get-tuple-element.364), channel_id=1, source_target_pairs={{0,4},{4,0},{8,12},{12,8},{16,20},{20,16},{24,28},{28,24},{1,5},{5... | collective-permute-start | bytes 786440 | tf_op jit(solution)/shard_map/ppermute | solution.py:587
  873.1 44.2 %collective-permute-start.45 = (bf16[32,2048]{1,0:T(8,128)(2,1)}, bf16[32,2048]{1,0:T(8,128)(2,1)S(1)}, u32[]{:S(2)}, u32[]{:S(2)}) collective-permute-start(bf16[32,2048]{1,0:T(8,128)(2,1)} %get-tuple-element.389), channel_id=1, source_target_pairs={{0,1},{1,2},{2,3},{3,0},{4,5},{5,6},{6,7},{7,4},{8,9},{9,10},{10,1... | collective-permute-start | bytes 393224 | tf_op jit(solution)/shard_map/ppermute | solution.py:780
  (99 other events, 2004.6 us)
Sparse Core Ops, SparseCore 0:
  9.9 74.0 all-gather.6
  85.9 61.8 all-gather.8
  149.6 54.8 all-gather.10
  522.2 71.0 reduce-scatter.5
  597.1 71.2 reduce-scatter.3
  719.3 71.8 reduce-scatter.7

commit v6 on v5

--- a/solution.py
+++ b/solution.py
@@ -111,25 +111,27 @@
     )(places, x, cosine, sine, *pieces)
 
 
-def outer_kernel(mine, *refs):
+def outer_kernel(mine, *refs, count):
     out_ref = refs[-1]
+    pairs = [(refs[n], refs[n + 1]) for n in range(0, len(refs) - 1, 2)]
     at = 0
-    for n in range(len(refs) // 2):
-        columns = refs[2 * n + 1].shape[1]
-        out_ref[:, at : at + columns] = dot_tn(refs[2 * n][...], refs[2 * n + 1][...]).astype(bf16)
+    for a_ref, b_ref in pairs[:count]:
+        columns = b_ref.shape[1]
+        out_ref[:, at : at + columns] = dot_tn(a_ref[...], b_ref[...]).astype(bf16)
         at += columns
-
-
-def outer(*pairs):
+    out_ref[:, at:] = sum(dot_tn(a[...], b[...]) for a, b in pairs[count:]).astype(bf16)
+
+
+def outer(pairs, extra):
     tok = pairs[0][0].shape[0]
     mine = lax.axis_index("ctx").astype(jnp.int32).reshape(1)
     specs = []
-    for _, b in pairs:
+    for _, b in pairs + extra:
         specs.append(pl.BlockSpec((tok, 128), lambda m, mine: (0, m ^ mine[0])))
         specs.append(pl.BlockSpec(b.shape, lambda m, mine: (0, 0)))
-    columns = sum(b.shape[1] for _, b in pairs)
+    columns = sum(b.shape[1] for _, b in pairs) + extra[0][1].shape[1]
     return pl.pallas_call(
-        outer_kernel,
+        functools.partial(outer_kernel, count=len(pairs)),
         grid_spec=pltpu.PrefetchScalarGridSpec(
             num_scalar_prefetch=1,
             grid=(8,),
@@ -140,7 +142,7 @@
         compiler_params=pltpu.CompilerParams(vmem_limit_bytes=VMEM_LIMIT),
         cost_estimate=SMALL,
         name="outer",
-    )(mine, *[x for pair in pairs for x in pair])
+    )(mine, *[x for pair in pairs + extra for x in pair])
 
 
 def gather_keys(pieces, scratch, places, block_rows):
@@ -408,13 +410,22 @@
     df_ref,
     rank_ref,
     gate_ref,
-    *refs,
+    wg_ref,
+    wu_ref,
+    wd_ref,
+    mix_ref,
+    da_ref,
+    dg_ref,
+    x_ref,
+    dy_ref,
+    z_ref,
+    dgate_ref,
+    dup_ref,
+    mix_acc,
+    da_acc,
+    *,
     sizes,
-    pieces,
 ):
-    weights, refs = refs[: 3 * pieces], refs[3 * pieces :]
-    wg_refs, wu_refs, wd_refs = (weights[n * pieces : (n + 1) * pieces] for n in range(3))
-    mix_ref, da_ref, dg_ref, x_ref, dy_ref, z_ref, dgate_ref, dup_ref, mix_acc, da_acc = refs
     e = pl.program_id(0)
 
     @pl.when(e == 0)
@@ -432,9 +443,9 @@
         gate = jnp.sum(jnp.where(hit, gates, 0.0), 1, keepdims=True)
         x = dot(chosen, a2_ref[...]).astype(bf16)
         d_mix = resid_scale * dot(chosen, df_ref[...])
-        wg = jnp.concatenate([ref[:, 0].reshape(-1, FF) for ref in wg_refs], 0)
-        wu = jnp.concatenate([ref[:, 0].reshape(-1, FF) for ref in wu_refs], 0)
-        wd = jnp.concatenate([ref[c, 0] for ref in wd_refs for c in range(ref.shape[0])], 1)
+        wg = wg_ref[:, 0].reshape(MODEL_WIDTH, FF)
+        wu = wu_ref[:, 0].reshape(MODEL_WIDTH, FF)
+        wd = jnp.concatenate([wd_ref[c, 0] for c in range(wd_ref.shape[0])], 1)
         g = dot(x, wg)
         u = dot(x, wu)
         sig = jax.nn.sigmoid(g)
@@ -473,25 +484,23 @@
 
 def expert_pass(a2, df, rank, gates, wg, wu, wd, capacity):
     tok = a2.shape[0]
-    parts, experts = wg[0].shape[0], wg[0].shape[1]
-    pieces = len(wg)
+    parts, experts = wg.shape[0], wg.shape[1]
     sizes = sorted({min(size, capacity) for size in (128, 192, 256, capacity)})
     counts = (jnp.max(rank, 1) + 1.0).astype(jnp.int32)
     spec = pl.BlockSpec
     whole = spec((tok, MODEL_WIDTH), lambda e, *_: (0, 0))
     row = spec((1, 1, tok), lambda e, *_: (e, 0, 0))
-    width = wg[0].shape[2]
-    up = spec((parts, 1, width, FF), lambda e, *_: (0, e, 0, 0))
-    down = spec((parts, 1, FF, width), lambda e, *_: (0, e, 0, 0))
+    up = spec((parts, 1, MODEL_WIDTH // parts, FF), lambda e, *_: (0, e, 0, 0))
+    down = spec((parts, 1, FF, MODEL_WIDTH // parts), lambda e, *_: (0, e, 0, 0))
     rows_wide = spec((1, capacity, MODEL_WIDTH), lambda e, *_: (e, 0, 0))
     rows_thin = spec((1, capacity, FF), lambda e, *_: (e, 0, 0))
     shape = jax.ShapeDtypeStruct
     return pl.pallas_call(
-        functools.partial(expert_kernel, sizes=sizes, pieces=pieces),
+        functools.partial(expert_kernel, sizes=sizes),
         grid_spec=pltpu.PrefetchScalarGridSpec(
             num_scalar_prefetch=1,
             grid=(experts,),
-            in_specs=[whole, whole, row, row] + [up] * (2 * pieces) + [down] * pieces,
+            in_specs=[whole, whole, row, row, up, up, down],
             out_specs=[whole, whole, row, rows_wide, rows_wide, rows_thin, rows_thin, rows_thin],
             scratch_shapes=[
                 pltpu.VMEM((tok, MODEL_WIDTH), f32),
@@ -511,24 +520,21 @@
         compiler_params=pltpu.CompilerParams(vmem_limit_bytes=VMEM_LIMIT),
         cost_estimate=SMALL,
         name="expert_pass",
-    )(counts, a2, df, rank.reshape(experts, 1, tok), gates.reshape(experts, 1, tok), *wg, *wu, *wd)
-
-
-def up_grad_kernel(order, *refs, sources):
+    )(counts, a2, df, rank.reshape(experts, 1, tok), gates.reshape(experts, 1, tok), wg, wu, wd)
+
+
+def up_grad_kernel(*refs, sources):
     rows = refs[: 3 * sources]
     gate_ref, up_ref = refs[3 * sources :]
-    width = gate_ref.shape[2]
     for n, out_ref in ((1, gate_ref), (2, up_ref)):
         total = None
         for s in range(sources):
             term = dot_tn(rows[3 * s][0], rows[3 * s + n][0])
             total = term if total is None else total + term
-        total = total.astype(bf16)
-        for c in range(out_ref.shape[0]):
-            out_ref[order[c], 0] = total[c * width : (c + 1) * width]
-
-
-def down_grad_kernel(order, *refs, sources, parts):
+        out_ref[...] = total.astype(bf16).reshape(out_ref.shape)
+
+
+def down_grad_kernel(*refs, sources, parts):
     rows, down_ref = refs[: 2 * sources], refs[-1]
     width = MODEL_WIDTH // parts
     total = None
@@ -537,50 +543,42 @@
         total = term if total is None else total + term
     total = total.astype(bf16)
     for c in range(parts):
-        down_ref[order[c], 0] = total[:, c * width : (c + 1) * width]
+        down_ref[c, 0] = total[:, c * width : (c + 1) * width]
 
 
 def row_specs(rows):
-    return [pl.BlockSpec((1,) + a.shape[1:], lambda e, *_: (e, 0, 0)) for r in rows for a in r]
-
-
-def up_weight_grads(rows, order):
-    parts = order.shape[0]
+    return [pl.BlockSpec((1,) + a.shape[1:], lambda e: (e, 0, 0)) for r in rows for a in r]
+
+
+def up_weight_grads(rows, parts):
     experts = rows[0][0].shape[0]
     shape = (parts, experts, MODEL_WIDTH // parts, FF)
-    out = pl.BlockSpec((parts, 1) + shape[2:], lambda e, *_: (0, e, 0, 0))
+    out = pl.BlockSpec((parts, 1) + shape[2:], lambda e: (0, e, 0, 0))
     return pl.pallas_call(
         functools.partial(up_grad_kernel, sources=len(rows)),
-        grid_spec=pltpu.PrefetchScalarGridSpec(
-            num_scalar_prefetch=1,
-            grid=(experts,),
-            in_specs=row_specs(rows),
-            out_specs=[out, out],
-        ),
+        grid=(experts,),
+        in_specs=row_specs(rows),
+        out_specs=[out, out],
         out_shape=[jax.ShapeDtypeStruct(shape, bf16)] * 2,
         compiler_params=pltpu.CompilerParams(vmem_limit_bytes=VMEM_LIMIT),
         cost_estimate=SMALL,
         name="up_weight_grads",
-    )(order, *[a for r in rows for a in r])
-
-
-def down_weight_grads(rows, order):
-    parts = order.shape[0]
+    )(*[a for r in rows for a in r])
+
+
+def down_weight_grads(rows, parts):
     experts = rows[0][0].shape[0]
     shape = (parts, experts, FF, MODEL_WIDTH // parts)
     return pl.pallas_call(
         functools.partial(down_grad_kernel, sources=len(rows), parts=parts),
-        grid_spec=pltpu.PrefetchScalarGridSpec(
-            num_scalar_prefetch=1,
-            grid=(experts,),
-            in_specs=row_specs(rows),
-            out_specs=pl.BlockSpec((parts, 1) + shape[2:], lambda e, *_: (0, e, 0, 0)),
-        ),
+        grid=(experts,),
+        in_specs=row_specs(rows),
+        out_specs=pl.BlockSpec((parts, 1) + shape[2:], lambda e: (0, e, 0, 0)),
         out_shape=jax.ShapeDtypeStruct(shape, bf16),
         compiler_params=pltpu.CompilerParams(vmem_limit_bytes=VMEM_LIMIT),
         cost_estimate=SMALL,
         name="down_weight_grads",
-    )(order, *[a for r in rows for a in r])
+    )(*[a for r in rows for a in r])
 
 
 def swap(x, mask):
@@ -591,23 +589,6 @@
     if lax.axis_size("ctx") != 8:
         return lax.all_gather(x[:rows], "ctx", axis=0, tiled=True)
     return plane_gather(x, rows)
-
-
-def scatter_ctx(x):
-    if lax.axis_size("ctx") != 8:
-        return lax.psum_scatter(x, "ctx", scatter_dimension=0, tiled=True).astype(f32)
-    rows = x.shape[0] // 8
-    half = rows // 2
-    block = [x[m * rows : (m + 1) * rows] for m in range(8)]
-    diagonal, near, far, own = (
-        block[m].astype(f32) + swap(block[m + 1], 1).astype(f32) for m in (6, 2, 4, 0)
-    )
-    diagonal = diagonal.astype(bf16)
-    near_top = near[:half] + swap(diagonal[:half], 4).astype(f32)
-    far_end = far[half:] + swap(diagonal[half:], 2).astype(f32)
-    near = jnp.concatenate([near_top.astype(bf16), near[half:].astype(bf16)], 0)
-    far = jnp.concatenate([far[:half].astype(bf16), far_end.astype(bf16)], 0)
-    return own + swap(near, 2).astype(f32) + swap(far, 4).astype(f32)
 
 
 MESH = pl.DeviceIdType.MESH
@@ -775,6 +756,155 @@
     )(x)
 
 
+def sum_steps(copies, x_ref, key, sib, low, recv, out_ref):
+    rows = x_ref.shape[0] // 8
+    half = rows // 2
+    side, near, far = ({"ctx": partner(m)} for m in (1, 2, 4))
+
+    def blocks(ref, m, start=0, count=rows):
+        return ref.at[pl.ds(m * rows + start, count)]
+
+    def added(m, start, count):
+        ours = x_ref[m * rows + start : m * rows + start + count, :].astype(f32)
+        at = m // 2 * rows + start
+        return ours + sib[at : at + count, :].astype(f32)
+
+    def put(place, start, value, device):
+        at = place * rows + start
+        low[at : at + half, :] = value.astype(bf16)
+        copies.start(
+            (key, "low", place, start),
+            blocks(low, place, start, half),
+            blocks(recv, place, start, half),
+            device,
+        )
+
+    def first():
+        for m in (7, 3, 5, 1):
+            copies.start((key, m), blocks(x_ref, m), blocks(sib, m // 2), side)
+
+    def second():
+        copies.arrived((key, 7))
+        put(0, 0, added(6, 0, half), far)
+        put(0, half, added(6, half, half), near)
+
+    def third():
+        copies.arrived((key, 3))
+        put(1, half, added(2, half, half), near)
+        copies.arrived((key, 5))
+        put(2, 0, added(4, 0, half), far)
+
+    def fourth():
+        copies.arrived((key, "low", 0, 0))
+        put(1, 0, added(2, 0, half) + recv[0:half, :].astype(f32), near)
+        copies.arrived((key, "low", 0, half))
+        put(2, half, added(4, half, half) + recv[half:rows, :].astype(f32), far)
+
+    def last():
+        copies.arrived((key, 1))
+        for place in (1, 2):
+            for start in (0, half):
+                copies.arrived((key, "low", place, start))
+        out_ref[...] = (
+            added(0, 0, rows)
+            + recv[rows : 2 * rows, :].astype(f32)
+            + recv[2 * rows :, :].astype(f32)
+        )
+
+    return [first, second, third, fourth, last]
+
+
+def plane_sum_kernel(*refs, sets):
+    x_refs, out_refs = refs[:sets], refs[sets : 2 * sets]
+    sibs, lows, recvs = (refs[(2 + n) * sets : (3 + n) * sets] for n in range(3))
+    send, recv_sem = refs[5 * sets :]
+    greet([{"ctx": partner(m)} for m in (1, 2, 4)])
+    copies = Copies(send, recv_sem)
+    steps = [
+        sum_steps(copies, x_refs[n], n, sibs[n], lows[n], recvs[n], out_refs[n])
+        for n in range(sets)
+    ]
+    for n in range(5):
+        for one in steps:
+            one[n]()
+    copies.close()
+
+
+def plane_sum(arrays):
+    if lax.axis_size("ctx") != 8:
+        return [
+            lax.psum_scatter(x, "ctx", scatter_dimension=0, tiled=True).astype(f32)
+            for x in arrays
+        ]
+    sets = len(arrays)
+    rows, columns = arrays[0].shape[0] // 8, arrays[0].shape[1]
+    vmem = pl.BlockSpec(memory_space=pltpu.VMEM)
+    return pl.pallas_call(
+        functools.partial(plane_sum_kernel, sets=sets),
+        in_specs=[vmem] * sets,
+        out_specs=[vmem] * sets,
+        out_shape=[jax.ShapeDtypeStruct((rows, columns), f32)] * sets,
+        scratch_shapes=[pltpu.VMEM((4 * rows, columns), bf16)] * sets
+        + [pltpu.VMEM((3 * rows, columns), bf16)] * (2 * sets)
+        + [pltpu.SemaphoreType.DMA((10 * sets,)), pltpu.SemaphoreType.DMA((10 * sets,))],
+        compiler_params=pltpu.CompilerParams(
+            collective_id=3, has_side_effects=True, vmem_limit_bytes=VMEM_LIMIT
+        ),
+        cost_estimate=SMALL,
+        name="plane_sum",
+    )(*arrays)
+
+
+def full_sum_kernel(x_ref, out_ref, sib, low, recv, total, total_low, arrived, send, recv_sem):
+    rows = out_ref.shape[0]
+    greet(
+        [{"ctx": partner(m)} for m in (1, 2, 4)] + [{"wt": ahead(d)} for d in (1, 2, 3)]
+    )
+    copies = Copies(send, recv_sem)
+    for step in sum_steps(copies, x_ref, 0, sib, low, recv, total):
+        step()
+    total_low[...] = total[...].astype(bf16)
+    for d in (2, 1, 3):
+        copies.start(
+            d,
+            total_low.at[pl.ds(pl.multiple_of(ahead(d) * rows, rows), rows)],
+            arrived.at[pl.ds((d - 1) * rows, rows)],
+            {"wt": ahead(d)},
+        )
+    result = total[pl.ds(pl.multiple_of(ahead(0) * rows, rows), rows), :]
+    for d in (1, 3, 2):
+        copies.arrived(d)
+        result = result + arrived[(d - 1) * rows : d * rows, :].astype(f32)
+    out_ref[...] = result
+    copies.close()
+
+
+def full_sum(x):
+    rows, columns = x.shape[0] // 32, x.shape[1]
+    vmem = pl.BlockSpec(memory_space=pltpu.VMEM)
+    return pl.pallas_call(
+        full_sum_kernel,
+        in_specs=[vmem],
+        out_specs=vmem,
+        out_shape=jax.ShapeDtypeStruct((rows, columns), f32),
+        scratch_shapes=[
+            pltpu.VMEM((16 * rows, columns), bf16),
+            pltpu.VMEM((12 * rows, columns), bf16),
+            pltpu.VMEM((12 * rows, columns), bf16),
+            pltpu.VMEM((4 * rows, columns), f32),
+            pltpu.VMEM((4 * rows, columns), bf16),
+            pltpu.VMEM((3 * rows, columns), bf16),
+            pltpu.SemaphoreType.DMA((13,)),
+            pltpu.SemaphoreType.DMA((13,)),
+        ],
+        compiler_params=pltpu.CompilerParams(
+            collective_id=4, has_side_effects=True, vmem_limit_bytes=VMEM_LIMIT
+        ),
+        cost_estimate=SMALL,
+        name="full_sum",
+    )(x)
+
+
 def shift(x, distance):
     n = lax.axis_size("wt")
     return lax.ppermute(x, "wt", [(i, (i + distance) % n) for i in range(n)])
@@ -796,29 +926,13 @@
     return [packed_gather(x)], [32], places.reshape(-1).astype(jnp.int32)
 
 
-def outer_part(*pairs):
+def outer_sum(pairs, extra):
     if lax.axis_size("ctx") != 8 or lax.axis_size("wt") != 4:
-        return jnp.concatenate([dot_tn(a, b) for a, b in pairs], 1)
-    return scatter_ctx(outer(*pairs))
-
-
-def row_sum(part):
-    wt = lax.axis_size("wt")
-    if lax.axis_size("ctx") != 8 or wt != 4:
+        parts = [dot_tn(a, b) for a, b in pairs] + [sum(dot_tn(a, b) for a, b in extra)]
         return lax.psum_scatter(
-            part.astype(bf16), ALL, scatter_dimension=0, tiled=True
+            jnp.concatenate(parts, 1).astype(bf16), ALL, scatter_dimension=0, tiled=True
         ).astype(f32)
-    rows = part.shape[0] // wt
-    low = part.astype(bf16)
-    at = lambda d: ((lax.axis_index("wt") + d) % wt) * rows
-    total = lax.dynamic_slice_in_dim(part, at(0), rows, 0)
-    for d in range(1, wt):
-        total = total + shift(lax.dynamic_slice_in_dim(low, at(d), rows, 0), d).astype(f32)
-    return total
-
-
-def spread_sum(x):
-    return jnp.sum(lax.all_to_all(x, ALL, 0, 0, tiled=True), 0)
+    return full_sum(outer(pairs, extra))
 
 
 def after(x, *others):
@@ -850,7 +964,7 @@
 
 def norm_backward(values, inverse, gain, grad_out):
     scaled = gain * grad_out
-    gain_grad = jnp.sum(grad_out * values * inverse, 0)
+    gain_grad = (grad_out * values * inverse).astype(bf16)
     projection = jnp.mean(scaled * values, -1, keepdims=True)
     return (inverse * scaled - values * inverse * inverse * inverse * projection, gain_grad)
 
@@ -902,38 +1016,9 @@
     )
     pieces, counts, block_places = gather_all(packed)
 
-    core = ctx_index % 2
-    if context_size == 8:
-        chips = [[0, 2, 4, 6], [1, 3, 5, 7]]
-        expert_weights = [
-            [lax.all_gather(w, "ctx", axis=0, tiled=False, axis_index_groups=chips)]
-            for w in (gate_weight, up_weight, down_weight)
-        ]
-        four = 2 * jnp.arange(4, dtype=jnp.int32)
-        width_order = jnp.concatenate([four + core, four + 1 - core]).astype(jnp.int32)
-    else:
-        expert_weights = [
-            [lax.all_gather(w, "ctx", axis=0, tiled=False)]
-            for w in (gate_weight, up_weight, down_weight)
-        ]
-        width_order = jnp.arange(context_size, dtype=jnp.int32)
-
-    def to_line(x):
-        if context_size != 8:
-            return x
-        x = x.reshape(tok, 4, 2, 128)
-        ours, others = (x[:, :, n].reshape(tok, 512) for n in range(2))
-        return jnp.where(
-            core == 0, jnp.concatenate([ours, others], 1), jnp.concatenate([others, ours], 1)
-        )
-
-    def from_line(x):
-        if context_size != 8:
-            return x
-        ours, others = (x[:, 512 * n : 512 * n + 512].reshape(tok, 4, 128) for n in range(2))
-        return jnp.where(
-            core == 0, jnp.stack([ours, others], 2), jnp.stack([others, ours], 2)
-        ).reshape(tok, MODEL_WIDTH)
+    gate_full = lax.all_gather(gate_weight, "ctx", axis=0, tiled=False)
+    up_full = lax.all_gather(up_weight, "ctx", axis=0, tiled=False)
+    down_full = lax.all_gather(down_weight, "ctx", axis=0, tiled=False)
 
     mask = jnp.any(
         routes[:, :, None] == jnp.arange(EXPERTS, dtype=jnp.int32)[None, None, :], 1
@@ -945,8 +1030,7 @@
         rank.T.reshape(shard_count, expert_count, tok), "wt", 0, 0, tiled=True
     )
     last = shard_count - 1
-    out_line = to_line(out_low)
-    grads_in = {0: out_line, last: shift(after(out_line, pieces[0]), -1)}
+    grads_in = {0: out_low, last: shift(after(out_low, pieces[0], ranks), -1)}
 
     pieces, ranks = beside(pieces, ranks)
     local_rows = jnp.arange(tok, dtype=jnp.int32)
@@ -991,12 +1075,6 @@
         d = last - 1 - half
         grads_in[d] = shift(grads_in[d + 1], -1)
         result, grads_in[d] = beside(result, grads_in[d])
-        if context_size == 8:
-            for weights in expert_weights[half : 2 * half + 1]:
-                result, sibling = beside(
-                    result, swap(after(weights[0], turned_query, *kv_pieces), 1)
-                )
-                weights.append(sibling)
         if half == 0:
             turned_query = after(turned_query, result[0])
         heads.append(result)
@@ -1019,7 +1097,7 @@
     for d in range(shard_count):
         piece = lax.dynamic_index_in_dim(gates_out, (wt_index + d) % shard_count, 0, False)
         gates_in.append(shift(piece, d) if d else piece)
-    got = {0: to_line(normed_two)}
+    got = {0: normed_two}
     partial, mixed, gate_grads, rows = {}, {}, {}, []
     carried = None
 
@@ -1030,7 +1108,7 @@
         source = (wt_index - d) % shard_count
         rank_in = lax.dynamic_index_in_dim(ranks, source, 0, False)
         result = expert_pass(
-            got[d], grads_in[d], rank_in, gates_in[d], *expert_weights, capacity
+            got[d], grads_in[d], rank_in, gates_in[d], gate_full, up_full, down_full, capacity
         )
         coming = d - 1 if d else last
         if coming:
@@ -1048,18 +1126,18 @@
             got[coming] = after(got[coming], partial[d])
     carried = shift(add(carried, partial[2]), -1)
     (gate_grad, up_grad), carried = beside(
-        up_weight_grads([(after(r[0], partial[1]), r[3], r[4]) for r in rows], width_order),
+        up_weight_grads([(after(r[0], partial[1]), r[3], r[4]) for r in rows], context_size),
         carried,
     )
     carried = shift(add(carried, partial[1]), -1)
     down_grad, home = beside(
-        down_weight_grads([(after(r[2], gate_grad), r[1]) for r in rows], width_order), carried
+        down_weight_grads([(after(r[2], gate_grad), r[1]) for r in rows], context_size), carried
     )
 
     stacked = jnp.stack([gate_grads[d] for d in range(shard_count)], 0)
     stacked = jnp.roll(stacked, wt_index, 0).reshape(EXPERTS, tok).T
     grad_logits = (gates * (stacked - jnp.sum(gates * stacked, -1, keepdims=True))).astype(bf16)
-    grad_normed_two = from_line(partial[0].astype(f32) + home.astype(f32))
+    grad_normed_two = partial[0].astype(f32) + home.astype(f32)
     grad_normed_two = grad_normed_two + dot_nt(grad_logits, router_full)
     grad_mid_norm, second_gain_grad = norm_backward(
         middle, inverse_two, second_gain, grad_normed_two
@@ -1071,18 +1149,9 @@
         lax.psum_scatter(grad, "ctx", scatter_dimension=0, tiled=False).astype(f32)
         for grad in (gate_grad, up_grad, down_grad)
     )
-    devices = context_size * shard_count
-    small = jnp.concatenate(
-        [
-            dot_tn(normed_two, grad_logits).reshape(devices, own_rows * EXPERTS),
-            second_gain_grad.reshape(devices, own_rows),
-        ],
-        1,
-    )
-
-    carried = shift(after(mixed[last], home), -1)
-    query, carried = beside(after(turned_query, grad_attended), carried)
-    d_query, owned, ours = [], [], []
+    carried = None
+    query = after(turned_query, grad_attended)
+    d_query, d_kv, ours = [], [], []
     for half in range(2):
         result = attention_backward(
             query,
@@ -1098,21 +1167,19 @@
             block_rows,
             half,
         )
-        carried = shift(add(carried, mixed[last - 1 - half]), -1)
+        carried = shift(after(add(carried, mixed[last - half]), home), -1)
         result, carried = beside(result, carried)
-        d_q, d_kv, d_key_own, d_value_own = result
-        query = after(query, d_q)
-        if half == 0:
-            small = spread_sum(after(small, d_q))
-        d_query.append(d_q)
-        owned.append(scatter_ctx(d_kv))
-        ours.append((d_key_own, d_value_own))
+        query = after(query, result[0])
+        d_query.append(result[0])
+        d_kv.append(result[1])
+        ours.append(result[2:])
+    carried = shift(add(carried, mixed[last - 2]), -1)
+    owned, carried = beside(plane_sum(d_kv), carried)
     for d in range(last - 3, 0, -1):
         carried = shift(add(carried, mixed[d]), -1)
-    mixture = from_line(mixed[0].astype(f32) + carried.astype(f32))
+    mixture = mixed[0].astype(f32) + carried.astype(f32)
     layer_output = (middle + resid_scale * mixture).astype(bf16)
     d_query = jnp.concatenate(d_query, 1)
-    query_part = outer_part((normed_one, d_query), (after(grad_branch, d_query), attended))
     d_key, d_value = (
         jnp.concatenate(
             [
@@ -1127,26 +1194,31 @@
         bf16
     )
     grad_kv = jnp.concatenate([grad_key_low, d_value.astype(bf16)], 1)
-    grad_kv, query_part = beside(grad_kv, query_part)
-    kv_share = row_sum(outer_part((normed_one, grad_kv)))
-    query_share, output_share = jnp.split(row_sum(query_part), 2, 1)
     grad_normed_one = dot_nt(d_query, qkv_full[:, :1024]) + dot_nt(grad_kv, qkv_full[:, 1024:])
     grad_input_norm, first_gain_grad = norm_backward(
         inputs, inverse_one, first_gain, grad_normed_one
     )
     input_grad = (grad_middle + grad_input_norm).astype(bf16)
 
-    first_gain_share = spread_sum(first_gain_grad.reshape(devices, own_rows))
+    column = lax.broadcasted_iota(jnp.int32, (tok, 128), 1)
+    shares = outer_sum(
+        [(normed_one, d_query), (grad_branch, attended), (normed_one, grad_kv)],
+        [
+            (normed_two, jnp.pad(grad_logits, ((0, 0), (0, 128 - EXPERTS)))),
+            (second_gain_grad, (column == EXPERTS).astype(bf16)),
+            (first_gain_grad, (column == EXPERTS + 1).astype(bf16)),
+        ],
+    )
     return (
         layer_output[None],
         input_grad[None],
-        first_gain_share,
-        query_share,
-        kv_share[:, :KV_WIDTH],
-        kv_share[:, KV_WIDTH:],
-        output_share.T,
-        small[own_rows * EXPERTS :],
-        small[: own_rows * EXPERTS].reshape(own_rows, EXPERTS),
+        shares[:, 3073 + EXPERTS],
+        shares[:, :1024],
+        shares[:, 2048 : 2048 + KV_WIDTH],
+        shares[:, 2048 + KV_WIDTH : 3072],
+        shares[:, 1024:2048].T,
+        shares[:, 3072 + EXPERTS],
+        shares[:, 3072 : 3072 + EXPERTS],
         gate_share,
         up_share,
         down_share,

time: 957 us -> 804 us (0.84)
  waiting for transfers between devices: 111 us -> 39.7 us
  Pallas kernels: 503 us -> 569 us
  local copies, waits for them, and re-layouts: 110 us -> 57.1 us
  other arithmetic: 95.5 us -> 47.7 us
  starting transfers between devices: 87.4 us -> 46.3 us
    pallas_call x6 -> x7, Pallas kernels: 193 us -> 258 us  [the longest x4 153 us: expert_pass(): pl.pallas_call(functools.partial(expert_kernel, sizes=sizes), grid_spec=p...]
    slice x23 -> x3, local copies, waits for them, and re-layouts: 37.9 us -> 4.35 us  [the longest x1 1.53 us: per_device(): shares[:, 2048 + KV_WIDTH:3072]]
    ppermute x35 -> x0, waiting for transfers between devices: 27.9 us -> none  [swap(): lax.ppermute(x, 'ctx', [(i, i ^ mask) for i in range(lax.axis_size('ctx'))])]
    all_to_all x1, waiting for transfers between devices: 24.5 us -> 0.01 us  [per_device(): lax.all_to_all(rank.T.reshape(shard_count, expert_count, tok), 'wt', 0, 0...]
    ppermute x35 -> x0, starting transfers between devices: 21.9 us -> none  [swap(): lax.ppermute(x, 'ctx', [(i, i ^ mask) for i in range(lax.axis_size('ctx'))])]
    add x11 -> x0, other arithmetic: 20.9 us -> none  [the longest x4 10.1 us: scatter_ctx(): block[m].astype(f32) + swap(block[m + 1], 1).astype(f32)]
    another operation x8 -> x0, local copies, waits for them, and re-layouts: 16.9 us -> none  [the longest x4 10.9 us: from_line(): jnp.stack([ours, others], 2)]
    select_n x3 -> x0, other arithmetic: 12.6 us -> none  [the longest x1 8.56 us: from_line(): jnp.where(core == 0, jnp.stack([ours, others], 2), jnp.stack([others, our...]
  transfers between devices with their start and end apart: 68 -> 25, of which waited for: 19 -> 3; matrix products, arithmetic and copies ran while one was open for 20% -> 14% of each run, Pallas kernels for 53% -> 72%
where the time goes in v6:
time: 804 us; the launch traced here: 794 us
  Pallas kernels  569 us (71%)
  local copies, waits for them, and re-layouts  57.1 us (7%)
  other arithmetic  47.7 us (6%)
  starting transfers between devices  46.3 us (6%)
  waiting for transfers between devices  39.7 us (5%)
  between operations  17.8 us (2%)
  matrix products  16.8 us (2%)
    pallas_call x4, Pallas kernels, expert_pass(): pl.pallas_call(functools.partial(expert_kernel, sizes=sizes), grid_spec=p...  153 us
    pallas_call x2, Pallas kernels, attention_backward(): pl.pallas_call(functools.partial(attention_backward_kernel, block_rows=bl...  98.1 us
    pallas_call x2, Pallas kernels, attention_forward(): pl.pallas_call(functools.partial(attention_forward_kernel, block_rows=blo...  53.2 us
    pallas_call x1, Pallas kernels, packed_gather(): pl.pallas_call(packed_gather_kernel, in_specs=[ANY], out_specs=ANY, out_s...  53 us
    pallas_call x1, Pallas kernels, full_sum(): pl.pallas_call(full_sum_kernel, in_specs=[vmem], out_specs=vmem, out_shap...  52.8 us
    pallas_call x1, Pallas kernels, up_weight_grads(): pl.pallas_call(functools.partial(up_grad_kernel, sources=len(rows)), grid...  40.6 us
    ppermute x18, starting transfers between devices, shift(): return lax.ppermute(x, 'wt', [(i, (i + distance) % n) for i in range(n)])  39.8 us
    pallas_call x1, Pallas kernels, plane_sum(): pl.pallas_call(functools.partial(plane_sum_kernel, sets=sets), in_specs=[...  38.2 us
  transfers between devices with their start and end apart: 25, of which 3 were waited for; matrix products, arithmetic and copies ran while one was open for 14% of the time, Pallas kernels for 72%

profile of v6, /device:TPU:0, one launch (start us, length us, event | category | flops | bytes accessed | tf_op | source)
XLA Modules:
  0.0 793.8 jit_solution(7846312050732742021)
XLA Ops:
  11.0 6.3 all-to-all-start
  18.4 53.0 %packed_gather.1.refs_0_ = bf16[1024,3200]{1,0:T(8,128)(2,1)} custom-call(bf16[32,3200]{1,0:T(8,128)(2,1)} %concatenate.45.x_ref), custom_call_target="tpu_custom_call" | custom-call | flops 1000000000 | bytes 1000000 | tf_op jit(solution)/shard_map/packed_gather/pallas_call | solution.py:743
  81.4 9.0 %project.1 = (bf16[768,1024]{1,0:T(8,128)(2,1)}, bf16[768,1024]{1,0:T(8,128)(2,1)}, bf16[768,1024]{1,0:T(8,128)(2,1)}, bf16[1024,2048]{1,0:T(8,128)(2,1)}, bf16[...) custom-call(s32[32]{0:T(128)} %add.223.places, bf16[768,1024]{1,0:T(8,128)(2,1)} %bitcast.130, ...), custom_call_target="tpu_custom_call" | custom-call | flops 1000000000 | bytes 1000000 | tf_op jit(solution)/shard_map/project/pallas_call | solution.py:95
  90.4 33.3 %plane_gather.1.refs_0_.refs_1_ = bf16[2048,1024]{1,0:T(8,128)(2,1)} custom-call(bf16[768,1024]{1,0:T(8,128)(2,1)} %get-tuple-element.162.x_ref), custom_call_target="tpu_custom_call" | custom-call | flops 1000000000 | bytes 1000000 | tf_op jit(solution)/shard_map/plane_gather/pallas_call | solution.py:688
  130.3 26.5 %attention_forward.2 = (bf16[768,512]{1,0:T(8,128)(2,1)}, f32[2,4,768]{2,1,0:T(4,128)}) custom-call(s32[16]{0:T(128)} %reshape.248.places, s32[4]{0:T(128)} %get-tuple-element.357.starts, bf16[768,1024]{1,0:T(8,128)(2,1)} %get-tuple-element.282.q_ref, bf16[2048,1024]{1,0:T(8,128)(2,1)} %plane_gather.1.refs_0_.refs_1_, ...), custom_call_target="tpu_custom_call" | custom-call | flops 1000000000 | bytes 1000000 | tf_op jit(solution)/shard_map/attention_forward/pallas_call | solution.py:228
  156.8 5.0 collective-permute-done.1.df_ref
  161.8 4.7 collective-permute-start.2
  167.9 26.7 %attention_forward.3 = (bf16[768,512]{1,0:T(8,128)(2,1)}, f32[2,4,768]{2,1,0:T(4,128)}) custom-call(s32[16]{0:T(128)} %reshape.248.places, s32[4]{0:T(128)} %get-tuple-element.357.starts, bf16[768,1024]{1,0:T(8,128)(2,1)} %get-tuple-element.282.q_ref, bf16[2048,1024]{1,0:T(8,128)(2,1)} %plane_gather.1.refs_0_.refs_1_, ...), custom_call_target="tpu_custom_call" | custom-call | flops 1000000000 | bytes 1000000 | tf_op jit(solution)/shard_map/attention_forward/pallas_call | solution.py:228
  194.7 5.1 collective-permute-done.2.df_ref
  228.8 38.1 %expert_pass.4 = (bf16[768,1024]{1,0:T(8,128)(2,1)}, bf16[768,1024]{1,0:T(8,128)(2,1)}, f32[8,1,768]{2,1,0:T(1,128)}, bf16[8,336,1024]{2,1,0:T(8,128)(2,1)}, bf1...) custom-call(s32[8]{0:T(128)} %get-tuple-element.361.counts, ...), custom_call_target="tpu_custom_call" | custom-call | flops 1000000000 | bytes 1000000 | tf_op jit(solution)/shard_map/expert_pass/pallas_call | solution.py:498
  270.6 38.7 %expert_pass.5 = (bf16[768,1024]{1,0:T(8,128)(2,1)}, bf16[768,1024]{1,0:T(8,128)(2,1)}, f32[8,1,768]{2,1,0:T(1,128)}, bf16[8,336,1024]{2,1,0:T(8,128)(2,1)}, bf1...) custom-call(s32[8]{0:T(128)} %get-tuple-element.358.counts, ...), custom_call_target="tpu_custom_call" | custom-call | flops 1000000000 | bytes 1000000 | tf_op jit(solution)/shard_map/expert_pass/pallas_call | solution.py:498
  309.3 6.5 collective-permute-start.8
  317.8 37.8 %expert_pass.6 = (bf16[768,1024]{1,0:T(8,128)(2,1)}, bf16[768,1024]{1,0:T(8,128)(2,1)}, f32[8,1,768]{2,1,0:T(1,128)}, bf16[8,336,1024]{2,1,0:T(8,128)(2,1)}, bf1...) custom-call(s32[8]{0:T(128)} %get-tuple-element.359.counts, ...), custom_call_target="tpu_custom_call" | custom-call | flops 1000000000 | bytes 1000000 | tf_op jit(solution)/shard_map/expert_pass/pallas_call | solution.py:498
  360.4 38.4 %expert_pass.7 = (bf16[768,1024]{1,0:T(8,128)(2,1)}, bf16[768,1024]{1,0:T(8,128)(2,1)}, f32[8,1,768]{2,1,0:T(1,128)}, bf16[8,336,1024]{2,1,0:T(8,128)(2,1)}, bf1...) custom-call(s32[8]{0:T(128)} %get-tuple-element.360.counts, ...), custom_call_target="tpu_custom_call" | custom-call | flops 1000000000 | bytes 1000000 | tf_op jit(solution)/shard_map/expert_pass/pallas_call | solution.py:498
  402.5 4.7 collective-permute-start.10
  407.1 40.6 %up_weight_grads.1 = (bf16[8,8,128,512]{3,2,1,0:T(8,128)(2,1)}, bf16[8,8,128,512]{3,2,1,0:T(8,128)(2,1)}) custom-call(bf16[8,336,1024]{2,1,0:T(8,128)(2,1)} %get-tuple-element.236.refs_0_, bf16[8,336,512]{2,1,0:T(8,128)(2,1)} %get-tuple-element.237.refs_1_, bf16[8,336,512]{2,1,0:T(8,128)(2,1)} %get-tuple-element.238.refs_2_, ...), custom_call_target="tpu_custom_call" | custom-call | flops 1000000000 | bytes 1000000 | tf_op jit(solution)/shard_map/up_weight_grads/pallas_call | solution.py:557
  460.7 26.9 %collective-permute-done.12 = f32[8,768]{1,0:T(8,128)S(1)} collective-permute-done((f32[8,768]{1,0:T(8,128)S(1)}, f32[8,768]{1,0:T(8,128)S(1)}, u32[]{:S(2)}, u32[]{:S(2)}) %collective-permute-start.12) | collective-permute-done | bytes 24608 | tf_op jit(solution)/shard_map/ppermute | solution.py:910
  490.1 23.4 %down_weight_grads.1 = bf16[8,8,512,128]{3,2,1,0:T(8,128)(2,1)} custom-call(bf16[8,336,512]{2,1,0:T(8,128)(2,1)} %get-tuple-element.255.refs_0_, bf16[8,336,1024]{2,1,0:T(8,128)(2,1)} %get-tuple-element.256.refs_1_, bf16[8,336,512]{2,1,0:T(8,128)(2,1)} %get-tuple-element.258.refs_2_, bf16[8,336,1024]{2,1,0:T(8,128)(2,1)} %get-tuple-element.259.refs_3_, ...), custom_call_target="tpu_custom_call" | custom-call | flops 1000000000 | bytes 1000000 | tf_op jit(solution)/shard_map/down_weight_grads/pallas_call | solution.py:572
  537.4 49.2 %attention_backward.2 = (bf16[768,512]{1,0:T(8,128)(2,1)}, bf16[2048,512]{1,0:T(8,128)(2,1)}, f32[512,256]{1,0:T(8,128)}, f32[512,256]{1,0:T(8,128)}) custom-call(s32[16]{0:T(128)} %reshape.248.places, s32[4]{0:T(128)} %get-tuple-element.357.starts, bf16[768,1024]{1,0:T(8,128)(2,1)} %get-tuple-element.282.q_ref, ...), custom_call_target="tpu_custom_call" | custom-call | flops 1000000000 | bytes 1000000 | tf_op jit(solution)/shard_map/attention_backward/pallas_call | solution.py:372
  590.5 48.9 %attention_backward.3 = (bf16[768,512]{1,0:T(8,128)(2,1)}, bf16[2048,512]{1,0:T(8,128)(2,1)}, f32[512,256]{1,0:T(8,128)}, f32[512,256]{1,0:T(8,128)}) custom-call(s32[16]{0:T(128)} %reshape.248.places, s32[4]{0:T(128)} %get-tuple-element.357.starts, bf16[768,1024]{1,0:T(8,128)(2,1)} %get-tuple-element.282.q_ref, ...), custom_call_target="tpu_custom_call" | custom-call | flops 1000000000 | bytes 1000000 | tf_op jit(solution)/shard_map/attention_backward/pallas_call | solution.py:372
  646.0 38.2 %plane_sum.1 = (f32[256,512]{1,0:T(8,128)}, f32[256,512]{1,0:T(8,128)}) custom-call(bf16[2048,512]{1,0:T(8,128)(2,1)} %get-tuple-element.280.refs_0_, bf16[2048,512]{1,0:T(8,128)(2,1)} %get-tuple-element.291.refs_1_), custom_call_target="tpu_custom_call" | custom-call | flops 1000000000 | bytes 1000000 | tf_op jit(solution)/shard_map/plane_sum/pallas_call | solution.py:842
  697.7 6.4 multiply_convert_fusion
  705.5 14.0 %outer.1.x_ref = bf16[1024,3200]{1,0:T(8,128)(2,1)} custom-call(s32[1]{0:T(128)} %bitcast.33.mine, bf16[768,1024]{1,0:T(8,128)(2,1)} %get-tuple-element.305.refs_0_.refs_4_, bf16[768,1024]{1,0:T(8,128)(2,1)} %constant_dynamic-update-slice_fusion.10.refs_1_, bf16[768,1024]{1,0:T(8,128)(2,1)} %copy-done.10, bf16[768,1024]{1,0:T(8,128)(2,1)} %copy-done.2, ...), custom_call_target="tpu_custom_call" | custom-call | flops 1000000000 | bytes 1000000 | tf_op jit(solution)/shard_map/outer/pallas_call | solution.py:133
  719.5 52.8 %full_sum.1 = f32[32,3200]{1,0:T(8,128)} custom-call(bf16[1024,3200]{1,0:T(8,128)(2,1)} %outer.1.x_ref), custom_call_target="tpu_custom_call" | custom-call | flops 1000000000 | bytes 1000000 | tf_op jit(solution)/shard_map/full_sum/pallas_call | solution.py:885
  (249 shorter events, 141.9 us)
Async XLA Ops:
  7.2 221.6 %all-gather.7.cloned.1.call-start = ((), (), s32[]{:S(2)}) async-start(), calls=%async_computation.7 | async-start | bytes 9437184 | tf_op jit(solution)/shard_map/all_gather | solution.py:1019
  8.0 220.8 %all-gather.9.cloned.1.call-start = ((), (), s32[]{:S(2)}) async-start(), calls=%async_computation.8 | async-start | bytes 9437184 | tf_op jit(solution)/shard_map/all_gather | solution.py:1020
  8.7 220.1 %all-gather.11.cloned.1.call-start = ((), (), s32[]{:S(2)}) async-start(), calls=%async_computation.9 | async-start | bytes 9437184 | tf_op jit(solution)/shard_map/all_gather | solution.py:1021
  11.0 60.4 %all-to-all-start = ((f32[4,8,768]{2,1,0:T(8,128)}), f32[4,8,768]{2,1,0:T(8,128)S(1)}, u32[]{:S(2)}, u32[]{:S(2)}) async-start(f32[4,8,768]{2,1,0:T(8,128)} %bitcast.14), calls=%async_computation | async-start | bytes 196608 | tf_op jit(solution)/shard_map/all_to_all | solution.py:1029
  17.4 761.1 %reduce-scatter.6.cloned.1.call-start = ((), (), s32[]{:S(2)}) async-start(), calls=%async_computation.5 | async-start | bytes 9437184 | tf_op jit(solution)/shard_map/reduce_scatter | solution.py:1149
  71.4 52.2 %collective-permute-start = (bf16[768,1024]{1,0:T(8,128)(2,1)S(1)}, bf16[768,1024]{1,0:T(8,128)(2,1)}, u32[]{:S(2)}, u32[]{:S(2)}) collective-permute-start(bf16[768,1024]{1,0:T(8,128)(2,1)S(1)} %bitcast.129), channel_id=1, source_target_pairs={{0,3},{1,0},{2,1},{3,2},{4,7},{5,4},{6,5},{7,6},{8,11},{9,8},{10,9... | collective-permute-start | bytes 4718600 | tf_op jit(solution)/shard_map/ppermute | solution.py:910
  123.7 38.1 %collective-permute-start.1 = (bf16[768,1024]{1,0:T(8,128)(2,1)}, bf16[768,1024]{1,0:T(8,128)(2,1)S(1)}, u32[]{:S(2)}, u32[]{:S(2)}) collective-permute-start(bf16[768,1024]{1,0:T(8,128)(2,1)} %collective-permute-done.df_ref), channel_id=1, source_target_pairs={{0,3},{1,0},{2,1},{3,2},{4,7},{5,4},{6,5},{7,6},{8,11},{9,8},{10,9... | collective-permute-start | bytes 4718600 | tf_op jit(solution)/shard_map/ppermute | solution.py:910
  161.8 38.1 %collective-permute-start.2 = (bf16[768,1024]{1,0:T(8,128)(2,1)S(1)}, bf16[768,1024]{1,0:T(8,128)(2,1)S(1)}, u32[]{:S(2)}, u32[]{:S(2)}) collective-permute-start(bf16[768,1024]{1,0:T(8,128)(2,1)S(1)} %collective-permute-done.1.df_ref), channel_id=1, source_target_pairs={{0,3},{1,0},{2,1},{3,2},{4,7},{5,4},{6,5},{7,6},{8,11},{9,8},{10,9... | collective-permute-start | bytes 4718600 | tf_op jit(solution)/shard_map/ppermute | solution.py:910
  207.5 59.5 %collective-permute-start.3 = (bf16[768,1024]{1,0:T(8,128)(2,1)}, bf16[768,1024]{1,0:T(8,128)(2,1)}, u32[]{:S(2)}, u32[]{:S(2)}) collective-permute-start(bf16[768,1024]{1,0:T(8,128)(2,1)} %multiply_convert_fusion.2.a2_ref.refs_6_), channel_id=1, source_target_pairs={{0,3},{1,0},{2,1},{3,2},{4,7},{5,4},{6,5},{7,6},{8,11},{9,8},{10,9... | collective-permute-start | bytes 4718600 | tf_op jit(solution)/shard_map/ppermute | solution.py:910
  225.0 42.0 %collective-permute-start.4 = (f32[8,768]{1,0:T(8,128)}, f32[8,768]{1,0:T(8,128)}, u32[]{:S(2)}, u32[]{:S(2)}) collective-permute-start(f32[8,768]{1,0:T(8,128)} %get-tuple-element.341), channel_id=1, source_target_pairs={{0,1},{1,2},{2,3},{3,0},{4,5},{5,6},{6,7},{7,4},{8,9},{9,10},{10,1... | collective-permute-start | bytes 73736 | tf_op jit(solution)/shard_map/ppermute | solution.py:910
  225.0 42.0 %collective-permute-start.5 = (f32[8,768]{1,0:T(8,128)}, f32[8,768]{1,0:T(8,128)}, u32[]{:S(2)}, u32[]{:S(2)}) collective-permute-start(f32[8,768]{1,0:T(8,128)} %get-tuple-element.340), channel_id=1, source_target_pairs={{0,2},{1,3},{2,0},{3,1},{4,6},{5,7},{6,4},{7,5},{8,10},{9,11},{10,... | collective-permute-start | bytes 73736 | tf_op jit(solution)/shard_map/ppermute | solution.py:910
  225.6 41.5 %collective-permute-start.6 = (f32[8,768]{1,0:T(8,128)}, f32[8,768]{1,0:T(8,128)}, u32[]{:S(2)}, u32[]{:S(2)}) collective-permute-start(f32[8,768]{1,0:T(8,128)} %get-tuple-element.339), channel_id=1, source_target_pairs={{0,3},{1,0},{2,1},{3,2},{4,7},{5,4},{6,5},{7,6},{8,11},{9,8},{10,9... | collective-permute-start | bytes 73736 | tf_op jit(solution)/shard_map/ppermute | solution.py:910
  267.0 42.3 %collective-permute-start.7 = (bf16[768,1024]{1,0:T(8,128)(2,1)}, bf16[768,1024]{1,0:T(8,128)(2,1)}, u32[]{:S(2)}, u32[]{:S(2)}) collective-permute-start(bf16[768,1024]{1,0:T(8,128)(2,1)} %collective-permute-done.3.a2_ref), channel_id=1, source_target_pairs={{0,3},{1,0},{2,1},{3,2},{4,7},{5,4},{6,5},{7,6},{8,11},{9,8},{10,9... | collective-permute-start | bytes 4718600 | tf_op jit(solution)/shard_map/ppermute | solution.py:910
  309.3 46.3 %collective-permute-start.8 = (bf16[768,1024]{1,0:T(8,128)(2,1)}, bf16[768,1024]{1,0:T(8,128)(2,1)}, u32[]{:S(2)}, u32[]{:S(2)}) collective-permute-start(bf16[768,1024]{1,0:T(8,128)(2,1)} %collective-permute-done.7.a2_ref), channel_id=1, source_target_pairs={{0,3},{1,0},{2,1},{3,2},{4,7},{5,4},{6,5},{7,6},{8,11},{9,8},{10,9... | collective-permute-start | bytes 4718600 | tf_op jit(solution)/shard_map/ppermute | solution.py:910
  355.6 43.2 %collective-permute-start.9 = (bf16[768,1024]{1,0:T(8,128)(2,1)}, bf16[768,1024]{1,0:T(8,128)(2,1)}, u32[]{:S(2)}, u32[]{:S(2)}) collective-permute-start(bf16[768,1024]{1,0:T(8,128)(2,1)} %get-tuple-element.234), channel_id=1, source_target_pairs={{0,3},{1,0},{2,1},{3,2},{4,7},{5,4},{6,5},{7,6},{8,11},{9,8},{10,9... | collective-permute-start | bytes 4718600 | tf_op jit(solution)/shard_map/ppermute | solution.py:910
  402.5 45.3 %collective-permute-start.10 = (bf16[768,1024]{1,0:T(8,128)(2,1)}, bf16[768,1024]{1,0:T(8,128)(2,1)}, u32[]{:S(2)}, u32[]{:S(2)}) collective-permute-start(bf16[768,1024]{1,0:T(8,128)(2,1)} %add_convert_fusion.4), channel_id=1, source_target_pairs={{0,3},{1,0},{2,1},{3,2},{4,7},{5,4},{6,5},{7,6},{8,11},{9,8},{10,9... | collective-permute-start | bytes 4718600 | tf_op jit(solution)/shard_map/ppermute | solution.py:910
  447.8 333.5 %reduce-scatter.4.cloned.1.call-start = ((), (), s32[]{:S(2)}) async-start(), calls=%async_computation.4 | async-start | bytes 9437184 | tf_op jit(solution)/shard_map/reduce_scatter | solution.py:1149
  448.4 335.7 %reduce-scatter.8.cloned.1.call-start = ((), (), s32[]{:S(2)}) async-start(), calls=%async_computation.6 | async-start | bytes 9437184 | tf_op jit(solution)/shard_map/reduce_scatter | solution.py:1149
  452.1 61.3 %collective-permute-start.11 = (bf16[768,1024]{1,0:T(8,128)(2,1)}, bf16[768,1024]{1,0:T(8,128)(2,1)}, u32[]{:S(2)}, u32[]{:S(2)}) collective-permute-start(bf16[768,1024]{1,0:T(8,128)(2,1)} %add_convert_fusion.3), channel_id=1, source_target_pairs={{0,3},{1,0},{2,1},{3,2},{4,7},{5,4},{6,5},{7,6},{8,11},{9,8},{10,9... | collective-permute-start | bytes 4718600 | tf_op jit(solution)/shard_map/ppermute | solution.py:910
  455.2 32.4 %collective-permute-start.12 = (f32[8,768]{1,0:T(8,128)S(1)}, f32[8,768]{1,0:T(8,128)S(1)}, u32[]{:S(2)}, u32[]{:S(2)}) collective-permute-start(f32[8,768]{1,0:T(8,128)S(1)} %bitcast.142), channel_id=1, source_target_pairs={{0,3},{1,0},{2,1},{3,2},{4,7},{5,4},{6,5},{7,6},{8,11},{9,8},{10,9... | collective-permute-start | bytes 73736 | tf_op jit(solution)/shard_map/ppermute | solution.py:910
  457.9 55.6 %collective-permute-start.14 = (f32[8,768]{1,0:T(8,128)}, f32[8,768]{1,0:T(8,128)}, u32[]{:S(2)}, u32[]{:S(2)}) collective-permute-start(f32[8,768]{1,0:T(8,128)} %bitcast.113), channel_id=1, source_target_pairs={{0,1},{1,2},{2,3},{3,0},{4,5},{5,6},{6,7},{7,4},{8,9},{9,10},{10,1... | collective-permute-start | bytes 73736 | tf_op jit(solution)/shard_map/ppermute | solution.py:910
  526.6 60.0 %collective-permute-start.15 = (bf16[768,1024]{1,0:T(8,128)(2,1)}, bf16[768,1024]{1,0:T(8,128)(2,1)}, u32[]{:S(2)}, u32[]{:S(2)}) collective-permute-start(bf16[768,1024]{1,0:T(8,128)(2,1)} %get-tuple-element.279), channel_id=1, source_target_pairs={{0,3},{1,0},{2,1},{3,2},{4,7},{5,4},{6,5},{7,6},{8,11},{9,8},{10,9... | collective-permute-start | bytes 4718600 | tf_op jit(solution)/shard_map/ppermute | solution.py:910
  590.4 49.0 %collective-permute-start.16 = (bf16[768,1024]{1,0:T(8,128)(2,1)}, bf16[768,1024]{1,0:T(8,128)(2,1)}, u32[]{:S(2)}, u32[]{:S(2)}) collective-permute-start(bf16[768,1024]{1,0:T(8,128)(2,1)} %add_convert_fusion.2), channel_id=1, source_target_pairs={{0,3},{1,0},{2,1},{3,2},{4,7},{5,4},{6,5},{7,6},{8,11},{9,8},{10,9... | collective-permute-start | bytes 4718600 | tf_op jit(solution)/shard_map/ppermute | solution.py:910
  643.3 43.1 %collective-permute-start.17 = (bf16[768,1024]{1,0:T(8,128)(2,1)}, bf16[768,1024]{1,0:T(8,128)(2,1)}, u32[]{:S(2)}, u32[]{:S(2)}) collective-permute-start(bf16[768,1024]{1,0:T(8,128)(2,1)} %add_convert_fusion.1), channel_id=1, source_target_pairs={{0,3},{1,0},{2,1},{3,2},{4,7},{5,4},{6,5},{7,6},{8,11},{9,8},{10,9... | collective-permute-start | bytes 4718600 | tf_op jit(solution)/shard_map/ppermute | solution.py:910
  (47 other events, 602.7 us)
Sparse Core Ops, SparseCore 0:
  9.9 75.7 all-gather.6
  87.6 62.5 all-gather.8
  152.1 54.3 all-gather.10
  447.9 72.8 reduce-scatter.5
  524.5 71.2 reduce-scatter.3
  599.2 82.6 reduce-scatter.7

commit v7 on v6

--- a/solution.py
+++ b/solution.py
@@ -18,6 +18,7 @@
 CONT_DEV = 2
 FF = 512
 QTILE = 128
+PARTS = 4
 KV_WIDTH = KEY_VALUE_HEADS * HEAD_SIZE
 ALL = ("ctx", "wt")
 
@@ -486,7 +487,7 @@
     tok = a2.shape[0]
     parts, experts = wg.shape[0], wg.shape[1]
     sizes = sorted({min(size, capacity) for size in (128, 192, 256, capacity)})
-    counts = (jnp.max(rank, 1) + 1.0).astype(jnp.int32)
+    counts = (jnp.max(rank, (1, 2)) + 1.0).astype(jnp.int32)
     spec = pl.BlockSpec
     whole = spec((tok, MODEL_WIDTH), lambda e, *_: (0, 0))
     row = spec((1, 1, tok), lambda e, *_: (e, 0, 0))
@@ -520,7 +521,7 @@
         compiler_params=pltpu.CompilerParams(vmem_limit_bytes=VMEM_LIMIT),
         cost_estimate=SMALL,
         name="expert_pass",
-    )(counts, a2, df, rank.reshape(experts, 1, tok), gates.reshape(experts, 1, tok), wg, wu, wd)
+    )(counts, a2, df, rank, gates, wg, wu, wd)
 
 
 def up_grad_kernel(*refs, sources):
@@ -756,22 +757,22 @@
     )(x)
 
 
-def sum_steps(copies, x_ref, key, sib, low, recv, out_ref):
+def sum_steps(copies, x_ref, key, sib, low, recv, out_ref, columns):
     rows = x_ref.shape[0] // 8
     half = rows // 2
     side, near, far = ({"ctx": partner(m)} for m in (1, 2, 4))
 
     def blocks(ref, m, start=0, count=rows):
-        return ref.at[pl.ds(m * rows + start, count)]
+        return ref.at[pl.ds(m * rows + start, count), columns]
 
     def added(m, start, count):
-        ours = x_ref[m * rows + start : m * rows + start + count, :].astype(f32)
+        ours = x_ref[m * rows + start : m * rows + start + count, columns].astype(f32)
         at = m // 2 * rows + start
-        return ours + sib[at : at + count, :].astype(f32)
+        return ours + sib[at : at + count, columns].astype(f32)
 
     def put(place, start, value, device):
         at = place * rows + start
-        low[at : at + half, :] = value.astype(bf16)
+        low[at : at + half, columns] = value.astype(bf16)
         copies.start(
             (key, "low", place, start),
             blocks(low, place, start, half),
@@ -796,19 +797,19 @@
 
     def fourth():
         copies.arrived((key, "low", 0, 0))
-        put(1, 0, added(2, 0, half) + recv[0:half, :].astype(f32), near)
+        put(1, 0, added(2, 0, half) + recv[0:half, columns].astype(f32), near)
         copies.arrived((key, "low", 0, half))
-        put(2, half, added(4, half, half) + recv[half:rows, :].astype(f32), far)
+        put(2, half, added(4, half, half) + recv[half:rows, columns].astype(f32), far)
 
     def last():
         copies.arrived((key, 1))
         for place in (1, 2):
             for start in (0, half):
                 copies.arrived((key, "low", place, start))
-        out_ref[...] = (
+        out_ref[:, columns] = (
             added(0, 0, rows)
-            + recv[rows : 2 * rows, :].astype(f32)
-            + recv[2 * rows :, :].astype(f32)
+            + recv[rows : 2 * rows, columns].astype(f32)
+            + recv[2 * rows :, columns].astype(f32)
         )
 
     return [first, second, third, fourth, last]
@@ -821,7 +822,7 @@
     greet([{"ctx": partner(m)} for m in (1, 2, 4)])
     copies = Copies(send, recv_sem)
     steps = [
-        sum_steps(copies, x_refs[n], n, sibs[n], lows[n], recvs[n], out_refs[n])
+        sum_steps(copies, x_refs[n], n, sibs[n], lows[n], recvs[n], out_refs[n], slice(None))
         for n in range(sets)
     ]
     for n in range(5):
@@ -861,21 +862,45 @@
         [{"ctx": partner(m)} for m in (1, 2, 4)] + [{"wt": ahead(d)} for d in (1, 2, 3)]
     )
     copies = Copies(send, recv_sem)
-    for step in sum_steps(copies, x_ref, 0, sib, low, recv, total):
-        step()
-    total_low[...] = total[...].astype(bf16)
-    for d in (2, 1, 3):
-        copies.start(
-            d,
-            total_low.at[pl.ds(pl.multiple_of(ahead(d) * rows, rows), rows)],
-            arrived.at[pl.ds((d - 1) * rows, rows)],
-            {"wt": ahead(d)},
-        )
-    result = total[pl.ds(pl.multiple_of(ahead(0) * rows, rows), rows), :]
-    for d in (1, 3, 2):
-        copies.arrived(d)
-        result = result + arrived[(d - 1) * rows : d * rows, :].astype(f32)
-    out_ref[...] = result
+    wide = x_ref.shape[1]
+    edges = [128 * (n * (wide // 128) // PARTS) for n in range(PARTS + 1)]
+    parts = [slice(a, b) for a, b in zip(edges, edges[1:])]
+    steps = [
+        sum_steps(copies, x_ref, n, sib, low, recv, total, columns)
+        for n, columns in enumerate(parts)
+    ]
+
+    def leave(n):
+        total_low[:, parts[n]] = total[:, parts[n]].astype(bf16)
+        for d in (2, 1, 3):
+            copies.start(
+                ("wt", n, d),
+                total_low.at[pl.ds(pl.multiple_of(ahead(d) * rows, rows), rows), parts[n]],
+                arrived.at[pl.ds((d - 1) * rows, rows), parts[n]],
+                {"wt": ahead(d)},
+            )
+
+    def finish(n):
+        own = pl.ds(pl.multiple_of(ahead(0) * rows, rows), rows)
+        result = total[own, parts[n]]
+        for d in (1, 3, 2):
+            copies.arrived(("wt", n, d))
+            result = result + arrived[(d - 1) * rows : d * rows, parts[n]].astype(f32)
+        out_ref[:, parts[n]] = result
+
+    for one in steps:
+        one[0]()
+    for n in range(PARTS + 2):
+        if n < PARTS:
+            steps[n][1]()
+            steps[n][2]()
+        if 1 <= n <= PARTS:
+            steps[n - 1][3]()
+        if n >= 2:
+            steps[n - 2][4]()
+            leave(n - 2)
+    for n in range(PARTS):
+        finish(n)
     copies.close()
 
 
@@ -894,8 +919,8 @@
             pltpu.VMEM((4 * rows, columns), f32),
             pltpu.VMEM((4 * rows, columns), bf16),
             pltpu.VMEM((3 * rows, columns), bf16),
-            pltpu.SemaphoreType.DMA((13,)),
-            pltpu.SemaphoreType.DMA((13,)),
+            pltpu.SemaphoreType.DMA((13 * PARTS,)),
+            pltpu.SemaphoreType.DMA((13 * PARTS,)),
         ],
         compiler_params=pltpu.CompilerParams(
             collective_id=4, has_side_effects=True, vmem_limit_bytes=VMEM_LIMIT
@@ -1027,7 +1052,7 @@
     before = (order[None, :] < order[:, None]).astype(bf16)
     rank = jnp.where(mask, dot(before, mask.astype(bf16)), -1.0)
     ranks = lax.all_to_all(
-        rank.T.reshape(shard_count, expert_count, tok), "wt", 0, 0, tiled=True
+        rank.T.reshape(shard_count, expert_count, 1, tok), "wt", 0, 0, tiled=True
     )
     last = shard_count - 1
     grads_in = {0: out_low, last: shift(after(out_low, pieces[0], ranks), -1)}
@@ -1092,7 +1117,7 @@
     raised = jnp.where(mask, jnp.exp(jnp.where(mask, logits - top, 0.0)), 0.0)
     gates = raised / jnp.sum(raised, -1, keepdims=True)
 
-    gates_out = gates.T.reshape(shard_count, expert_count, tok)
+    gates_out = gates.T.reshape(shard_count, expert_count, 1, tok)
     gates_in = []
     for d in range(shard_count):
         piece = lax.dynamic_index_in_dim(gates_out, (wt_index + d) % shard_count, 0, False)
@@ -1120,23 +1145,26 @@
             result, carried = beside(result, carried)
         mixed[d], partial[d], d_gate, *kept = result
         rows.append(kept)
-        d_gate = d_gate.reshape(expert_count, tok)
         gate_grads[d] = shift(d_gate, shard_count - d) if d else d_gate
         if coming:
             got[coming] = after(got[coming], partial[d])
     carried = shift(add(carried, partial[2]), -1)
-    (gate_grad, up_grad), carried = beside(
+    (gate_grad, up_grad), carried, gate_grads = beside(
         up_weight_grads([(after(r[0], partial[1]), r[3], r[4]) for r in rows], context_size),
         carried,
-    )
+        gate_grads,
+    )
+    stacked = jnp.stack([gate_grads[d] for d in range(shard_count)], 0)
+    for bit in (1, 2, 4):
+        if bit < shard_count:
+            stacked = jnp.where(wt_index & bit > 0, jnp.roll(stacked, bit, 0), stacked)
+    stacked = stacked.reshape(EXPERTS, tok).T
+    grad_logits = (gates * (stacked - jnp.sum(gates * stacked, -1, keepdims=True))).astype(bf16)
     carried = shift(add(carried, partial[1]), -1)
     down_grad, home = beside(
-        down_weight_grads([(after(r[2], gate_grad), r[1]) for r in rows], context_size), carried
-    )
-
-    stacked = jnp.stack([gate_grads[d] for d in range(shard_count)], 0)
-    stacked = jnp.roll(stacked, wt_index, 0).reshape(EXPERTS, tok).T
-    grad_logits = (gates * (stacked - jnp.sum(gates * stacked, -1, keepdims=True))).astype(bf16)
+        down_weight_grads([(after(r[2], gate_grad, grad_logits), r[1]) for r in rows], context_size), carried
+    )
+
     grad_normed_two = partial[0].astype(f32) + home.astype(f32)
     grad_normed_two = grad_normed_two + dot_nt(grad_logits, router_full)
     grad_mid_norm, second_gain_grad = norm_backward(

time: 804 us -> 760 us (0.945)
  waiting for transfers between devices: 39.7 us -> 12.7 us
  local copies, waits for them, and re-layouts: 57.1 us -> 39.9 us
  starting transfers between devices: 46.3 us -> 34.5 us
  Pallas kernels: 569 us -> 578 us
    ppermute x18, waiting for transfers between devices: 37.1 us -> 10.1 us  [shift(): return lax.ppermute(x, 'wt', [(i, (i + distance) % n) for i in range(n)])]
    pallas_call x4, Pallas kernels: 153 us -> 171 us  [expert_pass(): pl.pallas_call(functools.partial(expert_kernel, sizes=sizes), grid_spec=p...]
    ppermute x18, starting transfers between devices: 39.8 us -> 28 us  [shift(): return lax.ppermute(x, 'wt', [(i, (i + distance) % n) for i in range(n)])]
    unnamed x105 -> x96, local copies, waits for them, and re-layouts: 17.5 us -> 5.83 us
    reshape x10 -> x0, local copies, waits for them, and re-layouts: 10.6 us -> none  [the longest x4 4.7 us: expert_pass(): gates.reshape(experts, 1, tok)]
  transfers between devices with their start and end apart: 25 -> 25, of which waited for: 3 -> 2; matrix products, arithmetic and copies ran while one was open for 14% -> 13% of each run, Pallas kernels for 72% -> 77%
where the time goes in v7:
time: 760 us; the launch traced here: 751 us
  Pallas kernels  578 us (76%)
  other arithmetic  50.5 us (7%)
  local copies, waits for them, and re-layouts  39.9 us (5%)
  starting transfers between devices  34.5 us (5%)
  between operations  17.8 us (2%)
  matrix products  17.5 us (2%)
  waiting for transfers between devices  12.7 us (2%)
    pallas_call x4, Pallas kernels, expert_pass(): pl.pallas_call(functools.partial(expert_kernel, sizes=sizes), grid_spec=p...  171 us
    pallas_call x2, Pallas kernels, attention_backward(): pl.pallas_call(functools.partial(attention_backward_kernel, block_rows=bl...  97.6 us
    pallas_call x2, Pallas kernels, attention_forward(): pl.pallas_call(functools.partial(attention_forward_kernel, block_rows=blo...  53.3 us
    pallas_call x1, Pallas kernels, packed_gather(): pl.pallas_call(packed_gather_kernel, in_specs=[ANY], out_specs=ANY, out_s...  53 us
    pallas_call x1, Pallas kernels, full_sum(): pl.pallas_call(full_sum_kernel, in_specs=[vmem], out_specs=vmem, out_shap...  45.8 us
    pallas_call x1, Pallas kernels, up_weight_grads(): pl.pallas_call(functools.partial(up_grad_kernel, sources=len(rows)), grid...  40.6 us
    pallas_call x1, Pallas kernels, plane_sum(): pl.pallas_call(functools.partial(plane_sum_kernel, sets=sets), in_specs=[...  36.9 us
    pallas_call x1, Pallas kernels, plane_gather(): pl.pallas_call(plane_gather_kernel, in_specs=[ANY], out_specs=ANY, out_sh...  33.3 us
  transfers between devices with their start and end apart: 25, of which 2 were waited for; matrix products, arithmetic and copies ran while one was open for 13% of the time, Pallas kernels for 77%

profile of v7, /device:TPU:0, one launch (start us, length us, event | category | flops | bytes accessed | tf_op | source)
XLA Modules:
  0.0 751.1 jit_solution(5840738155918091093)
XLA Ops:
  11.0 6.3 all-to-all-start
  18.4 53.0 %packed_gather.1.refs_0_ = bf16[1024,3200]{1,0:T(8,128)(2,1)} custom-call(bf16[32,3200]{1,0:T(8,128)(2,1)} %concatenate.79.x_ref), custom_call_target="tpu_custom_call" | custom-call | flops 1000000000 | bytes 1000000 | tf_op jit(solution)/shard_map/packed_gather/pallas_call | solution.py:744
  81.4 9.0 %project.1 = (bf16[768,1024]{1,0:T(8,128)(2,1)}, bf16[768,1024]{1,0:T(8,128)(2,1)}, bf16[768,1024]{1,0:T(8,128)(2,1)}, bf16[1024,2048]{1,0:T(8,128)(2,1)}, bf16[...) custom-call(s32[32]{0:T(128)} %add.215.places, bf16[768,1024]{1,0:T(8,128)(2,1)} %bitcast.142, ...), custom_call_target="tpu_custom_call" | custom-call | flops 1000000000 | bytes 1000000 | tf_op jit(solution)/shard_map/project/pallas_call | solution.py:96
  90.4 33.3 %plane_gather.1.refs_0_.refs_1_ = bf16[2048,1024]{1,0:T(8,128)(2,1)} custom-call(bf16[768,1024]{1,0:T(8,128)(2,1)} %get-tuple-element.166.x_ref), custom_call_target="tpu_custom_call" | custom-call | flops 1000000000 | bytes 1000000 | tf_op jit(solution)/shard_map/plane_gather/pallas_call | solution.py:689
  130.3 26.5 %attention_forward.2 = (bf16[768,512]{1,0:T(8,128)(2,1)}, f32[2,4,768]{2,1,0:T(4,128)}) custom-call(s32[16]{0:T(128)} %reshape.357.places, s32[4]{0:T(128)} %get-tuple-element.367.starts, bf16[768,1024]{1,0:T(8,128)(2,1)} %get-tuple-element.290.q_ref, bf16[2048,1024]{1,0:T(8,128)(2,1)} %plane_gather.1.refs_0_.refs_1_, ...), custom_call_target="tpu_custom_call" | custom-call | flops 1000000000 | bytes 1000000 | tf_op jit(solution)/shard_map/attention_forward/pallas_call | solution.py:229
  156.8 5.0 collective-permute-done.1.df_ref
  161.8 4.7 collective-permute-start.2
  168.0 26.8 %attention_forward.3 = (bf16[768,512]{1,0:T(8,128)(2,1)}, f32[2,4,768]{2,1,0:T(4,128)}) custom-call(s32[16]{0:T(128)} %reshape.357.places, s32[4]{0:T(128)} %get-tuple-element.367.starts, bf16[768,1024]{1,0:T(8,128)(2,1)} %get-tuple-element.290.q_ref, bf16[2048,1024]{1,0:T(8,128)(2,1)} %plane_gather.1.refs_0_.refs_1_, ...), custom_call_target="tpu_custom_call" | custom-call | flops 1000000000 | bytes 1000000 | tf_op jit(solution)/shard_map/attention_forward/pallas_call | solution.py:229
  194.8 5.1 collective-permute-done.2.df_ref
  201.7 4.3 multiply_reduce_fusion.1
  207.5 4.3 collective-permute-start.3
  230.0 41.0 %expert_pass.4 = (bf16[768,1024]{1,0:T(8,128)(2,1)}, bf16[768,1024]{1,0:T(8,128)(2,1)}, f32[8,1,768]{2,1,0:T(1,128)}, bf16[8,336,1024]{2,1,0:T(8,128)(2,1)}, bf1...) custom-call(s32[8]{0:T(128)} %get-tuple-element.371.counts, ...), custom_call_target="tpu_custom_call" | custom-call | flops 1000000000 | bytes 1000000 | tf_op jit(solution)/shard_map/expert_pass/pallas_call | solution.py:499
  272.4 42.7 %expert_pass.5 = (bf16[768,1024]{1,0:T(8,128)(2,1)}, bf16[768,1024]{1,0:T(8,128)(2,1)}, f32[8,1,768]{2,1,0:T(1,128)}, bf16[8,336,1024]{2,1,0:T(8,128)(2,1)}, bf1...) custom-call(s32[8]{0:T(128)} %get-tuple-element.368.counts, ...), custom_call_target="tpu_custom_call" | custom-call | flops 1000000000 | bytes 1000000 | tf_op jit(solution)/shard_map/expert_pass/pallas_call | solution.py:499
  315.8 44.2 %expert_pass.6 = (bf16[768,1024]{1,0:T(8,128)(2,1)}, bf16[768,1024]{1,0:T(8,128)(2,1)}, f32[8,1,768]{2,1,0:T(1,128)}, bf16[8,336,1024]{2,1,0:T(8,128)(2,1)}, bf1...) custom-call(s32[8]{0:T(128)} %get-tuple-element.369.counts, ...), custom_call_target="tpu_custom_call" | custom-call | flops 1000000000 | bytes 1000000 | tf_op jit(solution)/shard_map/expert_pass/pallas_call | solution.py:499
  360.8 42.6 %expert_pass.7 = (bf16[768,1024]{1,0:T(8,128)(2,1)}, bf16[768,1024]{1,0:T(8,128)(2,1)}, f32[8,1,768]{2,1,0:T(1,128)}, bf16[8,336,1024]{2,1,0:T(8,128)(2,1)}, bf1...) custom-call(s32[8]{0:T(128)} %get-tuple-element.370.counts, ...), custom_call_target="tpu_custom_call" | custom-call | flops 1000000000 | bytes 1000000 | tf_op jit(solution)/shard_map/expert_pass/pallas_call | solution.py:499
  411.6 40.6 %up_weight_grads.1 = (bf16[8,8,128,512]{3,2,1,0:T(8,128)(2,1)}, bf16[8,8,128,512]{3,2,1,0:T(8,128)(2,1)}) custom-call(bf16[8,336,1024]{2,1,0:T(8,128)(2,1)} %get-tuple-element.240.refs_0_, bf16[8,336,512]{2,1,0:T(8,128)(2,1)} %get-tuple-element.241.refs_1_, bf16[8,336,512]{2,1,0:T(8,128)(2,1)} %get-tuple-element.242.refs_2_, ...), custom_call_target="tpu_custom_call" | custom-call | flops 1000000000 | bytes 1000000 | tf_op jit(solution)/shard_map/up_weight_grads/pallas_call | solution.py:558
  467.1 24.0 %down_weight_grads.1 = bf16[8,8,512,128]{3,2,1,0:T(8,128)(2,1)} custom-call(bf16[8,336,512]{2,1,0:T(8,128)(2,1)} %get-tuple-element.267.refs_0_, bf16[8,336,1024]{2,1,0:T(8,128)(2,1)} %get-tuple-element.268.refs_1_, bf16[8,336,512]{2,1,0:T(8,128)(2,1)} %get-tuple-element.270.refs_2_, bf16[8,336,1024]{2,1,0:T(8,128)(2,1)} %get-tuple-element.271.refs_3_, ...), custom_call_target="tpu_custom_call" | custom-call | flops 1000000000 | bytes 1000000 | tf_op jit(solution)/shard_map/down_weight_grads/pallas_call | solution.py:573
  502.5 48.7 %attention_backward.2 = (bf16[768,512]{1,0:T(8,128)(2,1)}, bf16[2048,512]{1,0:T(8,128)(2,1)}, f32[512,256]{1,0:T(8,128)}, f32[512,256]{1,0:T(8,128)}) custom-call(s32[16]{0:T(128)} %reshape.357.places, s32[4]{0:T(128)} %get-tuple-element.367.starts, bf16[768,1024]{1,0:T(8,128)(2,1)} %get-tuple-element.290.q_ref, ...), custom_call_target="tpu_custom_call" | custom-call | flops 1000000000 | bytes 1000000 | tf_op jit(solution)/shard_map/attention_backward/pallas_call | solution.py:373
  555.4 48.9 %attention_backward.3 = (bf16[768,512]{1,0:T(8,128)(2,1)}, bf16[2048,512]{1,0:T(8,128)(2,1)}, f32[512,256]{1,0:T(8,128)}, f32[512,256]{1,0:T(8,128)}) custom-call(s32[16]{0:T(128)} %reshape.357.places, s32[4]{0:T(128)} %get-tuple-element.367.starts, bf16[768,1024]{1,0:T(8,128)(2,1)} %get-tuple-element.290.q_ref, ...), custom_call_target="tpu_custom_call" | custom-call | flops 1000000000 | bytes 1000000 | tf_op jit(solution)/shard_map/attention_backward/pallas_call | solution.py:373
  604.3 3.8 add_convert_fusion.1
  611.3 36.9 %plane_sum.1 = (f32[256,512]{1,0:T(8,128)}, f32[256,512]{1,0:T(8,128)}) custom-call(bf16[2048,512]{1,0:T(8,128)(2,1)} %get-tuple-element.288.refs_0_, bf16[2048,512]{1,0:T(8,128)(2,1)} %get-tuple-element.299.refs_1_), custom_call_target="tpu_custom_call" | custom-call | flops 1000000000 | bytes 1000000 | tf_op jit(solution)/shard_map/plane_sum/pallas_call | solution.py:843
  661.9 6.6 multiply_convert_fusion
  669.9 14.0 %outer.1.x_ref = bf16[1024,3200]{1,0:T(8,128)(2,1)} custom-call(s32[1]{0:T(128)} %bitcast.31.mine, bf16[768,1024]{1,0:T(8,128)(2,1)} %get-tuple-element.313.refs_0_.refs_4_, bf16[768,1024]{1,0:T(8,128)(2,1)} %constant_dynamic-update-slice_fusion.2.refs_1_, bf16[768,1024]{1,0:T(8,128)(2,1)} %copy-done.10, bf16[768,1024]{1,0:T(8,128)(2,1)} %copy-done.2, ...), custom_call_target="tpu_custom_call" | custom-call | flops 1000000000 | bytes 1000000 | tf_op jit(solution)/shard_map/outer/pallas_call | solution.py:134
  683.9 45.8 %full_sum.1 = f32[32,3200]{1,0:T(8,128)} custom-call(bf16[1024,3200]{1,0:T(8,128)(2,1)} %outer.1.x_ref), custom_call_target="tpu_custom_call" | custom-call | flops 1000000000 | bytes 1000000 | tf_op jit(solution)/shard_map/full_sum/pallas_call | solution.py:910
  (241 shorter events, 115.2 us)
Async XLA Ops:
  7.2 222.8 %all-gather.7.cloned.1.call-start = ((), (), s32[]{:S(2)}) async-start(), calls=%async_computation.7 | async-start | bytes 9437184 | tf_op jit(solution)/shard_map/all_gather | solution.py:1044
  8.0 221.9 %all-gather.9.cloned.1.call-start = ((), (), s32[]{:S(2)}) async-start(), calls=%async_computation.8 | async-start | bytes 9437184 | tf_op jit(solution)/shard_map/all_gather | solution.py:1045
  8.7 221.2 %all-gather.11.cloned.1.call-start = ((), (), s32[]{:S(2)}) async-start(), calls=%async_computation.9 | async-start | bytes 9437184 | tf_op jit(solution)/shard_map/all_gather | solution.py:1046
  11.0 60.4 %all-to-all-start = ((f32[4,8,1,768]{3,1,2,0:T(8,128)}), f32[4,8,1,768]{3,1,2,0:T(8,128)S(1)}, u32[]{:S(2)}, u32[]{:S(2)}) async-start(f32[4,8,1,768]{3,1,2,0:T(8,128)} %bitcast.15), calls=%async_computation | async-start | bytes 196608 | tf_op jit(solution)/shard_map/all_to_all | solution.py:1054
  17.4 718.4 %reduce-scatter.6.cloned.1.call-start = ((), (), s32[]{:S(2)}) async-start(), calls=%async_computation.5 | async-start | bytes 9437184 | tf_op jit(solution)/shard_map/reduce_scatter | solution.py:1177
  71.4 52.3 %collective-permute-start = (bf16[768,1024]{1,0:T(8,128)(2,1)S(1)}, bf16[768,1024]{1,0:T(8,128)(2,1)}, u32[]{:S(2)}, u32[]{:S(2)}) collective-permute-start(bf16[768,1024]{1,0:T(8,128)(2,1)S(1)} %bitcast.141), channel_id=1, source_target_pairs={{0,3},{1,0},{2,1},{3,2},{4,7},{5,4},{6,5},{7,6},{8,11},{9,8},{10,9... | collective-permute-start | bytes 4718600 | tf_op jit(solution)/shard_map/ppermute | solution.py:935
  123.7 38.1 %collective-permute-start.1 = (bf16[768,1024]{1,0:T(8,128)(2,1)}, bf16[768,1024]{1,0:T(8,128)(2,1)S(1)}, u32[]{:S(2)}, u32[]{:S(2)}) collective-permute-start(bf16[768,1024]{1,0:T(8,128)(2,1)} %collective-permute-done.df_ref), channel_id=1, source_target_pairs={{0,3},{1,0},{2,1},{3,2},{4,7},{5,4},{6,5},{7,6},{8,11},{9,8},{10,9... | collective-permute-start | bytes 4718600 | tf_op jit(solution)/shard_map/ppermute | solution.py:935
  161.8 38.1 %collective-permute-start.2 = (bf16[768,1024]{1,0:T(8,128)(2,1)S(1)}, bf16[768,1024]{1,0:T(8,128)(2,1)S(1)}, u32[]{:S(2)}, u32[]{:S(2)}) collective-permute-start(bf16[768,1024]{1,0:T(8,128)(2,1)S(1)} %collective-permute-done.1.df_ref), channel_id=1, source_target_pairs={{0,3},{1,0},{2,1},{3,2},{4,7},{5,4},{6,5},{7,6},{8,11},{9,8},{10,9... | collective-permute-start | bytes 4718600 | tf_op jit(solution)/shard_map/ppermute | solution.py:935
  207.5 63.5 %collective-permute-start.3 = (bf16[768,1024]{1,0:T(8,128)(2,1)}, bf16[768,1024]{1,0:T(8,128)(2,1)}, u32[]{:S(2)}, u32[]{:S(2)}) collective-permute-start(bf16[768,1024]{1,0:T(8,128)(2,1)} %multiply_convert_fusion.2.a2_ref.refs_6_), channel_id=1, source_target_pairs={{0,3},{1,0},{2,1},{3,2},{4,7},{5,4},{6,5},{7,6},{8,11},{9,8},{10,9... | collective-permute-start | bytes 4718600 | tf_op jit(solution)/shard_map/ppermute | solution.py:935
  224.9 46.2 %collective-permute-start.4 = (f32[8,1,768]{2,1,0:T(1,128)}, f32[8,1,768]{2,1,0:T(1,128)}, u32[]{:S(2)}, u32[]{:S(2)}) collective-permute-start(f32[8,1,768]{2,1,0:T(1,128)} %squeeze.53), channel_id=1, source_target_pairs={{0,1},{1,2},{2,3},{3,0},{4,5},{5,6},{6,7},{7,4},{8,9},{9,10},{10,1... | collective-permute-start | bytes 73736 | tf_op jit(solution)/shard_map/ppermute | solution.py:935
  225.5 45.5 %collective-permute-start.5 = (f32[8,1,768]{2,1,0:T(1,128)}, f32[8,1,768]{2,1,0:T(1,128)}, u32[]{:S(2)}, u32[]{:S(2)}) collective-permute-start(f32[8,1,768]{2,1,0:T(1,128)} %squeeze.54), channel_id=1, source_target_pairs={{0,2},{1,3},{2,0},{3,1},{4,6},{5,7},{6,4},{7,5},{8,10},{9,11},{10,... | collective-permute-start | bytes 73736 | tf_op jit(solution)/shard_map/ppermute | solution.py:935
  226.7 44.4 %collective-permute-start.6 = (f32[8,1,768]{2,1,0:T(1,128)}, f32[8,1,768]{2,1,0:T(1,128)}, u32[]{:S(2)}, u32[]{:S(2)}) collective-permute-start(f32[8,1,768]{2,1,0:T(1,128)} %squeeze.55), channel_id=1, source_target_pairs={{0,3},{1,0},{2,1},{3,2},{4,7},{5,4},{6,5},{7,6},{8,11},{9,8},{10,9... | collective-permute-start | bytes 73736 | tf_op jit(solution)/shard_map/ppermute | solution.py:935
  271.1 44.1 %collective-permute-start.7 = (bf16[768,1024]{1,0:T(8,128)(2,1)}, bf16[768,1024]{1,0:T(8,128)(2,1)}, u32[]{:S(2)}, u32[]{:S(2)}) collective-permute-start(bf16[768,1024]{1,0:T(8,128)(2,1)} %collective-permute-done.3.a2_ref), channel_id=1, source_target_pairs={{0,3},{1,0},{2,1},{3,2},{4,7},{5,4},{6,5},{7,6},{8,11},{9,8},{10,9... | collective-permute-start | bytes 4718600 | tf_op jit(solution)/shard_map/ppermute | solution.py:935
  315.1 44.9 %collective-permute-start.8 = (bf16[768,1024]{1,0:T(8,128)(2,1)}, bf16[768,1024]{1,0:T(8,128)(2,1)}, u32[]{:S(2)}, u32[]{:S(2)}) collective-permute-start(bf16[768,1024]{1,0:T(8,128)(2,1)} %collective-permute-done.7.a2_ref), channel_id=1, source_target_pairs={{0,3},{1,0},{2,1},{3,2},{4,7},{5,4},{6,5},{7,6},{8,11},{9,8},{10,9... | collective-permute-start | bytes 4718600 | tf_op jit(solution)/shard_map/ppermute | solution.py:935
  360.1 43.4 %collective-permute-start.9 = (bf16[768,1024]{1,0:T(8,128)(2,1)}, bf16[768,1024]{1,0:T(8,128)(2,1)}, u32[]{:S(2)}, u32[]{:S(2)}) collective-permute-start(bf16[768,1024]{1,0:T(8,128)(2,1)} %get-tuple-element.238), channel_id=1, source_target_pairs={{0,3},{1,0},{2,1},{3,2},{4,7},{5,4},{6,5},{7,6},{8,11},{9,8},{10,9... | collective-permute-start | bytes 4718600 | tf_op jit(solution)/shard_map/ppermute | solution.py:935
  407.2 45.1 %collective-permute-start.10 = (bf16[768,1024]{1,0:T(8,128)(2,1)}, bf16[768,1024]{1,0:T(8,128)(2,1)}, u32[]{:S(2)}, u32[]{:S(2)}) collective-permute-start(bf16[768,1024]{1,0:T(8,128)(2,1)} %add_convert_fusion.4), channel_id=1, source_target_pairs={{0,3},{1,0},{2,1},{3,2},{4,7},{5,4},{6,5},{7,6},{8,11},{9,8},{10,9... | collective-permute-start | bytes 4718600 | tf_op jit(solution)/shard_map/ppermute | solution.py:935
  407.2 45.0 %collective-permute-start.13 = (f32[8,1,768]{2,1,0:T(1,128)S(1)}, f32[8,1,768]{2,1,0:T(1,128)}, u32[]{:S(2)}, u32[]{:S(2)}) collective-permute-start(f32[8,1,768]{2,1,0:T(1,128)S(1)} %copy-done.43), channel_id=1, source_target_pairs={{0,1},{1,2},{2,3},{3,0},{4,5},{5,6},{6,7},{7,4},{8,9},{9,10},{10,1... | collective-permute-start | bytes 73736 | tf_op jit(solution)/shard_map/ppermute | solution.py:935
  409.2 43.0 %collective-permute-start.12 = (f32[8,1,768]{2,1,0:T(1,128)S(1)}, f32[8,1,768]{2,1,0:T(1,128)}, u32[]{:S(2)}, u32[]{:S(2)}) collective-permute-start(f32[8,1,768]{2,1,0:T(1,128)S(1)} %copy-done.44), channel_id=1, source_target_pairs={{0,2},{1,3},{2,0},{3,1},{4,6},{5,7},{6,4},{7,5},{8,10},{9,11},{10,... | collective-permute-start | bytes 73736 | tf_op jit(solution)/shard_map/ppermute | solution.py:935
  409.2 43.0 %collective-permute-start.11 = (f32[8,1,768]{2,1,0:T(1,128)S(1)}, f32[8,1,768]{2,1,0:T(1,128)}, u32[]{:S(2)}, u32[]{:S(2)}) collective-permute-start(f32[8,1,768]{2,1,0:T(1,128)S(1)} %copy-done.45), channel_id=1, source_target_pairs={{0,3},{1,0},{2,1},{3,2},{4,7},{5,4},{6,5},{7,6},{8,11},{9,8},{10,9... | collective-permute-start | bytes 73736 | tf_op jit(solution)/shard_map/ppermute | solution.py:935
  452.3 286.3 %reduce-scatter.4.cloned.1.call-start = ((), (), s32[]{:S(2)}) async-start(), calls=%async_computation.4 | async-start | bytes 9437184 | tf_op jit(solution)/shard_map/reduce_scatter | solution.py:1177
  452.9 288.5 %reduce-scatter.8.cloned.1.call-start = ((), (), s32[]{:S(2)}) async-start(), calls=%async_computation.6 | async-start | bytes 9437184 | tf_op jit(solution)/shard_map/reduce_scatter | solution.py:1177
  491.1 60.1 %collective-permute-start.15 = (bf16[768,1024]{1,0:T(8,128)(2,1)}, bf16[768,1024]{1,0:T(8,128)(2,1)}, u32[]{:S(2)}, u32[]{:S(2)}) collective-permute-start(bf16[768,1024]{1,0:T(8,128)(2,1)} %get-tuple-element.287), channel_id=1, source_target_pairs={{0,3},{1,0},{2,1},{3,2},{4,7},{5,4},{6,5},{7,6},{8,11},{9,8},{10,9... | collective-permute-start | bytes 4718600 | tf_op jit(solution)/shard_map/ppermute | solution.py:935
  554.9 49.4 %collective-permute-start.16 = (bf16[768,1024]{1,0:T(8,128)(2,1)}, bf16[768,1024]{1,0:T(8,128)(2,1)}, u32[]{:S(2)}, u32[]{:S(2)}) collective-permute-start(bf16[768,1024]{1,0:T(8,128)(2,1)} %add_convert_fusion.2), channel_id=1, source_target_pairs={{0,3},{1,0},{2,1},{3,2},{4,7},{5,4},{6,5},{7,6},{8,11},{9,8},{10,9... | collective-permute-start | bytes 4718600 | tf_op jit(solution)/shard_map/ppermute | solution.py:935
  608.1 42.4 %collective-permute-start.17 = (bf16[768,1024]{1,0:T(8,128)(2,1)}, bf16[768,1024]{1,0:T(8,128)(2,1)}, u32[]{:S(2)}, u32[]{:S(2)}) collective-permute-start(bf16[768,1024]{1,0:T(8,128)(2,1)} %add_convert_fusion.1), channel_id=1, source_target_pairs={{0,3},{1,0},{2,1},{3,2},{4,7},{5,4},{6,5},{7,6},{8,11},{9,8},{10,9... | collective-permute-start | bytes 4718600 | tf_op jit(solution)/shard_map/ppermute | solution.py:935
  (47 other events, 624.8 us)
Sparse Core Ops, SparseCore 0:
  9.9 75.7 all-gather.6
  87.6 62.5 all-gather.8
  152.1 54.3 all-gather.10
  452.4 72.8 reduce-scatter.5
  529.0 71.2 reduce-scatter.3
  603.7 79.0 reduce-scatter.7

commit v8 on v7

--- a/solution.py
+++ b/solution.py
@@ -18,7 +18,7 @@
 CONT_DEV = 2
 FF = 512
 QTILE = 128
-PARTS = 4
+PARTS = 2
 KV_WIDTH = KEY_VALUE_HEADS * HEAD_SIZE
 ALL = ("ctx", "wt")
 
@@ -112,6 +112,44 @@
     )(places, x, cosine, sine, *pieces)
 
 
+def middle_kernel(
+    a_ref, b_ref, x_ref, out_ref, rest_ref, gains_ref, mask_ref, middle_ref, normed_ref, inv_ref, gates_ref
+):
+    half = a_ref.shape[1]
+    branch = dot_nt(a_ref[...], out_ref[:, :half]) + dot_nt(b_ref[...], out_ref[:, half:])
+    middle = x_ref[...].astype(f32) + resid_scale * branch
+    middle_ref[...] = middle
+    inverse = lax.rsqrt(jnp.mean(middle * middle, -1, keepdims=True) + norm_eps)
+    inv_ref[...] = inverse
+    normed = (middle * inverse * gains_ref[1:2]).astype(bf16)
+    normed_ref[...] = normed
+    mask = mask_ref[...] > 0.0
+    logits = jnp.where(mask, dot(normed, rest_ref[...]), masked_score)
+    top = jnp.max(logits, -1, keepdims=True)
+    raised = jnp.where(mask, jnp.exp(logits - top), 0.0)
+    gates_ref[...] = (raised / jnp.sum(raised, -1, keepdims=True)).T[:EXPERTS]
+
+
+def to_gates(halves, x, output_t, rest, gain_rows, mask):
+    tok = x.shape[0]
+    shape = jax.ShapeDtypeStruct
+    whole = pl.BlockSpec(memory_space=pltpu.VMEM)
+    return pl.pallas_call(
+        middle_kernel,
+        in_specs=[whole] * 7,
+        out_specs=[whole] * 4,
+        out_shape=[
+            shape((tok, MODEL_WIDTH), f32),
+            shape((tok, MODEL_WIDTH), bf16),
+            shape((tok, 1), f32),
+            shape((EXPERTS, tok), f32),
+        ],
+        compiler_params=pltpu.CompilerParams(vmem_limit_bytes=VMEM_LIMIT),
+        cost_estimate=SMALL,
+        name="to_gates",
+    )(*halves, x, output_t, rest, gain_rows, mask)
+
+
 def outer_kernel(mine, *refs, count):
     out_ref = refs[-1]
     pairs = [(refs[n], refs[n + 1]) for n in range(0, len(refs) - 1, 2)]
@@ -120,17 +158,19 @@
         columns = b_ref.shape[1]
         out_ref[:, at : at + columns] = dot_tn(a_ref[...], b_ref[...]).astype(bf16)
         at += columns
-    out_ref[:, at:] = sum(dot_tn(a[...], b[...]) for a, b in pairs[count:]).astype(bf16)
-
-
-def outer(pairs, extra):
+    if pairs[count:]:
+        out_ref[:, at:] = sum(dot_tn(a[...], b[...]) for a, b in pairs[count:]).astype(bf16)
+
+
+def outer(pairs, extra=()):
     tok = pairs[0][0].shape[0]
     mine = lax.axis_index("ctx").astype(jnp.int32).reshape(1)
     specs = []
-    for _, b in pairs + extra:
+    everything = [*pairs, *extra]
+    for _, b in everything:
         specs.append(pl.BlockSpec((tok, 128), lambda m, mine: (0, m ^ mine[0])))
         specs.append(pl.BlockSpec(b.shape, lambda m, mine: (0, 0)))
-    columns = sum(b.shape[1] for _, b in pairs) + extra[0][1].shape[1]
+    columns = sum(b.shape[1] for _, b in [*pairs, *extra[:1]])
     return pl.pallas_call(
         functools.partial(outer_kernel, count=len(pairs)),
         grid_spec=pltpu.PrefetchScalarGridSpec(
@@ -143,7 +183,7 @@
         compiler_params=pltpu.CompilerParams(vmem_limit_bytes=VMEM_LIMIT),
         cost_estimate=SMALL,
         name="outer",
-    )(mine, *[x for pair in pairs + extra for x in pair])
+    )(mine, *[x for pair in everything for x in pair])
 
 
 def gather_keys(pieces, scratch, places, block_rows):
@@ -368,6 +408,7 @@
     own = kv_own.shape[0]
     spec = pl.BlockSpec
     wide = spec((tok, 256), lambda g, *_: (0, 2 * half + g))
+    narrow = spec((tok, 256), lambda g, *_: (0, g))
     ours = spec((own, 128), lambda g, *_: (0, g))
     table = spec((tok, 128), lambda g, *_: (0, 0))
     return pl.pallas_call(
@@ -377,7 +418,7 @@
         grid_spec=pltpu.PrefetchScalarGridSpec(
             num_scalar_prefetch=2,
             grid=(2,),
-            in_specs=[wide, wide, spec((1, 4, tok), lambda g, *_: (g, 0, 0)), wide, table, table]
+            in_specs=[wide, wide, spec((1, 4, tok), lambda g, *_: (g, 0, 0)), narrow, table, table]
             + key_specs(pieces, own, half),
             out_specs=[
                 spec((tok, 256), lambda g, *_: (0, g)),
@@ -822,7 +863,9 @@
     greet([{"ctx": partner(m)} for m in (1, 2, 4)])
     copies = Copies(send, recv_sem)
     steps = [
-        sum_steps(copies, x_refs[n], n, sibs[n], lows[n], recvs[n], out_refs[n], slice(None))
+        sum_steps(
+            copies, x_refs[n], n, sibs[n], lows[n], recvs[n], out_refs[n], slice(None)
+        )
         for n in range(sets)
     ]
     for n in range(5):
@@ -832,21 +875,19 @@
 
 
 def plane_sum(arrays):
-    if lax.axis_size("ctx") != 8:
-        return [
-            lax.psum_scatter(x, "ctx", scatter_dimension=0, tiled=True).astype(f32)
-            for x in arrays
-        ]
     sets = len(arrays)
-    rows, columns = arrays[0].shape[0] // 8, arrays[0].shape[1]
+    shapes = [(x.shape[0] // 8, x.shape[1]) for x in arrays]
     vmem = pl.BlockSpec(memory_space=pltpu.VMEM)
     return pl.pallas_call(
         functools.partial(plane_sum_kernel, sets=sets),
         in_specs=[vmem] * sets,
         out_specs=[vmem] * sets,
-        out_shape=[jax.ShapeDtypeStruct((rows, columns), f32)] * sets,
-        scratch_shapes=[pltpu.VMEM((4 * rows, columns), bf16)] * sets
-        + [pltpu.VMEM((3 * rows, columns), bf16)] * (2 * sets)
+        out_shape=[jax.ShapeDtypeStruct(shape, f32) for shape in shapes],
+        scratch_shapes=[
+            pltpu.VMEM((times * rows, columns), bf16)
+            for times in (4, 3, 3)
+            for rows, columns in shapes
+        ]
         + [pltpu.SemaphoreType.DMA((10 * sets,)), pltpu.SemaphoreType.DMA((10 * sets,))],
         compiler_params=pltpu.CompilerParams(
             collective_id=3, has_side_effects=True, vmem_limit_bytes=VMEM_LIMIT
@@ -856,8 +897,11 @@
     )(*arrays)
 
 
-def full_sum_kernel(x_ref, out_ref, sib, low, recv, total, total_low, arrived, send, recv_sem):
+def full_sum_kernel(
+    x_ref, ready_ref, out_ref, sib, low, recv, total, total_low, arrived, send, recv_sem
+):
     rows = out_ref.shape[0]
+    lead = ready_ref.shape[1]
     greet(
         [{"ctx": partner(m)} for m in (1, 2, 4)] + [{"wt": ahead(d)} for d in (1, 2, 3)]
     )
@@ -865,31 +909,32 @@
     wide = x_ref.shape[1]
     edges = [128 * (n * (wide // 128) // PARTS) for n in range(PARTS + 1)]
     parts = [slice(a, b) for a, b in zip(edges, edges[1:])]
+    places = [slice(lead + a, lead + b) for a, b in zip(edges, edges[1:])] + [slice(0, lead)]
+    own = pl.ds(pl.multiple_of(ahead(0) * rows, rows), rows)
     steps = [
         sum_steps(copies, x_ref, n, sib, low, recv, total, columns)
         for n, columns in enumerate(parts)
     ]
 
-    def leave(n):
-        total_low[:, parts[n]] = total[:, parts[n]].astype(bf16)
+    def leave(n, value):
+        total_low[:, places[n]] = value.astype(bf16)
         for d in (2, 1, 3):
             copies.start(
                 ("wt", n, d),
-                total_low.at[pl.ds(pl.multiple_of(ahead(d) * rows, rows), rows), parts[n]],
-                arrived.at[pl.ds((d - 1) * rows, rows), parts[n]],
+                total_low.at[pl.ds(pl.multiple_of(ahead(d) * rows, rows), rows), places[n]],
+                arrived.at[pl.ds((d - 1) * rows, rows), places[n]],
                 {"wt": ahead(d)},
             )
 
-    def finish(n):
-        own = pl.ds(pl.multiple_of(ahead(0) * rows, rows), rows)
-        result = total[own, parts[n]]
+    def finish(n, result):
         for d in (1, 3, 2):
             copies.arrived(("wt", n, d))
-            result = result + arrived[(d - 1) * rows : d * rows, parts[n]].astype(f32)
-        out_ref[:, parts[n]] = result
+            result = result + arrived[(d - 1) * rows : d * rows, places[n]].astype(f32)
+        out_ref[:, places[n]] = result
 
     for one in steps:
         one[0]()
+    leave(PARTS, ready_ref[...])
     for n in range(PARTS + 2):
         if n < PARTS:
             steps[n][1]()
@@ -898,36 +943,39 @@
             steps[n - 1][3]()
         if n >= 2:
             steps[n - 2][4]()
-            leave(n - 2)
+            leave(n - 2, total[:, parts[n - 2]])
+    finish(PARTS, ready_ref[own, :])
     for n in range(PARTS):
-        finish(n)
+        finish(n, total[own, parts[n]])
     copies.close()
 
 
-def full_sum(x):
+def full_sum(x, ready):
     rows, columns = x.shape[0] // 32, x.shape[1]
+    whole = ready.shape[1] + columns
     vmem = pl.BlockSpec(memory_space=pltpu.VMEM)
+    count = 13 * PARTS + 3
     return pl.pallas_call(
         full_sum_kernel,
-        in_specs=[vmem],
+        in_specs=[vmem, vmem],
         out_specs=vmem,
-        out_shape=jax.ShapeDtypeStruct((rows, columns), f32),
+        out_shape=jax.ShapeDtypeStruct((rows, whole), f32),
         scratch_shapes=[
             pltpu.VMEM((16 * rows, columns), bf16),
             pltpu.VMEM((12 * rows, columns), bf16),
             pltpu.VMEM((12 * rows, columns), bf16),
             pltpu.VMEM((4 * rows, columns), f32),
-            pltpu.VMEM((4 * rows, columns), bf16),
-            pltpu.VMEM((3 * rows, columns), bf16),
-            pltpu.SemaphoreType.DMA((13 * PARTS,)),
-            pltpu.SemaphoreType.DMA((13 * PARTS,)),
+            pltpu.VMEM((4 * rows, whole), bf16),
+            pltpu.VMEM((3 * rows, whole), bf16),
+            pltpu.SemaphoreType.DMA((count,)),
+            pltpu.SemaphoreType.DMA((count,)),
         ],
         compiler_params=pltpu.CompilerParams(
             collective_id=4, has_side_effects=True, vmem_limit_bytes=VMEM_LIMIT
         ),
         cost_estimate=SMALL,
         name="full_sum",
-    )(x)
+    )(x, ready)
 
 
 def shift(x, distance):
@@ -951,13 +999,24 @@
     return [packed_gather(x)], [32], places.reshape(-1).astype(jnp.int32)
 
 
-def outer_sum(pairs, extra):
+def keys_and_early(d_kv, pairs):
     if lax.axis_size("ctx") != 8 or lax.axis_size("wt") != 4:
-        parts = [dot_tn(a, b) for a, b in pairs] + [sum(dot_tn(a, b) for a, b in extra)]
+        owned = [
+            lax.psum_scatter(x, "ctx", scatter_dimension=0, tiled=True).astype(f32)
+            for x in d_kv
+        ]
+        return owned, jnp.concatenate([dot_tn(a, b) for a, b in pairs], 1)
+    *owned, early = plane_sum(d_kv + [outer(pairs)])
+    return owned, early
+
+
+def last_sum(early, pairs, extra):
+    if lax.axis_size("ctx") != 8 or lax.axis_size("wt") != 4:
+        parts = [early] + [dot_tn(a, b) for a, b in pairs] + [sum(dot_tn(a, b) for a, b in extra)]
         return lax.psum_scatter(
             jnp.concatenate(parts, 1).astype(bf16), ALL, scatter_dimension=0, tiled=True
         ).astype(f32)
-    return full_sum(outer(pairs, extra))
+    return full_sum(outer(pairs, extra), early)
 
 
 def after(x, *others):
@@ -1105,19 +1164,19 @@
         heads.append(result)
     for d in range(last - 3, 0, -1):
         grads_in[d] = shift(grads_in[d + 1], -1)
-    attended = jnp.concatenate([out for out, _ in heads], 1)
+    attended = [out for out, _ in heads]
     lse = [row for _, row in heads]
 
-    branch = dot_nt(attended, output_t)
-    middle = inputs + resid_scale * branch
-    normed_mid, inverse_two = norm_forward(middle, second_gain)
-    normed_two = normed_mid.astype(bf16)
-    logits = dot(normed_two, router_full)
-    top = jnp.max(jnp.where(mask, logits, masked_score), -1, keepdims=True)
-    raised = jnp.where(mask, jnp.exp(jnp.where(mask, logits - top, 0.0)), 0.0)
-    gates = raised / jnp.sum(raised, -1, keepdims=True)
-
-    gates_out = gates.T.reshape(shard_count, expert_count, 1, tok)
+    middle, normed_two, inverse_two, gates = to_gates(
+        attended,
+        layer_input[0],
+        output_t,
+        rest,
+        gain_rows,
+        jnp.pad(mask.astype(f32), ((0, 0), (0, 128 - EXPERTS))),
+    )
+
+    gates_out = gates.reshape(shard_count, expert_count, 1, tok)
     gates_in = []
     for d in range(shard_count):
         piece = lax.dynamic_index_in_dim(gates_out, (wt_index + d) % shard_count, 0, False)
@@ -1158,8 +1217,9 @@
     for bit in (1, 2, 4):
         if bit < shard_count:
             stacked = jnp.where(wt_index & bit > 0, jnp.roll(stacked, bit, 0), stacked)
-    stacked = stacked.reshape(EXPERTS, tok).T
-    grad_logits = (gates * (stacked - jnp.sum(gates * stacked, -1, keepdims=True))).astype(bf16)
+    stacked = stacked.reshape(EXPERTS, tok)
+    grad_logits = gates * (stacked - jnp.sum(gates * stacked, 0, keepdims=True))
+    grad_logits = grad_logits.T.astype(bf16)
     carried = shift(add(carried, partial[1]), -1)
     down_grad, home = beside(
         down_weight_grads([(after(r[2], gate_grad, grad_logits), r[1]) for r in rows], context_size), carried
@@ -1185,7 +1245,7 @@
             query,
             grad_attended,
             lse[half],
-            attended,
+            attended[half],
             cosine,
             sine,
             kv_pieces,
@@ -1202,12 +1262,18 @@
         d_kv.append(result[1])
         ours.append(result[2:])
     carried = shift(add(carried, mixed[last - 2]), -1)
-    owned, carried = beside(plane_sum(d_kv), carried)
+    d_query = jnp.concatenate(d_query, 1)
+    (owned, early), carried = beside(
+        keys_and_early(
+            d_kv,
+            [(normed_one, d_query), (grad_branch, attended[0]), (grad_branch, attended[1])],
+        ),
+        carried,
+    )
     for d in range(last - 3, 0, -1):
         carried = shift(add(carried, mixed[d]), -1)
     mixture = mixed[0].astype(f32) + carried.astype(f32)
     layer_output = (middle + resid_scale * mixture).astype(bf16)
-    d_query = jnp.concatenate(d_query, 1)
     d_key, d_value = (
         jnp.concatenate(
             [
@@ -1229,8 +1295,9 @@
     input_grad = (grad_middle + grad_input_norm).astype(bf16)
 
     column = lax.broadcasted_iota(jnp.int32, (tok, 128), 1)
-    shares = outer_sum(
-        [(normed_one, d_query), (grad_branch, attended), (normed_one, grad_kv)],
+    shares = last_sum(
+        early,
+        [(normed_one, grad_kv)],
         [
             (normed_two, jnp.pad(grad_logits, ((0, 0), (0, 128 - EXPERTS)))),
             (second_gain_grad, (column == EXPERTS).astype(bf16)),

time: 760 us -> 766 us (level)
  Pallas kernels: 578 us -> 594 us
  other arithmetic: 50.5 us -> 39.6 us
  local copies, waits for them, and re-layouts: 39.9 us -> 30.7 us
  starting transfers between devices: 34.5 us -> 42.7 us
    pallas_call x1, Pallas kernels: 36.9 us -> 68.7 us  [plane_sum(): pl.pallas_call(functools.partial(plane_sum_kernel, sets=sets), in_specs=[...]
    pallas_call x1 -> x2, Pallas kernels: 45.8 us -> 33.2 us  [the longest x1 25.3 us: full_sum(): pl.pallas_call(full_sum_kernel, in_specs=[vmem, vmem], out_specs=vmem, ou...]
    pallas_call x4, Pallas kernels: 171 us -> 160 us  [expert_pass(): pl.pallas_call(functools.partial(expert_kernel, sizes=sizes), grid_spec=p...]
    ppermute x18, starting transfers between devices: 28 us -> 36.1 us  [shift(): return lax.ppermute(x, 'wt', [(i, (i + distance) % n) for i in range(n)])]
    pallas_call x1 -> x2, Pallas kernels: 14 us -> 20.8 us  [outer(): pl.pallas_call(functools.partial(outer_kernel, count=len(pairs)), grid_sp...]
  transfers between devices with their start and end apart: 25 -> 25, of which waited for: 2 -> 3; matrix products, arithmetic and copies ran while one was open for 13% -> 10% of each run, Pallas kernels for 77% -> 78%
where the time goes in v8:
time: 766 us; the launch traced here: 757 us
  Pallas kernels  594 us (78%)
  starting transfers between devices  42.7 us (6%)
  other arithmetic  39.6 us (5%)
  local copies, waits for them, and re-layouts  30.7 us (4%)
  waiting for transfers between devices  20.3 us (3%)
  between operations  17.8 us (2%)
  matrix products  12.5 us (2%)
    pallas_call x4, Pallas kernels, expert_pass(): pl.pallas_call(functools.partial(expert_kernel, sizes=sizes), grid_spec=p...  160 us
    pallas_call x2, Pallas kernels, attention_backward(): pl.pallas_call(functools.partial(attention_backward_kernel, block_rows=bl...  97.4 us
    pallas_call x1, Pallas kernels, plane_sum(): pl.pallas_call(functools.partial(plane_sum_kernel, sets=sets), in_specs=[...  68.7 us
    pallas_call x2, Pallas kernels, attention_forward(): pl.pallas_call(functools.partial(attention_forward_kernel, block_rows=blo...  53.2 us
    pallas_call x1, Pallas kernels, packed_gather(): pl.pallas_call(packed_gather_kernel, in_specs=[ANY], out_specs=ANY, out_s...  53 us
    pallas_call x1, Pallas kernels, up_weight_grads(): pl.pallas_call(functools.partial(up_grad_kernel, sources=len(rows)), grid...  40.5 us
    ppermute x18, starting transfers between devices, shift(): return lax.ppermute(x, 'wt', [(i, (i + distance) % n) for i in range(n)])  36.1 us
    pallas_call x1, Pallas kernels, plane_gather(): pl.pallas_call(plane_gather_kernel, in_specs=[ANY], out_specs=ANY, out_sh...  33.3 us
  transfers between devices with their start and end apart: 25, of which 3 were waited for; matrix products, arithmetic and copies ran while one was open for 10% of the time, Pallas kernels for 78%

profile of v8, /device:TPU:0, one launch (start us, length us, event | category | flops | bytes accessed | tf_op | source)
XLA Modules:
  0.0 757.3 jit_solution(16071001372718871303)
XLA Ops:
  10.6 6.3 all-to-all-start
  17.9 53.0 %packed_gather.1.refs_0_ = bf16[1024,3200]{1,0:T(8,128)(2,1)} custom-call(bf16[32,3200]{1,0:T(8,128)(2,1)} %concatenate.76.x_ref), custom_call_target="tpu_custom_call" | custom-call | flops 1000000000 | bytes 1000000 | tf_op jit(solution)/shard_map/packed_gather/pallas_call | solution.py:785
  80.3 9.0 %project.1 = (bf16[768,1024]{1,0:T(8,128)(2,1)}, bf16[768,1024]{1,0:T(8,128)(2,1)}, bf16[768,1024]{1,0:T(8,128)(2,1)}, bf16[1024,2048]{1,0:T(8,128)(2,1)}, bf16[...) custom-call(s32[32]{0:T(128)} %add.207.places, bf16[768,1024]{1,0:T(8,128)(2,1)} %bitcast.118, ...), custom_call_target="tpu_custom_call" | custom-call | flops 1000000000 | bytes 1000000 | tf_op jit(solution)/shard_map/project/pallas_call | solution.py:96
  89.3 33.3 %plane_gather.1.refs_0_.refs_1_ = bf16[2048,1024]{1,0:T(8,128)(2,1)} custom-call(bf16[768,1024]{1,0:T(8,128)(2,1)} %get-tuple-element.172.x_ref), custom_call_target="tpu_custom_call" | custom-call | flops 1000000000 | bytes 1000000 | tf_op jit(solution)/shard_map/plane_gather/pallas_call | solution.py:730
  129.3 26.6 %attention_forward.2 = (bf16[768,512]{1,0:T(8,128)(2,1)}, f32[2,4,768]{2,1,0:T(4,128)}) custom-call(s32[16]{0:T(128)} %reshape.348.places, s32[4]{0:T(128)} %get-tuple-element.375.starts, bf16[768,1024]{1,0:T(8,128)(2,1)} %get-tuple-element.300.q_ref, bf16[2048,1024]{1,0:T(8,128)(2,1)} %plane_gather.1.refs_0_.refs_1_, ...), custom_call_target="tpu_custom_call" | custom-call | flops 1000000000 | bytes 1000000 | tf_op jit(solution)/shard_map/attention_forward/pallas_call | solution.py:269
  155.8 4.9 collective-permute-done.1.df_ref
  160.8 4.7 collective-permute-start.2
  166.4 26.6 %attention_forward.3 = (bf16[768,512]{1,0:T(8,128)(2,1)}, f32[2,4,768]{2,1,0:T(4,128)}) custom-call(s32[16]{0:T(128)} %reshape.348.places, s32[4]{0:T(128)} %get-tuple-element.375.starts, bf16[768,1024]{1,0:T(8,128)(2,1)} %get-tuple-element.300.q_ref, bf16[2048,1024]{1,0:T(8,128)(2,1)} %plane_gather.1.refs_0_.refs_1_, ...), custom_call_target="tpu_custom_call" | custom-call | flops 1000000000 | bytes 1000000 | tf_op jit(solution)/shard_map/attention_forward/pallas_call | solution.py:269
  193.1 5.7 collective-permute-done.2.df_ref
  198.8 8.0 %to_gates.1 = (f32[768,1024]{1,0:T(8,128)}, bf16[768,1024]{1,0:T(8,128)(2,1)}, f32[768,1]{1,0:T(8,128)}, f32[32,768]{1,0:T(8,128)}) custom-call(bf16[768,512]{1,0:T(8,128)(2,1)} %get-tuple-element.178.a_ref.o_ref.refs_3_, bf16[768,512]{1,0:T(8,128)(2,1)} %get-tuple-element.183.b_ref.o_ref.refs_5_, bf16[768,1024]{1,0:T(8,128)(2,1)} %bitcast.119, ...), custom_call_target="tpu_custom_call" | custom-call | flops 1000000000 | bytes 1000000 | tf_op jit(solution)/shard_map/to_gates/pallas_call | solution.py:137
  218.0 38.7 %expert_pass.4 = (bf16[768,1024]{1,0:T(8,128)(2,1)}, bf16[768,1024]{1,0:T(8,128)(2,1)}, f32[8,1,768]{2,1,0:T(1,128)}, bf16[8,336,1024]{2,1,0:T(8,128)(2,1)}, bf1...) custom-call(s32[8]{0:T(128)} %get-tuple-element.379.counts, ...), custom_call_target="tpu_custom_call" | custom-call | flops 1000000000 | bytes 1000000 | tf_op jit(solution)/shard_map/expert_pass/pallas_call | solution.py:540
  258.7 39.7 %expert_pass.5 = (bf16[768,1024]{1,0:T(8,128)(2,1)}, bf16[768,1024]{1,0:T(8,128)(2,1)}, f32[8,1,768]{2,1,0:T(1,128)}, bf16[8,336,1024]{2,1,0:T(8,128)(2,1)}, bf1...) custom-call(s32[8]{0:T(128)} %get-tuple-element.376.counts, ...), custom_call_target="tpu_custom_call" | custom-call | flops 1000000000 | bytes 1000000 | tf_op jit(solution)/shard_map/expert_pass/pallas_call | solution.py:540
  301.2 40.3 %expert_pass.6 = (bf16[768,1024]{1,0:T(8,128)(2,1)}, bf16[768,1024]{1,0:T(8,128)(2,1)}, f32[8,1,768]{2,1,0:T(1,128)}, bf16[8,336,1024]{2,1,0:T(8,128)(2,1)}, bf1...) custom-call(s32[8]{0:T(128)} %get-tuple-element.377.counts, ...), custom_call_target="tpu_custom_call" | custom-call | flops 1000000000 | bytes 1000000 | tf_op jit(solution)/shard_map/expert_pass/pallas_call | solution.py:540
  344.8 41.4 %expert_pass.7 = (bf16[768,1024]{1,0:T(8,128)(2,1)}, bf16[768,1024]{1,0:T(8,128)(2,1)}, f32[8,1,768]{2,1,0:T(1,128)}, bf16[8,336,1024]{2,1,0:T(8,128)(2,1)}, bf1...) custom-call(s32[8]{0:T(128)} %get-tuple-element.378.counts, ...), custom_call_target="tpu_custom_call" | custom-call | flops 1000000000 | bytes 1000000 | tf_op jit(solution)/shard_map/expert_pass/pallas_call | solution.py:540
  399.5 40.5 %up_weight_grads.1 = (bf16[8,8,128,512]{3,2,1,0:T(8,128)(2,1)}, bf16[8,8,128,512]{3,2,1,0:T(8,128)(2,1)}) custom-call(bf16[8,336,1024]{2,1,0:T(8,128)(2,1)} %get-tuple-element.250.refs_0_, bf16[8,336,512]{2,1,0:T(8,128)(2,1)} %get-tuple-element.251.refs_1_, bf16[8,336,512]{2,1,0:T(8,128)(2,1)} %get-tuple-element.252.refs_2_, ...), custom_call_target="tpu_custom_call" | custom-call | flops 1000000000 | bytes 1000000 | tf_op jit(solution)/shard_map/up_weight_grads/pallas_call | solution.py:599
  444.3 24.5 %down_weight_grads.1 = bf16[8,8,512,128]{3,2,1,0:T(8,128)(2,1)} custom-call(bf16[8,336,512]{2,1,0:T(8,128)(2,1)} %get-tuple-element.277.refs_0_, bf16[8,336,1024]{2,1,0:T(8,128)(2,1)} %get-tuple-element.278.refs_1_, bf16[8,336,512]{2,1,0:T(8,128)(2,1)} %get-tuple-element.280.refs_2_, bf16[8,336,1024]{2,1,0:T(8,128)(2,1)} %get-tuple-element.281.refs_3_, ...), custom_call_target="tpu_custom_call" | custom-call | flops 1000000000 | bytes 1000000 | tf_op jit(solution)/shard_map/down_weight_grads/pallas_call | solution.py:614
  468.8 7.0 collective-permute-done.14
  489.1 48.5 %attention_backward.2 = (bf16[768,512]{1,0:T(8,128)(2,1)}, bf16[2048,512]{1,0:T(8,128)(2,1)}, f32[512,256]{1,0:T(8,128)}, f32[512,256]{1,0:T(8,128)}) custom-call(s32[16]{0:T(128)} %reshape.348.places, s32[4]{0:T(128)} %get-tuple-element.375.starts, bf16[768,1024]{1,0:T(8,128)(2,1)} %get-tuple-element.300.q_ref, ...), custom_call_target="tpu_custom_call" | custom-call | flops 1000000000 | bytes 1000000 | tf_op jit(solution)/shard_map/attention_backward/pallas_call | solution.py:414
  541.4 48.9 %attention_backward.3 = (bf16[768,512]{1,0:T(8,128)(2,1)}, bf16[2048,512]{1,0:T(8,128)(2,1)}, f32[512,256]{1,0:T(8,128)}, f32[512,256]{1,0:T(8,128)}) custom-call(s32[16]{0:T(128)} %reshape.348.places, s32[4]{0:T(128)} %get-tuple-element.375.starts, bf16[768,1024]{1,0:T(8,128)(2,1)} %get-tuple-element.300.q_ref, ...), custom_call_target="tpu_custom_call" | custom-call | flops 1000000000 | bytes 1000000 | tf_op jit(solution)/shard_map/attention_backward/pallas_call | solution.py:414
  598.1 11.2 %outer.2.refs_2_ = bf16[1024,2048]{1,0:T(8,128)(2,1)} custom-call(s32[1]{0:T(128)} %bitcast.31.mine, bf16[768,1024]{1,0:T(8,128)(2,1)} %get-tuple-element.310.refs_0_, bf16[768,1024]{1,0:T(8,128)(2,1)} %constant_dynamic-update-slice_fusion.refs_1_, bf16[768,1024]{1,0:T(8,128)(2,1)} %copy-done.3, bf16[768,512]{1,0:T(8,128)(2,1)} %get-tuple-element.178.a_ref.o_ref.refs_3_, ...), custom_call_target="tpu_custom_call" | custom-call | flops 1000000000 | bytes 1000000 | tf_op jit(solution)/shard_map/outer/pallas_call | solution.py:174
  609.3 68.7 %plane_sum.1 = (f32[256,512]{1,0:T(8,128)}, f32[256,512]{1,0:T(8,128)}, f32[128,2048]{1,0:T(8,128)}) custom-call(bf16[2048,512]{1,0:T(8,128)(2,1)} %get-tuple-element.298.refs_0_, bf16[2048,512]{1,0:T(8,128)(2,1)} %get-tuple-element.309.refs_1_, bf16[1024,2048]{1,0:T(8,128)(2,1)} %outer.2.refs_2_), custom_call_target="tpu_custom_call" | custom-call | flops 1000000000 | bytes 1000000 | tf_op jit(solution)/shard_map/plane_sum/pallas_call | solution.py:881
  693.4 6.3 multiply_convert_fusion
  701.1 9.6 %outer.3.x_ref = bf16[1024,1152]{1,0:T(8,128)(2,1)} custom-call(s32[1]{0:T(128)} %bitcast.31.mine, bf16[768,1024]{1,0:T(8,128)(2,1)} %get-tuple-element.310.refs_0_, bf16[768,1024]{1,0:T(8,128)(2,1)} %maximum_maximum_fusion.1.refs_1_, bf16[768,1024]{1,0:T(8,128)(2,1)} %get-tuple-element.189.a2_ref.refs_2_, bf16[768,128]{1,0:T(8,128)(2,1)} %pad.12.refs_3_, ...), custom_call_target="tpu_custom_call" | custom-call | flops 1000000000 | bytes 1000000 | tf_op jit(solution)/shard_map/outer/pallas_call | solution.py:174
  710.7 25.3 %full_sum.1 = f32[32,3200]{1,0:T(8,128)} custom-call(bf16[1024,1152]{1,0:T(8,128)(2,1)} %outer.3.x_ref, f32[128,2048]{1,0:T(8,128)} %get-tuple-element.325.ready_ref), custom_call_target="tpu_custom_call" | custom-call | flops 1000000000 | bytes 1000000 | tf_op jit(solution)/shard_map/full_sum/pallas_call | solution.py:958
  (233 shorter events, 110.9 us)
Async XLA Ops:
  7.3 210.7 %all-gather.7.cloned.1.call-start = ((), (), s32[]{:S(2)}) async-start(), calls=%async_computation.7 | async-start | bytes 9437184 | tf_op jit(solution)/shard_map/all_gather | solution.py:1103
  8.0 210.0 %all-gather.9.cloned.1.call-start = ((), (), s32[]{:S(2)}) async-start(), calls=%async_computation.8 | async-start | bytes 9437184 | tf_op jit(solution)/shard_map/all_gather | solution.py:1104
  8.7 209.2 %all-gather.11.cloned.1.call-start = ((), (), s32[]{:S(2)}) async-start(), calls=%async_computation.9 | async-start | bytes 9437184 | tf_op jit(solution)/shard_map/all_gather | solution.py:1105
  10.6 60.4 %all-to-all-start = ((f32[4,8,1,768]{3,1,2,0:T(8,128)}), f32[4,8,1,768]{3,1,2,0:T(8,128)S(1)}, u32[]{:S(2)}, u32[]{:S(2)}) async-start(f32[4,8,1,768]{3,1,2,0:T(8,128)} %fusion.28), calls=%async_computation | async-start | bytes 196608 | tf_op jit(solution)/shard_map/all_to_all | solution.py:1113
  16.9 725.0 %reduce-scatter.6.cloned.1.call-start = ((), (), s32[]{:S(2)}) async-start(), calls=%async_computation.5 | async-start | bytes 9437184 | tf_op jit(solution)/shard_map/reduce_scatter | solution.py:1237
  71.0 51.6 %collective-permute-start = (bf16[768,1024]{1,0:T(8,128)(2,1)S(1)}, bf16[768,1024]{1,0:T(8,128)(2,1)}, u32[]{:S(2)}, u32[]{:S(2)}) collective-permute-start(bf16[768,1024]{1,0:T(8,128)(2,1)S(1)} %bitcast.121), channel_id=1, source_target_pairs={{0,3},{1,0},{2,1},{3,2},{4,7},{5,4},{6,5},{7,6},{8,11},{9,8},{10,9... | collective-permute-start | bytes 4718600 | tf_op jit(solution)/shard_map/ppermute | solution.py:983
  122.6 38.1 %collective-permute-start.1 = (bf16[768,1024]{1,0:T(8,128)(2,1)}, bf16[768,1024]{1,0:T(8,128)(2,1)S(1)}, u32[]{:S(2)}, u32[]{:S(2)}) collective-permute-start(bf16[768,1024]{1,0:T(8,128)(2,1)} %collective-permute-done.df_ref), channel_id=1, source_target_pairs={{0,3},{1,0},{2,1},{3,2},{4,7},{5,4},{6,5},{7,6},{8,11},{9,8},{10,9... | collective-permute-start | bytes 4718600 | tf_op jit(solution)/shard_map/ppermute | solution.py:983
  160.8 38.1 %collective-permute-start.2 = (bf16[768,1024]{1,0:T(8,128)(2,1)S(1)}, bf16[768,1024]{1,0:T(8,128)(2,1)S(1)}, u32[]{:S(2)}, u32[]{:S(2)}) collective-permute-start(bf16[768,1024]{1,0:T(8,128)(2,1)S(1)} %collective-permute-done.1.df_ref), channel_id=1, source_target_pairs={{0,3},{1,0},{2,1},{3,2},{4,7},{5,4},{6,5},{7,6},{8,11},{9,8},{10,9... | collective-permute-start | bytes 4718600 | tf_op jit(solution)/shard_map/ppermute | solution.py:983
  206.8 49.9 %collective-permute-start.3 = (bf16[768,1024]{1,0:T(8,128)(2,1)}, bf16[768,1024]{1,0:T(8,128)(2,1)S(1)}, u32[]{:S(2)}, u32[]{:S(2)}) collective-permute-start(bf16[768,1024]{1,0:T(8,128)(2,1)} %get-tuple-element.189.a2_ref.refs_2_), channel_id=1, source_target_pairs={{0,3},{1,0},{2,1},{3,2},{4,7},{5,4},{6,5},{7,6},{8,11},{9,8},{10,9... | collective-permute-start | bytes 4718600 | tf_op jit(solution)/shard_map/ppermute | solution.py:983
  213.9 42.8 %collective-permute-start.4 = (f32[8,1,768]{2,1,0:T(1,128)S(1)}, f32[8,1,768]{2,1,0:T(1,128)S(1)}, u32[]{:S(2)}, u32[]{:S(2)}) collective-permute-start(f32[8,1,768]{2,1,0:T(1,128)S(1)} %bitcast.143), channel_id=1, source_target_pairs={{0,1},{1,2},{2,3},{3,0},{4,5},{5,6},{6,7},{7,4},{8,9},{9,10},{10,1... | collective-permute-start | bytes 73736 | tf_op jit(solution)/shard_map/ppermute | solution.py:983
  214.0 42.7 %collective-permute-start.5 = (f32[8,1,768]{2,1,0:T(1,128)S(1)}, f32[8,1,768]{2,1,0:T(1,128)S(1)}, u32[]{:S(2)}, u32[]{:S(2)}) collective-permute-start(f32[8,1,768]{2,1,0:T(1,128)S(1)} %bitcast.144), channel_id=1, source_target_pairs={{0,2},{1,3},{2,0},{3,1},{4,6},{5,7},{6,4},{7,5},{8,10},{9,11},{10,... | collective-permute-start | bytes 73736 | tf_op jit(solution)/shard_map/ppermute | solution.py:983
  214.8 41.9 %collective-permute-start.6 = (f32[8,1,768]{2,1,0:T(1,128)S(1)}, f32[8,1,768]{2,1,0:T(1,128)S(1)}, u32[]{:S(2)}, u32[]{:S(2)}) collective-permute-start(f32[8,1,768]{2,1,0:T(1,128)S(1)} %bitcast.145), channel_id=1, source_target_pairs={{0,3},{1,0},{2,1},{3,2},{4,7},{5,4},{6,5},{7,6},{8,11},{9,8},{10,9... | collective-permute-start | bytes 73736 | tf_op jit(solution)/shard_map/ppermute | solution.py:983
  256.7 41.6 %collective-permute-start.7 = (bf16[768,1024]{1,0:T(8,128)(2,1)S(1)}, bf16[768,1024]{1,0:T(8,128)(2,1)S(1)}, u32[]{:S(2)}, u32[]{:S(2)}) collective-permute-start(bf16[768,1024]{1,0:T(8,128)(2,1)S(1)} %collective-permute-done.3.a2_ref), channel_id=1, source_target_pairs={{0,3},{1,0},{2,1},{3,2},{4,7},{5,4},{6,5},{7,6},{8,11},{9,8},{10,9... | collective-permute-start | bytes 4718600 | tf_op jit(solution)/shard_map/ppermute | solution.py:983
  298.4 43.1 %collective-permute-start.8 = (bf16[768,1024]{1,0:T(8,128)(2,1)S(1)}, bf16[768,1024]{1,0:T(8,128)(2,1)S(1)}, u32[]{:S(2)}, u32[]{:S(2)}) collective-permute-start(bf16[768,1024]{1,0:T(8,128)(2,1)S(1)} %collective-permute-done.7.a2_ref), channel_id=1, source_target_pairs={{0,3},{1,0},{2,1},{3,2},{4,7},{5,4},{6,5},{7,6},{8,11},{9,8},{10,9... | collective-permute-start | bytes 4718600 | tf_op jit(solution)/shard_map/ppermute | solution.py:983
  341.5 44.7 %collective-permute-start.9 = (bf16[768,1024]{1,0:T(8,128)(2,1)}, bf16[768,1024]{1,0:T(8,128)(2,1)S(1)}, u32[]{:S(2)}, u32[]{:S(2)}) collective-permute-start(bf16[768,1024]{1,0:T(8,128)(2,1)} %get-tuple-element.248), channel_id=1, source_target_pairs={{0,3},{1,0},{2,1},{3,2},{4,7},{5,4},{6,5},{7,6},{8,11},{9,8},{10,9... | collective-permute-start | bytes 4718600 | tf_op jit(solution)/shard_map/ppermute | solution.py:983
  388.1 52.0 %collective-permute-start.10 = (bf16[768,1024]{1,0:T(8,128)(2,1)}, bf16[768,1024]{1,0:T(8,128)(2,1)S(1)}, u32[]{:S(2)}, u32[]{:S(2)}) collective-permute-start(bf16[768,1024]{1,0:T(8,128)(2,1)} %add_convert_fusion.4), channel_id=1, source_target_pairs={{0,3},{1,0},{2,1},{3,2},{4,7},{5,4},{6,5},{7,6},{8,11},{9,8},{10,9... | collective-permute-start | bytes 4718600 | tf_op jit(solution)/shard_map/ppermute | solution.py:983
  391.0 49.0 %collective-permute-start.13 = (f32[8,1,768]{2,1,0:T(1,128)S(1)}, f32[8,1,768]{2,1,0:T(1,128)S(1)}, u32[]{:S(2)}, u32[]{:S(2)}) collective-permute-start(f32[8,1,768]{2,1,0:T(1,128)S(1)} %copy-done.42), channel_id=1, source_target_pairs={{0,1},{1,2},{2,3},{3,0},{4,5},{5,6},{6,7},{7,4},{8,9},{9,10},{10,1... | collective-permute-start | bytes 73736 | tf_op jit(solution)/shard_map/ppermute | solution.py:983
  395.1 45.0 %collective-permute-start.12 = (f32[8,1,768]{2,1,0:T(1,128)S(1)}, f32[8,1,768]{2,1,0:T(1,128)S(1)}, u32[]{:S(2)}, u32[]{:S(2)}) collective-permute-start(f32[8,1,768]{2,1,0:T(1,128)S(1)} %copy-done.43), channel_id=1, source_target_pairs={{0,2},{1,3},{2,0},{3,1},{4,6},{5,7},{6,4},{7,5},{8,10},{9,11},{10,... | collective-permute-start | bytes 73736 | tf_op jit(solution)/shard_map/ppermute | solution.py:983
  396.6 43.4 %collective-permute-start.11 = (f32[8,1,768]{2,1,0:T(1,128)S(1)}, f32[8,1,768]{2,1,0:T(1,128)S(1)}, u32[]{:S(2)}, u32[]{:S(2)}) collective-permute-start(f32[8,1,768]{2,1,0:T(1,128)S(1)} %copy-done.44), channel_id=1, source_target_pairs={{0,3},{1,0},{2,1},{3,2},{4,7},{5,4},{6,5},{7,6},{8,11},{9,8},{10,9... | collective-permute-start | bytes 73736 | tf_op jit(solution)/shard_map/ppermute | solution.py:983
  440.1 304.7 %reduce-scatter.4.cloned.1.call-start = ((), (), s32[]{:S(2)}) async-start(), calls=%async_computation.4 | async-start | bytes 9437184 | tf_op jit(solution)/shard_map/reduce_scatter | solution.py:1237
  440.7 306.9 %reduce-scatter.8.cloned.1.call-start = ((), (), s32[]{:S(2)}) async-start(), calls=%async_computation.6 | async-start | bytes 9437184 | tf_op jit(solution)/shard_map/reduce_scatter | solution.py:1237
  478.1 59.5 %collective-permute-start.15 = (bf16[768,1024]{1,0:T(8,128)(2,1)}, bf16[768,1024]{1,0:T(8,128)(2,1)}, u32[]{:S(2)}, u32[]{:S(2)}) collective-permute-start(bf16[768,1024]{1,0:T(8,128)(2,1)} %get-tuple-element.297), channel_id=1, source_target_pairs={{0,3},{1,0},{2,1},{3,2},{4,7},{5,4},{6,5},{7,6},{8,11},{9,8},{10,9... | collective-permute-start | bytes 4718600 | tf_op jit(solution)/shard_map/ppermute | solution.py:983
  541.3 49.0 %collective-permute-start.16 = (bf16[768,1024]{1,0:T(8,128)(2,1)}, bf16[768,1024]{1,0:T(8,128)(2,1)}, u32[]{:S(2)}, u32[]{:S(2)}) collective-permute-start(bf16[768,1024]{1,0:T(8,128)(2,1)} %add_convert_fusion.2), channel_id=1, source_target_pairs={{0,3},{1,0},{2,1},{3,2},{4,7},{5,4},{6,5},{7,6},{8,11},{9,8},{10,9... | collective-permute-start | bytes 4718600 | tf_op jit(solution)/shard_map/ppermute | solution.py:983
  594.7 83.3 %collective-permute-start.17 = (bf16[768,1024]{1,0:T(8,128)(2,1)}, bf16[768,1024]{1,0:T(8,128)(2,1)}, u32[]{:S(2)}, u32[]{:S(2)}) collective-permute-start(bf16[768,1024]{1,0:T(8,128)(2,1)} %add_convert_fusion.1), channel_id=1, source_target_pairs={{0,3},{1,0},{2,1},{3,2},{4,7},{5,4},{6,5},{7,6},{8,11},{9,8},{10,9... | collective-permute-start | bytes 4718600 | tf_op jit(solution)/shard_map/ppermute | solution.py:983
  (46 other events, 576.0 us)
Sparse Core Ops, SparseCore 0:
  10.0 75.5 all-gather.6
  87.4 62.2 all-gather.8
  151.6 54.3 all-gather.10
  440.2 67.1 reduce-scatter.5
  511.1 71.2 reduce-scatter.3
  585.8 96.0 reduce-scatter.7

commit v9 on v7

--- a/solution.py
+++ b/solution.py
@@ -112,6 +112,44 @@
     )(places, x, cosine, sine, *pieces)
 
 
+def middle_kernel(
+    a_ref, b_ref, x_ref, out_ref, rest_ref, gains_ref, mask_ref, middle_ref, normed_ref, inv_ref, gates_ref
+):
+    half = a_ref.shape[1]
+    branch = dot_nt(a_ref[...], out_ref[:, :half]) + dot_nt(b_ref[...], out_ref[:, half:])
+    middle = x_ref[...].astype(f32) + resid_scale * branch
+    middle_ref[...] = middle
+    inverse = lax.rsqrt(jnp.mean(middle * middle, -1, keepdims=True) + norm_eps)
+    inv_ref[...] = inverse
+    normed = (middle * inverse * gains_ref[1:2]).astype(bf16)
+    normed_ref[...] = normed
+    mask = mask_ref[...] > 0.0
+    logits = jnp.where(mask, dot(normed, rest_ref[...]), masked_score)
+    top = jnp.max(logits, -1, keepdims=True)
+    raised = jnp.where(mask, jnp.exp(logits - top), 0.0)
+    gates_ref[...] = (raised / jnp.sum(raised, -1, keepdims=True)).T[:EXPERTS]
+
+
+def to_gates(halves, x, output_t, rest, gain_rows, mask):
+    tok = x.shape[0]
+    shape = jax.ShapeDtypeStruct
+    whole = pl.BlockSpec(memory_space=pltpu.VMEM)
+    return pl.pallas_call(
+        middle_kernel,
+        in_specs=[whole] * 7,
+        out_specs=[whole] * 4,
+        out_shape=[
+            shape((tok, MODEL_WIDTH), f32),
+            shape((tok, MODEL_WIDTH), bf16),
+            shape((tok, 1), f32),
+            shape((EXPERTS, tok), f32),
+        ],
+        compiler_params=pltpu.CompilerParams(vmem_limit_bytes=VMEM_LIMIT),
+        cost_estimate=SMALL,
+        name="to_gates",
+    )(*halves, x, output_t, rest, gain_rows, mask)
+
+
 def outer_kernel(mine, *refs, count):
     out_ref = refs[-1]
     pairs = [(refs[n], refs[n + 1]) for n in range(0, len(refs) - 1, 2)]
@@ -120,17 +158,19 @@
         columns = b_ref.shape[1]
         out_ref[:, at : at + columns] = dot_tn(a_ref[...], b_ref[...]).astype(bf16)
         at += columns
-    out_ref[:, at:] = sum(dot_tn(a[...], b[...]) for a, b in pairs[count:]).astype(bf16)
-
-
-def outer(pairs, extra):
+    if pairs[count:]:
+        out_ref[:, at:] = sum(dot_tn(a[...], b[...]) for a, b in pairs[count:]).astype(bf16)
+
+
+def outer(pairs, extra=()):
     tok = pairs[0][0].shape[0]
     mine = lax.axis_index("ctx").astype(jnp.int32).reshape(1)
     specs = []
-    for _, b in pairs + extra:
+    everything = [*pairs, *extra]
+    for _, b in everything:
         specs.append(pl.BlockSpec((tok, 128), lambda m, mine: (0, m ^ mine[0])))
         specs.append(pl.BlockSpec(b.shape, lambda m, mine: (0, 0)))
-    columns = sum(b.shape[1] for _, b in pairs) + extra[0][1].shape[1]
+    columns = sum(b.shape[1] for _, b in [*pairs, *extra[:1]])
     return pl.pallas_call(
         functools.partial(outer_kernel, count=len(pairs)),
         grid_spec=pltpu.PrefetchScalarGridSpec(
@@ -143,7 +183,7 @@
         compiler_params=pltpu.CompilerParams(vmem_limit_bytes=VMEM_LIMIT),
         cost_estimate=SMALL,
         name="outer",
-    )(mine, *[x for pair in pairs + extra for x in pair])
+    )(mine, *[x for pair in everything for x in pair])
 
 
 def gather_keys(pieces, scratch, places, block_rows):
@@ -368,6 +408,7 @@
     own = kv_own.shape[0]
     spec = pl.BlockSpec
     wide = spec((tok, 256), lambda g, *_: (0, 2 * half + g))
+    narrow = spec((tok, 256), lambda g, *_: (0, g))
     ours = spec((own, 128), lambda g, *_: (0, g))
     table = spec((tok, 128), lambda g, *_: (0, 0))
     return pl.pallas_call(
@@ -377,7 +418,7 @@
         grid_spec=pltpu.PrefetchScalarGridSpec(
             num_scalar_prefetch=2,
             grid=(2,),
-            in_specs=[wide, wide, spec((1, 4, tok), lambda g, *_: (g, 0, 0)), wide, table, table]
+            in_specs=[wide, wide, spec((1, 4, tok), lambda g, *_: (g, 0, 0)), narrow, table, table]
             + key_specs(pieces, own, half),
             out_specs=[
                 spec((tok, 256), lambda g, *_: (0, g)),
@@ -856,8 +897,10 @@
     )(*arrays)
 
 
-def full_sum_kernel(x_ref, out_ref, sib, low, recv, total, total_low, arrived, send, recv_sem):
-    rows = out_ref.shape[0]
+def full_sum_kernel(x_ref, *refs, widths):
+    out_refs, refs = refs[: len(widths)], refs[len(widths) :]
+    sib, low, recv, total, total_low, arrived, result_ref, send, recv_sem = refs
+    rows = result_ref.shape[0]
     greet(
         [{"ctx": partner(m)} for m in (1, 2, 4)] + [{"wt": ahead(d)} for d in (1, 2, 3)]
     )
@@ -886,7 +929,7 @@
         for d in (1, 3, 2):
             copies.arrived(("wt", n, d))
             result = result + arrived[(d - 1) * rows : d * rows, parts[n]].astype(f32)
-        out_ref[:, parts[n]] = result
+        result_ref[:, parts[n]] = result
 
     for one in steps:
         one[0]()
@@ -901,17 +944,21 @@
             leave(n - 2)
     for n in range(PARTS):
         finish(n)
+    at = 0
+    for out_ref, width in zip(out_refs, widths):
+        out_ref[...] = result_ref[:, at : at + width]
+        at += width
     copies.close()
 
 
-def full_sum(x):
+def full_sum(x, widths):
     rows, columns = x.shape[0] // 32, x.shape[1]
     vmem = pl.BlockSpec(memory_space=pltpu.VMEM)
     return pl.pallas_call(
-        full_sum_kernel,
+        functools.partial(full_sum_kernel, widths=widths),
         in_specs=[vmem],
-        out_specs=vmem,
-        out_shape=jax.ShapeDtypeStruct((rows, columns), f32),
+        out_specs=[vmem] * len(widths),
+        out_shape=[jax.ShapeDtypeStruct((rows, width), f32) for width in widths],
         scratch_shapes=[
             pltpu.VMEM((16 * rows, columns), bf16),
             pltpu.VMEM((12 * rows, columns), bf16),
@@ -919,6 +966,7 @@
             pltpu.VMEM((4 * rows, columns), f32),
             pltpu.VMEM((4 * rows, columns), bf16),
             pltpu.VMEM((3 * rows, columns), bf16),
+            pltpu.VMEM((rows, columns), f32),
             pltpu.SemaphoreType.DMA((13 * PARTS,)),
             pltpu.SemaphoreType.DMA((13 * PARTS,)),
         ],
@@ -951,13 +999,15 @@
     return [packed_gather(x)], [32], places.reshape(-1).astype(jnp.int32)
 
 
-def outer_sum(pairs, extra):
+def outer_sum(pairs, extra, widths):
     if lax.axis_size("ctx") != 8 or lax.axis_size("wt") != 4:
         parts = [dot_tn(a, b) for a, b in pairs] + [sum(dot_tn(a, b) for a, b in extra)]
-        return lax.psum_scatter(
+        result = lax.psum_scatter(
             jnp.concatenate(parts, 1).astype(bf16), ALL, scatter_dimension=0, tiled=True
         ).astype(f32)
-    return full_sum(outer(pairs, extra))
+        edges = [sum(widths[: n + 1]) for n in range(len(widths) - 1)]
+        return jnp.split(result, edges, 1)
+    return full_sum(outer(pairs, extra), widths)
 
 
 def after(x, *others):
@@ -1105,19 +1155,19 @@
         heads.append(result)
     for d in range(last - 3, 0, -1):
         grads_in[d] = shift(grads_in[d + 1], -1)
-    attended = jnp.concatenate([out for out, _ in heads], 1)
+    attended = [out for out, _ in heads]
     lse = [row for _, row in heads]
 
-    branch = dot_nt(attended, output_t)
-    middle = inputs + resid_scale * branch
-    normed_mid, inverse_two = norm_forward(middle, second_gain)
-    normed_two = normed_mid.astype(bf16)
-    logits = dot(normed_two, router_full)
-    top = jnp.max(jnp.where(mask, logits, masked_score), -1, keepdims=True)
-    raised = jnp.where(mask, jnp.exp(jnp.where(mask, logits - top, 0.0)), 0.0)
-    gates = raised / jnp.sum(raised, -1, keepdims=True)
-
-    gates_out = gates.T.reshape(shard_count, expert_count, 1, tok)
+    middle, normed_two, inverse_two, gates = to_gates(
+        attended,
+        layer_input[0],
+        output_t,
+        rest,
+        gain_rows,
+        jnp.pad(mask.astype(f32), ((0, 0), (0, 128 - EXPERTS))),
+    )
+
+    gates_out = gates.reshape(shard_count, expert_count, 1, tok)
     gates_in = []
     for d in range(shard_count):
         piece = lax.dynamic_index_in_dim(gates_out, (wt_index + d) % shard_count, 0, False)
@@ -1158,8 +1208,9 @@
     for bit in (1, 2, 4):
         if bit < shard_count:
             stacked = jnp.where(wt_index & bit > 0, jnp.roll(stacked, bit, 0), stacked)
-    stacked = stacked.reshape(EXPERTS, tok).T
-    grad_logits = (gates * (stacked - jnp.sum(gates * stacked, -1, keepdims=True))).astype(bf16)
+    stacked = stacked.reshape(EXPERTS, tok)
+    grad_logits = gates * (stacked - jnp.sum(gates * stacked, 0, keepdims=True))
+    grad_logits = grad_logits.T.astype(bf16)
     carried = shift(add(carried, partial[1]), -1)
     down_grad, home = beside(
         down_weight_grads([(after(r[2], gate_grad, grad_logits), r[1]) for r in rows], context_size), carried
@@ -1185,7 +1236,7 @@
             query,
             grad_attended,
             lse[half],
-            attended,
+            attended[half],
             cosine,
             sine,
             kv_pieces,
@@ -1229,24 +1280,25 @@
     input_grad = (grad_middle + grad_input_norm).astype(bf16)
 
     column = lax.broadcasted_iota(jnp.int32, (tok, 128), 1)
-    shares = outer_sum(
-        [(normed_one, d_query), (grad_branch, attended), (normed_one, grad_kv)],
+    query_share, output_share, key_share, value_share, small = outer_sum(
+        [(normed_one, d_query), (grad_branch, attended[0]), (grad_branch, attended[1]), (normed_one, grad_kv)],
         [
             (normed_two, jnp.pad(grad_logits, ((0, 0), (0, 128 - EXPERTS)))),
             (second_gain_grad, (column == EXPERTS).astype(bf16)),
             (first_gain_grad, (column == EXPERTS + 1).astype(bf16)),
         ],
+        (1024, 1024, KV_WIDTH, KV_WIDTH, 128),
     )
     return (
         layer_output[None],
         input_grad[None],
-        shares[:, 3073 + EXPERTS],
-        shares[:, :1024],
-        shares[:, 2048 : 2048 + KV_WIDTH],
-        shares[:, 2048 + KV_WIDTH : 3072],
-        shares[:, 1024:2048].T,
-        shares[:, 3072 + EXPERTS],
-        shares[:, 3072 : 3072 + EXPERTS],
+        small[:, EXPERTS + 1],
+        query_share,
+        key_share,
+        value_share,
+        output_share.T,
+        small[:, EXPERTS],
+        small[:, :EXPERTS],
         gate_share,
         up_share,
         down_share,

time: 760 us -> 739 us (0.972)
  other arithmetic: 50.5 us -> 37.5 us
  local copies, waits for them, and re-layouts: 39.9 us -> 31.3 us
  waiting for transfers between devices: 12.7 us -> 20.3 us
    pallas_call x4, Pallas kernels: 171 us -> 158 us  [expert_pass(): pl.pallas_call(functools.partial(expert_kernel, sizes=sizes), grid_spec=p...]
    pallas_call x1 -> x2, Pallas kernels: 45.8 us -> 54.9 us  [the longest x1 46.9 us: full_sum(): pl.pallas_call(functools.partial(full_sum_kernel, widths=widths), in_spec...]
  transfers between devices with their start and end apart: 25 -> 25, of which waited for: 2 -> 3; matrix products, arithmetic and copies ran while one was open for 13% -> 9% of each run, Pallas kernels for 77% -> 78%
where the time goes in v9:
time: 739 us; the launch traced here: 731 us
  Pallas kernels  572 us (77%)
  starting transfers between devices  41.5 us (6%)
  other arithmetic  37.5 us (5%)
  local copies, waits for them, and re-layouts  31.3 us (4%)
  waiting for transfers between devices  20.3 us (3%)
  between operations  17.8 us (2%)
  matrix products  11 us (1%)
    pallas_call x4, Pallas kernels, expert_pass(): pl.pallas_call(functools.partial(expert_kernel, sizes=sizes), grid_spec=p...  158 us
    pallas_call x2, Pallas kernels, attention_backward(): pl.pallas_call(functools.partial(attention_backward_kernel, block_rows=bl...  97.4 us
    pallas_call x2, Pallas kernels, attention_forward(): pl.pallas_call(functools.partial(attention_forward_kernel, block_rows=blo...  53.2 us
    pallas_call x1, Pallas kernels, packed_gather(): pl.pallas_call(packed_gather_kernel, in_specs=[ANY], out_specs=ANY, out_s...  53.1 us
    pallas_call x1, Pallas kernels, full_sum(): pl.pallas_call(functools.partial(full_sum_kernel, widths=widths), in_spec...  46.9 us
    pallas_call x1, Pallas kernels, up_weight_grads(): pl.pallas_call(functools.partial(up_grad_kernel, sources=len(rows)), grid...  40.6 us
    ppermute x18, starting transfers between devices, shift(): return lax.ppermute(x, 'wt', [(i, (i + distance) % n) for i in range(n)])  34.9 us
    pallas_call x1, Pallas kernels, plane_gather(): pl.pallas_call(plane_gather_kernel, in_specs=[ANY], out_specs=ANY, out_sh...  33.3 us
  transfers between devices with their start and end apart: 25, of which 3 were waited for; matrix products, arithmetic and copies ran while one was open for 9% of the time, Pallas kernels for 78%

profile of v9, /device:TPU:0, one launch (start us, length us, event | category | flops | bytes accessed | tf_op | source)
XLA Modules:
  0.0 731.1 jit_solution(13540458008965832022)
XLA Ops:
  10.6 6.3 all-to-all-start
  17.9 53.1 %packed_gather.1.refs_0_ = bf16[1024,3200]{1,0:T(8,128)(2,1)} custom-call(bf16[32,3200]{1,0:T(8,128)(2,1)} %concatenate.76.x_ref), custom_call_target="tpu_custom_call" | custom-call | flops 1000000000 | bytes 1000000 | tf_op jit(solution)/shard_map/packed_gather/pallas_call | solution.py:785
  80.4 9.0 %project.1 = (bf16[768,1024]{1,0:T(8,128)(2,1)}, bf16[768,1024]{1,0:T(8,128)(2,1)}, bf16[768,1024]{1,0:T(8,128)(2,1)}, bf16[1024,2048]{1,0:T(8,128)(2,1)}, bf16[...) custom-call(s32[32]{0:T(128)} %add.207.places, bf16[768,1024]{1,0:T(8,128)(2,1)} %bitcast.118, ...), custom_call_target="tpu_custom_call" | custom-call | flops 1000000000 | bytes 1000000 | tf_op jit(solution)/shard_map/project/pallas_call | solution.py:96
  89.4 33.3 %plane_gather.1.refs_0_.refs_1_ = bf16[2048,1024]{1,0:T(8,128)(2,1)} custom-call(bf16[768,1024]{1,0:T(8,128)(2,1)} %get-tuple-element.175.x_ref), custom_call_target="tpu_custom_call" | custom-call | flops 1000000000 | bytes 1000000 | tf_op jit(solution)/shard_map/plane_gather/pallas_call | solution.py:730
  129.4 26.5 %attention_forward.2 = (bf16[768,512]{1,0:T(8,128)(2,1)}, f32[2,4,768]{2,1,0:T(4,128)}) custom-call(s32[16]{0:T(128)} %reshape.347.places, s32[4]{0:T(128)} %get-tuple-element.377.starts, bf16[768,1024]{1,0:T(8,128)(2,1)} %get-tuple-element.303.q_ref, bf16[2048,1024]{1,0:T(8,128)(2,1)} %plane_gather.1.refs_0_.refs_1_, ...), custom_call_target="tpu_custom_call" | custom-call | flops 1000000000 | bytes 1000000 | tf_op jit(solution)/shard_map/attention_forward/pallas_call | solution.py:269
  155.9 5.0 collective-permute-done.1.df_ref
  160.9 4.7 collective-permute-start.2
  166.6 26.6 %attention_forward.3 = (bf16[768,512]{1,0:T(8,128)(2,1)}, f32[2,4,768]{2,1,0:T(4,128)}) custom-call(s32[16]{0:T(128)} %reshape.347.places, s32[4]{0:T(128)} %get-tuple-element.377.starts, bf16[768,1024]{1,0:T(8,128)(2,1)} %get-tuple-element.303.q_ref, bf16[2048,1024]{1,0:T(8,128)(2,1)} %plane_gather.1.refs_0_.refs_1_, ...), custom_call_target="tpu_custom_call" | custom-call | flops 1000000000 | bytes 1000000 | tf_op jit(solution)/shard_map/attention_forward/pallas_call | solution.py:269
  193.3 5.7 collective-permute-done.2.df_ref
  199.0 8.0 %to_gates.1 = (f32[768,1024]{1,0:T(8,128)}, bf16[768,1024]{1,0:T(8,128)(2,1)}, f32[768,1]{1,0:T(8,128)}, f32[32,768]{1,0:T(8,128)}) custom-call(bf16[768,512]{1,0:T(8,128)(2,1)} %get-tuple-element.181.a_ref.o_ref.refs_3_, bf16[768,512]{1,0:T(8,128)(2,1)} %get-tuple-element.186.b_ref.o_ref.refs_5_, bf16[768,1024]{1,0:T(8,128)(2,1)} %bitcast.119, ...), custom_call_target="tpu_custom_call" | custom-call | flops 1000000000 | bytes 1000000 | tf_op jit(solution)/shard_map/to_gates/pallas_call | solution.py:137
  218.2 38.8 %expert_pass.4 = (bf16[768,1024]{1,0:T(8,128)(2,1)}, bf16[768,1024]{1,0:T(8,128)(2,1)}, f32[8,1,768]{2,1,0:T(1,128)}, bf16[8,336,1024]{2,1,0:T(8,128)(2,1)}, bf1...) custom-call(s32[8]{0:T(128)} %get-tuple-element.381.counts, ...), custom_call_target="tpu_custom_call" | custom-call | flops 1000000000 | bytes 1000000 | tf_op jit(solution)/shard_map/expert_pass/pallas_call | solution.py:540
  258.4 38.5 %expert_pass.5 = (bf16[768,1024]{1,0:T(8,128)(2,1)}, bf16[768,1024]{1,0:T(8,128)(2,1)}, f32[8,1,768]{2,1,0:T(1,128)}, bf16[8,336,1024]{2,1,0:T(8,128)(2,1)}, bf1...) custom-call(s32[8]{0:T(128)} %get-tuple-element.378.counts, ...), custom_call_target="tpu_custom_call" | custom-call | flops 1000000000 | bytes 1000000 | tf_op jit(solution)/shard_map/expert_pass/pallas_call | solution.py:540
  297.0 6.3 collective-permute-start.8
  304.0 40.7 %expert_pass.6 = (bf16[768,1024]{1,0:T(8,128)(2,1)}, bf16[768,1024]{1,0:T(8,128)(2,1)}, f32[8,1,768]{2,1,0:T(1,128)}, bf16[8,336,1024]{2,1,0:T(8,128)(2,1)}, bf1...) custom-call(s32[8]{0:T(128)} %get-tuple-element.379.counts, ...), custom_call_target="tpu_custom_call" | custom-call | flops 1000000000 | bytes 1000000 | tf_op jit(solution)/shard_map/expert_pass/pallas_call | solution.py:540
  346.5 40.1 %expert_pass.7 = (bf16[768,1024]{1,0:T(8,128)(2,1)}, bf16[768,1024]{1,0:T(8,128)(2,1)}, f32[8,1,768]{2,1,0:T(1,128)}, bf16[8,336,1024]{2,1,0:T(8,128)(2,1)}, bf1...) custom-call(s32[8]{0:T(128)} %get-tuple-element.380.counts, ...), custom_call_target="tpu_custom_call" | custom-call | flops 1000000000 | bytes 1000000 | tf_op jit(solution)/shard_map/expert_pass/pallas_call | solution.py:540
  396.3 40.6 %up_weight_grads.1 = (bf16[8,8,128,512]{3,2,1,0:T(8,128)(2,1)}, bf16[8,8,128,512]{3,2,1,0:T(8,128)(2,1)}) custom-call(bf16[8,336,1024]{2,1,0:T(8,128)(2,1)} %get-tuple-element.253.refs_0_, bf16[8,336,512]{2,1,0:T(8,128)(2,1)} %get-tuple-element.254.refs_1_, bf16[8,336,512]{2,1,0:T(8,128)(2,1)} %get-tuple-element.255.refs_2_, ...), custom_call_target="tpu_custom_call" | custom-call | flops 1000000000 | bytes 1000000 | tf_op jit(solution)/shard_map/up_weight_grads/pallas_call | solution.py:599
  441.7 24.0 %down_weight_grads.1 = bf16[8,8,512,128]{3,2,1,0:T(8,128)(2,1)} custom-call(bf16[8,336,512]{2,1,0:T(8,128)(2,1)} %get-tuple-element.280.refs_0_, bf16[8,336,1024]{2,1,0:T(8,128)(2,1)} %get-tuple-element.281.refs_1_, bf16[8,336,512]{2,1,0:T(8,128)(2,1)} %get-tuple-element.283.refs_2_, bf16[8,336,1024]{2,1,0:T(8,128)(2,1)} %get-tuple-element.284.refs_3_, ...), custom_call_target="tpu_custom_call" | custom-call | flops 1000000000 | bytes 1000000 | tf_op jit(solution)/shard_map/down_weight_grads/pallas_call | solution.py:614
  465.7 6.9 collective-permute-done.14
  485.1 48.6 %attention_backward.2 = (bf16[768,512]{1,0:T(8,128)(2,1)}, bf16[2048,512]{1,0:T(8,128)(2,1)}, f32[512,256]{1,0:T(8,128)}, f32[512,256]{1,0:T(8,128)}) custom-call(s32[16]{0:T(128)} %reshape.347.places, s32[4]{0:T(128)} %get-tuple-element.377.starts, bf16[768,1024]{1,0:T(8,128)(2,1)} %get-tuple-element.303.q_ref, ...), custom_call_target="tpu_custom_call" | custom-call | flops 1000000000 | bytes 1000000 | tf_op jit(solution)/shard_map/attention_backward/pallas_call | solution.py:414
  538.3 48.8 %attention_backward.3 = (bf16[768,512]{1,0:T(8,128)(2,1)}, bf16[2048,512]{1,0:T(8,128)(2,1)}, f32[512,256]{1,0:T(8,128)}, f32[512,256]{1,0:T(8,128)}) custom-call(s32[16]{0:T(128)} %reshape.347.places, s32[4]{0:T(128)} %get-tuple-element.377.starts, bf16[768,1024]{1,0:T(8,128)(2,1)} %get-tuple-element.303.q_ref, ...), custom_call_target="tpu_custom_call" | custom-call | flops 1000000000 | bytes 1000000 | tf_op jit(solution)/shard_map/attention_backward/pallas_call | solution.py:414
  593.5 33.2 %plane_sum.1 = (f32[256,512]{1,0:T(8,128)}, f32[256,512]{1,0:T(8,128)}) custom-call(bf16[2048,512]{1,0:T(8,128)(2,1)} %get-tuple-element.301.refs_0_, bf16[2048,512]{1,0:T(8,128)(2,1)} %get-tuple-element.312.refs_1_), custom_call_target="tpu_custom_call" | custom-call | flops 1000000000 | bytes 1000000 | tf_op jit(solution)/shard_map/plane_sum/pallas_call | solution.py:884
  641.1 6.4 multiply_convert_fusion
  648.9 15.0 %outer.1.x_ref = bf16[1024,3200]{1,0:T(8,128)(2,1)} custom-call(s32[1]{0:T(128)} %bitcast.34.mine, bf16[768,1024]{1,0:T(8,128)(2,1)} %get-tuple-element.326.refs_0_.refs_6_, bf16[768,1024]{1,0:T(8,128)(2,1)} %constant_dynamic-update-slice_fusion.refs_1_, bf16[768,1024]{1,0:T(8,128)(2,1)} %copy-done.3, ...), custom_call_target="tpu_custom_call" | custom-call | flops 1000000000 | bytes 1000000 | tf_op jit(solution)/shard_map/outer/pallas_call | solution.py:174
  663.9 46.9 %full_sum.1 = (f32[32,1024]{1,0:T(8,128)}, f32[32,1024]{1,0:T(8,128)}, f32[32,512]{1,0:T(8,128)}, f32[32,512]{1,0:T(8,128)}, f32[32,128]{1,0:T(8,128)}) custom-call(bf16[1024,3200]{1,0:T(8,128)(2,1)} %outer.1.x_ref), custom_call_target="tpu_custom_call" | custom-call | flops 1000000000 | bytes 1000000 | tf_op jit(solution)/shard_map/full_sum/pallas_call | solution.py:957
  (244 shorter events, 100.1 us)
Async XLA Ops:
  7.3 210.9 %all-gather.7.cloned.1.call-start = ((), (), s32[]{:S(2)}) async-start(), calls=%async_computation.7 | async-start | bytes 9437184 | tf_op jit(solution)/shard_map/all_gather | solution.py:1094
  8.0 210.2 %all-gather.9.cloned.1.call-start = ((), (), s32[]{:S(2)}) async-start(), calls=%async_computation.8 | async-start | bytes 9437184 | tf_op jit(solution)/shard_map/all_gather | solution.py:1095
  8.7 209.4 %all-gather.11.cloned.1.call-start = ((), (), s32[]{:S(2)}) async-start(), calls=%async_computation.9 | async-start | bytes 9437184 | tf_op jit(solution)/shard_map/all_gather | solution.py:1096
  10.6 60.4 %all-to-all-start = ((f32[4,8,1,768]{3,1,2,0:T(8,128)}), f32[4,8,1,768]{3,1,2,0:T(8,128)S(1)}, u32[]{:S(2)}, u32[]{:S(2)}) async-start(f32[4,8,1,768]{3,1,2,0:T(8,128)} %fusion.28), calls=%async_computation | async-start | bytes 196608 | tf_op jit(solution)/shard_map/all_to_all | solution.py:1104
  16.9 695.4 %reduce-scatter.6.cloned.1.call-start = ((), (), s32[]{:S(2)}) async-start(), calls=%async_computation.5 | async-start | bytes 9437184 | tf_op jit(solution)/shard_map/reduce_scatter | solution.py:1228
  71.0 51.6 %collective-permute-start = (bf16[768,1024]{1,0:T(8,128)(2,1)S(1)}, bf16[768,1024]{1,0:T(8,128)(2,1)}, u32[]{:S(2)}, u32[]{:S(2)}) collective-permute-start(bf16[768,1024]{1,0:T(8,128)(2,1)S(1)} %bitcast.121), channel_id=1, source_target_pairs={{0,3},{1,0},{2,1},{3,2},{4,7},{5,4},{6,5},{7,6},{8,11},{9,8},{10,9... | collective-permute-start | bytes 4718600 | tf_op jit(solution)/shard_map/ppermute | solution.py:983
  122.7 38.2 %collective-permute-start.1 = (bf16[768,1024]{1,0:T(8,128)(2,1)}, bf16[768,1024]{1,0:T(8,128)(2,1)S(1)}, u32[]{:S(2)}, u32[]{:S(2)}) collective-permute-start(bf16[768,1024]{1,0:T(8,128)(2,1)} %collective-permute-done.df_ref), channel_id=1, source_target_pairs={{0,3},{1,0},{2,1},{3,2},{4,7},{5,4},{6,5},{7,6},{8,11},{9,8},{10,9... | collective-permute-start | bytes 4718600 | tf_op jit(solution)/shard_map/ppermute | solution.py:983
  160.9 38.1 %collective-permute-start.2 = (bf16[768,1024]{1,0:T(8,128)(2,1)S(1)}, bf16[768,1024]{1,0:T(8,128)(2,1)S(1)}, u32[]{:S(2)}, u32[]{:S(2)}) collective-permute-start(bf16[768,1024]{1,0:T(8,128)(2,1)S(1)} %collective-permute-done.1.df_ref), channel_id=1, source_target_pairs={{0,3},{1,0},{2,1},{3,2},{4,7},{5,4},{6,5},{7,6},{8,11},{9,8},{10,9... | collective-permute-start | bytes 4718600 | tf_op jit(solution)/shard_map/ppermute | solution.py:983
  207.0 50.0 %collective-permute-start.3 = (bf16[768,1024]{1,0:T(8,128)(2,1)}, bf16[768,1024]{1,0:T(8,128)(2,1)S(1)}, u32[]{:S(2)}, u32[]{:S(2)}) collective-permute-start(bf16[768,1024]{1,0:T(8,128)(2,1)} %get-tuple-element.192.a2_ref.refs_8_), channel_id=1, source_target_pairs={{0,3},{1,0},{2,1},{3,2},{4,7},{5,4},{6,5},{7,6},{8,11},{9,8},{10,9... | collective-permute-start | bytes 4718600 | tf_op jit(solution)/shard_map/ppermute | solution.py:983
  214.1 42.9 %collective-permute-start.4 = (f32[8,1,768]{2,1,0:T(1,128)S(1)}, f32[8,1,768]{2,1,0:T(1,128)S(1)}, u32[]{:S(2)}, u32[]{:S(2)}) collective-permute-start(f32[8,1,768]{2,1,0:T(1,128)S(1)} %bitcast.145), channel_id=1, source_target_pairs={{0,1},{1,2},{2,3},{3,0},{4,5},{5,6},{6,7},{7,4},{8,9},{9,10},{10,1... | collective-permute-start | bytes 73736 | tf_op jit(solution)/shard_map/ppermute | solution.py:983
  214.2 42.8 %collective-permute-start.5 = (f32[8,1,768]{2,1,0:T(1,128)S(1)}, f32[8,1,768]{2,1,0:T(1,128)S(1)}, u32[]{:S(2)}, u32[]{:S(2)}) collective-permute-start(f32[8,1,768]{2,1,0:T(1,128)S(1)} %bitcast.146), channel_id=1, source_target_pairs={{0,2},{1,3},{2,0},{3,1},{4,6},{5,7},{6,4},{7,5},{8,10},{9,11},{10,... | collective-permute-start | bytes 73736 | tf_op jit(solution)/shard_map/ppermute | solution.py:983
  215.0 42.1 %collective-permute-start.6 = (f32[8,1,768]{2,1,0:T(1,128)S(1)}, f32[8,1,768]{2,1,0:T(1,128)S(1)}, u32[]{:S(2)}, u32[]{:S(2)}) collective-permute-start(f32[8,1,768]{2,1,0:T(1,128)S(1)} %bitcast.147), channel_id=1, source_target_pairs={{0,3},{1,0},{2,1},{3,2},{4,7},{5,4},{6,5},{7,6},{8,11},{9,8},{10,9... | collective-permute-start | bytes 73736 | tf_op jit(solution)/shard_map/ppermute | solution.py:983
  257.1 39.9 %collective-permute-start.7 = (bf16[768,1024]{1,0:T(8,128)(2,1)S(1)}, bf16[768,1024]{1,0:T(8,128)(2,1)S(1)}, u32[]{:S(2)}, u32[]{:S(2)}) collective-permute-start(bf16[768,1024]{1,0:T(8,128)(2,1)S(1)} %collective-permute-done.3.a2_ref), channel_id=1, source_target_pairs={{0,3},{1,0},{2,1},{3,2},{4,7},{5,4},{6,5},{7,6},{8,11},{9,8},{10,9... | collective-permute-start | bytes 4718600 | tf_op jit(solution)/shard_map/ppermute | solution.py:983
  297.0 47.7 %collective-permute-start.8 = (bf16[768,1024]{1,0:T(8,128)(2,1)S(1)}, bf16[768,1024]{1,0:T(8,128)(2,1)S(1)}, u32[]{:S(2)}, u32[]{:S(2)}) collective-permute-start(bf16[768,1024]{1,0:T(8,128)(2,1)S(1)} %collective-permute-done.7.a2_ref), channel_id=1, source_target_pairs={{0,3},{1,0},{2,1},{3,2},{4,7},{5,4},{6,5},{7,6},{8,11},{9,8},{10,9... | collective-permute-start | bytes 4718600 | tf_op jit(solution)/shard_map/ppermute | solution.py:983
  345.9 40.7 %collective-permute-start.9 = (bf16[768,1024]{1,0:T(8,128)(2,1)}, bf16[768,1024]{1,0:T(8,128)(2,1)S(1)}, u32[]{:S(2)}, u32[]{:S(2)}) collective-permute-start(bf16[768,1024]{1,0:T(8,128)(2,1)} %get-tuple-element.251), channel_id=1, source_target_pairs={{0,3},{1,0},{2,1},{3,2},{4,7},{5,4},{6,5},{7,6},{8,11},{9,8},{10,9... | collective-permute-start | bytes 4718600 | tf_op jit(solution)/shard_map/ppermute | solution.py:983
  388.4 48.5 %collective-permute-start.10 = (bf16[768,1024]{1,0:T(8,128)(2,1)}, bf16[768,1024]{1,0:T(8,128)(2,1)S(1)}, u32[]{:S(2)}, u32[]{:S(2)}) collective-permute-start(bf16[768,1024]{1,0:T(8,128)(2,1)} %add_convert_fusion.4), channel_id=1, source_target_pairs={{0,3},{1,0},{2,1},{3,2},{4,7},{5,4},{6,5},{7,6},{8,11},{9,8},{10,9... | collective-permute-start | bytes 4718600 | tf_op jit(solution)/shard_map/ppermute | solution.py:983
  390.0 46.9 %collective-permute-start.13 = (f32[8,1,768]{2,1,0:T(1,128)S(1)}, f32[8,1,768]{2,1,0:T(1,128)S(1)}, u32[]{:S(2)}, u32[]{:S(2)}) collective-permute-start(f32[8,1,768]{2,1,0:T(1,128)S(1)} %copy-done.47), channel_id=1, source_target_pairs={{0,1},{1,2},{2,3},{3,0},{4,5},{5,6},{6,7},{7,4},{8,9},{9,10},{10,1... | collective-permute-start | bytes 73736 | tf_op jit(solution)/shard_map/ppermute | solution.py:983
  391.3 45.7 %collective-permute-start.12 = (f32[8,1,768]{2,1,0:T(1,128)S(1)}, f32[8,1,768]{2,1,0:T(1,128)S(1)}, u32[]{:S(2)}, u32[]{:S(2)}) collective-permute-start(f32[8,1,768]{2,1,0:T(1,128)S(1)} %copy-done.48), channel_id=1, source_target_pairs={{0,2},{1,3},{2,0},{3,1},{4,6},{5,7},{6,4},{7,5},{8,10},{9,11},{10,... | collective-permute-start | bytes 73736 | tf_op jit(solution)/shard_map/ppermute | solution.py:983
  395.4 41.5 %collective-permute-start.11 = (f32[8,1,768]{2,1,0:T(1,128)S(1)}, f32[8,1,768]{2,1,0:T(1,128)S(1)}, u32[]{:S(2)}, u32[]{:S(2)}) collective-permute-start(f32[8,1,768]{2,1,0:T(1,128)S(1)} %copy-done.49), channel_id=1, source_target_pairs={{0,3},{1,0},{2,1},{3,2},{4,7},{5,4},{6,5},{7,6},{8,11},{9,8},{10,9... | collective-permute-start | bytes 73736 | tf_op jit(solution)/shard_map/ppermute | solution.py:983
  437.0 278.1 %reduce-scatter.4.cloned.1.call-start = ((), (), s32[]{:S(2)}) async-start(), calls=%async_computation.4 | async-start | bytes 9437184 | tf_op jit(solution)/shard_map/reduce_scatter | solution.py:1228
  437.6 280.4 %reduce-scatter.8.cloned.1.call-start = ((), (), s32[]{:S(2)}) async-start(), calls=%async_computation.6 | async-start | bytes 9437184 | tf_op jit(solution)/shard_map/reduce_scatter | solution.py:1228
  474.8 58.8 %collective-permute-start.15 = (bf16[768,1024]{1,0:T(8,128)(2,1)}, bf16[768,1024]{1,0:T(8,128)(2,1)}, u32[]{:S(2)}, u32[]{:S(2)}) collective-permute-start(bf16[768,1024]{1,0:T(8,128)(2,1)} %get-tuple-element.300), channel_id=1, source_target_pairs={{0,3},{1,0},{2,1},{3,2},{4,7},{5,4},{6,5},{7,6},{8,11},{9,8},{10,9... | collective-permute-start | bytes 4718600 | tf_op jit(solution)/shard_map/ppermute | solution.py:983
  537.3 49.8 %collective-permute-start.16 = (bf16[768,1024]{1,0:T(8,128)(2,1)}, bf16[768,1024]{1,0:T(8,128)(2,1)}, u32[]{:S(2)}, u32[]{:S(2)}) collective-permute-start(bf16[768,1024]{1,0:T(8,128)(2,1)} %add_convert_fusion.2), channel_id=1, source_target_pairs={{0,3},{1,0},{2,1},{3,2},{4,7},{5,4},{6,5},{7,6},{8,11},{9,8},{10,9... | collective-permute-start | bytes 4718600 | tf_op jit(solution)/shard_map/ppermute | solution.py:983
  591.0 38.0 %collective-permute-start.17 = (bf16[768,1024]{1,0:T(8,128)(2,1)}, bf16[768,1024]{1,0:T(8,128)(2,1)}, u32[]{:S(2)}, u32[]{:S(2)}) collective-permute-start(bf16[768,1024]{1,0:T(8,128)(2,1)} %add_convert_fusion.1), channel_id=1, source_target_pairs={{0,3},{1,0},{2,1},{3,2},{4,7},{5,4},{6,5},{7,6},{8,11},{9,8},{10,9... | collective-permute-start | bytes 4718600 | tf_op jit(solution)/shard_map/ppermute | solution.py:983
  (51 other events, 520.7 us)
Sparse Core Ops, SparseCore 0:
  10.0 75.5 all-gather.6
  87.4 62.2 all-gather.8
  151.6 54.3 all-gather.10
  437.1 72.5 reduce-scatter.5
  513.4 71.2 reduce-scatter.3
  588.1 77.5 reduce-scatter.7

commit v10 on v9

--- a/solution.py
+++ b/solution.py
@@ -148,42 +148,6 @@
         cost_estimate=SMALL,
         name="to_gates",
     )(*halves, x, output_t, rest, gain_rows, mask)
-
-
-def outer_kernel(mine, *refs, count):
-    out_ref = refs[-1]
-    pairs = [(refs[n], refs[n + 1]) for n in range(0, len(refs) - 1, 2)]
-    at = 0
-    for a_ref, b_ref in pairs[:count]:
-        columns = b_ref.shape[1]
-        out_ref[:, at : at + columns] = dot_tn(a_ref[...], b_ref[...]).astype(bf16)
-        at += columns
-    if pairs[count:]:
-        out_ref[:, at:] = sum(dot_tn(a[...], b[...]) for a, b in pairs[count:]).astype(bf16)
-
-
-def outer(pairs, extra=()):
-    tok = pairs[0][0].shape[0]
-    mine = lax.axis_index("ctx").astype(jnp.int32).reshape(1)
-    specs = []
-    everything = [*pairs, *extra]
-    for _, b in everything:
-        specs.append(pl.BlockSpec((tok, 128), lambda m, mine: (0, m ^ mine[0])))
-        specs.append(pl.BlockSpec(b.shape, lambda m, mine: (0, 0)))
-    columns = sum(b.shape[1] for _, b in [*pairs, *extra[:1]])
-    return pl.pallas_call(
-        functools.partial(outer_kernel, count=len(pairs)),
-        grid_spec=pltpu.PrefetchScalarGridSpec(
-            num_scalar_prefetch=1,
-            grid=(8,),
-            in_specs=specs,
-            out_specs=pl.BlockSpec((128, columns), lambda m, mine: (m, 0)),
-        ),
-        out_shape=jax.ShapeDtypeStruct((MODEL_WIDTH, columns), bf16),
-        compiler_params=pltpu.CompilerParams(vmem_limit_bytes=VMEM_LIMIT),
-        cost_estimate=SMALL,
-        name="outer",
-    )(mine, *[x for pair in everything for x in pair])
 
 
 def gather_keys(pieces, scratch, places, block_rows):
@@ -639,7 +603,11 @@
 
 def partner(mask):
     me = lax.axis_index("ctx")
-    return me + mask - 2 * mask * ((me // mask) % 2)
+    other = me
+    for bit in (1, 2, 4):
+        if mask & bit:
+            other = other + bit - 2 * bit * ((me // bit) % 2)
+    return other
 
 
 def ahead(distance):
@@ -821,9 +789,12 @@
             device,
         )
 
+    def send_one(m):
+        copies.start((key, m), blocks(x_ref, m), blocks(sib, m // 2), side)
+
     def first():
         for m in (7, 3, 5, 1):
-            copies.start((key, m), blocks(x_ref, m), blocks(sib, m // 2), side)
+            send_one(m)
 
     def second():
         copies.arrived((key, 7))
@@ -853,7 +824,7 @@
             + recv[2 * rows :, columns].astype(f32)
         )
 
-    return [first, second, third, fourth, last]
+    return [first, second, third, fourth, last, send_one]
 
 
 def plane_sum_kernel(*refs, sets):
@@ -897,9 +868,13 @@
     )(*arrays)
 
 
-def full_sum_kernel(x_ref, *refs, widths):
-    out_refs, refs = refs[: len(widths)], refs[len(widths) :]
-    sib, low, recv, total, total_low, arrived, result_ref, send, recv_sem = refs
+def full_sum_kernel(*refs, sides, count, widths):
+    arrays = sum(sides)
+    out_refs = refs[arrays : arrays + len(widths)]
+    a_refs, b_refs = refs[: sides[0]], refs[sides[0] : arrays]
+    x_ref, sib, low, recv, total, total_low, arrived, result_ref, send, recv_sem = refs[
+        arrays + len(widths) :
+    ]
     rows = result_ref.shape[0]
     greet(
         [{"ctx": partner(m)} for m in (1, 2, 4)] + [{"wt": ahead(d)} for d in (1, 2, 3)]
@@ -931,17 +906,32 @@
             result = result + arrived[(d - 1) * rows : d * rows, parts[n]].astype(f32)
         result_ref[:, parts[n]] = result
 
+    def make(m):
+        lanes = pl.ds(pl.multiple_of(partner(m) * 128, 128), 128)
+        block = slice(m * 4 * rows, (m + 1) * 4 * rows)
+        terms = [dot_tn(a[:, lanes], b[...]) for a, b in zip(a_refs, b_refs)]
+        at = 0
+        for term in terms[:count] + [sum(terms[count:])]:
+            x_ref[block, at : at + term.shape[1]] = term.astype(bf16)
+            at += term.shape[1]
+
+    for m in (7, 3, 5, 1):
+        make(m)
+        for one in steps:
+            one[5](m)
+    make(6)
     for one in steps:
-        one[0]()
-    for n in range(PARTS + 2):
-        if n < PARTS:
-            steps[n][1]()
-            steps[n][2]()
-        if 1 <= n <= PARTS:
-            steps[n - 1][3]()
-        if n >= 2:
-            steps[n - 2][4]()
-            leave(n - 2)
+        one[1]()
+    make(2)
+    make(4)
+    for one in steps:
+        one[2]()
+    make(0)
+    for one in steps:
+        one[3]()
+    for n in range(PARTS):
+        steps[n][4]()
+        leave(n)
     for n in range(PARTS):
         finish(n)
     at = 0
@@ -951,15 +941,20 @@
     copies.close()
 
 
-def full_sum(x, widths):
-    rows, columns = x.shape[0] // 32, x.shape[1]
+def full_sum(pairs, extra, widths):
+    rows, columns = MODEL_WIDTH // 32, sum(widths)
     vmem = pl.BlockSpec(memory_space=pltpu.VMEM)
+    lefts = [a for a, _ in [*pairs, *extra]]
+    rights = [b for _, b in [*pairs, *extra]]
     return pl.pallas_call(
-        functools.partial(full_sum_kernel, widths=widths),
-        in_specs=[vmem],
+        functools.partial(
+            full_sum_kernel, sides=(len(lefts), len(rights)), count=len(pairs), widths=widths
+        ),
+        in_specs=[vmem] * (len(lefts) + len(rights)),
         out_specs=[vmem] * len(widths),
         out_shape=[jax.ShapeDtypeStruct((rows, width), f32) for width in widths],
         scratch_shapes=[
+            pltpu.VMEM((32 * rows, columns), bf16),
             pltpu.VMEM((16 * rows, columns), bf16),
             pltpu.VMEM((12 * rows, columns), bf16),
             pltpu.VMEM((12 * rows, columns), bf16),
@@ -975,7 +970,7 @@
         ),
         cost_estimate=SMALL,
         name="full_sum",
-    )(x)
+    )(*lefts, *rights)
 
 
 def shift(x, distance):
@@ -1007,7 +1002,7 @@
         ).astype(f32)
         edges = [sum(widths[: n + 1]) for n in range(len(widths) - 1)]
         return jnp.split(result, edges, 1)
-    return full_sum(outer(pairs, extra), widths)
+    return full_sum(pairs, extra, widths)
 
 
 def after(x, *others):

time: 739 us -> 741 us (level)
  Pallas kernels: 572 us -> 585 us
  starting transfers between devices: 41.5 us -> 33.2 us
    pallas_call x4, Pallas kernels: 158 us -> 174 us  [expert_pass(): pl.pallas_call(functools.partial(expert_kernel, sizes=sizes), grid_spec=p...]
    ppermute x18, starting transfers between devices: 34.9 us -> 26.7 us  [shift(): return lax.ppermute(x, 'wt', [(i, (i + distance) % n) for i in range(n)])]
    pallas_call x2 -> x1, Pallas kernels: 61.9 us -> 56 us  [full_sum(): pl.pallas_call(functools.partial(full_sum_kernel, sides=(len(lefts), len(...]
  transfers between devices with their start and end apart: 25 -> 25, of which waited for: 3 -> 3; matrix products, arithmetic and copies ran while one was open for 9% -> 9% of each run, Pallas kernels for 78% -> 80%
where the time goes in v10:
time: 741 us; the launch traced here: 735 us
  Pallas kernels  585 us (79%)
  other arithmetic  37.4 us (5%)
  starting transfers between devices  33.2 us (4%)
  local copies, waits for them, and re-layouts  30.9 us (4%)
  waiting for transfers between devices  20 us (3%)
  between operations  17.8 us (2%)
  matrix products  11.2 us (2%)
    pallas_call x4, Pallas kernels, expert_pass(): pl.pallas_call(functools.partial(expert_kernel, sizes=sizes), grid_spec=p...  174 us
    pallas_call x2, Pallas kernels, attention_backward(): pl.pallas_call(functools.partial(attention_backward_kernel, block_rows=bl...  97.9 us
    pallas_call x1, Pallas kernels, full_sum(): pl.pallas_call(functools.partial(full_sum_kernel, sides=(len(lefts), len(...  56 us
    pallas_call x2, Pallas kernels, attention_forward(): pl.pallas_call(functools.partial(attention_forward_kernel, block_rows=blo...  53.1 us
    pallas_call x1, Pallas kernels, packed_gather(): pl.pallas_call(packed_gather_kernel, in_specs=[ANY], out_specs=ANY, out_s...  53.1 us
    pallas_call x1, Pallas kernels, up_weight_grads(): pl.pallas_call(functools.partial(up_grad_kernel, sources=len(rows)), grid...  40.6 us
    pallas_call x1, Pallas kernels, plane_sum(): pl.pallas_call(functools.partial(plane_sum_kernel, sets=sets), in_specs=[...  35 us
    pallas_call x1, Pallas kernels, plane_gather(): pl.pallas_call(plane_gather_kernel, in_specs=[ANY], out_specs=ANY, out_sh...  33.3 us
  transfers between devices with their start and end apart: 25, of which 3 were waited for; matrix products, arithmetic and copies ran while one was open for 9% of the time, Pallas kernels for 80%

profile of v10, /device:TPU:0, one launch (start us, length us, event | category | flops | bytes accessed | tf_op | source)
XLA Modules:
  0.0 735.0 jit_solution(5425327531277427068)
XLA Ops:
  10.6 6.3 all-to-all-start
  17.9 53.1 %packed_gather.1.refs_0_ = bf16[1024,3200]{1,0:T(8,128)(2,1)} custom-call(bf16[32,3200]{1,0:T(8,128)(2,1)} %concatenate.76.x_ref), custom_call_target="tpu_custom_call" | custom-call | flops 1000000000 | bytes 1000000 | tf_op jit(solution)/shard_map/packed_gather/pallas_call | solution.py:753
  80.4 9.0 %project.1 = (bf16[768,1024]{1,0:T(8,128)(2,1)}, bf16[768,1024]{1,0:T(8,128)(2,1)}, bf16[768,1024]{1,0:T(8,128)(2,1)}, bf16[1024,2048]{1,0:T(8,128)(2,1)}, bf16[...) custom-call(s32[32]{0:T(128)} %add.207.places, bf16[768,1024]{1,0:T(8,128)(2,1)} %bitcast.117, ...), custom_call_target="tpu_custom_call" | custom-call | flops 1000000000 | bytes 1000000 | tf_op jit(solution)/shard_map/project/pallas_call | solution.py:96
  89.4 33.3 %plane_gather.1.refs_0_.refs_1_ = bf16[2048,1024]{1,0:T(8,128)(2,1)} custom-call(bf16[768,1024]{1,0:T(8,128)(2,1)} %get-tuple-element.175.x_ref), custom_call_target="tpu_custom_call" | custom-call | flops 1000000000 | bytes 1000000 | tf_op jit(solution)/shard_map/plane_gather/pallas_call | solution.py:698
  129.2 26.5 %attention_forward.2 = (bf16[768,512]{1,0:T(8,128)(2,1)}, f32[2,4,768]{2,1,0:T(4,128)}) custom-call(s32[16]{0:T(128)} %reshape.344.places, s32[4]{0:T(128)} %get-tuple-element.377.starts, bf16[768,1024]{1,0:T(8,128)(2,1)} %get-tuple-element.303.q_ref, bf16[2048,1024]{1,0:T(8,128)(2,1)} %plane_gather.1.refs_0_.refs_1_, ...), custom_call_target="tpu_custom_call" | custom-call | flops 1000000000 | bytes 1000000 | tf_op jit(solution)/shard_map/attention_forward/pallas_call | solution.py:233
  155.8 5.0 collective-permute-done.1.df_ref
  160.8 4.5 collective-permute-start.2
  166.2 26.6 %attention_forward.3 = (bf16[768,512]{1,0:T(8,128)(2,1)}, f32[2,4,768]{2,1,0:T(4,128)}) custom-call(s32[16]{0:T(128)} %reshape.344.places, s32[4]{0:T(128)} %get-tuple-element.377.starts, bf16[768,1024]{1,0:T(8,128)(2,1)} %get-tuple-element.303.q_ref, bf16[2048,1024]{1,0:T(8,128)(2,1)} %plane_gather.1.refs_0_.refs_1_, ...), custom_call_target="tpu_custom_call" | custom-call | flops 1000000000 | bytes 1000000 | tf_op jit(solution)/shard_map/attention_forward/pallas_call | solution.py:233
  192.8 5.8 collective-permute-done.2.df_ref
  198.6 8.0 %to_gates.1 = (f32[768,1024]{1,0:T(8,128)}, bf16[768,1024]{1,0:T(8,128)(2,1)}, f32[768,1]{1,0:T(8,128)}, f32[32,768]{1,0:T(8,128)}) custom-call(bf16[768,512]{1,0:T(8,128)(2,1)} %get-tuple-element.181.a_ref.o_ref.refs_8_, bf16[768,512]{1,0:T(8,128)(2,1)} %get-tuple-element.186.b_ref.o_ref.refs_9_, bf16[768,1024]{1,0:T(8,128)(2,1)} %bitcast.118, ...), custom_call_target="tpu_custom_call" | custom-call | flops 1000000000 | bytes 1000000 | tf_op jit(solution)/shard_map/to_gates/pallas_call | solution.py:137
  206.6 4.3 collective-permute-start.3
  217.8 50.5 %expert_pass.4 = (bf16[768,1024]{1,0:T(8,128)(2,1)}, bf16[768,1024]{1,0:T(8,128)(2,1)}, f32[8,1,768]{2,1,0:T(1,128)}, bf16[8,336,1024]{2,1,0:T(8,128)(2,1)}, bf1...) custom-call(s32[8]{0:T(128)} %get-tuple-element.381.counts, ...), custom_call_target="tpu_custom_call" | custom-call | flops 1000000000 | bytes 1000000 | tf_op jit(solution)/shard_map/expert_pass/pallas_call | solution.py:504
  269.9 41.2 %expert_pass.5 = (bf16[768,1024]{1,0:T(8,128)(2,1)}, bf16[768,1024]{1,0:T(8,128)(2,1)}, f32[8,1,768]{2,1,0:T(1,128)}, bf16[8,336,1024]{2,1,0:T(8,128)(2,1)}, bf1...) custom-call(s32[8]{0:T(128)} %get-tuple-element.378.counts, ...), custom_call_target="tpu_custom_call" | custom-call | flops 1000000000 | bytes 1000000 | tf_op jit(solution)/shard_map/expert_pass/pallas_call | solution.py:504
  312.3 42.5 %expert_pass.6 = (bf16[768,1024]{1,0:T(8,128)(2,1)}, bf16[768,1024]{1,0:T(8,128)(2,1)}, f32[8,1,768]{2,1,0:T(1,128)}, bf16[8,336,1024]{2,1,0:T(8,128)(2,1)}, bf1...) custom-call(s32[8]{0:T(128)} %get-tuple-element.379.counts, ...), custom_call_target="tpu_custom_call" | custom-call | flops 1000000000 | bytes 1000000 | tf_op jit(solution)/shard_map/expert_pass/pallas_call | solution.py:504
  356.6 40.2 %expert_pass.7 = (bf16[768,1024]{1,0:T(8,128)(2,1)}, bf16[768,1024]{1,0:T(8,128)(2,1)}, f32[8,1,768]{2,1,0:T(1,128)}, bf16[8,336,1024]{2,1,0:T(8,128)(2,1)}, bf1...) custom-call(s32[8]{0:T(128)} %get-tuple-element.380.counts, ...), custom_call_target="tpu_custom_call" | custom-call | flops 1000000000 | bytes 1000000 | tf_op jit(solution)/shard_map/expert_pass/pallas_call | solution.py:504
  404.5 40.6 %up_weight_grads.1 = (bf16[8,8,128,512]{3,2,1,0:T(8,128)(2,1)}, bf16[8,8,128,512]{3,2,1,0:T(8,128)(2,1)}) custom-call(bf16[8,336,1024]{2,1,0:T(8,128)(2,1)} %get-tuple-element.253.refs_0_, bf16[8,336,512]{2,1,0:T(8,128)(2,1)} %get-tuple-element.254.refs_1_, bf16[8,336,512]{2,1,0:T(8,128)(2,1)} %get-tuple-element.255.refs_2_, ...), custom_call_target="tpu_custom_call" | custom-call | flops 1000000000 | bytes 1000000 | tf_op jit(solution)/shard_map/up_weight_grads/pallas_call | solution.py:563
  449.8 24.2 %down_weight_grads.1 = bf16[8,8,512,128]{3,2,1,0:T(8,128)(2,1)} custom-call(bf16[8,336,512]{2,1,0:T(8,128)(2,1)} %get-tuple-element.280.refs_0_, bf16[8,336,1024]{2,1,0:T(8,128)(2,1)} %get-tuple-element.281.refs_1_, bf16[8,336,512]{2,1,0:T(8,128)(2,1)} %get-tuple-element.283.refs_2_, bf16[8,336,1024]{2,1,0:T(8,128)(2,1)} %get-tuple-element.284.refs_3_, ...), custom_call_target="tpu_custom_call" | custom-call | flops 1000000000 | bytes 1000000 | tf_op jit(solution)/shard_map/down_weight_grads/pallas_call | solution.py:578
  474.0 6.5 collective-permute-done.14
  493.4 48.5 %attention_backward.2 = (bf16[768,512]{1,0:T(8,128)(2,1)}, bf16[2048,512]{1,0:T(8,128)(2,1)}, f32[512,256]{1,0:T(8,128)}, f32[512,256]{1,0:T(8,128)}) custom-call(s32[16]{0:T(128)} %reshape.344.places, s32[4]{0:T(128)} %get-tuple-element.377.starts, bf16[768,1024]{1,0:T(8,128)(2,1)} %get-tuple-element.303.q_ref, ...), custom_call_target="tpu_custom_call" | custom-call | flops 1000000000 | bytes 1000000 | tf_op jit(solution)/shard_map/attention_backward/pallas_call | solution.py:378
  546.5 49.4 %attention_backward.3 = (bf16[768,512]{1,0:T(8,128)(2,1)}, bf16[2048,512]{1,0:T(8,128)(2,1)}, f32[512,256]{1,0:T(8,128)}, f32[512,256]{1,0:T(8,128)}) custom-call(s32[16]{0:T(128)} %reshape.344.places, s32[4]{0:T(128)} %get-tuple-element.377.starts, bf16[768,1024]{1,0:T(8,128)(2,1)} %get-tuple-element.303.q_ref, ...), custom_call_target="tpu_custom_call" | custom-call | flops 1000000000 | bytes 1000000 | tf_op jit(solution)/shard_map/attention_backward/pallas_call | solution.py:378
  595.9 3.8 add_convert_fusion.1
  602.0 35.0 %plane_sum.1 = (f32[256,512]{1,0:T(8,128)}, f32[256,512]{1,0:T(8,128)}) custom-call(bf16[2048,512]{1,0:T(8,128)(2,1)} %get-tuple-element.301.refs_0_, bf16[2048,512]{1,0:T(8,128)(2,1)} %get-tuple-element.312.refs_1_), custom_call_target="tpu_custom_call" | custom-call | flops 1000000000 | bytes 1000000 | tf_op jit(solution)/shard_map/plane_sum/pallas_call | solution.py:855
  650.8 6.4 multiply_convert_fusion
  658.7 56.0 %full_sum.1 = (f32[32,1024]{1,0:T(8,128)}, f32[32,1024]{1,0:T(8,128)}, f32[32,512]{1,0:T(8,128)}, f32[32,512]{1,0:T(8,128)}, f32[32,128]{1,0:T(8,128)}) custom-call(bf16[768,1024]{1,0:T(8,128)(2,1)} %get-tuple-element.326.refs_0_.refs_3_, bf16[768,1024]{1,0:T(8,128)(2,1)} %copy-done.7, bf16[768,1024]{1,0:T(8,128)(2,1)} %copy-done.7, ...), custom_call_target="tpu_custom_call" | custom-call | flops 1000000000 | bytes 1000000 | tf_op jit(solution)/shard_map/full_sum/pallas_call | solution.py:949
  (243 shorter events, 90.1 us)
Async XLA Ops:
  7.3 210.5 %all-gather.7.cloned.1.call-start = ((), (), s32[]{:S(2)}) async-start(), calls=%async_computation.7 | async-start | bytes 9437184 | tf_op jit(solution)/shard_map/all_gather | solution.py:1089
  8.0 209.8 %all-gather.9.cloned.1.call-start = ((), (), s32[]{:S(2)}) async-start(), calls=%async_computation.8 | async-start | bytes 9437184 | tf_op jit(solution)/shard_map/all_gather | solution.py:1090
  8.7 209.0 %all-gather.11.cloned.1.call-start = ((), (), s32[]{:S(2)}) async-start(), calls=%async_computation.9 | async-start | bytes 9437184 | tf_op jit(solution)/shard_map/all_gather | solution.py:1091
  10.6 60.4 %all-to-all-start = ((f32[4,8,1,768]{3,1,2,0:T(8,128)}), f32[4,8,1,768]{3,1,2,0:T(8,128)S(1)}, u32[]{:S(2)}, u32[]{:S(2)}) async-start(f32[4,8,1,768]{3,1,2,0:T(8,128)} %fusion.28), calls=%async_computation | async-start | bytes 196608 | tf_op jit(solution)/shard_map/all_to_all | solution.py:1099
  16.9 699.3 %reduce-scatter.6.cloned.1.call-start = ((), (), s32[]{:S(2)}) async-start(), calls=%async_computation.5 | async-start | bytes 9437184 | tf_op jit(solution)/shard_map/reduce_scatter | solution.py:1223
  71.0 51.6 %collective-permute-start = (bf16[768,1024]{1,0:T(8,128)(2,1)S(1)}, bf16[768,1024]{1,0:T(8,128)(2,1)}, u32[]{:S(2)}, u32[]{:S(2)}) collective-permute-start(bf16[768,1024]{1,0:T(8,128)(2,1)S(1)} %bitcast.120), channel_id=1, source_target_pairs={{0,3},{1,0},{2,1},{3,2},{4,7},{5,4},{6,5},{7,6},{8,11},{9,8},{10,9... | collective-permute-start | bytes 4718600 | tf_op jit(solution)/shard_map/ppermute | solution.py:978
  122.7 38.1 %collective-permute-start.1 = (bf16[768,1024]{1,0:T(8,128)(2,1)}, bf16[768,1024]{1,0:T(8,128)(2,1)S(1)}, u32[]{:S(2)}, u32[]{:S(2)}) collective-permute-start(bf16[768,1024]{1,0:T(8,128)(2,1)} %collective-permute-done.df_ref), channel_id=1, source_target_pairs={{0,3},{1,0},{2,1},{3,2},{4,7},{5,4},{6,5},{7,6},{8,11},{9,8},{10,9... | collective-permute-start | bytes 4718600 | tf_op jit(solution)/shard_map/ppermute | solution.py:978
  160.8 37.8 %collective-permute-start.2 = (bf16[768,1024]{1,0:T(8,128)(2,1)S(1)}, bf16[768,1024]{1,0:T(8,128)(2,1)S(1)}, u32[]{:S(2)}, u32[]{:S(2)}) collective-permute-start(bf16[768,1024]{1,0:T(8,128)(2,1)S(1)} %collective-permute-done.1.df_ref), channel_id=1, source_target_pairs={{0,3},{1,0},{2,1},{3,2},{4,7},{5,4},{6,5},{7,6},{8,11},{9,8},{10,9... | collective-permute-start | bytes 4718600 | tf_op jit(solution)/shard_map/ppermute | solution.py:978
  206.6 61.7 %collective-permute-start.3 = (bf16[768,1024]{1,0:T(8,128)(2,1)}, bf16[768,1024]{1,0:T(8,128)(2,1)S(1)}, u32[]{:S(2)}, u32[]{:S(2)}) collective-permute-start(bf16[768,1024]{1,0:T(8,128)(2,1)} %get-tuple-element.192.a2_ref.refs_4_), channel_id=1, source_target_pairs={{0,3},{1,0},{2,1},{3,2},{4,7},{5,4},{6,5},{7,6},{8,11},{9,8},{10,9... | collective-permute-start | bytes 4718600 | tf_op jit(solution)/shard_map/ppermute | solution.py:978
  213.7 54.6 %collective-permute-start.4 = (f32[8,1,768]{2,1,0:T(1,128)S(1)}, f32[8,1,768]{2,1,0:T(1,128)S(1)}, u32[]{:S(2)}, u32[]{:S(2)}) collective-permute-start(f32[8,1,768]{2,1,0:T(1,128)S(1)} %bitcast.144), channel_id=1, source_target_pairs={{0,1},{1,2},{2,3},{3,0},{4,5},{5,6},{6,7},{7,4},{8,9},{9,10},{10,1... | collective-permute-start | bytes 73736 | tf_op jit(solution)/shard_map/ppermute | solution.py:978
  213.8 54.5 %collective-permute-start.5 = (f32[8,1,768]{2,1,0:T(1,128)S(1)}, f32[8,1,768]{2,1,0:T(1,128)S(1)}, u32[]{:S(2)}, u32[]{:S(2)}) collective-permute-start(f32[8,1,768]{2,1,0:T(1,128)S(1)} %bitcast.145), channel_id=1, source_target_pairs={{0,2},{1,3},{2,0},{3,1},{4,6},{5,7},{6,4},{7,5},{8,10},{9,11},{10,... | collective-permute-start | bytes 73736 | tf_op jit(solution)/shard_map/ppermute | solution.py:978
  214.6 53.8 %collective-permute-start.6 = (f32[8,1,768]{2,1,0:T(1,128)S(1)}, f32[8,1,768]{2,1,0:T(1,128)S(1)}, u32[]{:S(2)}, u32[]{:S(2)}) collective-permute-start(f32[8,1,768]{2,1,0:T(1,128)S(1)} %bitcast.146), channel_id=1, source_target_pairs={{0,3},{1,0},{2,1},{3,2},{4,7},{5,4},{6,5},{7,6},{8,11},{9,8},{10,9... | collective-permute-start | bytes 73736 | tf_op jit(solution)/shard_map/ppermute | solution.py:978
  268.3 42.8 %collective-permute-start.7 = (bf16[768,1024]{1,0:T(8,128)(2,1)S(1)}, bf16[768,1024]{1,0:T(8,128)(2,1)S(1)}, u32[]{:S(2)}, u32[]{:S(2)}) collective-permute-start(bf16[768,1024]{1,0:T(8,128)(2,1)S(1)} %collective-permute-done.3.a2_ref), channel_id=1, source_target_pairs={{0,3},{1,0},{2,1},{3,2},{4,7},{5,4},{6,5},{7,6},{8,11},{9,8},{10,9... | collective-permute-start | bytes 4718600 | tf_op jit(solution)/shard_map/ppermute | solution.py:978
  311.2 43.7 %collective-permute-start.8 = (bf16[768,1024]{1,0:T(8,128)(2,1)S(1)}, bf16[768,1024]{1,0:T(8,128)(2,1)S(1)}, u32[]{:S(2)}, u32[]{:S(2)}) collective-permute-start(bf16[768,1024]{1,0:T(8,128)(2,1)S(1)} %collective-permute-done.7.a2_ref), channel_id=1, source_target_pairs={{0,3},{1,0},{2,1},{3,2},{4,7},{5,4},{6,5},{7,6},{8,11},{9,8},{10,9... | collective-permute-start | bytes 4718600 | tf_op jit(solution)/shard_map/ppermute | solution.py:978
  356.0 40.8 %collective-permute-start.9 = (bf16[768,1024]{1,0:T(8,128)(2,1)}, bf16[768,1024]{1,0:T(8,128)(2,1)S(1)}, u32[]{:S(2)}, u32[]{:S(2)}) collective-permute-start(bf16[768,1024]{1,0:T(8,128)(2,1)} %get-tuple-element.251), channel_id=1, source_target_pairs={{0,3},{1,0},{2,1},{3,2},{4,7},{5,4},{6,5},{7,6},{8,11},{9,8},{10,9... | collective-permute-start | bytes 4718600 | tf_op jit(solution)/shard_map/ppermute | solution.py:978
  398.6 46.4 %collective-permute-start.10 = (bf16[768,1024]{1,0:T(8,128)(2,1)}, bf16[768,1024]{1,0:T(8,128)(2,1)S(1)}, u32[]{:S(2)}, u32[]{:S(2)}) collective-permute-start(bf16[768,1024]{1,0:T(8,128)(2,1)} %add_convert_fusion.4), channel_id=1, source_target_pairs={{0,3},{1,0},{2,1},{3,2},{4,7},{5,4},{6,5},{7,6},{8,11},{9,8},{10,9... | collective-permute-start | bytes 4718600 | tf_op jit(solution)/shard_map/ppermute | solution.py:978
  398.7 46.4 %collective-permute-start.13 = (f32[8,1,768]{2,1,0:T(1,128)S(1)}, f32[8,1,768]{2,1,0:T(1,128)S(1)}, u32[]{:S(2)}, u32[]{:S(2)}) collective-permute-start(f32[8,1,768]{2,1,0:T(1,128)S(1)} %copy-done.47), channel_id=1, source_target_pairs={{0,1},{1,2},{2,3},{3,0},{4,5},{5,6},{6,7},{7,4},{8,9},{9,10},{10,1... | collective-permute-start | bytes 73736 | tf_op jit(solution)/shard_map/ppermute | solution.py:978
  400.7 44.4 %collective-permute-start.12 = (f32[8,1,768]{2,1,0:T(1,128)S(1)}, f32[8,1,768]{2,1,0:T(1,128)S(1)}, u32[]{:S(2)}, u32[]{:S(2)}) collective-permute-start(f32[8,1,768]{2,1,0:T(1,128)S(1)} %copy-done.48), channel_id=1, source_target_pairs={{0,2},{1,3},{2,0},{3,1},{4,6},{5,7},{6,4},{7,5},{8,10},{9,11},{10,... | collective-permute-start | bytes 73736 | tf_op jit(solution)/shard_map/ppermute | solution.py:978
  401.6 43.5 %collective-permute-start.11 = (f32[8,1,768]{2,1,0:T(1,128)S(1)}, f32[8,1,768]{2,1,0:T(1,128)S(1)}, u32[]{:S(2)}, u32[]{:S(2)}) collective-permute-start(f32[8,1,768]{2,1,0:T(1,128)S(1)} %copy-done.49), channel_id=1, source_target_pairs={{0,3},{1,0},{2,1},{3,2},{4,7},{5,4},{6,5},{7,6},{8,11},{9,8},{10,9... | collective-permute-start | bytes 73736 | tf_op jit(solution)/shard_map/ppermute | solution.py:978
  445.1 274.0 %reduce-scatter.4.cloned.1.call-start = ((), (), s32[]{:S(2)}) async-start(), calls=%async_computation.4 | async-start | bytes 9437184 | tf_op jit(solution)/shard_map/reduce_scatter | solution.py:1223
  445.7 276.2 %reduce-scatter.8.cloned.1.call-start = ((), (), s32[]{:S(2)}) async-start(), calls=%async_computation.6 | async-start | bytes 9437184 | tf_op jit(solution)/shard_map/reduce_scatter | solution.py:1223
  482.7 59.2 %collective-permute-start.15 = (bf16[768,1024]{1,0:T(8,128)(2,1)}, bf16[768,1024]{1,0:T(8,128)(2,1)}, u32[]{:S(2)}, u32[]{:S(2)}) collective-permute-start(bf16[768,1024]{1,0:T(8,128)(2,1)} %get-tuple-element.300), channel_id=1, source_target_pairs={{0,3},{1,0},{2,1},{3,2},{4,7},{5,4},{6,5},{7,6},{8,11},{9,8},{10,9... | collective-permute-start | bytes 4718600 | tf_op jit(solution)/shard_map/ppermute | solution.py:978
  545.6 50.3 %collective-permute-start.16 = (bf16[768,1024]{1,0:T(8,128)(2,1)}, bf16[768,1024]{1,0:T(8,128)(2,1)}, u32[]{:S(2)}, u32[]{:S(2)}) collective-permute-start(bf16[768,1024]{1,0:T(8,128)(2,1)} %add_convert_fusion.2), channel_id=1, source_target_pairs={{0,3},{1,0},{2,1},{3,2},{4,7},{5,4},{6,5},{7,6},{8,11},{9,8},{10,9... | collective-permute-start | bytes 4718600 | tf_op jit(solution)/shard_map/ppermute | solution.py:978
  599.7 39.7 %collective-permute-start.17 = (bf16[768,1024]{1,0:T(8,128)(2,1)}, bf16[768,1024]{1,0:T(8,128)(2,1)}, u32[]{:S(2)}, u32[]{:S(2)}) collective-permute-start(bf16[768,1024]{1,0:T(8,128)(2,1)} %add_convert_fusion.1), channel_id=1, source_target_pairs={{0,3},{1,0},{2,1},{3,2},{4,7},{5,4},{6,5},{7,6},{8,11},{9,8},{10,9... | collective-permute-start | bytes 4718600 | tf_op jit(solution)/shard_map/ppermute | solution.py:978
  (51 other events, 513.6 us)
Sparse Core Ops, SparseCore 0:
  10.0 75.5 all-gather.6
  87.4 62.2 all-gather.8
  151.6 54.3 all-gather.10
  445.2 74.2 reduce-scatter.5
  523.2 71.2 reduce-scatter.3
  597.8 76.3 reduce-scatter.7

commit v11 on v9

--- a/solution.py
+++ b/solution.py
@@ -1106,6 +1106,7 @@
     )
     last = shard_count - 1
     grads_in = {0: out_low, last: shift(after(out_low, pieces[0], ranks), -1)}
+    grads_in[1] = shift(after(out_low, pieces[0], ranks), 1)
 
     pieces, ranks = beside(pieces, ranks)
     local_rows = jnp.arange(tok, dtype=jnp.int32)
@@ -1147,13 +1148,12 @@
         result = attention_forward(
             turned_query, kv_pieces, kv_own, places, starts, block_rows, half
         )
-        d = last - 1 - half
-        grads_in[d] = shift(grads_in[d + 1], -1)
-        result, grads_in[d] = beside(result, grads_in[d])
+        if half == 0:
+            result, grads_in[1] = beside(result, grads_in[1])
         if half == 0:
             turned_query = after(turned_query, result[0])
         heads.append(result)
-    for d in range(last - 3, 0, -1):
+    for d in range(last - 1, 1, -1):
         grads_in[d] = shift(grads_in[d + 1], -1)
     attended = [out for out, _ in heads]
     lse = [row for _, row in heads]
@@ -1167,6 +1167,7 @@
         jnp.pad(mask.astype(f32), ((0, 0), (0, 128 - EXPERTS))),
     )
 
+    normed_two, grads_in[last - 1] = beside(normed_two, grads_in[last - 1])
     gates_out = gates.reshape(shard_count, expert_count, 1, tok)
     gates_in = []
     for d in range(shard_count):

time: 739 us -> 736 us (level)
    ppermute x18, waiting for transfers between devices: 17.6 us -> 10 us  [shift(): return lax.ppermute(x, 'wt', [(i, (i + distance) % n) for i in range(n)])]
  transfers between devices with their start and end apart: 25 -> 25, of which waited for: 3 -> 2; matrix products, arithmetic and copies ran while one was open for 9% -> 9% of each run, Pallas kernels for 78% -> 78%
where the time goes in v11:
time: 736 us; the launch traced here: 728 us
  Pallas kernels  571 us (78%)
  starting transfers between devices  42 us (6%)
  other arithmetic  37.7 us (5%)
  local copies, waits for them, and re-layouts  30.5 us (4%)
  waiting for transfers between devices  18.1 us (2%)
  between operations  17.8 us (2%)
  matrix products  11 us (1%)
    pallas_call x4, Pallas kernels, expert_pass(): pl.pallas_call(functools.partial(expert_kernel, sizes=sizes), grid_spec=p...  154 us
    pallas_call x2, Pallas kernels, attention_backward(): pl.pallas_call(functools.partial(attention_backward_kernel, block_rows=bl...  97.6 us
    pallas_call x2, Pallas kernels, attention_forward(): pl.pallas_call(functools.partial(attention_forward_kernel, block_rows=blo...  53.5 us
    pallas_call x1, Pallas kernels, packed_gather(): pl.pallas_call(packed_gather_kernel, in_specs=[ANY], out_specs=ANY, out_s...  53.1 us
    pallas_call x1, Pallas kernels, full_sum(): pl.pallas_call(functools.partial(full_sum_kernel, widths=widths), in_spec...  44.1 us
    pallas_call x1, Pallas kernels, up_weight_grads(): pl.pallas_call(functools.partial(up_grad_kernel, sources=len(rows)), grid...  40.6 us
    pallas_call x1, Pallas kernels, plane_sum(): pl.pallas_call(functools.partial(plane_sum_kernel, sets=sets), in_specs=[...  39.1 us
    ppermute x18, starting transfers between devices, shift(): return lax.ppermute(x, 'wt', [(i, (i + distance) % n) for i in range(n)])  35.5 us
  transfers between devices with their start and end apart: 25, of which 2 were waited for; matrix products, arithmetic and copies ran while one was open for 9% of the time, Pallas kernels for 78%

profile of v11, /device:TPU:0, one launch (start us, length us, event | category | flops | bytes accessed | tf_op | source)
XLA Modules:
  0.0 728.4 jit_solution(7603735474720890299)
XLA Ops:
  10.6 6.3 all-to-all-start
  17.9 53.1 %packed_gather.1.refs_0_ = bf16[1024,3200]{1,0:T(8,128)(2,1)} custom-call(bf16[32,3200]{1,0:T(8,128)(2,1)} %concatenate.76.x_ref), custom_call_target="tpu_custom_call" | custom-call | flops 1000000000 | bytes 1000000 | tf_op jit(solution)/shard_map/packed_gather/pallas_call | solution.py:785
  82.0 9.1 %project.1 = (bf16[768,1024]{1,0:T(8,128)(2,1)}, bf16[768,1024]{1,0:T(8,128)(2,1)}, bf16[768,1024]{1,0:T(8,128)(2,1)}, bf16[1024,2048]{1,0:T(8,128)(2,1)}, bf16[...) custom-call(s32[32]{0:T(128)} %add.207.places, bf16[768,1024]{1,0:T(8,128)(2,1)} %bitcast.118, ...), custom_call_target="tpu_custom_call" | custom-call | flops 1000000000 | bytes 1000000 | tf_op jit(solution)/shard_map/project/pallas_call | solution.py:96
  91.1 34.6 %plane_gather.1.refs_0_.refs_1_ = bf16[2048,1024]{1,0:T(8,128)(2,1)} custom-call(bf16[768,1024]{1,0:T(8,128)(2,1)} %get-tuple-element.174.x_ref), custom_call_target="tpu_custom_call" | custom-call | flops 1000000000 | bytes 1000000 | tf_op jit(solution)/shard_map/plane_gather/pallas_call | solution.py:730
  130.9 26.6 %attention_forward.2 = (bf16[768,512]{1,0:T(8,128)(2,1)}, f32[2,4,768]{2,1,0:T(4,128)}) custom-call(s32[16]{0:T(128)} %reshape.347.places, s32[4]{0:T(128)} %get-tuple-element.375.starts, bf16[768,1024]{1,0:T(8,128)(2,1)} %get-tuple-element.301.q_ref, bf16[2048,1024]{1,0:T(8,128)(2,1)} %plane_gather.1.refs_0_.refs_1_, ...), custom_call_target="tpu_custom_call" | custom-call | flops 1000000000 | bytes 1000000 | tf_op jit(solution)/shard_map/attention_forward/pallas_call | solution.py:269
  157.6 26.9 %attention_forward.3 = (bf16[768,512]{1,0:T(8,128)(2,1)}, f32[2,4,768]{2,1,0:T(4,128)}) custom-call(s32[16]{0:T(128)} %reshape.347.places, s32[4]{0:T(128)} %get-tuple-element.375.starts, bf16[768,1024]{1,0:T(8,128)(2,1)} %get-tuple-element.301.q_ref, bf16[2048,1024]{1,0:T(8,128)(2,1)} %plane_gather.1.refs_0_.refs_1_, ...), custom_call_target="tpu_custom_call" | custom-call | flops 1000000000 | bytes 1000000 | tf_op jit(solution)/shard_map/attention_forward/pallas_call | solution.py:269
  184.4 7.4 %to_gates.1 = (f32[768,1024]{1,0:T(8,128)}, bf16[768,1024]{1,0:T(8,128)(2,1)}, f32[768,1]{1,0:T(8,128)}, f32[32,768]{1,0:T(8,128)}) custom-call(bf16[768,512]{1,0:T(8,128)(2,1)} %get-tuple-element.179.a_ref.o_ref.refs_3_, bf16[768,512]{1,0:T(8,128)(2,1)} %get-tuple-element.181.b_ref.o_ref.refs_5_, bf16[768,1024]{1,0:T(8,128)(2,1)} %bitcast.119, ...), custom_call_target="tpu_custom_call" | custom-call | flops 1000000000 | bytes 1000000 | tf_op jit(solution)/shard_map/to_gates/pallas_call | solution.py:137
  200.7 5.4 all-gather.11.cloned.1.call-done
  206.1 37.8 %expert_pass.4 = (bf16[768,1024]{1,0:T(8,128)(2,1)}, bf16[768,1024]{1,0:T(8,128)(2,1)}, f32[8,1,768]{2,1,0:T(1,128)}, bf16[8,336,1024]{2,1,0:T(8,128)(2,1)}, bf1...) custom-call(s32[8]{0:T(128)} %get-tuple-element.379.counts, ...), custom_call_target="tpu_custom_call" | custom-call | flops 1000000000 | bytes 1000000 | tf_op jit(solution)/shard_map/expert_pass/pallas_call | solution.py:540
  244.0 5.3 collective-permute-start.7
  250.4 39.9 %expert_pass.5 = (bf16[768,1024]{1,0:T(8,128)(2,1)}, bf16[768,1024]{1,0:T(8,128)(2,1)}, f32[8,1,768]{2,1,0:T(1,128)}, bf16[8,336,1024]{2,1,0:T(8,128)(2,1)}, bf1...) custom-call(s32[8]{0:T(128)} %get-tuple-element.376.counts, ...), custom_call_target="tpu_custom_call" | custom-call | flops 1000000000 | bytes 1000000 | tf_op jit(solution)/shard_map/expert_pass/pallas_call | solution.py:540
  294.6 38.1 %expert_pass.6 = (bf16[768,1024]{1,0:T(8,128)(2,1)}, bf16[768,1024]{1,0:T(8,128)(2,1)}, f32[8,1,768]{2,1,0:T(1,128)}, bf16[8,336,1024]{2,1,0:T(8,128)(2,1)}, bf1...) custom-call(s32[8]{0:T(128)} %get-tuple-element.377.counts, ...), custom_call_target="tpu_custom_call" | custom-call | flops 1000000000 | bytes 1000000 | tf_op jit(solution)/shard_map/expert_pass/pallas_call | solution.py:540
  337.9 38.0 %expert_pass.7 = (bf16[768,1024]{1,0:T(8,128)(2,1)}, bf16[768,1024]{1,0:T(8,128)(2,1)}, f32[8,1,768]{2,1,0:T(1,128)}, bf16[8,336,1024]{2,1,0:T(8,128)(2,1)}, bf1...) custom-call(s32[8]{0:T(128)} %get-tuple-element.378.counts, ...), custom_call_target="tpu_custom_call" | custom-call | flops 1000000000 | bytes 1000000 | tf_op jit(solution)/shard_map/expert_pass/pallas_call | solution.py:540
  377.8 5.4 collective-permute-start.10
  387.3 40.6 %up_weight_grads.1 = (bf16[8,8,128,512]{3,2,1,0:T(8,128)(2,1)}, bf16[8,8,128,512]{3,2,1,0:T(8,128)(2,1)}) custom-call(bf16[8,336,1024]{2,1,0:T(8,128)(2,1)} %get-tuple-element.251.refs_0_, bf16[8,336,512]{2,1,0:T(8,128)(2,1)} %get-tuple-element.252.refs_1_, bf16[8,336,512]{2,1,0:T(8,128)(2,1)} %get-tuple-element.253.refs_2_, ...), custom_call_target="tpu_custom_call" | custom-call | flops 1000000000 | bytes 1000000 | tf_op jit(solution)/shard_map/up_weight_grads/pallas_call | solution.py:599
  432.6 24.1 %down_weight_grads.1 = bf16[8,8,512,128]{3,2,1,0:T(8,128)(2,1)} custom-call(bf16[8,336,512]{2,1,0:T(8,128)(2,1)} %get-tuple-element.278.refs_0_, bf16[8,336,1024]{2,1,0:T(8,128)(2,1)} %get-tuple-element.279.refs_1_, bf16[8,336,512]{2,1,0:T(8,128)(2,1)} %get-tuple-element.281.refs_2_, bf16[8,336,1024]{2,1,0:T(8,128)(2,1)} %get-tuple-element.282.refs_3_, ...), custom_call_target="tpu_custom_call" | custom-call | flops 1000000000 | bytes 1000000 | tf_op jit(solution)/shard_map/down_weight_grads/pallas_call | solution.py:614
  456.7 10.0 %collective-permute-done.14 = bf16[768,1024]{1,0:T(8,128)(2,1)} collective-permute-done((bf16[768,1024]{1,0:T(8,128)(2,1)}, bf16[768,1024]{1,0:T(8,128)(2,1)}, u32[]{:S(2)}, u32[]{:S(2)}) %collective-permute-start.14) | collective-permute-done | bytes 1572896 | tf_op jit(solution)/shard_map/ppermute | solution.py:983
  480.8 48.5 %attention_backward.2 = (bf16[768,512]{1,0:T(8,128)(2,1)}, bf16[2048,512]{1,0:T(8,128)(2,1)}, f32[512,256]{1,0:T(8,128)}, f32[512,256]{1,0:T(8,128)}) custom-call(s32[16]{0:T(128)} %reshape.347.places, s32[4]{0:T(128)} %get-tuple-element.375.starts, bf16[768,1024]{1,0:T(8,128)(2,1)} %get-tuple-element.301.q_ref, ...), custom_call_target="tpu_custom_call" | custom-call | flops 1000000000 | bytes 1000000 | tf_op jit(solution)/shard_map/attention_backward/pallas_call | solution.py:414
  529.3 3.9 add_convert_fusion.2
  533.3 49.1 %attention_backward.3 = (bf16[768,512]{1,0:T(8,128)(2,1)}, bf16[2048,512]{1,0:T(8,128)(2,1)}, f32[512,256]{1,0:T(8,128)}, f32[512,256]{1,0:T(8,128)}) custom-call(s32[16]{0:T(128)} %reshape.347.places, s32[4]{0:T(128)} %get-tuple-element.375.starts, bf16[768,1024]{1,0:T(8,128)(2,1)} %get-tuple-element.301.q_ref, ...), custom_call_target="tpu_custom_call" | custom-call | flops 1000000000 | bytes 1000000 | tf_op jit(solution)/shard_map/attention_backward/pallas_call | solution.py:414
  589.0 39.1 %plane_sum.1 = (f32[256,512]{1,0:T(8,128)}, f32[256,512]{1,0:T(8,128)}) custom-call(bf16[2048,512]{1,0:T(8,128)(2,1)} %get-tuple-element.299.refs_0_, bf16[2048,512]{1,0:T(8,128)(2,1)} %get-tuple-element.310.refs_1_), custom_call_target="tpu_custom_call" | custom-call | flops 1000000000 | bytes 1000000 | tf_op jit(solution)/shard_map/plane_sum/pallas_call | solution.py:884
  641.8 6.4 multiply_convert_fusion
  649.7 14.4 %outer.1.x_ref = bf16[1024,3200]{1,0:T(8,128)(2,1)} custom-call(s32[1]{0:T(128)} %bitcast.34.mine, bf16[768,1024]{1,0:T(8,128)(2,1)} %get-tuple-element.324.refs_0_.refs_6_, bf16[768,1024]{1,0:T(8,128)(2,1)} %constant_dynamic-update-slice_fusion.refs_1_, bf16[768,1024]{1,0:T(8,128)(2,1)} %copy-done.3, ...), custom_call_target="tpu_custom_call" | custom-call | flops 1000000000 | bytes 1000000 | tf_op jit(solution)/shard_map/outer/pallas_call | solution.py:174
  664.1 44.1 %full_sum.1 = (f32[32,1024]{1,0:T(8,128)}, f32[32,1024]{1,0:T(8,128)}, f32[32,512]{1,0:T(8,128)}, f32[32,512]{1,0:T(8,128)}, f32[32,128]{1,0:T(8,128)}) custom-call(bf16[1024,3200]{1,0:T(8,128)(2,1)} %outer.1.x_ref), custom_call_target="tpu_custom_call" | custom-call | flops 1000000000 | bytes 1000000 | tf_op jit(solution)/shard_map/full_sum/pallas_call | solution.py:957
  (240 shorter events, 96.5 us)
Async XLA Ops:
  7.3 193.4 %all-gather.7.cloned.1.call-start = ((), (), s32[]{:S(2)}) async-start(), calls=%async_computation.7 | async-start | bytes 9437184 | tf_op jit(solution)/shard_map/all_gather | solution.py:1094
  8.0 192.7 %all-gather.9.cloned.1.call-start = ((), (), s32[]{:S(2)}) async-start(), calls=%async_computation.8 | async-start | bytes 9437184 | tf_op jit(solution)/shard_map/all_gather | solution.py:1095
  8.7 197.4 %all-gather.11.cloned.1.call-start = ((), (), s32[]{:S(2)}) async-start(), calls=%async_computation.9 | async-start | bytes 9437184 | tf_op jit(solution)/shard_map/all_gather | solution.py:1096
  10.6 60.4 %all-to-all-start = ((f32[4,8,1,768]{3,1,2,0:T(8,128)}), f32[4,8,1,768]{3,1,2,0:T(8,128)S(1)}, u32[]{:S(2)}, u32[]{:S(2)}) async-start(f32[4,8,1,768]{3,1,2,0:T(8,128)} %fusion.28), calls=%async_computation | async-start | bytes 196608 | tf_op jit(solution)/shard_map/all_to_all | solution.py:1104
  16.9 692.7 %reduce-scatter.6.cloned.1.call-start = ((), (), s32[]{:S(2)}) async-start(), calls=%async_computation.5 | async-start | bytes 9437184 | tf_op jit(solution)/shard_map/reduce_scatter | solution.py:1229
  71.0 54.7 %collective-permute-start = (bf16[768,1024]{1,0:T(8,128)(2,1)S(1)}, bf16[768,1024]{1,0:T(8,128)(2,1)}, u32[]{:S(2)}, u32[]{:S(2)}) collective-permute-start(bf16[768,1024]{1,0:T(8,128)(2,1)S(1)} %bitcast.121), channel_id=1, source_target_pairs={{0,3},{1,0},{2,1},{3,2},{4,7},{5,4},{6,5},{7,6},{8,11},{9,8},{10,9... | collective-permute-start | bytes 4718600 | tf_op jit(solution)/shard_map/ppermute | solution.py:983
  79.4 78.1 %collective-permute-start.1 = (bf16[768,1024]{1,0:T(8,128)(2,1)S(1)}, bf16[768,1024]{1,0:T(8,128)(2,1)}, u32[]{:S(2)}, u32[]{:S(2)}) collective-permute-start(bf16[768,1024]{1,0:T(8,128)(2,1)S(1)} %bitcast.122), channel_id=1, source_target_pairs={{0,1},{1,2},{2,3},{3,0},{4,5},{5,6},{6,7},{7,4},{8,9},{9,10},{10,1... | collective-permute-start | bytes 4718600 | tf_op jit(solution)/shard_map/ppermute | solution.py:983
  125.7 66.1 %collective-permute-start.2 = (bf16[768,1024]{1,0:T(8,128)(2,1)}, bf16[768,1024]{1,0:T(8,128)(2,1)}, u32[]{:S(2)}, u32[]{:S(2)}) collective-permute-start(bf16[768,1024]{1,0:T(8,128)(2,1)} %collective-permute-done.df_ref), channel_id=1, source_target_pairs={{0,3},{1,0},{2,1},{3,2},{4,7},{5,4},{6,5},{7,6},{8,11},{9,8},{10,9... | collective-permute-start | bytes 4718600 | tf_op jit(solution)/shard_map/ppermute | solution.py:983
  191.9 52.0 %collective-permute-start.3 = (bf16[768,1024]{1,0:T(8,128)(2,1)}, bf16[768,1024]{1,0:T(8,128)(2,1)S(1)}, u32[]{:S(2)}, u32[]{:S(2)}) collective-permute-start(bf16[768,1024]{1,0:T(8,128)(2,1)} %get-tuple-element.189.a2_ref.refs_8_), channel_id=1, source_target_pairs={{0,3},{1,0},{2,1},{3,2},{4,7},{5,4},{6,5},{7,6},{8,11},{9,8},{10,9... | collective-permute-start | bytes 4718600 | tf_op jit(solution)/shard_map/ppermute | solution.py:983
  196.0 47.9 %collective-permute-start.4 = (f32[8,1,768]{2,1,0:T(1,128)S(1)}, f32[8,1,768]{2,1,0:T(1,128)S(1)}, u32[]{:S(2)}, u32[]{:S(2)}) collective-permute-start(f32[8,1,768]{2,1,0:T(1,128)S(1)} %bitcast.146), channel_id=1, source_target_pairs={{0,1},{1,2},{2,3},{3,0},{4,5},{5,6},{6,7},{7,4},{8,9},{9,10},{10,1... | collective-permute-start | bytes 73736 | tf_op jit(solution)/shard_map/ppermute | solution.py:983
  196.8 47.2 %collective-permute-start.5 = (f32[8,1,768]{2,1,0:T(1,128)S(1)}, f32[8,1,768]{2,1,0:T(1,128)S(1)}, u32[]{:S(2)}, u32[]{:S(2)}) collective-permute-start(f32[8,1,768]{2,1,0:T(1,128)S(1)} %bitcast.147), channel_id=1, source_target_pairs={{0,2},{1,3},{2,0},{3,1},{4,6},{5,7},{6,4},{7,5},{8,10},{9,11},{10,... | collective-permute-start | bytes 73736 | tf_op jit(solution)/shard_map/ppermute | solution.py:983
  197.7 46.2 %collective-permute-start.6 = (f32[8,1,768]{2,1,0:T(1,128)S(1)}, f32[8,1,768]{2,1,0:T(1,128)S(1)}, u32[]{:S(2)}, u32[]{:S(2)}) collective-permute-start(f32[8,1,768]{2,1,0:T(1,128)S(1)} %bitcast.148), channel_id=1, source_target_pairs={{0,3},{1,0},{2,1},{3,2},{4,7},{5,4},{6,5},{7,6},{8,11},{9,8},{10,9... | collective-permute-start | bytes 73736 | tf_op jit(solution)/shard_map/ppermute | solution.py:983
  244.0 46.4 %collective-permute-start.7 = (bf16[768,1024]{1,0:T(8,128)(2,1)S(1)}, bf16[768,1024]{1,0:T(8,128)(2,1)S(1)}, u32[]{:S(2)}, u32[]{:S(2)}) collective-permute-start(bf16[768,1024]{1,0:T(8,128)(2,1)S(1)} %collective-permute-done.3.a2_ref), channel_id=1, source_target_pairs={{0,3},{1,0},{2,1},{3,2},{4,7},{5,4},{6,5},{7,6},{8,11},{9,8},{10,9... | collective-permute-start | bytes 4718600 | tf_op jit(solution)/shard_map/ppermute | solution.py:983
  290.4 42.3 %collective-permute-start.8 = (bf16[768,1024]{1,0:T(8,128)(2,1)S(1)}, bf16[768,1024]{1,0:T(8,128)(2,1)S(1)}, u32[]{:S(2)}, u32[]{:S(2)}) collective-permute-start(bf16[768,1024]{1,0:T(8,128)(2,1)S(1)} %collective-permute-done.7.a2_ref), channel_id=1, source_target_pairs={{0,3},{1,0},{2,1},{3,2},{4,7},{5,4},{6,5},{7,6},{8,11},{9,8},{10,9... | collective-permute-start | bytes 4718600 | tf_op jit(solution)/shard_map/ppermute | solution.py:983
  333.8 42.1 %collective-permute-start.9 = (bf16[768,1024]{1,0:T(8,128)(2,1)}, bf16[768,1024]{1,0:T(8,128)(2,1)S(1)}, u32[]{:S(2)}, u32[]{:S(2)}) collective-permute-start(bf16[768,1024]{1,0:T(8,128)(2,1)} %get-tuple-element.249), channel_id=1, source_target_pairs={{0,3},{1,0},{2,1},{3,2},{4,7},{5,4},{6,5},{7,6},{8,11},{9,8},{10,9... | collective-permute-start | bytes 4718600 | tf_op jit(solution)/shard_map/ppermute | solution.py:983
  377.8 50.1 %collective-permute-start.10 = (bf16[768,1024]{1,0:T(8,128)(2,1)}, bf16[768,1024]{1,0:T(8,128)(2,1)S(1)}, u32[]{:S(2)}, u32[]{:S(2)}) collective-permute-start(bf16[768,1024]{1,0:T(8,128)(2,1)} %add_convert_fusion.4), channel_id=1, source_target_pairs={{0,3},{1,0},{2,1},{3,2},{4,7},{5,4},{6,5},{7,6},{8,11},{9,8},{10,9... | collective-permute-start | bytes 4718600 | tf_op jit(solution)/shard_map/ppermute | solution.py:983
  383.2 44.7 %collective-permute-start.13 = (f32[8,1,768]{2,1,0:T(1,128)S(1)}, f32[8,1,768]{2,1,0:T(1,128)S(1)}, u32[]{:S(2)}, u32[]{:S(2)}) collective-permute-start(f32[8,1,768]{2,1,0:T(1,128)S(1)} %copy-done.45), channel_id=1, source_target_pairs={{0,1},{1,2},{2,3},{3,0},{4,5},{5,6},{6,7},{7,4},{8,9},{9,10},{10,1... | collective-permute-start | bytes 73736 | tf_op jit(solution)/shard_map/ppermute | solution.py:983
  383.2 44.7 %collective-permute-start.12 = (f32[8,1,768]{2,1,0:T(1,128)S(1)}, f32[8,1,768]{2,1,0:T(1,128)S(1)}, u32[]{:S(2)}, u32[]{:S(2)}) collective-permute-start(f32[8,1,768]{2,1,0:T(1,128)S(1)} %copy-done.46), channel_id=1, source_target_pairs={{0,2},{1,3},{2,0},{3,1},{4,6},{5,7},{6,4},{7,5},{8,10},{9,11},{10,... | collective-permute-start | bytes 73736 | tf_op jit(solution)/shard_map/ppermute | solution.py:983
  386.4 41.5 %collective-permute-start.11 = (f32[8,1,768]{2,1,0:T(1,128)S(1)}, f32[8,1,768]{2,1,0:T(1,128)S(1)}, u32[]{:S(2)}, u32[]{:S(2)}) collective-permute-start(f32[8,1,768]{2,1,0:T(1,128)S(1)} %copy-done.47), channel_id=1, source_target_pairs={{0,3},{1,0},{2,1},{3,2},{4,7},{5,4},{6,5},{7,6},{8,11},{9,8},{10,9... | collective-permute-start | bytes 73736 | tf_op jit(solution)/shard_map/ppermute | solution.py:983
  427.9 284.5 %reduce-scatter.4.cloned.1.call-start = ((), (), s32[]{:S(2)}) async-start(), calls=%async_computation.4 | async-start | bytes 9437184 | tf_op jit(solution)/shard_map/reduce_scatter | solution.py:1229
  428.6 286.8 %reduce-scatter.8.cloned.1.call-start = ((), (), s32[]{:S(2)}) async-start(), calls=%async_computation.6 | async-start | bytes 9437184 | tf_op jit(solution)/shard_map/reduce_scatter | solution.py:1229
  468.9 60.4 %collective-permute-start.15 = (bf16[768,1024]{1,0:T(8,128)(2,1)}, bf16[768,1024]{1,0:T(8,128)(2,1)}, u32[]{:S(2)}, u32[]{:S(2)}) collective-permute-start(bf16[768,1024]{1,0:T(8,128)(2,1)} %get-tuple-element.298), channel_id=1, source_target_pairs={{0,3},{1,0},{2,1},{3,2},{4,7},{5,4},{6,5},{7,6},{8,11},{9,8},{10,9... | collective-permute-start | bytes 4718600 | tf_op jit(solution)/shard_map/ppermute | solution.py:983
  533.2 49.2 %collective-permute-start.16 = (bf16[768,1024]{1,0:T(8,128)(2,1)}, bf16[768,1024]{1,0:T(8,128)(2,1)}, u32[]{:S(2)}, u32[]{:S(2)}) collective-permute-start(bf16[768,1024]{1,0:T(8,128)(2,1)} %add_convert_fusion.2), channel_id=1, source_target_pairs={{0,3},{1,0},{2,1},{3,2},{4,7},{5,4},{6,5},{7,6},{8,11},{9,8},{10,9... | collective-permute-start | bytes 4718600 | tf_op jit(solution)/shard_map/ppermute | solution.py:983
  586.2 44.2 %collective-permute-start.17 = (bf16[768,1024]{1,0:T(8,128)(2,1)}, bf16[768,1024]{1,0:T(8,128)(2,1)}, u32[]{:S(2)}, u32[]{:S(2)}) collective-permute-start(bf16[768,1024]{1,0:T(8,128)(2,1)} %add_convert_fusion.1), channel_id=1, source_target_pairs={{0,3},{1,0},{2,1},{3,2},{4,7},{5,4},{6,5},{7,6},{8,11},{9,8},{10,9... | collective-permute-start | bytes 4718600 | tf_op jit(solution)/shard_map/ppermute | solution.py:983
  (49 other events, 511.6 us)
Sparse Core Ops, SparseCore 0:
  10.0 75.5 all-gather.6
  87.4 62.3 all-gather.8
  151.7 54.3 all-gather.10
  428.1 72.6 reduce-scatter.5
  504.4 71.2 reduce-scatter.3
  579.1 80.3 reduce-scatter.7

commit v12 on v11

--- a/solution.py
+++ b/solution.py
@@ -253,6 +253,33 @@
             total = jnp.sum(e, 1, keepdims=True)
             out = dot(e.astype(bf16), v_scr[:keys, lanes])
             store(start, block_rows, j, out, m, total, CONT_DEV * CLEN + half * block_rows)
+
+
+def finish_keys_kernel(*refs):
+    cos_ref, sin_ref, out_ref = refs[6:]
+    for half in range(2):
+        owned, key, value = refs[half], refs[2 + 2 * half], refs[3 + 2 * half]
+        for c in range(2):
+            lanes = slice(128 * c, 128 * (c + 1))
+            at = 256 * half + 128 * c
+            d_key = jnp.concatenate([owned[:, lanes], key[:, lanes]], 0)
+            d_key = turn_tile(d_key, cos_ref[...], sin_ref[...], -1.0)
+            d_value = jnp.concatenate([owned[:, 256 + 128 * c : 384 + 128 * c], value[:, lanes]], 0)
+            out_ref[:, at : at + 128] = d_key.astype(bf16)
+            out_ref[:, KV_WIDTH + at : KV_WIDTH + at + 128] = d_value.astype(bf16)
+
+
+def finish_keys(owned, ours, cosine, sine):
+    whole = pl.BlockSpec(memory_space=pltpu.VMEM)
+    return pl.pallas_call(
+        finish_keys_kernel,
+        in_specs=[whole] * 8,
+        out_specs=whole,
+        out_shape=jax.ShapeDtypeStruct((cosine.shape[0], 2 * KV_WIDTH), bf16),
+        compiler_params=pltpu.CompilerParams(vmem_limit_bytes=VMEM_LIMIT),
+        cost_estimate=SMALL,
+        name="finish_keys",
+    )(*owned, *ours[0], *ours[1], cosine, sine)
 
 
 def key_specs(pieces, own, half):
@@ -1260,20 +1287,7 @@
     mixture = mixed[0].astype(f32) + carried.astype(f32)
     layer_output = (middle + resid_scale * mixture).astype(bf16)
     d_query = jnp.concatenate(d_query, 1)
-    d_key, d_value = (
-        jnp.concatenate(
-            [
-                jnp.concatenate([owned[half][:, 256 * n : 256 * n + 256], ours[half][n]], 0)
-                for half in range(2)
-            ],
-            1,
-        )
-        for n in range(2)
-    )
-    grad_key_low = turn(d_key, jnp.tile(cosine, (1, 4)), jnp.tile(sine, (1, 4)), -1.0).astype(
-        bf16
-    )
-    grad_kv = jnp.concatenate([grad_key_low, d_value.astype(bf16)], 1)
+    grad_kv = finish_keys(owned, ours, cosine, sine)
     grad_normed_one = dot_nt(d_query, qkv_full[:, :1024]) + dot_nt(grad_kv, qkv_full[:, 1024:])
     grad_input_norm, first_gain_grad = norm_backward(
         inputs, inverse_one, first_gain, grad_normed_one

time: 736 us -> 727 us (0.988)
  Pallas kernels: 571 us -> 589 us
  starting transfers between devices: 42 us -> 24.7 us
    ppermute x18, starting transfers between devices: 35.5 us -> 18.2 us  [shift(): return lax.ppermute(x, 'wt', [(i, (i + distance) % n) for i in range(n)])]
    pallas_call x4, Pallas kernels: 154 us -> 170 us  [expert_pass(): pl.pallas_call(functools.partial(expert_kernel, sizes=sizes), grid_spec=p...]
  transfers between devices with their start and end apart: 25 -> 25, of which waited for: 2 -> 2; matrix products, arithmetic and copies ran while one was open for 9% -> 9% of each run, Pallas kernels for 78% -> 82%
where the time goes in v12:
time: 727 us; the launch traced here: 720 us
  Pallas kernels  589 us (81%)
  other arithmetic  35 us (5%)
  local copies, waits for them, and re-layouts  26.7 us (4%)
  starting transfers between devices  24.7 us (3%)
  between operations  17.7 us (2%)
  waiting for transfers between devices  13.6 us (2%)
  matrix products  13.3 us (2%)
    pallas_call x4, Pallas kernels, expert_pass(): pl.pallas_call(functools.partial(expert_kernel, sizes=sizes), grid_spec=p...  170 us
    pallas_call x2, Pallas kernels, attention_backward(): pl.pallas_call(functools.partial(attention_backward_kernel, block_rows=bl...  97.6 us
    pallas_call x2, Pallas kernels, attention_forward(): pl.pallas_call(functools.partial(attention_forward_kernel, block_rows=blo...  53.6 us
    pallas_call x1, Pallas kernels, packed_gather(): pl.pallas_call(packed_gather_kernel, in_specs=[ANY], out_specs=ANY, out_s...  53 us
    pallas_call x1, Pallas kernels, full_sum(): pl.pallas_call(functools.partial(full_sum_kernel, widths=widths), in_spec...  45.7 us
    pallas_call x1, Pallas kernels, up_weight_grads(): pl.pallas_call(functools.partial(up_grad_kernel, sources=len(rows)), grid...  40.6 us
    pallas_call x1, Pallas kernels, plane_gather(): pl.pallas_call(plane_gather_kernel, in_specs=[ANY], out_specs=ANY, out_sh...  34.6 us
    pallas_call x1, Pallas kernels, plane_sum(): pl.pallas_call(functools.partial(plane_sum_kernel, sets=sets), in_specs=[...  34 us
  transfers between devices with their start and end apart: 25, of which 2 were waited for; matrix products, arithmetic and copies ran while one was open for 9% of the time, Pallas kernels for 82%

profile of v12, /device:TPU:0, one launch (start us, length us, event | category | flops | bytes accessed | tf_op | source)
XLA Modules:
  0.0 720.3 jit_solution(17632344814035837268)
XLA Ops:
  10.6 6.3 all-to-all-start
  17.9 53.0 %packed_gather.1.refs_0_ = bf16[1024,3200]{1,0:T(8,128)(2,1)} custom-call(bf16[32,3200]{1,0:T(8,128)(2,1)} %concatenate.45.x_ref), custom_call_target="tpu_custom_call" | custom-call | flops 1000000000 | bytes 1000000 | tf_op jit(solution)/shard_map/packed_gather/pallas_call | solution.py:812
  82.0 9.1 %project.1 = (bf16[768,1024]{1,0:T(8,128)(2,1)}, bf16[768,1024]{1,0:T(8,128)(2,1)}, bf16[768,1024]{1,0:T(8,128)(2,1)}, bf16[1024,2048]{1,0:T(8,128)(2,1)}, bf16[...) custom-call(s32[32]{0:T(128)} %add.197.places, bf16[768,1024]{1,0:T(8,128)(2,1)} %bitcast.107, ...), custom_call_target="tpu_custom_call" | custom-call | flops 1000000000 | bytes 1000000 | tf_op jit(solution)/shard_map/project/pallas_call | solution.py:96
  91.1 34.6 %plane_gather.1.refs_0_.refs_1_ = bf16[2048,1024]{1,0:T(8,128)(2,1)} custom-call(bf16[768,1024]{1,0:T(8,128)(2,1)} %get-tuple-element.174.x_ref), custom_call_target="tpu_custom_call" | custom-call | flops 1000000000 | bytes 1000000 | tf_op jit(solution)/shard_map/plane_gather/pallas_call | solution.py:757
  130.9 26.7 %attention_forward.2 = (bf16[768,512]{1,0:T(8,128)(2,1)}, f32[2,4,768]{2,1,0:T(4,128)}) custom-call(s32[16]{0:T(128)} %reshape.335.places, s32[4]{0:T(128)} %get-tuple-element.373.starts, bf16[768,1024]{1,0:T(8,128)(2,1)} %get-tuple-element.301.q_ref, bf16[2048,1024]{1,0:T(8,128)(2,1)} %plane_gather.1.refs_0_.refs_1_, ...), custom_call_target="tpu_custom_call" | custom-call | flops 1000000000 | bytes 1000000 | tf_op jit(solution)/shard_map/attention_forward/pallas_call | solution.py:296
  157.6 26.9 %attention_forward.3 = (bf16[768,512]{1,0:T(8,128)(2,1)}, f32[2,4,768]{2,1,0:T(4,128)}) custom-call(s32[16]{0:T(128)} %reshape.335.places, s32[4]{0:T(128)} %get-tuple-element.373.starts, bf16[768,1024]{1,0:T(8,128)(2,1)} %get-tuple-element.301.q_ref, bf16[2048,1024]{1,0:T(8,128)(2,1)} %plane_gather.1.refs_0_.refs_1_, ...), custom_call_target="tpu_custom_call" | custom-call | flops 1000000000 | bytes 1000000 | tf_op jit(solution)/shard_map/attention_forward/pallas_call | solution.py:296
  184.5 7.4 %to_gates.1 = (f32[768,1024]{1,0:T(8,128)}, bf16[768,1024]{1,0:T(8,128)(2,1)}, f32[768,1]{1,0:T(8,128)}, f32[32,768]{1,0:T(8,128)}) custom-call(bf16[768,512]{1,0:T(8,128)(2,1)} %get-tuple-element.179.a_ref.o_ref.refs_3_, bf16[768,512]{1,0:T(8,128)(2,1)} %get-tuple-element.181.b_ref.o_ref.refs_5_, bf16[768,1024]{1,0:T(8,128)(2,1)} %bitcast.108, ...), custom_call_target="tpu_custom_call" | custom-call | flops 1000000000 | bytes 1000000 | tf_op jit(solution)/shard_map/to_gates/pallas_call | solution.py:137
  200.7 5.4 all-gather.11.cloned.1.call-done
  206.1 43.6 %expert_pass.4 = (bf16[768,1024]{1,0:T(8,128)(2,1)}, bf16[768,1024]{1,0:T(8,128)(2,1)}, f32[8,1,768]{2,1,0:T(1,128)}, bf16[8,336,1024]{2,1,0:T(8,128)(2,1)}, bf1...) custom-call(s32[8]{0:T(128)} %get-tuple-element.377.counts, ...), custom_call_target="tpu_custom_call" | custom-call | flops 1000000000 | bytes 1000000 | tf_op jit(solution)/shard_map/expert_pass/pallas_call | solution.py:567
  251.2 43.1 %expert_pass.5 = (bf16[768,1024]{1,0:T(8,128)(2,1)}, bf16[768,1024]{1,0:T(8,128)(2,1)}, f32[8,1,768]{2,1,0:T(1,128)}, bf16[8,336,1024]{2,1,0:T(8,128)(2,1)}, bf1...) custom-call(s32[8]{0:T(128)} %get-tuple-element.374.counts, ...), custom_call_target="tpu_custom_call" | custom-call | flops 1000000000 | bytes 1000000 | tf_op jit(solution)/shard_map/expert_pass/pallas_call | solution.py:567
  295.5 40.9 %expert_pass.6 = (bf16[768,1024]{1,0:T(8,128)(2,1)}, bf16[768,1024]{1,0:T(8,128)(2,1)}, f32[8,1,768]{2,1,0:T(1,128)}, bf16[8,336,1024]{2,1,0:T(8,128)(2,1)}, bf1...) custom-call(s32[8]{0:T(128)} %get-tuple-element.375.counts, ...), custom_call_target="tpu_custom_call" | custom-call | flops 1000000000 | bytes 1000000 | tf_op jit(solution)/shard_map/expert_pass/pallas_call | solution.py:567
  337.5 42.9 %expert_pass.7 = (bf16[768,1024]{1,0:T(8,128)(2,1)}, bf16[768,1024]{1,0:T(8,128)(2,1)}, f32[8,1,768]{2,1,0:T(1,128)}, bf16[8,336,1024]{2,1,0:T(8,128)(2,1)}, bf1...) custom-call(s32[8]{0:T(128)} %get-tuple-element.376.counts, ...), custom_call_target="tpu_custom_call" | custom-call | flops 1000000000 | bytes 1000000 | tf_op jit(solution)/shard_map/expert_pass/pallas_call | solution.py:567
  387.2 40.6 %up_weight_grads.1 = (bf16[8,8,128,512]{3,2,1,0:T(8,128)(2,1)}, bf16[8,8,128,512]{3,2,1,0:T(8,128)(2,1)}) custom-call(bf16[8,336,1024]{2,1,0:T(8,128)(2,1)} %get-tuple-element.251.refs_0_, bf16[8,336,512]{2,1,0:T(8,128)(2,1)} %get-tuple-element.252.refs_1_, bf16[8,336,512]{2,1,0:T(8,128)(2,1)} %get-tuple-element.253.refs_2_, ...), custom_call_target="tpu_custom_call" | custom-call | flops 1000000000 | bytes 1000000 | tf_op jit(solution)/shard_map/up_weight_grads/pallas_call | solution.py:626
  433.5 24.5 %down_weight_grads.1 = bf16[8,8,512,128]{3,2,1,0:T(8,128)(2,1)} custom-call(bf16[8,336,512]{2,1,0:T(8,128)(2,1)} %get-tuple-element.278.refs_0_, bf16[8,336,1024]{2,1,0:T(8,128)(2,1)} %get-tuple-element.279.refs_1_, bf16[8,336,512]{2,1,0:T(8,128)(2,1)} %get-tuple-element.281.refs_2_, bf16[8,336,1024]{2,1,0:T(8,128)(2,1)} %get-tuple-element.282.refs_3_, ...), custom_call_target="tpu_custom_call" | custom-call | flops 1000000000 | bytes 1000000 | tf_op jit(solution)/shard_map/down_weight_grads/pallas_call | solution.py:641
  458.0 5.5 collective-permute-done.14
  476.5 48.5 %attention_backward.2 = (bf16[768,512]{1,0:T(8,128)(2,1)}, bf16[2048,512]{1,0:T(8,128)(2,1)}, f32[512,256]{1,0:T(8,128)}, f32[512,256]{1,0:T(8,128)}) custom-call(s32[16]{0:T(128)} %reshape.335.places, s32[4]{0:T(128)} %get-tuple-element.373.starts, bf16[768,1024]{1,0:T(8,128)(2,1)} %get-tuple-element.301.q_ref, ...), custom_call_target="tpu_custom_call" | custom-call | flops 1000000000 | bytes 1000000 | tf_op jit(solution)/shard_map/attention_backward/pallas_call | solution.py:441
  525.0 4.0 add_convert_fusion.2
  529.1 49.1 %attention_backward.3 = (bf16[768,512]{1,0:T(8,128)(2,1)}, bf16[2048,512]{1,0:T(8,128)(2,1)}, f32[512,256]{1,0:T(8,128)}, f32[512,256]{1,0:T(8,128)}) custom-call(s32[16]{0:T(128)} %reshape.335.places, s32[4]{0:T(128)} %get-tuple-element.373.starts, bf16[768,1024]{1,0:T(8,128)(2,1)} %get-tuple-element.301.q_ref, ...), custom_call_target="tpu_custom_call" | custom-call | flops 1000000000 | bytes 1000000 | tf_op jit(solution)/shard_map/attention_backward/pallas_call | solution.py:441
  584.3 34.0 %plane_sum.1 = (f32[256,512]{1,0:T(8,128)}, f32[256,512]{1,0:T(8,128)}) custom-call(bf16[2048,512]{1,0:T(8,128)(2,1)} %get-tuple-element.299.refs_0_, bf16[2048,512]{1,0:T(8,128)(2,1)} %get-tuple-element.310.refs_1_), custom_call_target="tpu_custom_call" | custom-call | flops 1000000000 | bytes 1000000 | tf_op jit(solution)/shard_map/plane_sum/pallas_call | solution.py:911
  620.5 4.5 finish_keys.1.refs_7_
  625.0 4.0 fusion.11
  632.3 6.3 multiply_convert_fusion
  640.1 14.3 %outer.1.x_ref = bf16[1024,3200]{1,0:T(8,128)(2,1)} custom-call(s32[1]{0:T(128)} %bitcast.34.mine, bf16[768,1024]{1,0:T(8,128)(2,1)} %get-tuple-element.324.refs_0_.refs_6_, bf16[768,1024]{1,0:T(8,128)(2,1)} %constant_dynamic-update-slice_fusion.refs_1_, bf16[768,1024]{1,0:T(8,128)(2,1)} %copy-done.3, ...), custom_call_target="tpu_custom_call" | custom-call | flops 1000000000 | bytes 1000000 | tf_op jit(solution)/shard_map/outer/pallas_call | solution.py:174
  654.4 45.7 %full_sum.1 = (f32[32,1024]{1,0:T(8,128)}, f32[32,1024]{1,0:T(8,128)}, f32[32,512]{1,0:T(8,128)}, f32[32,512]{1,0:T(8,128)}, f32[32,128]{1,0:T(8,128)}) custom-call(bf16[1024,3200]{1,0:T(8,128)(2,1)} %outer.1.x_ref), custom_call_target="tpu_custom_call" | custom-call | flops 1000000000 | bytes 1000000 | tf_op jit(solution)/shard_map/full_sum/pallas_call | solution.py:984
  (213 shorter events, 81.6 us)
Async XLA Ops:
  7.3 193.4 %all-gather.7.cloned.1.call-start = ((), (), s32[]{:S(2)}) async-start(), calls=%async_computation.7 | async-start | bytes 9437184 | tf_op jit(solution)/shard_map/all_gather | solution.py:1121
  8.0 192.7 %all-gather.9.cloned.1.call-start = ((), (), s32[]{:S(2)}) async-start(), calls=%async_computation.8 | async-start | bytes 9437184 | tf_op jit(solution)/shard_map/all_gather | solution.py:1122
  8.7 197.4 %all-gather.11.cloned.1.call-start = ((), (), s32[]{:S(2)}) async-start(), calls=%async_computation.9 | async-start | bytes 9437184 | tf_op jit(solution)/shard_map/all_gather | solution.py:1123
  10.6 60.4 %all-to-all-start = ((f32[4,8,1,768]{3,1,2,0:T(8,128)}), f32[4,8,1,768]{3,1,2,0:T(8,128)S(1)}, u32[]{:S(2)}, u32[]{:S(2)}) async-start(f32[4,8,1,768]{3,1,2,0:T(8,128)} %fusion.21), calls=%async_computation | async-start | bytes 196608 | tf_op jit(solution)/shard_map/all_to_all | solution.py:1131
  16.9 684.7 %reduce-scatter.6.cloned.1.call-start = ((), (), s32[]{:S(2)}) async-start(), calls=%async_computation.5 | async-start | bytes 9437184 | tf_op jit(solution)/shard_map/reduce_scatter | solution.py:1256
  71.0 54.6 %collective-permute-start = (bf16[768,1024]{1,0:T(8,128)(2,1)S(1)}, bf16[768,1024]{1,0:T(8,128)(2,1)}, u32[]{:S(2)}, u32[]{:S(2)}) collective-permute-start(bf16[768,1024]{1,0:T(8,128)(2,1)S(1)} %bitcast.110), channel_id=1, source_target_pairs={{0,3},{1,0},{2,1},{3,2},{4,7},{5,4},{6,5},{7,6},{8,11},{9,8},{10,9... | collective-permute-start | bytes 4718600 | tf_op jit(solution)/shard_map/ppermute | solution.py:1010
  79.4 78.2 %collective-permute-start.1 = (bf16[768,1024]{1,0:T(8,128)(2,1)S(1)}, bf16[768,1024]{1,0:T(8,128)(2,1)}, u32[]{:S(2)}, u32[]{:S(2)}) collective-permute-start(bf16[768,1024]{1,0:T(8,128)(2,1)S(1)} %bitcast.111), channel_id=1, source_target_pairs={{0,1},{1,2},{2,3},{3,0},{4,5},{5,6},{6,7},{7,4},{8,9},{9,10},{10,1... | collective-permute-start | bytes 4718600 | tf_op jit(solution)/shard_map/ppermute | solution.py:1010
  125.7 66.2 %collective-permute-start.2 = (bf16[768,1024]{1,0:T(8,128)(2,1)}, bf16[768,1024]{1,0:T(8,128)(2,1)}, u32[]{:S(2)}, u32[]{:S(2)}) collective-permute-start(bf16[768,1024]{1,0:T(8,128)(2,1)} %collective-permute-done.df_ref), channel_id=1, source_target_pairs={{0,3},{1,0},{2,1},{3,2},{4,7},{5,4},{6,5},{7,6},{8,11},{9,8},{10,9... | collective-permute-start | bytes 4718600 | tf_op jit(solution)/shard_map/ppermute | solution.py:1010
  191.9 57.8 %collective-permute-start.3 = (bf16[768,1024]{1,0:T(8,128)(2,1)}, bf16[768,1024]{1,0:T(8,128)(2,1)S(1)}, u32[]{:S(2)}, u32[]{:S(2)}) collective-permute-start(bf16[768,1024]{1,0:T(8,128)(2,1)} %get-tuple-element.189.a2_ref.refs_8_), channel_id=1, source_target_pairs={{0,3},{1,0},{2,1},{3,2},{4,7},{5,4},{6,5},{7,6},{8,11},{9,8},{10,9... | collective-permute-start | bytes 4718600 | tf_op jit(solution)/shard_map/ppermute | solution.py:1010
  196.0 53.7 %collective-permute-start.4 = (f32[8,1,768]{2,1,0:T(1,128)S(1)}, f32[8,1,768]{2,1,0:T(1,128)S(1)}, u32[]{:S(2)}, u32[]{:S(2)}) collective-permute-start(f32[8,1,768]{2,1,0:T(1,128)S(1)} %bitcast.133), channel_id=1, source_target_pairs={{0,1},{1,2},{2,3},{3,0},{4,5},{5,6},{6,7},{7,4},{8,9},{9,10},{10,1... | collective-permute-start | bytes 73736 | tf_op jit(solution)/shard_map/ppermute | solution.py:1010
  196.8 52.9 %collective-permute-start.5 = (f32[8,1,768]{2,1,0:T(1,128)S(1)}, f32[8,1,768]{2,1,0:T(1,128)S(1)}, u32[]{:S(2)}, u32[]{:S(2)}) collective-permute-start(f32[8,1,768]{2,1,0:T(1,128)S(1)} %bitcast.134), channel_id=1, source_target_pairs={{0,2},{1,3},{2,0},{3,1},{4,6},{5,7},{6,4},{7,5},{8,10},{9,11},{10,... | collective-permute-start | bytes 73736 | tf_op jit(solution)/shard_map/ppermute | solution.py:1010
  197.7 52.0 %collective-permute-start.6 = (f32[8,1,768]{2,1,0:T(1,128)S(1)}, f32[8,1,768]{2,1,0:T(1,128)S(1)}, u32[]{:S(2)}, u32[]{:S(2)}) collective-permute-start(f32[8,1,768]{2,1,0:T(1,128)S(1)} %bitcast.135), channel_id=1, source_target_pairs={{0,3},{1,0},{2,1},{3,2},{4,7},{5,4},{6,5},{7,6},{8,11},{9,8},{10,9... | collective-permute-start | bytes 73736 | tf_op jit(solution)/shard_map/ppermute | solution.py:1010
  249.7 44.6 %collective-permute-start.7 = (bf16[768,1024]{1,0:T(8,128)(2,1)S(1)}, bf16[768,1024]{1,0:T(8,128)(2,1)S(1)}, u32[]{:S(2)}, u32[]{:S(2)}) collective-permute-start(bf16[768,1024]{1,0:T(8,128)(2,1)S(1)} %collective-permute-done.3.a2_ref), channel_id=1, source_target_pairs={{0,3},{1,0},{2,1},{3,2},{4,7},{5,4},{6,5},{7,6},{8,11},{9,8},{10,9... | collective-permute-start | bytes 4718600 | tf_op jit(solution)/shard_map/ppermute | solution.py:1010
  294.4 42.0 %collective-permute-start.8 = (bf16[768,1024]{1,0:T(8,128)(2,1)S(1)}, bf16[768,1024]{1,0:T(8,128)(2,1)S(1)}, u32[]{:S(2)}, u32[]{:S(2)}) collective-permute-start(bf16[768,1024]{1,0:T(8,128)(2,1)S(1)} %collective-permute-done.7.a2_ref), channel_id=1, source_target_pairs={{0,3},{1,0},{2,1},{3,2},{4,7},{5,4},{6,5},{7,6},{8,11},{9,8},{10,9... | collective-permute-start | bytes 4718600 | tf_op jit(solution)/shard_map/ppermute | solution.py:1010
  336.4 44.1 %collective-permute-start.9 = (bf16[768,1024]{1,0:T(8,128)(2,1)}, bf16[768,1024]{1,0:T(8,128)(2,1)S(1)}, u32[]{:S(2)}, u32[]{:S(2)}) collective-permute-start(bf16[768,1024]{1,0:T(8,128)(2,1)} %get-tuple-element.249), channel_id=1, source_target_pairs={{0,3},{1,0},{2,1},{3,2},{4,7},{5,4},{6,5},{7,6},{8,11},{9,8},{10,9... | collective-permute-start | bytes 4718600 | tf_op jit(solution)/shard_map/ppermute | solution.py:1010
  382.3 45.5 %collective-permute-start.10 = (bf16[768,1024]{1,0:T(8,128)(2,1)}, bf16[768,1024]{1,0:T(8,128)(2,1)S(1)}, u32[]{:S(2)}, u32[]{:S(2)}) collective-permute-start(bf16[768,1024]{1,0:T(8,128)(2,1)} %add_convert_fusion.4), channel_id=1, source_target_pairs={{0,3},{1,0},{2,1},{3,2},{4,7},{5,4},{6,5},{7,6},{8,11},{9,8},{10,9... | collective-permute-start | bytes 4718600 | tf_op jit(solution)/shard_map/ppermute | solution.py:1010
  382.3 45.4 %collective-permute-start.13 = (f32[8,1,768]{2,1,0:T(1,128)S(1)}, f32[8,1,768]{2,1,0:T(1,128)S(1)}, u32[]{:S(2)}, u32[]{:S(2)}) collective-permute-start(f32[8,1,768]{2,1,0:T(1,128)S(1)} %copy-done.38), channel_id=1, source_target_pairs={{0,1},{1,2},{2,3},{3,0},{4,5},{5,6},{6,7},{7,4},{8,9},{9,10},{10,1... | collective-permute-start | bytes 73736 | tf_op jit(solution)/shard_map/ppermute | solution.py:1010
  384.3 43.4 %collective-permute-start.12 = (f32[8,1,768]{2,1,0:T(1,128)S(1)}, f32[8,1,768]{2,1,0:T(1,128)S(1)}, u32[]{:S(2)}, u32[]{:S(2)}) collective-permute-start(f32[8,1,768]{2,1,0:T(1,128)S(1)} %copy-done.39), channel_id=1, source_target_pairs={{0,2},{1,3},{2,0},{3,1},{4,6},{5,7},{6,4},{7,5},{8,10},{9,11},{10,... | collective-permute-start | bytes 73736 | tf_op jit(solution)/shard_map/ppermute | solution.py:1010
  384.4 43.4 %collective-permute-start.11 = (f32[8,1,768]{2,1,0:T(1,128)S(1)}, f32[8,1,768]{2,1,0:T(1,128)S(1)}, u32[]{:S(2)}, u32[]{:S(2)}) collective-permute-start(f32[8,1,768]{2,1,0:T(1,128)S(1)} %copy-done.40), channel_id=1, source_target_pairs={{0,3},{1,0},{2,1},{3,2},{4,7},{5,4},{6,5},{7,6},{8,11},{9,8},{10,9... | collective-permute-start | bytes 73736 | tf_op jit(solution)/shard_map/ppermute | solution.py:1010
  427.8 276.6 %reduce-scatter.4.cloned.1.call-start = ((), (), s32[]{:S(2)}) async-start(), calls=%async_computation.4 | async-start | bytes 9437184 | tf_op jit(solution)/shard_map/reduce_scatter | solution.py:1256
  428.5 278.9 %reduce-scatter.8.cloned.1.call-start = ((), (), s32[]{:S(2)}) async-start(), calls=%async_computation.6 | async-start | bytes 9437184 | tf_op jit(solution)/shard_map/reduce_scatter | solution.py:1256
  465.5 59.5 %collective-permute-start.15 = (bf16[768,1024]{1,0:T(8,128)(2,1)}, bf16[768,1024]{1,0:T(8,128)(2,1)}, u32[]{:S(2)}, u32[]{:S(2)}) collective-permute-start(bf16[768,1024]{1,0:T(8,128)(2,1)} %get-tuple-element.298), channel_id=1, source_target_pairs={{0,3},{1,0},{2,1},{3,2},{4,7},{5,4},{6,5},{7,6},{8,11},{9,8},{10,9... | collective-permute-start | bytes 4718600 | tf_op jit(solution)/shard_map/ppermute | solution.py:1010
  529.0 49.2 %collective-permute-start.16 = (bf16[768,1024]{1,0:T(8,128)(2,1)}, bf16[768,1024]{1,0:T(8,128)(2,1)}, u32[]{:S(2)}, u32[]{:S(2)}) collective-permute-start(bf16[768,1024]{1,0:T(8,128)(2,1)} %add_convert_fusion.2), channel_id=1, source_target_pairs={{0,3},{1,0},{2,1},{3,2},{4,7},{5,4},{6,5},{7,6},{8,11},{9,8},{10,9... | collective-permute-start | bytes 4718600 | tf_op jit(solution)/shard_map/ppermute | solution.py:1010
  582.0 38.5 %collective-permute-start.17 = (bf16[768,1024]{1,0:T(8,128)(2,1)}, bf16[768,1024]{1,0:T(8,128)(2,1)}, u32[]{:S(2)}, u32[]{:S(2)}) collective-permute-start(bf16[768,1024]{1,0:T(8,128)(2,1)} %add_convert_fusion.1), channel_id=1, source_target_pairs={{0,3},{1,0},{2,1},{3,2},{4,7},{5,4},{6,5},{7,6},{8,11},{9,8},{10,9... | collective-permute-start | bytes 4718600 | tf_op jit(solution)/shard_map/ppermute | solution.py:1010
  (42 other events, 484.3 us)
Sparse Core Ops, SparseCore 0:
  10.0 75.5 all-gather.6
  87.4 62.3 all-gather.8
  151.7 54.3 all-gather.10
  427.9 68.5 reduce-scatter.5
  500.3 71.2 reduce-scatter.3
  574.9 78.1 reduce-scatter.7
